TPU v7x, 128 devices: a whole 4x4x4 slice. The times are simulated.
128 devices in a mesh: px: 8 (over x_hi, y), py: 16 (over z, x_lo, core).
Axes of the slice: x: 4 (x_hi: 2, x_lo: 2; x = x_hi * 2 + x_lo), y: 4, z: 4, core: 2. Of those that a mesh axis runs over, the one named last changes fastest.
Arguments:
- tokens: bfloat16 [128, 128, 6144], P('px', 'py'), may hold values from -6 to 6
- conv_weight: float32 [27, 192], replicated, may hold values from -1.2 to 1.2
- inner_weight: bfloat16 [2, 2, 96, 96], replicated, may hold values from -0.4375 to 0.4375
- outer_weight: bfloat16 [2, 2, 96, 96], replicated, may hold values from -0.625 to 0.625
Outputs:
- mixed: bfloat16 [128, 128, 6144], P('px', 'py')
All inputs are finite; a program needn't handle non-finite values.
Results may differ from a plain program's by a relative error of at most 0.0095.
Values may be sent and summed in bfloat16 or wider, within the bound.
No kernel may reach another device: no remote copies, remote signals or barrier semaphores. Data moves between devices by JAX's collectives and lax.ppermute only.
A program may use at most 64 MiB of HBM per device.

v0:
```python
import math

import jax
import jax.numpy as jnp
from jax import lax
from jax.sharding import PartitionSpec as P

shrink_level = 0.2


def extended(array, sides, width):
    for axis, dim in sides:
        peers, length = (lax.axis_size(axis), array.shape[dim])
        up = [(i, (i + 1) % peers) for i in range(peers - 1)]
        down = [(j, i) for i, j in up]
        last = lax.slice_in_dim(array, length - width, length, axis=dim)
        first = lax.slice_in_dim(array, 0, width, axis=dim)
        before = lax.ppermute(last, axis, up)
        after = lax.ppermute(first, axis, down)
        array = jnp.concatenate([before, array, after], axis=dim)
    return array


def wave_tables(length, modes, weights):
    grid = jnp.arange(length, dtype=jnp.int32)
    product = modes[:, None] * grid[None, :] % length
    angle = product.astype(jnp.float32) * (2.0 * math.pi / length)
    factor = weights[:, None] / math.sqrt(length)
    return (
        (jnp.cos(angle) * factor).astype(jnp.bfloat16),
        (jnp.sin(angle) * factor).astype(jnp.bfloat16),
    )


def depth_weights(count):
    return jnp.where(jnp.arange(count, dtype=jnp.int32) == 0, 1.0, 2.0).astype(jnp.float32)


def convolve(padded, weight):
    size_x = padded.shape[0] - 2
    size_y = padded.shape[1] - 2
    depth = padded.shape[2]
    padded = jnp.pad(padded, ((0, 0), (0, 0), (1, 1), (0, 0))).astype(jnp.float32)
    total = jnp.zeros((size_x, size_y, depth, padded.shape[3]), jnp.float32)
    for shift_a in range(3):
        for shift_b in range(3):
            for shift_e in range(3):
                window = padded[
                    shift_a : shift_a + size_x,
                    shift_b : shift_b + size_y,
                    shift_e : shift_e + depth,
                ]
                total = total + window * weight[shift_a * 9 + shift_b * 3 + shift_e]
    return total.astype(jnp.bfloat16)


def ein(form, left, right):
    return jnp.einsum(form, left, right, preferred_element_type=jnp.float32)


def filter_spectrum(spec_r, spec_i, inner_weight, outer_weight):
    lead = spec_r.shape[:3]
    blocks = inner_weight.shape[1]
    block_size = inner_weight.shape[2]
    block_r = spec_r.reshape(lead + (blocks, block_size))
    block_i = spec_i.reshape(lead + (blocks, block_size))
    form = "pqkbc,bcd->pqkbd"
    hidden_r = jnp.tanh(
        ein(form, block_r, inner_weight[0]) - ein(form, block_i, inner_weight[1])
    ).astype(jnp.bfloat16)
    hidden_i = jnp.tanh(
        ein(form, block_r, inner_weight[1]) + ein(form, block_i, inner_weight[0])
    ).astype(jnp.bfloat16)
    out_r = ein(form, hidden_r, outer_weight[0]) - ein(form, hidden_i, outer_weight[1])
    out_i = ein(form, hidden_r, outer_weight[1]) + ein(form, hidden_i, outer_weight[0])
    shrunk_r = out_r - jnp.clip(out_r, -shrink_level, shrink_level)
    shrunk_i = out_i - jnp.clip(out_i, -shrink_level, shrink_level)
    return (
        shrunk_r.reshape(lead + (blocks * block_size,)),
        shrunk_i.reshape(lead + (blocks * block_size,)),
    )


def body(tokens, conv_weight, inner_weight, outer_weight):
    local_x, local_y, merged = tokens.shape
    channels = conv_weight.shape[1]
    depth = merged // channels
    width_x = local_x * lax.axis_size("px")
    width_y = local_y * lax.axis_size("py")
    modes_z = depth // 2
    padded = extended(tokens, (("px", 0), ("py", 1)), 1)
    padded = padded.reshape(local_x + 2, local_y + 2, depth, channels)
    field = convolve(padded, conv_weight)
    freq_z = jnp.arange(modes_z, dtype=jnp.int32)
    cos_z, sin_z = wave_tables(depth, freq_z, jnp.ones((modes_z,), jnp.float32))
    real_z = ein("xyzc,kz->xykc", field, cos_z).astype(jnp.bfloat16)
    imag_z = (-ein("xyzc,kz->xykc", field, sin_z)).astype(jnp.bfloat16)
    real_z, imag_z = (
        lax.all_to_all(real_z, "py", split_axis=2, concat_axis=1, tiled=True),
        lax.all_to_all(imag_z, "py", split_axis=2, concat_axis=1, tiled=True),
    )
    modes_y = jnp.arange(width_y, dtype=jnp.int32)
    modes_x = jnp.arange(width_x, dtype=jnp.int32)
    cos_y, sin_y = wave_tables(width_y, modes_y, jnp.ones((modes_y.shape[0],), jnp.float32))
    cos_x, sin_x = wave_tables(width_x, modes_x, jnp.ones((modes_x.shape[0],), jnp.float32))
    real_y = (ein("xykc,qy->xqkc", real_z, cos_y) + ein("xykc,qy->xqkc", imag_z, sin_y)).astype(
        jnp.bfloat16
    )
    imag_y = (ein("xykc,qy->xqkc", imag_z, cos_y) - ein("xykc,qy->xqkc", real_z, sin_y)).astype(
        jnp.bfloat16
    )
    real_y, imag_y = (
        lax.all_to_all(real_y, "px", split_axis=1, concat_axis=0, tiled=True),
        lax.all_to_all(imag_y, "px", split_axis=1, concat_axis=0, tiled=True),
    )
    spec_r = (ein("xqkc,px->pqkc", real_y, cos_x) + ein("xqkc,px->pqkc", imag_y, sin_x)).astype(
        jnp.bfloat16
    )
    spec_i = (ein("xqkc,px->pqkc", imag_y, cos_x) - ein("xqkc,px->pqkc", real_y, sin_x)).astype(
        jnp.bfloat16
    )
    shrunk_r, shrunk_i = filter_spectrum(spec_r, spec_i, inner_weight, outer_weight)
    rows_here = spec_r.shape[1]
    quarter_x = width_x // 4
    quarter_y = width_y // 4
    index_p = jnp.arange(spec_r.shape[0], dtype=jnp.int32)
    index_q = lax.axis_index("px") * rows_here + jnp.arange(rows_here, dtype=jnp.int32)
    keep_p = (index_p < quarter_x) | (index_p >= width_x - quarter_x)
    keep_q = (index_q < quarter_y) | (index_q >= width_y - quarter_y)
    keep = (keep_p[:, None] & keep_q[None, :])[:, :, None, None]
    shrunk_r = jnp.where(keep, shrunk_r, 0.0)
    shrunk_i = jnp.where(keep, shrunk_i, 0.0)
    filt_r = shrunk_r.astype(jnp.bfloat16)
    filt_i = shrunk_i.astype(jnp.bfloat16)
    back_xr = (ein("pqkc,px->xqkc", filt_r, cos_x) - ein("pqkc,px->xqkc", filt_i, sin_x)).astype(
        jnp.bfloat16
    )
    back_xi = (ein("pqkc,px->xqkc", filt_i, cos_x) + ein("pqkc,px->xqkc", filt_r, sin_x)).astype(
        jnp.bfloat16
    )
    back_xr, back_xi = (
        lax.all_to_all(back_xr, "px", split_axis=0, concat_axis=1, tiled=True),
        lax.all_to_all(back_xi, "px", split_axis=0, concat_axis=1, tiled=True),
    )
    back_yr = (ein("xqkc,qy->xykc", back_xr, cos_y) - ein("xqkc,qy->xykc", back_xi, sin_y)).astype(
        jnp.bfloat16
    )
    back_yi = (ein("xqkc,qy->xykc", back_xi, cos_y) + ein("xqkc,qy->xykc", back_xr, sin_y)).astype(
        jnp.bfloat16
    )
    back_yr, back_yi = (
        lax.all_to_all(back_yr, "py", split_axis=1, concat_axis=2, tiled=True),
        lax.all_to_all(back_yi, "py", split_axis=1, concat_axis=2, tiled=True),
    )
    icos_z, isin_z = wave_tables(depth, freq_z, depth_weights(modes_z))
    result = ein("xykc,kz->xyzc", back_yr, icos_z) - ein("xykc,kz->xyzc", back_yi, isin_z)
    mixed = (result + field.astype(jnp.float32)).astype(jnp.bfloat16)
    return mixed.reshape(local_x, local_y, merged)


def solution(mesh):
    in_specs = (P("px", "py", None), P(), P(), P())
    out_specs = P("px", "py", None)
    return jax.shard_map(body, mesh=mesh, in_specs=in_specs, out_specs=out_specs, check_vma=False)
```

profile of v0, /device:TPU:1, one launch (start us, length us, event | category | flops | bytes accessed | tf_op | source)
XLA Modules:
  0.0 266.2 jit_solution(2076494639407197248)
XLA Ops:
  2.3 4.7 %collective-permute-start = (bf16[1,8,6144]{2,1,0:T(8,128)(2,1)S(1)}, bf16[1,8,6144]{2,1,0:T(8,128)(2,1)S(1)}, u32[]{:S(2)}, u32[]{:S(2)}) collective-permute-start(bf16[1,8,6144]{2,1,0:T(8,128)(2,1)S(1)} %get-tuple-element.7), channel_id=1, source_target_pairs={{0,16},{16,32},{32,48},{48,64},{64,80},{80,96},{96,112},{1,17},{17... | collective-permute-start | bytes 294920 | tf_op jit(solution)/shard_map/ppermute | solution.py:18
  10.8 3.2 %collective-permute-start.3 = (bf16[18,1,6144]{2,0,1:T(8,128)(2,1)S(1)}, bf16[18,1,6144]{2,0,1:T(8,128)(2,1)S(1)}, u32[]{:S(2)}, u32[]{:S(2)}) collective-permute-start(bf16[18,1,6144]{2,0,1:T(8,128)(2,1)S(1)} %get-tuple-element.6), channel_id=1, source_target_pairs={{1,0},{2,1},{3,2},{4,3},{5,4},{6,5},{7,6},{8,7},{9,8},{10,9},{11,1... | collective-permute-start | bytes 663560 | tf_op jit(solution)/shard_map/ppermute | solution.py:19
  14.0 3.1 %collective-permute-start.2 = (bf16[18,1,6144]{2,0,1:T(8,128)(2,1)S(1)}, bf16[18,1,6144]{2,0,1:T(8,128)(2,1)S(1)}, u32[]{:S(2)}, u32[]{:S(2)}) collective-permute-start(bf16[18,1,6144]{2,0,1:T(8,128)(2,1)S(1)} %get-tuple-element.5), channel_id=1, source_target_pairs={{0,1},{1,2},{2,3},{3,4},{4,5},{5,6},{6,7},{7,8},{8,9},{9,10},{10,1... | collective-permute-start | bytes 663560 | tf_op jit(solution)/shard_map/ppermute | solution.py:18
  21.9 4.6 %reshape.213 = bf16[18,10,32,192]{3,2,0,1:T(8,128)(2,1)} reshape(bf16[18,10,6144]{2,0,1:T(8,128)(2,1)S(1)} %pad_maximum_fusion) | data formatting | bytes 4423680 | tf_op jit(solution)/shard_map/reshape | solution.py:92
  26.5 3.1 %pad_convert_fusion = f32[18,10,34,192]{3,2,1,0:T(8,128)S(1)} fusion(bf16[18,10,32,192]{3,2,0,1:T(8,128)(2,1)} %reshape.213), kind=kLoop, calls=%fused_computation.56 | loop fusion | flops 1175040 | bytes 6912000 | tf_op jit(solution)/shard_map/convert_element_type | solution.py:43
  29.6 14.6 %fusion.1 = bf16[16,8,32,192]{3,2,1,0:T(8,128)(2,1)S(1)} fusion(f32[18,10,34,192]{3,2,1,0:T(8,128)S(1)} %pad_convert_fusion, f32[192]{0:T(256)S(1)} %bitcast.333, f32[192]{0:T(256)S(1)} %bitcast.334, f32[192]{0:T(256)S(1)} %bitcast.309, f32[192]{0:T(256)S(1)} %bitcast.310, f32[192]{0:T(256)S(1)} %bitcast.311, f32[192]{0:T(256)S(1)} %bitcast.312, ...), kind=kLoop, calls=%fused_computation.2 | loop fusion | flops 42467328 | bytes 86528256 | tf_op jit(solution)/shard_map/convert_element_type | solution.py:54
  46.0 8.2 %all-to-all-start = ((bf16[16,8,16,192]{3,1,0,2:T(8,128)(2,1)}), bf16[16,8,16,192]{3,1,0,2:T(8,128)(2,1)S(1)}, u32[]{:S(2)}, u32[]{:S(2)}) async-start(bf16[16,8,16,192]{3,1,0,2:T(8,128)(2,1)} %copy.107), calls=%async_computation | async-start | bytes 2097152 | tf_op jit(solution)/shard_map/all_to_all | solution.py:99
  56.0 14.1 %all-to-all-done = bf16[16,8,16,192]{3,1,0,2:T(8,128)(2,1)S(1)} async-done(((bf16[16,8,16,192]{3,1,0,2:T(8,128)(2,1)}), bf16[16,8,16,192]{3,1,0,2:T(8,128)(2,1)S(1)}, u32[]{:S(2)}, u32[]{:S(2)}) %all-to-all-start) | async-done | bytes 786464 | tf_op jit(solution)/shard_map/all_to_all | solution.py:99
  70.0 4.9 %all-to-all-start.1 = ((bf16[16,8,16,192]{3,1,0,2:T(8,128)(2,1)}), bf16[16,8,16,192]{3,1,0,2:T(8,128)(2,1)}, u32[]{:S(2)}, u32[]{:S(2)}) async-start(bf16[16,8,16,192]{3,1,0,2:T(8,128)(2,1)} %copy.110), calls=%async_computation.1 | async-start | bytes 2097152 | tf_op jit(solution)/shard_map/all_to_all | solution.py:100
  77.6 13.3 %all-to-all-done.1 = bf16[16,8,16,192]{3,1,0,2:T(8,128)(2,1)} async-done(((bf16[16,8,16,192]{3,1,0,2:T(8,128)(2,1)}), bf16[16,8,16,192]{3,1,0,2:T(8,128)(2,1)}, u32[]{:S(2)}, u32[]{:S(2)}) %all-to-all-start.1) | async-done | bytes 786464 | tf_op jit(solution)/shard_map/all_to_all | solution.py:100
  91.0 2.3 copy_bitcast_fusion
  98.9 2.6 copy.119
  101.5 9.9 %all-to-all-start.3 = ((bf16[16,128,1,192]{3,0,2,1:T(8,128)(2,1)}), bf16[16,128,1,192]{3,0,2,1:T(8,128)(2,1)}, u32[]{:S(2)}, u32[]{:S(2)}) async-start(bf16[16,128,1,192]{3,0,2,1:T(8,128)(2,1)} %copy.119), calls=%async_computation.3 | async-start | bytes 2097152 | tf_op jit(solution)/shard_map/all_to_all | solution.py:114
  115.7 10.0 %all-to-all-done.3 = bf16[16,128,1,192]{3,0,2,1:T(8,128)(2,1)} async-done(((bf16[16,128,1,192]{3,0,2,1:T(8,128)(2,1)}), bf16[16,128,1,192]{3,0,2,1:T(8,128)(2,1)}, u32[]{:S(2)}, u32[]{:S(2)}) %all-to-all-start.3) | async-done | bytes 786464 | tf_op jit(solution)/shard_map/all_to_all | solution.py:114
  125.7 6.0 %all-to-all-start.2 = ((bf16[16,128,1,192]{3,0,2,1:T(8,128)(2,1)}), bf16[16,128,1,192]{3,0,2,1:T(8,128)(2,1)}, u32[]{:S(2)}, u32[]{:S(2)}) async-start(bf16[16,128,1,192]{3,0,2,1:T(8,128)(2,1)} %copy.113), calls=%async_computation.2 | async-start | bytes 2097152 | tf_op jit(solution)/shard_map/all_to_all | solution.py:113
  139.9 6.3 %all-to-all-done.2 = bf16[16,128,1,192]{3,0,2,1:T(8,128)(2,1)} async-done(((bf16[16,128,1,192]{3,0,2,1:T(8,128)(2,1)}), bf16[16,128,1,192]{3,0,2,1:T(8,128)(2,1)}, u32[]{:S(2)}, u32[]{:S(2)}) %all-to-all-start.2) | async-done | bytes 786464 | tf_op jit(solution)/shard_map/all_to_all | solution.py:113
  159.3 2.6 copy.135
  161.9 5.8 %all-to-all-start.4 = ((bf16[128,16,1,192]{3,1,2,0:T(8,128)(2,1)}), bf16[128,16,1,192]{3,1,2,0:T(8,128)(2,1)}, u32[]{:S(2)}, u32[]{:S(2)}) async-start(bf16[128,16,1,192]{3,1,2,0:T(8,128)(2,1)} %copy.135), calls=%async_computation.4 | async-start | bytes 2097152 | tf_op jit(solution)/shard_map/all_to_all | solution.py:142
  171.9 10.3 %all-to-all-done.4 = bf16[128,16,1,192]{3,1,2,0:T(8,128)(2,1)} async-done(((bf16[128,16,1,192]{3,1,2,0:T(8,128)(2,1)}), bf16[128,16,1,192]{3,1,2,0:T(8,128)(2,1)}, u32[]{:S(2)}, u32[]{:S(2)}) %all-to-all-start.4) | async-done | bytes 786464 | tf_op jit(solution)/shard_map/all_to_all | solution.py:142
  182.2 5.7 %all-to-all-start.5 = ((bf16[128,16,1,192]{3,1,2,0:T(8,128)(2,1)}), bf16[128,16,1,192]{3,1,2,0:T(8,128)(2,1)}, u32[]{:S(2)}, u32[]{:S(2)}) async-start(bf16[128,16,1,192]{3,1,2,0:T(8,128)(2,1)} %copy.138), calls=%async_computation.5 | async-start | bytes 2097152 | tf_op jit(solution)/shard_map/all_to_all | solution.py:143
  188.0 2.3 copy.136
  193.6 8.7 %all-to-all-done.5 = bf16[128,16,1,192]{3,1,2,0:T(8,128)(2,1)} async-done(((bf16[128,16,1,192]{3,1,2,0:T(8,128)(2,1)}), bf16[128,16,1,192]{3,1,2,0:T(8,128)(2,1)}, u32[]{:S(2)}, u32[]{:S(2)}) %all-to-all-start.5) | async-done | bytes 786464 | tf_op jit(solution)/shard_map/all_to_all | solution.py:143
  202.3 2.3 copy.139
  208.6 2.5 fusion.43
  211.2 2.6 copy.141
  213.7 6.6 %all-to-all-start.6 = ((bf16[16,128,1,192]{3,0,2,1:T(8,128)(2,1)}), bf16[16,128,1,192]{3,0,2,1:T(8,128)(2,1)}, u32[]{:S(2)}, u32[]{:S(2)}) async-start(bf16[16,128,1,192]{3,0,2,1:T(8,128)(2,1)} %copy.141), calls=%async_computation.6 | async-start | bytes 2097152 | tf_op jit(solution)/shard_map/all_to_all | solution.py:152
  224.5 11.8 %all-to-all-done.6 = bf16[16,128,1,192]{3,0,2,1:T(8,128)(2,1)} async-done(((bf16[16,128,1,192]{3,0,2,1:T(8,128)(2,1)}), bf16[16,128,1,192]{3,0,2,1:T(8,128)(2,1)}, u32[]{:S(2)}, u32[]{:S(2)}) %all-to-all-start.6) | async-done | bytes 786464 | tf_op jit(solution)/shard_map/all_to_all | solution.py:152
  236.3 4.3 %all-to-all-start.7 = ((bf16[16,128,1,192]{3,0,2,1:T(8,128)(2,1)}), bf16[16,128,1,192]{3,0,2,1:T(8,128)(2,1)S(1)}, u32[]{:S(2)}, u32[]{:S(2)}) async-start(bf16[16,128,1,192]{3,0,2,1:T(8,128)(2,1)} %copy.146), calls=%async_computation.7 | async-start | bytes 2097152 | tf_op jit(solution)/shard_map/all_to_all | solution.py:153
  240.7 4.6 %fusion.35 = f32[32,16,8,192]{3,0,2,1:T(8,128)} fusion(bf16[16,16,8,1,192]{4,0,2,1,3:T(8,128)(2,1)} %bitcast.139, f32[16]{0:T(128)S(1)} %fusion.115), kind=kOutput, calls=%fused_computation.81 | convolution fusion | flops 25174016 | bytes 3932224 | tf_op jit(solution)/shard_map/xykc,kz->xyzc/dot_general | solution.py:58
  245.2 11.3 %all-to-all-done.7 = bf16[16,128,1,192]{3,0,2,1:T(8,128)(2,1)S(1)} async-done(((bf16[16,128,1,192]{3,0,2,1:T(8,128)(2,1)}), bf16[16,128,1,192]{3,0,2,1:T(8,128)(2,1)S(1)}, u32[]{:S(2)}, u32[]{:S(2)}) %all-to-all-start.7) | async-done | bytes 786464 | tf_op jit(solution)/shard_map/all_to_all | solution.py:153
  256.6 5.1 %fusion.27 = bf16[16,8,32,192]{3,2,1,0:T(8,128)(2,1)} fusion(bf16[16,8,32,192]{3,2,1,0:T(8,128)(2,1)S(1)} %fusion.1, f32[32,16,8,192]{3,0,2,1:T(8,128)} %fusion.35, bf16[16,16,8,1,192]{4,0,2,1,3:T(8,128)(2,1)S(1)} %bitcast.301, f32[16]{0:T(128)S(1)} %fusion.115), kind=kOutput, calls=%fused_computation.55 | convolution fusion | flops 28319744 | bytes 7077952 | tf_op jit(solution)/shard_map/xykc,kz->xyzc/dot_general | solution.py:58
  261.7 4.5 %reshape.226 = bf16[16,8,6144]{2,1,0:T(8,128)(2,1)} reshape(bf16[16,8,32,192]{3,2,1,0:T(8,128)(2,1)} %fusion.27) | data formatting | bytes 3145728 | tf_op jit(solution)/shard_map/reshape | solution.py:158
  (79 shorter events, 63.8 us)
Async XLA Ops:
  1.0 9.3 %collective-permute-start.1 = (bf16[1,8,6144]{2,1,0:T(8,128)(2,1)S(1)}, bf16[1,8,6144]{2,1,0:T(8,128)(2,1)S(1)}, u32[]{:S(2)}, u32[]{:S(2)}) collective-permute-start(bf16[1,8,6144]{2,1,0:T(8,128)(2,1)S(1)} %get-tuple-element.8), channel_id=1, source_target_pairs={{16,0},{32,16},{48,32},{64,48},{80,64},{96,80},{112,96},{17,1},{33... | collective-permute-start | bytes 294920 | tf_op jit(solution)/shard_map/ppermute | solution.py:19
  2.3 8.2 %collective-permute-start = (bf16[1,8,6144]{2,1,0:T(8,128)(2,1)S(1)}, bf16[1,8,6144]{2,1,0:T(8,128)(2,1)S(1)}, u32[]{:S(2)}, u32[]{:S(2)}) collective-permute-start(bf16[1,8,6144]{2,1,0:T(8,128)(2,1)S(1)} %get-tuple-element.7), channel_id=1, source_target_pairs={{0,16},{16,32},{32,48},{48,64},{64,80},{80,96},{96,112},{1,17},{17... | collective-permute-start | bytes 294920 | tf_op jit(solution)/shard_map/ppermute | solution.py:18
  10.8 8.8 %collective-permute-start.3 = (bf16[18,1,6144]{2,0,1:T(8,128)(2,1)S(1)}, bf16[18,1,6144]{2,0,1:T(8,128)(2,1)S(1)}, u32[]{:S(2)}, u32[]{:S(2)}) collective-permute-start(bf16[18,1,6144]{2,0,1:T(8,128)(2,1)S(1)} %get-tuple-element.6), channel_id=1, source_target_pairs={{1,0},{2,1},{3,2},{4,3},{5,4},{6,5},{7,6},{8,7},{9,8},{10,9},{11,1... | collective-permute-start | bytes 663560 | tf_op jit(solution)/shard_map/ppermute | solution.py:19
  14.0 6.8 %collective-permute-start.2 = (bf16[18,1,6144]{2,0,1:T(8,128)(2,1)S(1)}, bf16[18,1,6144]{2,0,1:T(8,128)(2,1)S(1)}, u32[]{:S(2)}, u32[]{:S(2)}) collective-permute-start(bf16[18,1,6144]{2,0,1:T(8,128)(2,1)S(1)} %get-tuple-element.5), channel_id=1, source_target_pairs={{0,1},{1,2},{2,3},{3,4},{4,5},{5,6},{6,7},{7,8},{8,9},{9,10},{10,1... | collective-permute-start | bytes 663560 | tf_op jit(solution)/shard_map/ppermute | solution.py:18
  46.0 24.0 %all-to-all-start = ((bf16[16,8,16,192]{3,1,0,2:T(8,128)(2,1)}), bf16[16,8,16,192]{3,1,0,2:T(8,128)(2,1)S(1)}, u32[]{:S(2)}, u32[]{:S(2)}) async-start(bf16[16,8,16,192]{3,1,0,2:T(8,128)(2,1)} %copy.107), calls=%async_computation | async-start | bytes 2097152 | tf_op jit(solution)/shard_map/all_to_all | solution.py:99
  70.0 21.0 %all-to-all-start.1 = ((bf16[16,8,16,192]{3,1,0,2:T(8,128)(2,1)}), bf16[16,8,16,192]{3,1,0,2:T(8,128)(2,1)}, u32[]{:S(2)}, u32[]{:S(2)}) async-start(bf16[16,8,16,192]{3,1,0,2:T(8,128)(2,1)} %copy.110), calls=%async_computation.1 | async-start | bytes 2097152 | tf_op jit(solution)/shard_map/all_to_all | solution.py:100
  101.5 24.2 %all-to-all-start.3 = ((bf16[16,128,1,192]{3,0,2,1:T(8,128)(2,1)}), bf16[16,128,1,192]{3,0,2,1:T(8,128)(2,1)}, u32[]{:S(2)}, u32[]{:S(2)}) async-start(bf16[16,128,1,192]{3,0,2,1:T(8,128)(2,1)} %copy.119), calls=%async_computation.3 | async-start | bytes 2097152 | tf_op jit(solution)/shard_map/all_to_all | solution.py:114
  125.7 20.4 %all-to-all-start.2 = ((bf16[16,128,1,192]{3,0,2,1:T(8,128)(2,1)}), bf16[16,128,1,192]{3,0,2,1:T(8,128)(2,1)}, u32[]{:S(2)}, u32[]{:S(2)}) async-start(bf16[16,128,1,192]{3,0,2,1:T(8,128)(2,1)} %copy.113), calls=%async_computation.2 | async-start | bytes 2097152 | tf_op jit(solution)/shard_map/all_to_all | solution.py:113
  150.7 1.4 copy-start.2
  150.7 1.6 copy-start.3
  152.1 1.4 copy-start.1
  152.7 1.4 copy-start.4
  156.8 0.9 copy-start
  161.9 20.3 %all-to-all-start.4 = ((bf16[128,16,1,192]{3,1,2,0:T(8,128)(2,1)}), bf16[128,16,1,192]{3,1,2,0:T(8,128)(2,1)}, u32[]{:S(2)}, u32[]{:S(2)}) async-start(bf16[128,16,1,192]{3,1,2,0:T(8,128)(2,1)} %copy.135), calls=%async_computation.4 | async-start | bytes 2097152 | tf_op jit(solution)/shard_map/all_to_all | solution.py:142
  182.2 20.1 %all-to-all-start.5 = ((bf16[128,16,1,192]{3,1,2,0:T(8,128)(2,1)}), bf16[128,16,1,192]{3,1,2,0:T(8,128)(2,1)}, u32[]{:S(2)}, u32[]{:S(2)}) async-start(bf16[128,16,1,192]{3,1,2,0:T(8,128)(2,1)} %copy.138), calls=%async_computation.5 | async-start | bytes 2097152 | tf_op jit(solution)/shard_map/all_to_all | solution.py:143
  213.7 22.6 %all-to-all-start.6 = ((bf16[16,128,1,192]{3,0,2,1:T(8,128)(2,1)}), bf16[16,128,1,192]{3,0,2,1:T(8,128)(2,1)}, u32[]{:S(2)}, u32[]{:S(2)}) async-start(bf16[16,128,1,192]{3,0,2,1:T(8,128)(2,1)} %copy.141), calls=%async_computation.6 | async-start | bytes 2097152 | tf_op jit(solution)/shard_map/all_to_all | solution.py:152
  236.3 20.2 %all-to-all-start.7 = ((bf16[16,128,1,192]{3,0,2,1:T(8,128)(2,1)}), bf16[16,128,1,192]{3,0,2,1:T(8,128)(2,1)S(1)}, u32[]{:S(2)}, u32[]{:S(2)}) async-start(bf16[16,128,1,192]{3,0,2,1:T(8,128)(2,1)} %copy.146), calls=%async_computation.7 | async-start | bytes 2097152 | tf_op jit(solution)/shard_map/all_to_all | solution.py:153
where the time goes:
time: 268 us; the launch traced here: 266 us
  waiting for transfers between devices  88.6 us (33%)
  starting transfers between devices  63.7 us (24%)
  local copies, waits for them, and re-layouts  55.8 us (21%)
  matrix products  32.5 us (12%)
  other arithmetic  25.1 us (9%)
    unnamed x16, matrix products  18.7 us
    another operation x8, local copies, waits for them, and re-layouts  14.8 us
    convert_element_type x1, other arithmetic, convolve(): return total.astype(jnp.bfloat16)  14.6 us
    all_to_all x1, waiting for transfers between devices, body(): lax.all_to_all(real_z, 'py', split_axis=2, concat_axis=1, tiled=True)  14.1 us
    dot_general x12, matrix products, ein(): return jnp.einsum(form, left, right, preferred_element_type=jnp.float32)  13.8 us
    all_to_all x1, waiting for transfers between devices, body(): lax.all_to_all(imag_z, 'py', split_axis=2, concat_axis=1, tiled=True)  13.3 us
    all_to_all x1, waiting for transfers between devices, body(): lax.all_to_all(back_yr, 'py', split_axis=1, concat_axis=2, tiled=True)  11.8 us
    all_to_all x1, waiting for transfers between devices, body(): lax.all_to_all(back_yi, 'py', split_axis=1, concat_axis=2, tiled=True)  11.3 us
  transfers between devices with their start and end apart: 12, of which 10 were waited for; matrix products, arithmetic and copies ran while one was open for 15% of the time, Pallas kernels for 0%

commit v1 on v0

v1 whole, which is shorter than its diff:
```python
import functools
import math

import jax
import jax.numpy as jnp
import ml_dtypes
import numpy as np
from jax import lax
from jax.experimental import pallas as pl
from jax.experimental.pallas import tpu as pltpu
from jax.sharding import PartitionSpec as P

shrink_level = 0.2
F32 = jnp.float32
BF16 = jnp.bfloat16
VMEM = pltpu.VMEM

PX, PY = 8, 16
LX, LY = 16, 8
Z, KZ, C, CB = 32, 16, 192, 96
W = 2 * C
MERGED = Z * C
XP = LX // 2
ZH = Z // 2
Q = 64


def tables(length, modes, weights):
    product = np.asarray(modes)[:, None] * np.arange(length)[None, :] % length
    angle = product.astype(np.float32) * np.float32(2.0 * math.pi / length)
    factor = np.asarray(weights, np.float32)[:, None] / np.float32(math.sqrt(length))
    rounded = [(f(angle) * factor).astype(ml_dtypes.bfloat16) for f in (np.cos, np.sin)]
    return [t.astype(np.float64) for t in rounded]


def kept(length):
    return np.concatenate([np.arange(length // 4), np.arange(length - length // 4, length)])


def forward(cos, sin):
    return np.stack([np.stack([cos, sin], 1), np.stack([-sin, cos], 1)])


def backward(cos, sin):
    cos, sin = cos.T, sin.T
    return np.stack([np.stack([cos, -sin], 1), np.stack([sin, cos], 1)])


def as_bf16(matrix):
    return np.ascontiguousarray(matrix).astype(ml_dtypes.bfloat16)


@functools.cache
def matrices():
    eye = np.eye(LY)
    one = np.ones(KZ)
    cz, sz = tables(Z, np.arange(KZ), one)
    both = np.stack([cz, -sz], 1).reshape(KZ, 2, ZH, 2)
    z_fwd = np.einsum("kpzs,yw->kpyszw", both, eye).reshape(KZ * 2 * LY, 2 * ZH * LY)
    two = np.where(np.arange(KZ) == 0, 1.0, 2.0)
    cz, sz = tables(Z, np.arange(KZ), two)
    both = np.stack([cz, -sz], 1).reshape(KZ, 2, ZH, 2)
    z_inv = np.einsum("kpzs,yw->szykpw", both, eye).reshape(2 * ZH * LY, KZ * 2 * LY)
    n = PY * LY
    cy, sy = tables(n, kept(n), np.ones(Q))
    y_fwd = forward(cy, sy).reshape(2, Q, 2, PY, LY).transpose(0, 1, 3, 2, 4).reshape(2 * Q, 2 * n)
    y_inv = backward(cy, sy).reshape(2, PY, LY, 2, PX, Q // PX)
    y_inv = y_inv.transpose(1, 0, 2, 4, 3, 5).reshape(2 * n, 2 * Q)
    n = PX * LX
    cx, sx = tables(n, kept(n), np.ones(Q))
    x_fwd = forward(cx, sx).reshape(2, Q, 2, PX, XP, 2)
    x_fwd = x_fwd.transpose(5, 0, 1, 3, 2, 4).reshape(4 * Q, 2 * PX * XP)
    x_inv = backward(cx, sx).reshape(2, PX, XP, 2, 2, Q)
    x_inv = x_inv.transpose(3, 0, 1, 2, 4, 5).reshape(4 * PX * XP, 2 * Q)
    return [as_bf16(m) for m in (z_fwd, z_inv, y_fwd, y_inv, x_fwd, x_inv)]


def dot(a, b):
    return jnp.dot(a, b, preferred_element_type=F32)


def low_half(rows):
    return lax.broadcasted_iota(jnp.int32, (rows, W), 1) < C


def swap(value):
    return pltpu.roll(value, C, 1)


def conv_kernel(tok, xlo, xhi, ylo, yhi, weight, z_fwd, field, freq, shifted, ylo_s, yhi_s, edge, conv):
    pad = jnp.zeros((LY, C), F32)
    for i in range(LX + 2):
        row = xlo[0] if i == 0 else xhi[0] if i == LX + 1 else tok[i - 1]
        shifted[i, :, :] = jnp.concatenate([pad, row.astype(F32), pad], axis=1)
    pad = jnp.zeros((LX + 2, C), F32)
    ylo_s[...] = jnp.concatenate([pad, ylo[...].astype(F32), pad], axis=1)
    yhi_s[...] = jnp.concatenate([pad, yhi[...].astype(F32), pad], axis=1)
    row_at = lax.broadcasted_iota(jnp.int32, (LY, 128), 0)

    @pl.loop(0, MERGED // 128)
    def _(j):
        at = pl.multiple_of(j * 128, 128)
        after = pl.multiple_of(j * 128 + W, 128)
        here = pl.ds(at, 128)
        phase = pl.multiple_of(lax.rem(j, 3) * 128, 128)
        taps = [weight[t : t + 1, pl.ds(phase, 128)] for t in range(27)]
        for side, rows, rows_s, b in ((0, ylo, ylo_s, 0), (1, yhi, yhi_s, 2)):
            mid = rows[:, here].astype(F32)
            before = rows_s[:, here]
            behind = rows_s[:, pl.ds(after, 128)]
            total = None
            for a in range(3):
                t = a * 9 + b * 3
                term = before * taps[t] + mid * taps[t + 1] + behind * taps[t + 2]
                term = term[a : a + LX]
                total = term if total is None else total + term
            edge[side] = total
        wide = [jnp.broadcast_to(t, (LY, 128)) for t in taps]
        sums = {}
        for i in range(LX + 2):
            ref = xlo if i == 0 else xhi if i == LX + 1 else tok
            mid = ref[0 if i in (0, LX + 1) else i - 1, :, here].astype(F32)
            before = shifted[i, :, here]
            behind = shifted[i, :, pl.ds(after, 128)]
            for a in range(3):
                x = i - a
                if not 0 <= x < LX:
                    continue
                for b in range(3):
                    t = a * 9 + b * 3
                    term = before * wide[t] + mid * wide[t + 1] + behind * wide[t + 2]
                    sums[x, b] = sums[x, b] + term if (x, b) in sums else term
            x = i - 2
            if x >= 0:
                down = pltpu.roll(sums.pop((x, 0)), 1, 0)
                up = pltpu.roll(sums.pop((x, 2)), LY - 1, 0)
                down = jnp.where(row_at == 0, edge[0, x : x + 1, :], down)
                up = jnp.where(row_at == LY - 1, edge[1, x : x + 1, :], up)
                conv[x, :, here] = sums.pop((x, 1)) + down + up

    low = low_half(ZH * LY)

    @pl.loop(0, XP)
    def _(xp):
        parts = []
        for x in (2 * xp, 2 * xp + 1):
            part = jnp.concatenate([conv[x, :, z * W : (z + 1) * W] for z in range(ZH)], axis=0)
            field[x] = part.astype(BF16)
            parts.append(part)
        first, second = parts
        even = jnp.where(low, first, swap(second)).astype(BF16)
        odd = jnp.where(low, swap(first), second).astype(BF16)
        out = dot(z_fwd[...], jnp.concatenate([even, odd], axis=0))
        freq[:, xp] = out.astype(BF16).reshape(KZ, 2 * LY, W)


def y_forward_kernel(given, y_fwd, out, rows):
    for xp in range(XP):
        data = given[:, xp].reshape(2 * PY * LY, W)
        value = dot(y_fwd[...], data)
        for part in range(2):
            for t in range(W // 128):
                rows[t, pl.ds(part * XP + xp, Q, stride=2 * XP), :] = value[
                    part * Q : (part + 1) * Q, t * 128 : (t + 1) * 128
                ]
    gather(rows, out)


def gather(rows, out):
    count = 2 * XP * Q // PX
    for d in range(PX):
        block = [rows[t, pl.ds(d * count, count), :] for t in range(W // 128)]
        out[d] = jnp.concatenate(block, axis=1).astype(BF16).reshape(out.shape[1:])


def shrink(v):
    return v - jnp.clip(v, -shrink_level, shrink_level)


def spectrum_kernel(given, x_fwd, x_inv, inner, outer, out, rows):
    low = low_half(2 * PX * XP)
    for q in range(Q // PX):
        data = given[:, q].reshape(2 * PX * XP, W)
        both = dot(x_fwd[...], data)
        spec = both[: 2 * Q] + swap(both[2 * Q :])
        spec = spec[:, :256].astype(BF16)
        mixed = dot(spec, inner[...])
        hidden_r = jnp.tanh(mixed[:Q, :256] - mixed[Q:, 256:])
        hidden_i = jnp.tanh(mixed[:Q, 256:] + mixed[Q:, :256])
        hidden = jnp.concatenate([hidden_r, hidden_i], axis=0).astype(BF16)
        mixed = dot(hidden, outer[...])
        filt_r = shrink(mixed[:Q, :W] - mixed[Q:, W:])
        filt_i = shrink(mixed[:Q, W:] + mixed[Q:, :W])
        filt = jnp.concatenate([filt_r, filt_i], axis=0).astype(BF16)
        both = dot(x_inv[...], filt)
        back = jnp.where(low, both[: 2 * PX * XP], both[2 * PX * XP :])
        for part in range(2):
            for t in range(W // 128):
                rows[t, pl.ds(part * (Q // PX) + q, PX * XP, stride=2 * (Q // PX)), :] = back[
                    part * PX * XP : (part + 1) * PX * XP, t * 128 : (t + 1) * 128
                ]
    gather(rows, out)


def y_inverse_kernel(given, y_inv, out):
    for xp in range(XP):
        data = given[:, xp].reshape(2 * Q, W)
        out[:, xp] = dot(y_inv[...], data).astype(BF16).reshape(PY, 2 * LY, W)


def z_inverse_kernel(given, z_inv, field, out):
    low = low_half(ZH * LY)

    @pl.loop(0, XP)
    def _(xp):
        data = given[:, xp].reshape(2 * KZ * LY, W)
        value = dot(z_inv[...], data)
        even, odd = value[: ZH * LY], value[ZH * LY :]
        first = jnp.where(low, even, swap(odd)) + field[2 * xp].astype(F32)
        second = jnp.where(low, swap(even), odd) + field[2 * xp + 1].astype(F32)
        for x, value in ((2 * xp, first), (2 * xp + 1, second)):
            for z in range(ZH):
                out[x, :, z * W : (z + 1) * W] = value[z * LY : (z + 1) * LY].astype(BF16)


def call(kernel, outs, scratch=(), name=None):
    return pl.pallas_call(
        kernel,
        out_shape=outs,
        scratch_shapes=list(scratch),
        compiler_params=pltpu.CompilerParams(vmem_limit_bytes=50 * 2**20),
        name=name,
    )


def shape(*dims):
    return jax.ShapeDtypeStruct(dims, BF16)


def block_diagonal(weight):
    full = jnp.zeros((2, C, C), weight.dtype)
    for b in range(C // CB):
        full = full.at[:, b * CB : (b + 1) * CB, b * CB : (b + 1) * CB].set(weight[:, b])
    return full


def halos(tokens):
    up_x = [(i, i + 1) for i in range(PX - 1)]
    down_x = [(j, i) for i, j in up_x]
    up_y = [(i, i + 1) for i in range(PY - 1)]
    down_y = [(j, i) for i, j in up_y]
    xlo = lax.ppermute(tokens[LX - 1 :], "px", up_x)
    xhi = lax.ppermute(tokens[:1], "px", down_x)
    first, last = (
        jnp.concatenate([xlo[:, y], tokens[:, y], xhi[:, y]], axis=0) for y in (0, LY - 1)
    )
    ylo = lax.ppermute(last, "py", up_y)
    yhi = lax.ppermute(first, "py", down_y)
    return xlo, xhi, ylo, yhi


def body(tokens, conv_weight, inner_weight, outer_weight):
    z_fwd, z_inv, y_fwd, y_inv, x_fwd, x_inv = (jnp.asarray(m) for m in matrices())
    weight = jnp.concatenate([conv_weight, conv_weight], axis=1)
    inner = block_diagonal(inner_weight)
    inner = jnp.pad(inner, ((0, 0), (0, 256 - C), (0, 256 - C)))
    inner = jnp.concatenate([inner[0], inner[1]], axis=1)
    outer = block_diagonal(outer_weight)
    outer = jnp.pad(outer, ((0, 0), (0, 256 - C), (0, 0)))
    outer = jnp.concatenate([outer[0], outer[0], outer[1], outer[1]], axis=1)

    xlo, xhi, ylo, yhi = halos(tokens)
    wide = MERGED + 2 * C
    field, freq = call(
        conv_kernel,
        [shape(LX, ZH * LY, W), shape(KZ, XP, 2 * LY, W)],
        [
            VMEM((LX + 2, LY, wide), F32),
            VMEM((LX + 2, wide), F32),
            VMEM((LX + 2, wide), F32),
            VMEM((2, LX, 128), F32),
            VMEM((LX, LY, MERGED), F32),
        ],
        name="conv_z",
    )(tokens, xlo, xhi, ylo, yhi, weight, z_fwd)
    rows = VMEM((W // 128, 2 * XP * Q, 128), F32)
    freq = lax.all_to_all(freq, "py", 0, 0, tiled=True)
    freq = call(y_forward_kernel, shape(PX, Q // PX, 2 * XP, W), [rows], name="y_fwd")(freq, y_fwd)
    freq = lax.all_to_all(freq, "px", 0, 0, tiled=True)
    freq = call(spectrum_kernel, shape(PX, XP, 2 * Q // PX, W), [rows], name="spec")(
        freq, x_fwd, x_inv, inner, outer
    )
    freq = lax.all_to_all(freq, "px", 0, 0, tiled=True)
    freq = call(y_inverse_kernel, shape(PY, XP, 2 * LY, W), name="y_inv")(freq, y_inv)
    freq = lax.all_to_all(freq, "py", 0, 0, tiled=True)
    return call(z_inverse_kernel, shape(LX, LY, MERGED), name="z_inv")(freq, z_inv, field)


def solution(mesh):
    in_specs = (P("px", "py", None), P(), P(), P())
    out_specs = P("px", "py", None)
    return jax.shard_map(body, mesh=mesh, in_specs=in_specs, out_specs=out_specs, check_vma=False)
```

time: 268 us -> 142 us (0.53)
  waiting for transfers between devices: 88.6 us -> 34.2 us
  local copies, waits for them, and re-layouts: 55.8 us -> 6.79 us
  blocking collectives: 0 us -> 45.4 us
  starting transfers between devices: 63.7 us -> 29.1 us
  matrix products: 32.5 us -> 0 us
  Pallas kernels: 0 us -> 25 us
  other arithmetic: 25.1 us -> 0.49 us
    all_to_all x8 -> x2, waiting for transfers between devices: 85.8 us -> 29.5 us  [the longest x1 21.4 us: body(): freq = lax.all_to_all(freq, 'py', 0, 0, tiled=True)]
    all_to_all x0 -> x2, blocking collectives: none -> 45.4 us  [the longest x1 26.6 us: body(): freq = lax.all_to_all(freq, 'py', 0, 0, tiled=True)]
    all_to_all x8 -> x2, starting transfers between devices: 51.5 us -> 16.7 us  [the longest x1 8.73 us: body(): freq = lax.all_to_all(freq, 'px', 0, 0, tiled=True)]
    pallas_call x0 -> x5, Pallas kernels: none -> 25 us  [the longest x1 13.1 us: body(): call(conv_kernel, [shape(LX, ZH * LY, W), shape(KZ, XP, 2 * LY, W)], [VME...]
    convert_element_type x11 -> x0, other arithmetic: 23.7 us -> none  [the longest x1 14.6 us: convolve(): return total.astype(jnp.bfloat16)]
    unnamed x16 -> x0, matrix products: 18.7 us -> none
    convert_element_type x8 -> x0, local copies, waits for them, and re-layouts: 15.5 us -> none  [the longest x1 2.59 us: body(): (ein('xykc,qy->xqkc', imag_z, cos_y) - ein('xykc,qy->xqkc', real_z, sin_y...]
    another operation x8 -> x2, local copies, waits for them, and re-layouts: 14.8 us -> 0.02 us
  transfers between devices with their start and end apart: 12 -> 6, of which waited for: 10 -> 5; matrix products, arithmetic and copies ran while one was open for 15% -> 4% of each run, Pallas kernels for 0% -> 0%
where the time goes in v1:
time: 142 us; the launch traced here: 141 us
  blocking collectives  45.4 us (32%)
  waiting for transfers between devices  34.2 us (24%)
  starting transfers between devices  29.1 us (20%)
  Pallas kernels  25 us (18%)
  local copies, waits for them, and re-layouts  6.79 us (5%)
    all_to_all x1, blocking collectives, body(): freq = lax.all_to_all(freq, 'py', 0, 0, tiled=True)  26.6 us
    all_to_all x1, waiting for transfers between devices, body(): freq = lax.all_to_all(freq, 'py', 0, 0, tiled=True)  21.4 us
    all_to_all x1, blocking collectives, body(): freq = lax.all_to_all(freq, 'px', 0, 0, tiled=True)  18.8 us
    pallas_call x1, Pallas kernels, body(): call(conv_kernel, [shape(LX, ZH * LY, W), shape(KZ, XP, 2 * LY, W)], [VME...  13.1 us
    all_to_all x1, starting transfers between devices, body(): freq = lax.all_to_all(freq, 'px', 0, 0, tiled=True)  8.73 us
    all_to_all x1, waiting for transfers between devices, body(): freq = lax.all_to_all(freq, 'px', 0, 0, tiled=True)  8.02 us
    all_to_all x1, starting transfers between devices, body(): freq = lax.all_to_all(freq, 'py', 0, 0, tiled=True)  7.97 us
    pallas_call x1, Pallas kernels, body(): call(spectrum_kernel, shape(PX, XP, 2 * Q // PX, W), [rows], name='spec')  5.88 us
  transfers between devices with their start and end apart: 6, of which 5 were waited for; matrix products, arithmetic and copies ran while one was open for 4% of the time, Pallas kernels for 0%

profile of v1, /device:TPU:1, one launch (start us, length us, event | category | flops | bytes accessed | tf_op | source)
XLA Modules:
  0.0 141.1 jit_solution(17309806625791085315)
XLA Ops:
  0.0 1.0 fusion.5
  1.0 4.0 %collective-permute-start = (bf16[1,8,6144]{2,1,0:T(8,128)(2,1)S(1)}, bf16[1,8,6144]{2,1,0:T(8,128)(2,1)S(1)}, u32[]{:S(2)}, u32[]{:S(2)}) collective-permute-start(bf16[1,8,6144]{2,1,0:T(8,128)(2,1)S(1)} %get-tuple-element.60), channel_id=1, source_target_pairs={{0,16},{16,32},{32,48},{48,64},{64,80},{80,96},{96,112},{1,17},{17... | collective-permute-start | bytes 294920 | tf_op jit(solution)/shard_map/ppermute | solution.py:252
  5.0 1.3 collective-permute-start.1
  6.3 2.6 %fusion.4 = (bf16[16,1,6144]{2,1,0:T(2,128)(2,1)S(1)}, bf16[16,1,6144]{2,1,0:T(2,128)(2,1)S(1)}) fusion(bf16[16,8,6144]{2,1,0:T(8,128)(2,1)} %tok.1), kind=kLoop, calls=%fused_computation.23 | loop fusion | bytes 786432 | tf_op jit(solution)/shard_map/slice | solution.py:255
  8.9 0.0 copy-start.1
  8.9 0.1 copy.25
  9.0 0.1 copy.26
  9.2 1.2 collective-permute-done.1.xhi
  10.4 0.1 pad_maximum_fusion.2
  10.5 4.0 %collective-permute-start.3 = (bf16[18,6144]{1,0:T(8,128)(2,1)S(1)}, bf16[18,6144]{1,0:T(8,128)(2,1)S(1)}, u32[]{:S(2)}, u32[]{:S(2)}) collective-permute-start(bf16[18,6144]{1,0:T(8,128)(2,1)S(1)} %pad_maximum_fusion.2), channel_id=1, source_target_pairs={{1,0},{2,1},{3,2},{4,3},{5,4},{6,5},{7,6},{8,7},{9,8},{10,9},{11,1... | collective-permute-start | bytes 663560 | tf_op jit(solution)/shard_map/ppermute | solution.py:258
  14.5 0.1 pad_maximum_fusion.1
  14.7 3.0 %collective-permute-start.2 = (bf16[18,6144]{1,0:T(8,128)(2,1)S(1)}, bf16[18,6144]{1,0:T(8,128)(2,1)S(1)}, u32[]{:S(2)}, u32[]{:S(2)}) collective-permute-start(bf16[18,6144]{1,0:T(8,128)(2,1)S(1)} %pad_maximum_fusion.1), channel_id=1, source_target_pairs={{0,1},{1,2},{2,3},{3,4},{4,5},{5,6},{6,7},{7,8},{8,9},{9,10},{10,1... | collective-permute-start | bytes 663560 | tf_op jit(solution)/shard_map/ppermute | solution.py:257
  17.7 0.1 pad_maximum_fusion.4.weight
  17.8 2.3 %collective-permute-done.3.yhi = bf16[18,6144]{1,0:T(8,128)(2,1)S(1)} collective-permute-done((bf16[18,6144]{1,0:T(8,128)(2,1)S(1)}, bf16[18,6144]{1,0:T(8,128)(2,1)S(1)}, u32[]{:S(2)}, u32[]{:S(2)}) %collective-permute-start.3) | collective-permute-done | bytes 221216 | tf_op jit(solution)/shard_map/ppermute | solution.py:258
  20.0 1.3 collective-permute-done.2.ylo
  21.3 13.1 %conv_z.1 = (bf16[16,128,384]{2,1,0:T(8,128)(2,1)S(1)}, bf16[16,8,16,384]{3,2,1,0:T(8,128)(2,1)}) custom-call(bf16[16,8,6144]{2,1,0:T(8,128)(2,1)} %tok.1, bf16[1,8,6144]{2,1,0:T(8,128)(2,1)S(1)} %collective-permute-done.xlo, bf16[1,8,6144]{2,1,0:T(8,128)(2,1)S(1)} %collective-permute-done.1.xhi, bf16[18,6144]{1,0:T(8,128)(2,1)S(1)} %collective-permute-done.2.ylo, ...), custom_call_target="tpu_custom_call" | custom-call | tf_op jit(solution)/shard_map/conv_z/pallas_call | solution.py:274
  34.5 8.0 %all-to-all-start = ((bf16[16,8,16,384]{3,2,1,0:T(8,128)(2,1)}), bf16[16,8,16,384]{3,2,1,0:T(8,128)(2,1)S(1)}, u32[]{:S(2)}, u32[]{:S(2)}) async-start(bf16[16,8,16,384]{3,2,1,0:T(8,128)(2,1)} %get-tuple-element.55), calls=%async_computation | async-start | bytes 3145728 | tf_op jit(solution)/shard_map/all_to_all | solution.py:287
  42.5 21.4 %all-to-all-done.given = bf16[16,8,16,384]{3,2,1,0:T(8,128)(2,1)S(1)} async-done(((bf16[16,8,16,384]{3,2,1,0:T(8,128)(2,1)}), bf16[16,8,16,384]{3,2,1,0:T(8,128)(2,1)S(1)}, u32[]{:S(2)}, u32[]{:S(2)}) %all-to-all-start) | async-done | bytes 1572896 | tf_op jit(solution)/shard_map/all_to_all | solution.py:287
  64.0 1.7 %y_fwd.2 = bf16[8,8,16,384]{3,2,1,0:T(8,128)(2,1)} custom-call(bf16[16,8,16,384]{3,2,1,0:T(8,128)(2,1)S(1)} %all-to-all-done.given, bf16[128,256]{1,0:T(8,128)(2,1)S(1)} %copy-done.5), custom_call_target="tpu_custom_call" | custom-call | tf_op jit(solution)/shard_map/y_fwd/pallas_call | solution.py:288
  65.7 8.7 %all-to-all-start.1 = ((bf16[8,8,16,384]{3,2,1,0:T(8,128)(2,1)}), bf16[8,8,16,384]{3,2,1,0:T(8,128)(2,1)S(1)}, u32[]{:S(2)}, u32[]{:S(2)}) async-start(bf16[8,8,16,384]{3,2,1,0:T(8,128)(2,1)} %y_fwd.2), calls=%async_computation.1 | async-start | bytes 1572864 | tf_op jit(solution)/shard_map/all_to_all | solution.py:289
  74.4 0.0 copy-start.3
  74.4 0.0 copy-start.4
  74.5 1.4 scatter.19
  75.9 1.4 scatter.15
  77.4 0.2 pad_maximum_fusion.outer
  77.6 0.0 copy-start.2
  77.6 8.0 %all-to-all-done.1.given = bf16[8,8,16,384]{3,2,1,0:T(8,128)(2,1)S(1)} async-done(((bf16[8,8,16,384]{3,2,1,0:T(8,128)(2,1)}), bf16[8,8,16,384]{3,2,1,0:T(8,128)(2,1)S(1)}, u32[]{:S(2)}, u32[]{:S(2)}) %all-to-all-start.1) | async-done | bytes 786464 | tf_op jit(solution)/shard_map/all_to_all | solution.py:289
  85.6 5.9 %spec.1 = bf16[8,8,16,384]{3,2,1,0:T(8,128)(2,1)S(1)} custom-call(bf16[8,8,16,384]{3,2,1,0:T(8,128)(2,1)S(1)} %all-to-all-done.1.given, bf16[256,128]{1,0:T(8,128)(2,1)S(1)} %copy-done.3, bf16[256,128]{1,0:T(8,128)(2,1)S(1)} %copy-done.4, bf16[256,512]{1,0:T(8,128)(2,1)S(1)} %pad_maximum_fusion.3.inner, bf16[256,768]{1,0:T(8,128)(2,1)S(1)} %pad_maximum_fusion.outer), custom_call_target="tpu_custom_call" | custom-call | tf_op jit(solution)/shard_map/spec/pallas_call | solution.py:290
  91.5 18.8 %all_to_all.20.given = bf16[8,8,16,384]{3,2,1,0:T(8,128)(2,1)S(1)} all-to-all(bf16[8,8,16,384]{3,2,1,0:T(8,128)(2,1)S(1)} %spec.1), channel_id=1, replica_groups=mesh['px'=8,'py'=16] {'px'}, dimensions={0} | all-to-all | bytes 1572864 | tf_op jit(solution)/shard_map/all_to_all | solution.py:293
  110.3 0.6 y_inv.2
  110.9 26.6 %all_to_all.21.given = bf16[16,8,16,384]{3,2,1,0:T(8,128)(2,1)S(1)} all-to-all(bf16[16,8,16,384]{3,2,1,0:T(8,128)(2,1)S(1)} %y_inv.2), channel_id=1, replica_groups=mesh['px'=8,'py'=16] {'py'}, dimensions={0} | all-to-all | bytes 3145728 | tf_op jit(solution)/shard_map/all_to_all | solution.py:295
  137.4 3.7 %z_inv.2 = bf16[16,8,6144]{2,1,0:T(8,128)(2,1)} custom-call(bf16[16,8,16,384]{3,2,1,0:T(8,128)(2,1)S(1)} %all_to_all.21.given, bf16[256,256]{1,0:T(8,128)(2,1)S(1)} %copy-done, bf16[16,128,384]{2,1,0:T(8,128)(2,1)S(1)} %get-tuple-element.56.field), custom_call_target="tpu_custom_call" | custom-call | tf_op jit(solution)/shard_map/z_inv/pallas_call | solution.py:296
  (24 shorter events, 0.3 us)
Async XLA Ops:
  1.0 8.2 %collective-permute-start = (bf16[1,8,6144]{2,1,0:T(8,128)(2,1)S(1)}, bf16[1,8,6144]{2,1,0:T(8,128)(2,1)S(1)}, u32[]{:S(2)}, u32[]{:S(2)}) collective-permute-start(bf16[1,8,6144]{2,1,0:T(8,128)(2,1)S(1)} %get-tuple-element.60), channel_id=1, source_target_pairs={{0,16},{16,32},{32,48},{48,64},{64,80},{80,96},{96,112},{1,17},{17... | collective-permute-start | bytes 294920 | tf_op jit(solution)/shard_map/ppermute | solution.py:252
  5.0 5.4 %collective-permute-start.1 = (bf16[1,8,6144]{2,1,0:T(8,128)(2,1)S(1)}, bf16[1,8,6144]{2,1,0:T(8,128)(2,1)S(1)}, u32[]{:S(2)}, u32[]{:S(2)}) collective-permute-start(bf16[1,8,6144]{2,1,0:T(8,128)(2,1)S(1)} %get-tuple-element.59), channel_id=1, source_target_pairs={{16,0},{32,16},{48,32},{64,48},{80,64},{96,80},{112,96},{17,1},{33... | collective-permute-start | bytes 294920 | tf_op jit(solution)/shard_map/ppermute | solution.py:253
  8.9 8.8 %copy-start.8 = (f32[27,192]{1,0:T(8,128)S(1)}, f32[27,192]{1,0:T(8,128)}, u32[]{:S(2)}) copy-start(f32[27,192]{1,0:T(8,128)} %param.19) | copy-start | bytes 62212
  8.9 12.5 %copy-start.1 = (bf16[256,256]{1,0:T(8,128)(2,1)S(1)}, bf16[256,256]{1,0:T(8,128)(2,1)}, u32[]{:S(2)}) copy-start(bf16[256,256]{1,0:T(8,128)(2,1)} %constant.116.clone.z_fwd) | copy-start | bytes 393220
  10.5 9.5 %collective-permute-start.3 = (bf16[18,6144]{1,0:T(8,128)(2,1)S(1)}, bf16[18,6144]{1,0:T(8,128)(2,1)S(1)}, u32[]{:S(2)}, u32[]{:S(2)}) collective-permute-start(bf16[18,6144]{1,0:T(8,128)(2,1)S(1)} %pad_maximum_fusion.2), channel_id=1, source_target_pairs={{1,0},{2,1},{3,2},{4,3},{5,4},{6,5},{7,6},{8,7},{9,8},{10,9},{11,1... | collective-permute-start | bytes 663560 | tf_op jit(solution)/shard_map/ppermute | solution.py:258
  14.7 6.7 %collective-permute-start.2 = (bf16[18,6144]{1,0:T(8,128)(2,1)S(1)}, bf16[18,6144]{1,0:T(8,128)(2,1)S(1)}, u32[]{:S(2)}, u32[]{:S(2)}) collective-permute-start(bf16[18,6144]{1,0:T(8,128)(2,1)S(1)} %pad_maximum_fusion.1), channel_id=1, source_target_pairs={{0,1},{1,2},{2,3},{3,4},{4,5},{5,6},{6,7},{7,8},{8,9},{9,10},{10,1... | collective-permute-start | bytes 663560 | tf_op jit(solution)/shard_map/ppermute | solution.py:257
  34.5 8.0 %copy-start.6 = (bf16[2,2,96,96]{3,2,1,0:T(8,128)(2,1)S(1)}, bf16[2,2,96,96]{3,2,1,0:T(8,128)(2,1)}, u32[]{:S(2)}) copy-start(bf16[2,2,96,96]{3,2,1,0:T(8,128)(2,1)} %param.21) | copy-start | bytes 221188
  34.5 29.5 %copy-start.5 = (bf16[128,256]{1,0:T(8,128)(2,1)S(1)}, bf16[128,256]{1,0:T(8,128)(2,1)}, u32[]{:S(2)}) copy-start(bf16[128,256]{1,0:T(8,128)(2,1)} %constant.118.clone.y_fwd) | copy-start | bytes 196612
  34.5 29.5 %all-to-all-start = ((bf16[16,8,16,384]{3,2,1,0:T(8,128)(2,1)}), bf16[16,8,16,384]{3,2,1,0:T(8,128)(2,1)S(1)}, u32[]{:S(2)}, u32[]{:S(2)}) async-start(bf16[16,8,16,384]{3,2,1,0:T(8,128)(2,1)} %get-tuple-element.55), calls=%async_computation | async-start | bytes 3145728 | tf_op jit(solution)/shard_map/all_to_all | solution.py:287
  42.5 31.9 %copy-start.7 = (bf16[2,2,96,96]{3,2,1,0:T(8,128)(2,1)S(1)}, bf16[2,2,96,96]{3,2,1,0:T(8,128)(2,1)}, u32[]{:S(2)}) copy-start(bf16[2,2,96,96]{3,2,1,0:T(8,128)(2,1)} %param.20) | copy-start | bytes 221188
  65.7 19.9 %all-to-all-start.1 = ((bf16[8,8,16,384]{3,2,1,0:T(8,128)(2,1)}), bf16[8,8,16,384]{3,2,1,0:T(8,128)(2,1)S(1)}, u32[]{:S(2)}, u32[]{:S(2)}) async-start(bf16[8,8,16,384]{3,2,1,0:T(8,128)(2,1)} %y_fwd.2), calls=%async_computation.1 | async-start | bytes 1572864 | tf_op jit(solution)/shard_map/all_to_all | solution.py:289
  74.4 11.2 %copy-start.3 = (bf16[256,128]{1,0:T(8,128)(2,1)S(1)}, bf16[256,128]{1,0:T(8,128)(2,1)}, u32[]{:S(2)}) copy-start(bf16[256,128]{1,0:T(8,128)(2,1)} %constant.120.clone.x_fwd) | copy-start | bytes 196612
  74.4 11.2 %copy-start.4 = (bf16[256,128]{1,0:T(8,128)(2,1)S(1)}, bf16[256,128]{1,0:T(8,128)(2,1)}, u32[]{:S(2)}) copy-start(bf16[256,128]{1,0:T(8,128)(2,1)} %constant.121.clone.x_inv) | copy-start | bytes 196612
  77.6 32.7 %copy-start.2 = (bf16[256,128]{1,0:T(8,128)(2,1)S(1)}, bf16[256,128]{1,0:T(8,128)(2,1)}, u32[]{:S(2)}) copy-start(bf16[256,128]{1,0:T(8,128)(2,1)} %constant.119.clone.y_inv) | copy-start | bytes 196612
  110.8 26.6 %copy-start = (bf16[256,256]{1,0:T(8,128)(2,1)S(1)}, bf16[256,256]{1,0:T(8,128)(2,1)}, u32[]{:S(2)}) copy-start(bf16[256,256]{1,0:T(8,128)(2,1)} %constant.117.clone.z_inv) | copy-start | bytes 393220

commit v2 on v1

--- a/solution.py
+++ b/solution.py
@@ -87,14 +87,11 @@
     return pltpu.roll(value, C, 1)
 
 
-def conv_kernel(tok, xlo, xhi, ylo, yhi, weight, z_fwd, field, freq, shifted, ylo_s, yhi_s, edge, conv):
+def conv_rows(rows, weight, out, shifted):
     pad = jnp.zeros((LY, C), F32)
-    for i in range(LX + 2):
-        row = xlo[0] if i == 0 else xhi[0] if i == LX + 1 else tok[i - 1]
-        shifted[i, :, :] = jnp.concatenate([pad, row.astype(F32), pad], axis=1)
-    pad = jnp.zeros((LX + 2, C), F32)
-    ylo_s[...] = jnp.concatenate([pad, ylo[...].astype(F32), pad], axis=1)
-    yhi_s[...] = jnp.concatenate([pad, yhi[...].astype(F32), pad], axis=1)
+    flat = [row for run in rows for row in run]
+    for i, (ref, x) in enumerate(flat):
+        shifted[i] = jnp.concatenate([pad, ref[x].astype(F32), pad], axis=1)
     row_at = lax.broadcasted_iota(jnp.int32, (LY, 128), 0)
 
     @pl.loop(0, MERGED // 128)
@@ -103,7 +100,54 @@
         after = pl.multiple_of(j * 128 + W, 128)
         here = pl.ds(at, 128)
         phase = pl.multiple_of(lax.rem(j, 3) * 128, 128)
-        taps = [weight[t : t + 1, pl.ds(phase, 128)] for t in range(27)]
+        wide = [jnp.broadcast_to(weight[t : t + 1, pl.ds(phase, 128)], (LY, 128)) for t in range(27)]
+        done = slot = 0
+        for run in rows:
+            sums = {}
+            for i, (ref, x) in enumerate(run):
+                mid = ref[x, :, here].astype(F32)
+                before = shifted[slot, :, here]
+                behind = shifted[slot, :, pl.ds(after, 128)]
+                slot += 1
+                for a in range(3):
+                    to = i - a
+                    if not 0 <= to < len(run) - 2:
+                        continue
+                    for b in range(3):
+                        t = a * 9 + b * 3
+                        term = before * wide[t] + mid * wide[t + 1] + behind * wide[t + 2]
+                        sums[to, b] = sums[to, b] + term if (to, b) in sums else term
+                if i >= 2:
+                    to = i - 2
+                    down = pltpu.roll(sums.pop((to, 0)), 1, 0)
+                    up = pltpu.roll(sums.pop((to, 2)), LY - 1, 0)
+                    down = jnp.where(row_at == 0, 0.0, down)
+                    up = jnp.where(row_at == LY - 1, 0.0, up)
+                    out[done, :, here] = sums.pop((to, 1)) + down + up
+                    done += 1
+
+
+def near_kernel(tok, weight, out, shifted):
+    conv_rows([[(tok, x) for x in range(0, LX // 2 + 1)]], weight, out, shifted)
+
+
+def far_kernel(tok, xlo, xhi, weight, out, shifted):
+    start = [(xlo, 0), (tok, 0), (tok, 1)]
+    end = [(tok, x) for x in range(LX // 2 - 1, LX)] + [(xhi, 0)]
+    conv_rows([start, end], weight, out, shifted)
+
+
+def edge_kernel(near, far, ylo, yhi, weight, z_fwd, field, freq, ylo_s, yhi_s, edge):
+    pad = jnp.zeros((LX + 2, C), F32)
+    ylo_s[...] = jnp.concatenate([pad, ylo[...].astype(F32), pad], axis=1)
+    yhi_s[...] = jnp.concatenate([pad, yhi[...].astype(F32), pad], axis=1)
+
+    @pl.loop(0, MERGED // 128)
+    def _(j):
+        at = pl.multiple_of(j * 128, 128)
+        after = pl.multiple_of(j * 128 + W, 128)
+        here = pl.ds(at, 128)
+        phase = pl.multiple_of(lax.rem(j, 3) * 128, 128)
         for side, rows, rows_s, b in ((0, ylo, ylo_s, 0), (1, yhi, yhi_s, 2)):
             mid = rows[:, here].astype(F32)
             before = rows_s[:, here]
@@ -111,40 +155,25 @@
             total = None
             for a in range(3):
                 t = a * 9 + b * 3
-                term = before * taps[t] + mid * taps[t + 1] + behind * taps[t + 2]
+                taps = [weight[t + e : t + e + 1, pl.ds(phase, 128)] for e in range(3)]
+                term = before * taps[0] + mid * taps[1] + behind * taps[2]
                 term = term[a : a + LX]
                 total = term if total is None else total + term
-            edge[side] = total
-        wide = [jnp.broadcast_to(t, (LY, 128)) for t in taps]
-        sums = {}
-        for i in range(LX + 2):
-            ref = xlo if i == 0 else xhi if i == LX + 1 else tok
-            mid = ref[0 if i in (0, LX + 1) else i - 1, :, here].astype(F32)
-            before = shifted[i, :, here]
-            behind = shifted[i, :, pl.ds(after, 128)]
-            for a in range(3):
-                x = i - a
-                if not 0 <= x < LX:
-                    continue
-                for b in range(3):
-                    t = a * 9 + b * 3
-                    term = before * wide[t] + mid * wide[t + 1] + behind * wide[t + 2]
-                    sums[x, b] = sums[x, b] + term if (x, b) in sums else term
-            x = i - 2
-            if x >= 0:
-                down = pltpu.roll(sums.pop((x, 0)), 1, 0)
-                up = pltpu.roll(sums.pop((x, 2)), LY - 1, 0)
-                down = jnp.where(row_at == 0, edge[0, x : x + 1, :], down)
-                up = jnp.where(row_at == LY - 1, edge[1, x : x + 1, :], up)
-                conv[x, :, here] = sums.pop((x, 1)) + down + up
+            edge[side, :, here] = total
 
     low = low_half(ZH * LY)
-
-    @pl.loop(0, XP)
-    def _(xp):
+    row_at = lax.broadcasted_iota(jnp.int32, (LY, W), 0)
+    for xp in range(XP):
         parts = []
         for x in (2 * xp, 2 * xp + 1):
-            part = jnp.concatenate([conv[x, :, z * W : (z + 1) * W] for z in range(ZH)], axis=0)
+            ref, at = (far, x and x - LX // 2 + 1) if x == 0 or x >= LX // 2 else (near, x - 1)
+            pieces = []
+            for z in range(ZH):
+                here = slice(z * W, (z + 1) * W)
+                more = jnp.where(row_at == 0, edge[0, x : x + 1, here], 0.0)
+                more = jnp.where(row_at == LY - 1, edge[1, x : x + 1, here], more)
+                pieces.append(ref[at, :, here] + more)
+            part = jnp.concatenate(pieces, axis=0)
             field[x] = part.astype(BF16)
             parts.append(part)
         first, second = parts
@@ -178,25 +207,30 @@
 
 
 def spectrum_kernel(given, x_fwd, x_inv, inner, outer, out, rows):
+    count = Q // PX
     low = low_half(2 * PX * XP)
-    for q in range(Q // PX):
-        data = given[:, q].reshape(2 * PX * XP, W)
-        both = dot(x_fwd[...], data)
-        spec = both[: 2 * Q] + swap(both[2 * Q :])
-        spec = spec[:, :256].astype(BF16)
-        mixed = dot(spec, inner[...])
-        hidden_r = jnp.tanh(mixed[:Q, :256] - mixed[Q:, 256:])
-        hidden_i = jnp.tanh(mixed[:Q, 256:] + mixed[Q:, :256])
-        hidden = jnp.concatenate([hidden_r, hidden_i], axis=0).astype(BF16)
-        mixed = dot(hidden, outer[...])
-        filt_r = shrink(mixed[:Q, :W] - mixed[Q:, W:])
-        filt_i = shrink(mixed[:Q, W:] + mixed[Q:, :W])
-        filt = jnp.concatenate([filt_r, filt_i], axis=0).astype(BF16)
-        both = dot(x_inv[...], filt)
-        back = jnp.where(low, both[: 2 * PX * XP], both[2 * PX * XP :])
+    data = [given[:, q].reshape(2 * PX * XP, W) for q in range(count)]
+    both = dot(x_fwd[...], jnp.concatenate(data, axis=1))
+    spec = []
+    for q in range(count):
+        part = both[:, q * W : (q + 1) * W]
+        part = part[: 2 * Q] + swap(part[2 * Q :])
+        spec.append(part[:, :256].astype(BF16))
+    mixed = dot(jnp.concatenate(spec, axis=0), inner[...]).reshape(count, 2, Q, 512)
+    hidden_r = jnp.tanh(mixed[:, 0, :, :256] - mixed[:, 1, :, 256:])
+    hidden_i = jnp.tanh(mixed[:, 0, :, 256:] + mixed[:, 1, :, :256])
+    hidden = jnp.stack([hidden_r, hidden_i], axis=1).astype(BF16).reshape(count * 2 * Q, 256)
+    mixed = dot(hidden, outer[...]).reshape(count, 2, Q, 2 * W)
+    filt_r = shrink(mixed[:, 0, :, :W] - mixed[:, 1, :, W:]).astype(BF16)
+    filt_i = shrink(mixed[:, 0, :, W:] + mixed[:, 1, :, :W]).astype(BF16)
+    filt = [jnp.concatenate([filt_r[q], filt_i[q]], axis=0) for q in range(count)]
+    both = dot(x_inv[...], jnp.concatenate(filt, axis=1))
+    for q in range(count):
+        part = both[:, q * W : (q + 1) * W]
+        back = jnp.where(low, part[: 2 * PX * XP], part[2 * PX * XP :])
         for part in range(2):
             for t in range(W // 128):
-                rows[t, pl.ds(part * (Q // PX) + q, PX * XP, stride=2 * (Q // PX)), :] = back[
+                rows[t, pl.ds(part * count + q, PX * XP, stride=2 * count), :] = back[
                     part * PX * XP : (part + 1) * PX * XP, t * 128 : (t + 1) * 128
                 ]
     gather(rows, out)
@@ -210,9 +244,7 @@
 
 def z_inverse_kernel(given, z_inv, field, out):
     low = low_half(ZH * LY)
-
-    @pl.loop(0, XP)
-    def _(xp):
+    for xp in range(given.shape[1]):
         data = given[:, xp].reshape(2 * KZ * LY, W)
         value = dot(z_inv[...], data)
         even, odd = value[: ZH * LY], value[ZH * LY :]
@@ -237,52 +269,60 @@
     return jax.ShapeDtypeStruct(dims, BF16)
 
 
-def block_diagonal(weight):
-    full = jnp.zeros((2, C, C), weight.dtype)
+def block_diagonal(weight, width):
+    total = 0
     for b in range(C // CB):
-        full = full.at[:, b * CB : (b + 1) * CB, b * CB : (b + 1) * CB].set(weight[:, b])
-    return full
-
-
-def halos(tokens):
-    up_x = [(i, i + 1) for i in range(PX - 1)]
-    down_x = [(j, i) for i, j in up_x]
-    up_y = [(i, i + 1) for i in range(PY - 1)]
-    down_y = [(j, i) for i, j in up_y]
-    xlo = lax.ppermute(tokens[LX - 1 :], "px", up_x)
-    xhi = lax.ppermute(tokens[:1], "px", down_x)
+        total = total + jnp.pad(weight[b], ((b * CB, 256 - (b + 1) * CB), (b * CB, width - (b + 1) * CB)))
+    return total
+
+
+def pairs(count, step):
+    return [(i, i + step) for i in range(count) if 0 <= i + step < count]
+
+
+def halos_x(tokens):
+    return (
+        lax.ppermute(tokens[LX - 1 :], "px", pairs(PX, 1)),
+        lax.ppermute(tokens[:1], "px", pairs(PX, -1)),
+    )
+
+
+def halos_y(tokens, xlo, xhi):
     first, last = (
         jnp.concatenate([xlo[:, y], tokens[:, y], xhi[:, y]], axis=0) for y in (0, LY - 1)
     )
-    ylo = lax.ppermute(last, "py", up_y)
-    yhi = lax.ppermute(first, "py", down_y)
-    return xlo, xhi, ylo, yhi
+    return lax.ppermute(last, "py", pairs(PY, 1)), lax.ppermute(first, "py", pairs(PY, -1))
 
 
 def body(tokens, conv_weight, inner_weight, outer_weight):
     z_fwd, z_inv, y_fwd, y_inv, x_fwd, x_inv = (jnp.asarray(m) for m in matrices())
     weight = jnp.concatenate([conv_weight, conv_weight], axis=1)
-    inner = block_diagonal(inner_weight)
-    inner = jnp.pad(inner, ((0, 0), (0, 256 - C), (0, 256 - C)))
-    inner = jnp.concatenate([inner[0], inner[1]], axis=1)
-    outer = block_diagonal(outer_weight)
-    outer = jnp.pad(outer, ((0, 0), (0, 256 - C), (0, 0)))
+    inner = jnp.concatenate([block_diagonal(w, 256) for w in inner_weight], axis=1)
+    outer = [block_diagonal(w, C) for w in outer_weight]
     outer = jnp.concatenate([outer[0], outer[0], outer[1], outer[1]], axis=1)
 
-    xlo, xhi, ylo, yhi = halos(tokens)
     wide = MERGED + 2 * C
+    xlo, xhi = halos_x(tokens)
+    near = call(
+        near_kernel,
+        jax.ShapeDtypeStruct((LX // 2 - 1, LY, MERGED), F32),
+        [VMEM((LX // 2 + 1, LY, wide), F32)],
+        name="near",
+    )(tokens, weight)
+    ylo, yhi = halos_y(tokens, xlo, xhi)
+    far = call(
+        far_kernel,
+        jax.ShapeDtypeStruct((LX // 2 + 1, LY, MERGED), F32),
+        [VMEM((LX // 2 + 5, LY, wide), F32)],
+        name="far",
+    )(tokens, xlo, xhi, weight)
+    near, inner, outer = lax.optimization_barrier((near, inner, outer))
     field, freq = call(
-        conv_kernel,
+        edge_kernel,
         [shape(LX, ZH * LY, W), shape(KZ, XP, 2 * LY, W)],
-        [
-            VMEM((LX + 2, LY, wide), F32),
-            VMEM((LX + 2, wide), F32),
-            VMEM((LX + 2, wide), F32),
-            VMEM((2, LX, 128), F32),
-            VMEM((LX, LY, MERGED), F32),
-        ],
-        name="conv_z",
-    )(tokens, xlo, xhi, ylo, yhi, weight, z_fwd)
+        [VMEM((LX + 2, wide), F32), VMEM((LX + 2, wide), F32), VMEM((2, LX, MERGED), F32)],
+        name="edge_z",
+    )(near, far, ylo, yhi, weight, z_fwd)
     rows = VMEM((W // 128, 2 * XP * Q, 128), F32)
     freq = lax.all_to_all(freq, "py", 0, 0, tiled=True)
     freq = call(y_forward_kernel, shape(PX, Q // PX, 2 * XP, W), [rows], name="y_fwd")(freq, y_fwd)
@@ -293,7 +333,20 @@
     freq = lax.all_to_all(freq, "px", 0, 0, tiled=True)
     freq = call(y_inverse_kernel, shape(PY, XP, 2 * LY, W), name="y_inv")(freq, y_inv)
     freq = lax.all_to_all(freq, "py", 0, 0, tiled=True)
-    return call(z_inverse_kernel, shape(LX, LY, MERGED), name="z_inv")(freq, z_inv, field)
+    steps = 4
+    return pl.pallas_call(
+        z_inverse_kernel,
+        out_shape=shape(LX, LY, MERGED),
+        grid=(steps,),
+        in_specs=[
+            pl.BlockSpec((KZ, XP // steps, 2 * LY, W), lambda i: (0, i, 0, 0)),
+            pl.BlockSpec(z_inv.shape, lambda i: (0, 0)),
+            pl.BlockSpec((LX // steps, ZH * LY, W), lambda i: (i, 0, 0)),
+        ],
+        out_specs=pl.BlockSpec((LX // steps, LY, MERGED), lambda i: (i, 0, 0)),
+        compiler_params=pltpu.CompilerParams(vmem_limit_bytes=50 * 2**20),
+        name="z_inv",
+    )(freq, z_inv, field)
 
 
 def solution(mesh):

time: 142 us -> 131 us (0.923)
  blocking collectives: 45.4 us -> 91.6 us
  waiting for transfers between devices: 34.2 us -> 0.91 us
  starting transfers between devices: 29.1 us -> 12.4 us
  Pallas kernels: 25 us -> 20 us
  local copies, waits for them, and re-layouts: 6.79 us -> 5.12 us
    all_to_all x1 -> x2, blocking collectives: 26.6 us -> 57 us  [body(): freq = lax.all_to_all(freq, 'py', 0, 0, tiled=True)]
    all_to_all x2 -> x0, waiting for transfers between devices: 29.5 us -> none  [the longest x1 21.4 us: body(): freq = lax.all_to_all(freq, 'py', 0, 0, tiled=True)]
    all_to_all x2 -> x0, starting transfers between devices: 16.7 us -> none  [the longest x1 8.73 us: body(): freq = lax.all_to_all(freq, 'px', 0, 0, tiled=True)]
    all_to_all x1 -> x2, blocking collectives: 18.8 us -> 34.6 us  [body(): freq = lax.all_to_all(freq, 'px', 0, 0, tiled=True)]
    ppermute x4, waiting for transfers between devices: 4.71 us -> 0.91 us  [the longest x1 0.91 us: halos_y(): lax.ppermute(first, 'py', pairs(PY, -1))]
    pallas_call x1, Pallas kernels: 5.88 us -> 2.4 us  [body(): call(spectrum_kernel, shape(PX, XP, 2 * Q // PX, W), [rows], name='spec')]
    scatter x4 -> x0, local copies, waits for them, and re-layouts: 2.82 us -> none  [block_diagonal(): full.at[:, b * CB:(b + 1) * CB, b * CB:(b + 1) * CB].set(weight[:, b])]
    pallas_call x2 -> x4, Pallas kernels: 16.8 us -> 16.2 us  [the longest x1 5.39 us: body(): call(edge_kernel, [shape(LX, ZH * LY, W), shape(KZ, XP, 2 * LY, W)], [VME...]
  transfers between devices with their start and end apart: 6 -> 4, of which waited for: 5 -> 1; matrix products, arithmetic and copies ran while one was open for 4% -> 3% of each run, Pallas kernels for 0% -> 6%
where the time goes in v2:
time: 131 us
  blocking collectives  91.6 us (70%)
  Pallas kernels  20 us (15%)
  starting transfers between devices  12.4 us (9%)
  local copies, waits for them, and re-layouts  5.12 us (4%)
    all_to_all x2, blocking collectives, body(): freq = lax.all_to_all(freq, 'py', 0, 0, tiled=True)  57 us
    all_to_all x2, blocking collectives, body(): freq = lax.all_to_all(freq, 'px', 0, 0, tiled=True)  34.6 us
    pallas_call x1, Pallas kernels, body(): call(edge_kernel, [shape(LX, ZH * LY, W), shape(KZ, XP, 2 * LY, W)], [VME...  5.39 us
    ppermute x1, starting transfers between devices, halos_x(): lax.ppermute(tokens[LX - 1:], 'px', pairs(PX, 1))  4.8 us
    ppermute x1, starting transfers between devices, halos_y(): lax.ppermute(last, 'py', pairs(PY, 1))  4.4 us
    pallas_call x1, Pallas kernels, body(): call(far_kernel, jax.ShapeDtypeStruct((LX // 2 + 1, LY, MERGED), F32), [V...  4.36 us
    pallas_call x1, Pallas kernels, body(): call(near_kernel, jax.ShapeDtypeStruct((LX // 2 - 1, LY, MERGED), F32), [...  3.53 us
    pallas_call x1, Pallas kernels, body(): pl.pallas_call(z_inverse_kernel, out_shape=shape(LX, LY, MERGED), grid=(s...  2.91 us
  transfers between devices with their start and end apart: 4, of which 1 were waited for; matrix products, arithmetic and copies ran while one was open for 3% of the time, Pallas kernels for 6%

profile of v2, /device:TPU:1, one launch (start us, length us, event | category | flops | bytes accessed | tf_op | source)
XLA Modules:
  0.0 131.0 jit_solution(6704492248329760504)
XLA Ops:
  0.0 1.0 fusion.1
  1.0 1.3 collective-permute-start.1
  2.3 0.0 copy-start
  2.3 4.8 %collective-permute-start = (bf16[1,8,6144]{2,1,0:T(8,128)(2,1)S(1)}, bf16[1,8,6144]{2,1,0:T(8,128)(2,1)S(1)}, u32[]{:S(2)}, u32[]{:S(2)}) collective-permute-start(bf16[1,8,6144]{2,1,0:T(8,128)(2,1)S(1)} %get-tuple-element.18), channel_id=1, source_target_pairs={{0,16},{16,32},{32,48},{48,64},{64,80},{80,96},{96,112},{1,17},{17... | collective-permute-start | bytes 294920 | tf_op jit(solution)/shard_map/ppermute | solution.py:285
  7.1 2.5 %fusion = (bf16[16,1,6144]{2,1,0:T(2,128)(2,1)S(1)}, bf16[16,1,6144]{2,1,0:T(2,128)(2,1)S(1)}) fusion(bf16[16,8,6144]{2,1,0:T(8,128)(2,1)} %tok.3), kind=kLoop, calls=%fused_computation.23 | loop fusion | bytes 786432 | tf_op jit(solution)/shard_map/slice | solution.py:292
  9.7 0.1 pad_maximum_fusion.4.weight
  9.8 0.1 copy.17
  9.9 0.1 copy.18
  10.0 3.5 %near.1 = f32[7,8,6144]{2,1,0:T(8,128)S(1)} custom-call(bf16[16,8,6144]{2,1,0:T(8,128)(2,1)S(1)} %copy-done, f32[27,384]{1,0:T(8,128)S(1)} %pad_maximum_fusion.4.weight), custom_call_target="tpu_custom_call" | custom-call | tf_op jit(solution)/shard_map/near/pallas_call | solution.py:306
  13.6 0.1 pad_add_fusion.2
  13.7 0.0 collective-permute-done.1.xhi
  13.8 0.0 collective-permute-done.xlo
  13.8 0.1 pad_maximum_fusion.1
  13.9 4.4 %collective-permute-start.2 = (bf16[18,6144]{1,0:T(8,128)(2,1)S(1)}, bf16[18,6144]{1,0:T(8,128)(2,1)S(1)}, u32[]{:S(2)}, u32[]{:S(2)}) collective-permute-start(bf16[18,6144]{1,0:T(8,128)(2,1)S(1)} %pad_maximum_fusion.1), channel_id=1, source_target_pairs={{0,1},{1,2},{2,3},{3,4},{4,5},{5,6},{6,7},{7,8},{8,9},{9,10},{10,1... | collective-permute-start | bytes 663560 | tf_op jit(solution)/shard_map/ppermute | solution.py:294
  18.4 0.1 pad_maximum_fusion.2
  18.5 1.9 %collective-permute-start.3 = (bf16[18,6144]{1,0:T(8,128)(2,1)S(1)}, bf16[18,6144]{1,0:T(8,128)(2,1)S(1)}, u32[]{:S(2)}, u32[]{:S(2)}) collective-permute-start(bf16[18,6144]{1,0:T(8,128)(2,1)S(1)} %pad_maximum_fusion.2), channel_id=1, source_target_pairs={{1,0},{2,1},{3,2},{4,3},{5,4},{6,5},{7,6},{8,7},{9,8},{10,9},{11,1... | collective-permute-start | bytes 663560 | tf_op jit(solution)/shard_map/ppermute | solution.py:294
  20.4 0.1 pad_add_fusion
  20.5 0.2 pad_maximum_fusion.outer
  20.7 0.0 copy-start.3
  20.7 4.4 %far.1 = f32[9,8,6144]{2,1,0:T(8,128)S(1)} custom-call(bf16[16,8,6144]{2,1,0:T(8,128)(2,1)S(1)} %copy-done, bf16[1,8,6144]{2,1,0:T(8,128)(2,1)S(1)} %collective-permute-done.xlo, bf16[1,8,6144]{2,1,0:T(8,128)(2,1)S(1)} %collective-permute-done.1.xhi, f32[27,384]{1,0:T(8,128)S(1)} %pad_maximum_fusion.4.weight), custom_call_target="tpu_custom_call" | custom-call | tf_op jit(solution)/shard_map/far/pallas_call | solution.py:313
  25.1 1.2 copy-done.1
  26.3 0.9 collective-permute-done.3.yhi
  27.2 5.4 %edge_z.1 = (bf16[16,128,384]{2,1,0:T(8,128)(2,1)S(1)}, bf16[16,8,16,384]{3,2,1,0:T(8,128)(2,1)}) custom-call(f32[7,8,6144]{2,1,0:T(8,128)S(1)} %near.1, f32[9,8,6144]{2,1,0:T(8,128)} %copy-done.1, bf16[18,6144]{1,0:T(8,128)(2,1)S(1)} %collective-permute-done.2.ylo, bf16[18,6144]{1,0:T(8,128)(2,1)S(1)} %collective-permute-done.3.yhi, ...), custom_call_target="tpu_custom_call" | custom-call | tf_op jit(solution)/shard_map/edge_z/pallas_call | solution.py:320
  32.6 27.7 %all_to_all.20.given = bf16[16,8,16,384]{3,2,1,0:T(8,128)(2,1)S(1)} all-to-all(bf16[16,8,16,384]{3,2,1,0:T(8,128)(2,1)} %get-tuple-element.11), channel_id=1, replica_groups=mesh['px'=8,'py'=16] {'py'}, dimensions={0} | all-to-all | bytes 3145728 | tf_op jit(solution)/shard_map/all_to_all | solution.py:327
  60.3 0.8 y_fwd.2
  61.1 19.4 %all_to_all.21.given = bf16[8,8,16,384]{3,2,1,0:T(8,128)(2,1)S(1)} all-to-all(bf16[8,8,16,384]{3,2,1,0:T(8,128)(2,1)S(1)} %y_fwd.2), channel_id=1, replica_groups=mesh['px'=8,'py'=16] {'px'}, dimensions={0} | all-to-all | bytes 1572864 | tf_op jit(solution)/shard_map/all_to_all | solution.py:329
  80.6 2.4 %spec.1 = bf16[8,8,16,384]{3,2,1,0:T(8,128)(2,1)S(1)} custom-call(bf16[8,8,16,384]{3,2,1,0:T(8,128)(2,1)S(1)} %all_to_all.21.given, bf16[256,128]{1,0:T(8,128)(2,1)S(1)} %copy-done.6, bf16[256,128]{1,0:T(8,128)(2,1)S(1)} %copy-done.5, bf16[256,512]{1,0:T(8,128)(2,1)S(1)} %pad_maximum_fusion.3.inner, bf16[256,768]{1,0:T(8,128)(2,1)S(1)} %pad_maximum_fusion.outer), custom_call_target="tpu_custom_call" | custom-call | tf_op jit(solution)/shard_map/spec/pallas_call | solution.py:330
  83.0 15.2 %all_to_all.22.given = bf16[8,8,16,384]{3,2,1,0:T(8,128)(2,1)S(1)} all-to-all(bf16[8,8,16,384]{3,2,1,0:T(8,128)(2,1)S(1)} %spec.1), channel_id=1, replica_groups=mesh['px'=8,'py'=16] {'px'}, dimensions={0} | all-to-all | bytes 1572864 | tf_op jit(solution)/shard_map/all_to_all | solution.py:333
  98.2 0.6 y_inv.2
  98.7 0.0 copy-start.2
  98.7 29.3 %all_to_all.23.given = bf16[16,8,16,384]{3,2,1,0:T(8,128)(2,1)S(1)} all-to-all(bf16[16,8,16,384]{3,2,1,0:T(8,128)(2,1)S(1)} %y_inv.2), channel_id=1, replica_groups=mesh['px'=8,'py'=16] {'py'}, dimensions={0} | all-to-all | bytes 3145728 | tf_op jit(solution)/shard_map/all_to_all | solution.py:335
  128.1 2.9 %z_inv.2 = bf16[16,8,6144]{2,1,0:T(8,128)(2,1)} custom-call(bf16[16,8,16,384]{3,2,1,0:T(8,128)(2,1)S(1)} %all_to_all.23.given, bf16[256,256]{1,0:T(8,128)(2,1)S(1)} %copy-done.2, bf16[16,128,384]{2,1,0:T(8,128)(2,1)S(1)} %get-tuple-element.14.field), custom_call_target="tpu_custom_call" | custom-call | tf_op jit(solution)/shard_map/z_inv/pallas_call | solution.py:337
  (24 shorter events, 0.1 us)
Async XLA Ops:
  0.0 9.7 %copy-start.10 = (f32[27,192]{1,0:T(8,128)S(1)}, f32[27,192]{1,0:T(8,128)}, u32[]{:S(2)}) copy-start(f32[27,192]{1,0:T(8,128)} %param.11) | copy-start | bytes 62212
  0.0 9.7 %copy-start.8 = (bf16[2,2,96,96]{3,2,1,0:T(8,128)(2,1)S(1)}, bf16[2,2,96,96]{3,2,1,0:T(8,128)(2,1)}, u32[]{:S(2)}) copy-start(bf16[2,2,96,96]{3,2,1,0:T(8,128)(2,1)} %param.12) | copy-start | bytes 221188
  0.0 9.8 %copy-start.9 = (bf16[2,2,96,96]{3,2,1,0:T(8,128)(2,1)S(1)}, bf16[2,2,96,96]{3,2,1,0:T(8,128)(2,1)}, u32[]{:S(2)}) copy-start(bf16[2,2,96,96]{3,2,1,0:T(8,128)(2,1)} %param.13) | copy-start | bytes 221188
  1.0 12.7 %collective-permute-start.1 = (bf16[1,8,6144]{2,1,0:T(8,128)(2,1)S(1)}, bf16[1,8,6144]{2,1,0:T(8,128)(2,1)S(1)}, u32[]{:S(2)}, u32[]{:S(2)}) collective-permute-start(bf16[1,8,6144]{2,1,0:T(8,128)(2,1)S(1)} %get-tuple-element.17), channel_id=1, source_target_pairs={{16,0},{32,16},{48,32},{64,48},{80,64},{96,80},{112,96},{17,1},{33... | collective-permute-start | bytes 294920 | tf_op jit(solution)/shard_map/ppermute | solution.py:286
  2.3 7.7 %copy-start = (bf16[16,8,6144]{2,1,0:T(8,128)(2,1)S(1)}, bf16[16,8,6144]{2,1,0:T(8,128)(2,1)}, u32[]{:S(2)}) copy-start(bf16[16,8,6144]{2,1,0:T(8,128)(2,1)} %tok.3) | copy-start | bytes 4718596
  2.3 11.4 %collective-permute-start = (bf16[1,8,6144]{2,1,0:T(8,128)(2,1)S(1)}, bf16[1,8,6144]{2,1,0:T(8,128)(2,1)S(1)}, u32[]{:S(2)}, u32[]{:S(2)}) collective-permute-start(bf16[1,8,6144]{2,1,0:T(8,128)(2,1)S(1)} %get-tuple-element.18), channel_id=1, source_target_pairs={{0,16},{16,32},{32,48},{48,64},{64,80},{80,96},{96,112},{1,17},{17... | collective-permute-start | bytes 294920 | tf_op jit(solution)/shard_map/ppermute | solution.py:285
  13.9 12.4 %collective-permute-start.2 = (bf16[18,6144]{1,0:T(8,128)(2,1)S(1)}, bf16[18,6144]{1,0:T(8,128)(2,1)S(1)}, u32[]{:S(2)}, u32[]{:S(2)}) collective-permute-start(bf16[18,6144]{1,0:T(8,128)(2,1)S(1)} %pad_maximum_fusion.1), channel_id=1, source_target_pairs={{0,1},{1,2},{2,3},{3,4},{4,5},{5,6},{6,7},{7,8},{8,9},{9,10},{10,1... | collective-permute-start | bytes 663560 | tf_op jit(solution)/shard_map/ppermute | solution.py:294
  18.5 8.7 %collective-permute-start.3 = (bf16[18,6144]{1,0:T(8,128)(2,1)S(1)}, bf16[18,6144]{1,0:T(8,128)(2,1)S(1)}, u32[]{:S(2)}, u32[]{:S(2)}) collective-permute-start(bf16[18,6144]{1,0:T(8,128)(2,1)S(1)} %pad_maximum_fusion.2), channel_id=1, source_target_pairs={{1,0},{2,1},{3,2},{4,3},{5,4},{6,5},{7,6},{8,7},{9,8},{10,9},{11,1... | collective-permute-start | bytes 663560 | tf_op jit(solution)/shard_map/ppermute | solution.py:294
  20.7 6.5 %copy-start.3 = (bf16[256,256]{1,0:T(8,128)(2,1)S(1)}, bf16[256,256]{1,0:T(8,128)(2,1)}, u32[]{:S(2)}) copy-start(bf16[256,256]{1,0:T(8,128)(2,1)} %constant.15.clone.z_fwd) | copy-start | bytes 393220
  25.1 1.2 copy-start.1
  32.6 27.7 %copy-start.7 = (bf16[128,256]{1,0:T(8,128)(2,1)S(1)}, bf16[128,256]{1,0:T(8,128)(2,1)}, u32[]{:S(2)}) copy-start(bf16[128,256]{1,0:T(8,128)(2,1)} %constant.17.clone.y_fwd) | copy-start | bytes 196612
  60.3 20.3 %copy-start.5 = (bf16[256,128]{1,0:T(8,128)(2,1)S(1)}, bf16[256,128]{1,0:T(8,128)(2,1)}, u32[]{:S(2)}) copy-start(bf16[256,128]{1,0:T(8,128)(2,1)} %constant.20.clone.x_inv) | copy-start | bytes 196612
  60.3 20.3 %copy-start.6 = (bf16[256,128]{1,0:T(8,128)(2,1)S(1)}, bf16[256,128]{1,0:T(8,128)(2,1)}, u32[]{:S(2)}) copy-start(bf16[256,128]{1,0:T(8,128)(2,1)} %constant.19.clone.x_fwd) | copy-start | bytes 196612
  80.6 17.6 %copy-start.4 = (bf16[256,128]{1,0:T(8,128)(2,1)S(1)}, bf16[256,128]{1,0:T(8,128)(2,1)}, u32[]{:S(2)}) copy-start(bf16[256,128]{1,0:T(8,128)(2,1)} %constant.18.clone.y_inv) | copy-start | bytes 196612
  98.7 29.4 %copy-start.2 = (bf16[256,256]{1,0:T(8,128)(2,1)S(1)}, bf16[256,256]{1,0:T(8,128)(2,1)}, u32[]{:S(2)}) copy-start(bf16[256,256]{1,0:T(8,128)(2,1)} %constant.16.clone.z_inv) | copy-start | bytes 393220

commit v3 on v2

--- a/solution.py
+++ b/solution.py
@@ -72,7 +72,11 @@
     x_fwd = x_fwd.transpose(5, 0, 1, 3, 2, 4).reshape(4 * Q, 2 * PX * XP)
     x_inv = backward(cx, sx).reshape(2, PX, XP, 2, 2, Q)
     x_inv = x_inv.transpose(3, 0, 1, 2, 4, 5).reshape(4 * PX * XP, 2 * Q)
-    return [as_bf16(m) for m in (z_fwd, z_inv, y_fwd, y_inv, x_fwd, x_inv)]
+    pick = np.zeros((64, LX + 2, LY))
+    for i in range(LX + 2):
+        pick[i, i, 0] = pick[32 + i, i, LY - 1] = 1
+    pick = pick.reshape(64, (LX + 2) * LY)
+    return [as_bf16(m) for m in (z_fwd, z_inv, y_fwd, y_inv, x_fwd, x_inv, pick)]
 
 
 def dot(a, b):
@@ -127,17 +131,61 @@
                     done += 1
 
 
-def near_kernel(tok, weight, out, shifted):
-    conv_rows([[(tok, x) for x in range(0, LX // 2 + 1)]], weight, out, shifted)
-
-
-def far_kernel(tok, xlo, xhi, weight, out, shifted):
-    start = [(xlo, 0), (tok, 0), (tok, 1)]
-    end = [(tok, x) for x in range(LX // 2 - 1, LX)] + [(xhi, 0)]
-    conv_rows([start, end], weight, out, shifted)
-
-
-def edge_kernel(near, far, ylo, yhi, weight, z_fwd, field, freq, ylo_s, yhi_s, edge):
+PIECES = (((1, 5),), ((5, 8),), ((8, 11),), ((0, 1), (11, 16)))
+
+
+def piece_kernel(runs, *refs):
+    if len(refs) == 4:
+        tok, weight, out, shifted = refs
+    else:
+        tok, xlo, xhi, weight, out, shifted = refs
+    rows = []
+    for first, end in runs:
+        run = [(tok, x) for x in range(max(first - 1, 0), min(end + 1, LX))]
+        if first == 0:
+            run = [(xlo, 0)] + run
+        if end == LX:
+            run = run + [(xhi, 0)]
+        rows.append(run)
+    conv_rows(rows, weight, out, shifted)
+
+
+def piece(at, *operands):
+    runs = PIECES[at]
+    made = sum(end - first for first, end in runs)
+    wide = MERGED + 2 * C
+    return call(
+        functools.partial(piece_kernel, runs),
+        jax.ShapeDtypeStruct((made, LY, MERGED), F32),
+        [VMEM((made + 2 * len(runs), LY, wide), F32)],
+        name=f"conv{at}",
+        cost=pl.CostEstimate(flops=1, bytes_accessed=1, transcendentals=0),
+    )(*operands)
+
+
+def find(x):
+    for at, runs in enumerate(PIECES):
+        row = 0
+        for first, end in runs:
+            if first <= x < end:
+                return at, row + x - first
+            row += end - first
+
+
+def rows_kernel(tok, xlo, xhi, pick, first, last):
+    step = MERGED // 4
+    for j in range(4):
+        here = slice(j * step, (j + 1) * step)
+        parts = [ref[:, :, here].astype(F32) for ref in (xlo, tok, xhi)]
+        data = jnp.concatenate(parts, axis=0).reshape((LX + 2) * LY, step).astype(BF16)
+        out = dot(pick[...], data).astype(BF16)
+        first[:, here] = out[: LX + 2]
+        last[:, here] = out[32 : 32 + LX + 2]
+
+
+def edge_kernel(*refs):
+    pieces, refs = refs[: len(PIECES)], refs[len(PIECES) :]
+    ylo, yhi, weight, z_fwd, field, freq, ylo_s, yhi_s, edge = refs
     pad = jnp.zeros((LX + 2, C), F32)
     ylo_s[...] = jnp.concatenate([pad, ylo[...].astype(F32), pad], axis=1)
     yhi_s[...] = jnp.concatenate([pad, yhi[...].astype(F32), pad], axis=1)
@@ -166,14 +214,15 @@
     for xp in range(XP):
         parts = []
         for x in (2 * xp, 2 * xp + 1):
-            ref, at = (far, x and x - LX // 2 + 1) if x == 0 or x >= LX // 2 else (near, x - 1)
-            pieces = []
+            ref, at = find(x)
+            ref = pieces[ref]
+            rows = []
             for z in range(ZH):
                 here = slice(z * W, (z + 1) * W)
                 more = jnp.where(row_at == 0, edge[0, x : x + 1, here], 0.0)
                 more = jnp.where(row_at == LY - 1, edge[1, x : x + 1, here], more)
-                pieces.append(ref[at, :, here] + more)
-            part = jnp.concatenate(pieces, axis=0)
+                rows.append(ref[at, :, here] + more)
+            part = jnp.concatenate(rows, axis=0)
             field[x] = part.astype(BF16)
             parts.append(part)
         first, second = parts
@@ -255,12 +304,13 @@
                 out[x, :, z * W : (z + 1) * W] = value[z * LY : (z + 1) * LY].astype(BF16)
 
 
-def call(kernel, outs, scratch=(), name=None):
+def call(kernel, outs, scratch=(), name=None, cost=None):
     return pl.pallas_call(
         kernel,
         out_shape=outs,
         scratch_shapes=list(scratch),
-        compiler_params=pltpu.CompilerParams(vmem_limit_bytes=50 * 2**20),
+        compiler_params=pltpu.CompilerParams(vmem_limit_bytes=20 * 2**20),
+        cost_estimate=cost,
         name=name,
     )
 
@@ -280,49 +330,35 @@
     return [(i, i + step) for i in range(count) if 0 <= i + step < count]
 
 
-def halos_x(tokens):
-    return (
-        lax.ppermute(tokens[LX - 1 :], "px", pairs(PX, 1)),
-        lax.ppermute(tokens[:1], "px", pairs(PX, -1)),
-    )
-
-
-def halos_y(tokens, xlo, xhi):
-    first, last = (
-        jnp.concatenate([xlo[:, y], tokens[:, y], xhi[:, y]], axis=0) for y in (0, LY - 1)
-    )
-    return lax.ppermute(last, "py", pairs(PY, 1)), lax.ppermute(first, "py", pairs(PY, -1))
-
-
 def body(tokens, conv_weight, inner_weight, outer_weight):
-    z_fwd, z_inv, y_fwd, y_inv, x_fwd, x_inv = (jnp.asarray(m) for m in matrices())
+    z_fwd, z_inv, y_fwd, y_inv, x_fwd, x_inv, pick = (jnp.asarray(m) for m in matrices())
     weight = jnp.concatenate([conv_weight, conv_weight], axis=1)
     inner = jnp.concatenate([block_diagonal(w, 256) for w in inner_weight], axis=1)
     outer = [block_diagonal(w, C) for w in outer_weight]
     outer = jnp.concatenate([outer[0], outer[0], outer[1], outer[1]], axis=1)
 
     wide = MERGED + 2 * C
-    xlo, xhi = halos_x(tokens)
-    near = call(
-        near_kernel,
-        jax.ShapeDtypeStruct((LX // 2 - 1, LY, MERGED), F32),
-        [VMEM((LX // 2 + 1, LY, wide), F32)],
-        name="near",
-    )(tokens, weight)
-    ylo, yhi = halos_y(tokens, xlo, xhi)
-    far = call(
-        far_kernel,
-        jax.ShapeDtypeStruct((LX // 2 + 1, LY, MERGED), F32),
-        [VMEM((LX // 2 + 5, LY, wide), F32)],
-        name="far",
-    )(tokens, xlo, xhi, weight)
-    near, inner, outer = lax.optimization_barrier((near, inner, outer))
+    xlo = lax.ppermute(tokens[LX - 1 :], "px", pairs(PX, 1))
+    piece0 = piece(0, tokens, weight)
+    piece0, bottom, xlo = lax.optimization_barrier((piece0, tokens[:1], xlo))
+    xhi = lax.ppermute(bottom, "px", pairs(PX, -1))
+    tokens, bottom = lax.optimization_barrier((tokens, bottom))
+    piece1 = piece(1, tokens, weight)
+    piece1, xlo, xhi = lax.optimization_barrier((piece1, xlo, xhi))
+    first, last = call(rows_kernel, [shape(LX + 2, MERGED)] * 2, name="y_rows")(tokens, xlo, xhi, pick)
+    ylo = lax.ppermute(last, "py", pairs(PY, 1))
+    tokens, last = lax.optimization_barrier((tokens, last))
+    piece2 = piece(2, tokens, weight)
+    piece2, first = lax.optimization_barrier((piece2, first))
+    yhi = lax.ppermute(first, "py", pairs(PY, -1))
+    piece3 = piece(3, tokens, xlo, xhi, weight)
+    piece3, inner, outer = lax.optimization_barrier((piece3, inner, outer))
     field, freq = call(
         edge_kernel,
         [shape(LX, ZH * LY, W), shape(KZ, XP, 2 * LY, W)],
         [VMEM((LX + 2, wide), F32), VMEM((LX + 2, wide), F32), VMEM((2, LX, MERGED), F32)],
         name="edge_z",
-    )(near, far, ylo, yhi, weight, z_fwd)
+    )(piece0, piece1, piece2, piece3, ylo, yhi, weight, z_fwd)
     rows = VMEM((W // 128, 2 * XP * Q, 128), F32)
     freq = lax.all_to_all(freq, "py", 0, 0, tiled=True)
     freq = call(y_forward_kernel, shape(PX, Q // PX, 2 * XP, W), [rows], name="y_fwd")(freq, y_fwd)
@@ -344,7 +380,7 @@
             pl.BlockSpec((LX // steps, ZH * LY, W), lambda i: (i, 0, 0)),
         ],
         out_specs=pl.BlockSpec((LX // steps, LY, MERGED), lambda i: (i, 0, 0)),
-        compiler_params=pltpu.CompilerParams(vmem_limit_bytes=50 * 2**20),
+        compiler_params=pltpu.CompilerParams(vmem_limit_bytes=20 * 2**20),
         name="z_inv",
     )(freq, z_inv, field)
 

time: 131 us -> 136 us (1.038)
  waiting for transfers between devices: 0.91 us -> 4.68 us
  blocking collectives: 91.6 us -> 93.2 us
    ppermute x4, waiting for transfers between devices: 0.91 us -> 4.68 us  [the longest x1 2.61 us: body(): yhi = lax.ppermute(first, 'py', pairs(PY, -1))]
    pallas_call x1, Pallas kernels: 5.39 us -> 2.75 us  [body(): call(edge_kernel, [shape(LX, ZH * LY, W), shape(KZ, XP, 2 * LY, W)], [VME...]
    slice x2 -> x1, local copies, waits for them, and re-layouts: 3.52 us -> 0.95 us  [body(): xlo = lax.ppermute(tokens[LX - 1:], 'px', pairs(PX, 1))]
    pallas_call x2 -> x5, Pallas kernels: 7.89 us -> 9.87 us  [the longest x4 9.49 us: piece(): call(functools.partial(piece_kernel, runs), jax.ShapeDtypeStruct((made, L...]
    squeeze x2, local copies, waits for them, and re-layouts: 0.02 us -> 1.6 us  [block_diagonal(): weight[b]]
  transfers between devices with their start and end apart: 4 -> 4, of which waited for: 1 -> 2; matrix products, arithmetic and copies ran while one was open for 3% -> 2% of each run, Pallas kernels for 6% -> 7%
where the time goes in v3:
time: 136 us; the launch traced here: 135 us
  blocking collectives  93.2 us (69%)
  Pallas kernels  19.3 us (14%)
  starting transfers between devices  12.4 us (9%)
  waiting for transfers between devices  4.68 us (3%)
  local copies, waits for them, and re-layouts  3.99 us (3%)
    all_to_all x2, blocking collectives, body(): freq = lax.all_to_all(freq, 'py', 0, 0, tiled=True)  57.5 us
    all_to_all x2, blocking collectives, body(): freq = lax.all_to_all(freq, 'px', 0, 0, tiled=True)  35.7 us
    pallas_call x4, Pallas kernels, piece(): call(functools.partial(piece_kernel, runs), jax.ShapeDtypeStruct((made, L...  9.49 us
    ppermute x1, starting transfers between devices, body(): ylo = lax.ppermute(last, 'py', pairs(PY, 1))  5.1 us
    ppermute x1, starting transfers between devices, body(): xlo = lax.ppermute(tokens[LX - 1:], 'px', pairs(PX, 1))  4.04 us
    pallas_call x1, Pallas kernels, body(): pl.pallas_call(z_inverse_kernel, out_shape=shape(LX, LY, MERGED), grid=(s...  2.91 us
    pallas_call x1, Pallas kernels, body(): call(edge_kernel, [shape(LX, ZH * LY, W), shape(KZ, XP, 2 * LY, W)], [VME...  2.75 us
  transfers between devices with their start and end apart: 4, of which 2 were waited for; matrix products, arithmetic and copies ran while one was open for 2% of the time, Pallas kernels for 7%

profile of v3, /device:TPU:1, one launch (start us, length us, event | category | flops | bytes accessed | tf_op | source)
XLA Modules:
  0.0 135.1 jit_solution(18151943502268929637)
XLA Ops:
  0.0 1.0 fusion
  1.0 4.0 %collective-permute-start = (bf16[1,8,6144]{2,1,0:T(8,128)(2,1)S(1)}, bf16[1,8,6144]{2,1,0:T(8,128)(2,1)S(1)}, u32[]{:S(2)}, u32[]{:S(2)}) collective-permute-start(bf16[1,8,6144]{2,1,0:T(8,128)(2,1)S(1)} %get-tuple-element.39), channel_id=1, source_target_pairs={{0,16},{16,32},{32,48},{48,64},{64,80},{80,96},{96,112},{1,17},{17... | collective-permute-start | bytes 294920 | tf_op jit(solution)/shard_map/ppermute | solution.py:341
  5.0 0.9 pad_maximum_fusion.2.refs_1_.refs_3_.refs_6_
  5.9 0.8 slice_bitcast_fusion.7
  6.7 0.8 slice_bitcast_fusion.3
  7.5 1.4 %copy-done = bf16[16,8,6144]{2,1,0:T(8,128)(2,1)S(1)} copy-done((bf16[16,8,6144]{2,1,0:T(8,128)(2,1)S(1)}, bf16[16,8,6144]{2,1,0:T(8,128)(2,1)}, u32[]{:S(2)}) %copy-start) | copy-done | bytes 1572888
  8.9 2.4 %conv0.1.refs_0_ = f32[4,8,6144]{2,1,0:T(8,128)S(1)} custom-call(bf16[16,8,6144]{2,1,0:T(8,128)(2,1)S(1)} %copy-done, f32[27,384]{1,0:T(8,128)S(1)} %pad_maximum_fusion.2.refs_1_.refs_3_.refs_6_), custom_call_target="tpu_custom_call" | custom-call | flops 1 | bytes 1 | tf_op jit(solution)/shard_map/conv0/pallas_call | solution.py:157
  11.3 0.0 copy-start.7
  11.3 0.1 pad_add_fusion.2
  11.4 1.3 collective-permute-start.1
  12.7 2.0 %conv1.1.refs_1_ = f32[3,8,6144]{2,1,0:T(8,128)S(1)} custom-call(bf16[16,8,6144]{2,1,0:T(8,128)(2,1)S(1)} %copy-done, f32[27,384]{1,0:T(8,128)S(1)} %pad_maximum_fusion.2.refs_1_.refs_3_.refs_6_), custom_call_target="tpu_custom_call" | custom-call | flops 1 | bytes 1 | tf_op jit(solution)/shard_map/conv1/pallas_call | solution.py:157
  14.7 2.1 %collective-permute-done.1.xhi.refs_2_ = bf16[1,8,6144]{2,1,0:T(8,128)(2,1)S(1)} collective-permute-done((bf16[1,8,6144]{2,1,0:T(8,128)(2,1)S(1)}, bf16[1,8,6144]{2,1,0:T(8,128)(2,1)S(1)}, u32[]{:S(2)}, u32[]{:S(2)}) %collective-permute-start.1) | collective-permute-done | bytes 98336 | tf_op jit(solution)/shard_map/ppermute | solution.py:344
  16.8 0.4 y_rows.1
  17.2 5.1 %collective-permute-start.2 = (bf16[18,6144]{1,0:T(8,128)(2,1)S(1)}, bf16[18,6144]{1,0:T(8,128)(2,1)S(1)}, u32[]{:S(2)}, u32[]{:S(2)}) collective-permute-start(bf16[18,6144]{1,0:T(8,128)(2,1)S(1)} %get-tuple-element.29), channel_id=1, source_target_pairs={{0,1},{1,2},{2,3},{3,4},{4,5},{5,6},{6,7},{7,8},{8,9},{9,10},{10,1... | collective-permute-start | bytes 663560 | tf_op jit(solution)/shard_map/ppermute | solution.py:349
  22.3 2.0 %conv2.1.refs_2_ = f32[3,8,6144]{2,1,0:T(8,128)S(1)} custom-call(bf16[16,8,6144]{2,1,0:T(8,128)(2,1)S(1)} %copy-done, f32[27,384]{1,0:T(8,128)S(1)} %pad_maximum_fusion.2.refs_1_.refs_3_.refs_6_), custom_call_target="tpu_custom_call" | custom-call | flops 1 | bytes 1 | tf_op jit(solution)/shard_map/conv2/pallas_call | solution.py:157
  24.3 1.9 %collective-permute-start.3 = (bf16[18,6144]{1,0:T(8,128)(2,1)S(1)}, bf16[18,6144]{1,0:T(8,128)(2,1)S(1)}, u32[]{:S(2)}, u32[]{:S(2)}) collective-permute-start(bf16[18,6144]{1,0:T(8,128)(2,1)S(1)} %get-tuple-element.34), channel_id=1, source_target_pairs={{1,0},{2,1},{3,2},{4,3},{5,4},{6,5},{7,6},{8,7},{9,8},{10,9},{11,1... | collective-permute-start | bytes 663560 | tf_op jit(solution)/shard_map/ppermute | solution.py:353
  26.2 0.1 pad_add_fusion
  26.3 0.2 pad_maximum_fusion.outer
  26.5 0.0 copy-start.2
  26.5 3.2 %conv3.1.refs_3_ = f32[6,8,6144]{2,1,0:T(8,128)S(1)} custom-call(bf16[16,8,6144]{2,1,0:T(8,128)(2,1)S(1)} %copy-done, bf16[1,8,6144]{2,1,0:T(8,128)(2,1)S(1)} %collective-permute-done.xlo.refs_1_, bf16[1,8,6144]{2,1,0:T(8,128)(2,1)S(1)} %collective-permute-done.1.xhi.refs_2_, f32[27,384]{1,0:T(8,128)S(1)} %pad_maximum_fusion.2.refs_1_.refs_3_.refs_6_), custom_call_target="tpu_custom_call" | custom-call | flops 1 | bytes 1 | tf_op jit(solution)/shard_map/conv3/pallas_call | solution.py:157
  29.7 2.6 %collective-permute-done.3.refs_5_ = bf16[18,6144]{1,0:T(8,128)(2,1)S(1)} collective-permute-done((bf16[18,6144]{1,0:T(8,128)(2,1)S(1)}, bf16[18,6144]{1,0:T(8,128)(2,1)S(1)}, u32[]{:S(2)}, u32[]{:S(2)}) %collective-permute-start.3) | collective-permute-done | bytes 221216 | tf_op jit(solution)/shard_map/ppermute | solution.py:353
  32.3 2.7 %edge_z.1 = (bf16[16,128,384]{2,1,0:T(8,128)(2,1)S(1)}, bf16[16,8,16,384]{3,2,1,0:T(8,128)(2,1)S(1)}) custom-call(f32[4,8,6144]{2,1,0:T(8,128)S(1)} %conv0.1.refs_0_, f32[3,8,6144]{2,1,0:T(8,128)S(1)} %conv1.1.refs_1_, f32[3,8,6144]{2,1,0:T(8,128)S(1)} %conv2.1.refs_2_, f32[6,8,6144]{2,1,0:T(8,128)S(1)} %conv3.1.refs_3_, ...), custom_call_target="tpu_custom_call" | custom-call | tf_op jit(solution)/shard_map/edge_z/pallas_call | solution.py:356
  35.1 0.0 copy-start.6
  35.1 28.2 %all_to_all.20.given = bf16[16,8,16,384]{3,2,1,0:T(8,128)(2,1)S(1)} all-to-all(bf16[16,8,16,384]{3,2,1,0:T(8,128)(2,1)S(1)} %get-tuple-element.35), channel_id=1, replica_groups=mesh['px'=8,'py'=16] {'py'}, dimensions={0} | all-to-all | bytes 3145728 | tf_op jit(solution)/shard_map/all_to_all | solution.py:363
  63.2 0.8 y_fwd.2
  64.1 20.5 %all_to_all.21.given = bf16[8,8,16,384]{3,2,1,0:T(8,128)(2,1)S(1)} all-to-all(bf16[8,8,16,384]{3,2,1,0:T(8,128)(2,1)S(1)} %y_fwd.2), channel_id=1, replica_groups=mesh['px'=8,'py'=16] {'px'}, dimensions={0} | all-to-all | bytes 1572864 | tf_op jit(solution)/shard_map/all_to_all | solution.py:365
  84.6 2.4 %spec.1 = bf16[8,8,16,384]{3,2,1,0:T(8,128)(2,1)S(1)} custom-call(bf16[8,8,16,384]{3,2,1,0:T(8,128)(2,1)S(1)} %all_to_all.21.given, bf16[256,128]{1,0:T(8,128)(2,1)S(1)} %copy-done.5, bf16[256,128]{1,0:T(8,128)(2,1)S(1)} %copy-done.4, bf16[256,512]{1,0:T(8,128)(2,1)S(1)} %pad_maximum_fusion.1.inner, bf16[256,768]{1,0:T(8,128)(2,1)S(1)} %pad_maximum_fusion.outer), custom_call_target="tpu_custom_call" | custom-call | tf_op jit(solution)/shard_map/spec/pallas_call | solution.py:366
  87.0 15.2 %all_to_all.22.given = bf16[8,8,16,384]{3,2,1,0:T(8,128)(2,1)S(1)} all-to-all(bf16[8,8,16,384]{3,2,1,0:T(8,128)(2,1)S(1)} %spec.1), channel_id=1, replica_groups=mesh['px'=8,'py'=16] {'px'}, dimensions={0} | all-to-all | bytes 1572864 | tf_op jit(solution)/shard_map/all_to_all | solution.py:369
  102.2 0.6 y_inv.2
  102.8 0.0 copy-start.1
  102.8 29.3 %all_to_all.23.given = bf16[16,8,16,384]{3,2,1,0:T(8,128)(2,1)S(1)} all-to-all(bf16[16,8,16,384]{3,2,1,0:T(8,128)(2,1)S(1)} %y_inv.2), channel_id=1, replica_groups=mesh['px'=8,'py'=16] {'py'}, dimensions={0} | all-to-all | bytes 3145728 | tf_op jit(solution)/shard_map/all_to_all | solution.py:371
  132.1 2.9 %z_inv.2 = bf16[16,8,6144]{2,1,0:T(8,128)(2,1)} custom-call(bf16[16,8,16,384]{3,2,1,0:T(8,128)(2,1)S(1)} %all_to_all.23.given, bf16[256,256]{1,0:T(8,128)(2,1)S(1)} %copy-done.1, bf16[16,128,384]{2,1,0:T(8,128)(2,1)S(1)} %get-tuple-element.38.field), custom_call_target="tpu_custom_call" | custom-call | tf_op jit(solution)/shard_map/z_inv/pallas_call | solution.py:373
  (14 shorter events, 0.0 us)
Async XLA Ops:
  1.0 10.5 %collective-permute-start = (bf16[1,8,6144]{2,1,0:T(8,128)(2,1)S(1)}, bf16[1,8,6144]{2,1,0:T(8,128)(2,1)S(1)}, u32[]{:S(2)}, u32[]{:S(2)}) collective-permute-start(bf16[1,8,6144]{2,1,0:T(8,128)(2,1)S(1)} %get-tuple-element.39), channel_id=1, source_target_pairs={{0,16},{16,32},{32,48},{48,64},{64,80},{80,96},{96,112},{1,17},{17... | collective-permute-start | bytes 294920 | tf_op jit(solution)/shard_map/ppermute | solution.py:341
  7.5 1.4 %copy-start = (bf16[16,8,6144]{2,1,0:T(8,128)(2,1)S(1)}, bf16[16,8,6144]{2,1,0:T(8,128)(2,1)}, u32[]{:S(2)}) copy-start(bf16[16,8,6144]{2,1,0:T(8,128)(2,1)} %refs_0_.4) | copy-start | bytes 4718596
  11.3 5.5 %copy-start.7 = (bf16[64,144]{1,0:T(8,128)(2,1)S(1)}, bf16[64,144]{1,0:T(8,128)(2,1)}, u32[]{:S(2)}) copy-start(bf16[64,144]{1,0:T(8,128)(2,1)} %constant.23.clone.pick) | copy-start | bytes 55300
  11.4 5.4 %collective-permute-start.1 = (bf16[1,8,6144]{2,1,0:T(8,128)(2,1)S(1)}, bf16[1,8,6144]{2,1,0:T(8,128)(2,1)S(1)}, u32[]{:S(2)}, u32[]{:S(2)}) collective-permute-start(bf16[1,8,6144]{2,1,0:T(8,128)(2,1)S(1)} %get-tuple-element.23), channel_id=1, source_target_pairs={{16,0},{32,16},{48,32},{64,48},{80,64},{96,80},{112,96},{17,1},{33... | collective-permute-start | bytes 294920 | tf_op jit(solution)/shard_map/ppermute | solution.py:344
  17.2 12.5 %collective-permute-start.2 = (bf16[18,6144]{1,0:T(8,128)(2,1)S(1)}, bf16[18,6144]{1,0:T(8,128)(2,1)S(1)}, u32[]{:S(2)}, u32[]{:S(2)}) collective-permute-start(bf16[18,6144]{1,0:T(8,128)(2,1)S(1)} %get-tuple-element.29), channel_id=1, source_target_pairs={{0,1},{1,2},{2,3},{3,4},{4,5},{5,6},{6,7},{7,8},{8,9},{9,10},{10,1... | collective-permute-start | bytes 663560 | tf_op jit(solution)/shard_map/ppermute | solution.py:349
  24.3 8.0 %collective-permute-start.3 = (bf16[18,6144]{1,0:T(8,128)(2,1)S(1)}, bf16[18,6144]{1,0:T(8,128)(2,1)S(1)}, u32[]{:S(2)}, u32[]{:S(2)}) collective-permute-start(bf16[18,6144]{1,0:T(8,128)(2,1)S(1)} %get-tuple-element.34), channel_id=1, source_target_pairs={{1,0},{2,1},{3,2},{4,3},{5,4},{6,5},{7,6},{8,7},{9,8},{10,9},{11,1... | collective-permute-start | bytes 663560 | tf_op jit(solution)/shard_map/ppermute | solution.py:353
  26.5 5.8 %copy-start.2 = (bf16[256,256]{1,0:T(8,128)(2,1)S(1)}, bf16[256,256]{1,0:T(8,128)(2,1)}, u32[]{:S(2)}) copy-start(bf16[256,256]{1,0:T(8,128)(2,1)} %constant.17.clone.refs_7_) | copy-start | bytes 393220
  35.1 28.2 %copy-start.6 = (bf16[128,256]{1,0:T(8,128)(2,1)S(1)}, bf16[128,256]{1,0:T(8,128)(2,1)}, u32[]{:S(2)}) copy-start(bf16[128,256]{1,0:T(8,128)(2,1)} %constant.19.clone.y_fwd) | copy-start | bytes 196612
  63.2 21.4 %copy-start.4 = (bf16[256,128]{1,0:T(8,128)(2,1)S(1)}, bf16[256,128]{1,0:T(8,128)(2,1)}, u32[]{:S(2)}) copy-start(bf16[256,128]{1,0:T(8,128)(2,1)} %constant.22.clone.x_inv) | copy-start | bytes 196612
  63.2 21.4 %copy-start.5 = (bf16[256,128]{1,0:T(8,128)(2,1)S(1)}, bf16[256,128]{1,0:T(8,128)(2,1)}, u32[]{:S(2)}) copy-start(bf16[256,128]{1,0:T(8,128)(2,1)} %constant.21.clone.x_fwd) | copy-start | bytes 196612
  84.6 17.6 %copy-start.3 = (bf16[256,128]{1,0:T(8,128)(2,1)S(1)}, bf16[256,128]{1,0:T(8,128)(2,1)}, u32[]{:S(2)}) copy-start(bf16[256,128]{1,0:T(8,128)(2,1)} %constant.20.clone.y_inv) | copy-start | bytes 196612
  102.8 29.4 %copy-start.1 = (bf16[256,256]{1,0:T(8,128)(2,1)S(1)}, bf16[256,256]{1,0:T(8,128)(2,1)}, u32[]{:S(2)}) copy-start(bf16[256,256]{1,0:T(8,128)(2,1)} %constant.18.clone.z_inv) | copy-start | bytes 393220

commit v4 on v3

--- a/solution.py
+++ b/solution.py
@@ -91,7 +91,8 @@
     return pltpu.roll(value, C, 1)
 
 
-def conv_rows(rows, weight, out, shifted):
+def conv_rows(rows, narrow, out, shifted, weight):
+    weight[...] = jnp.concatenate([narrow[...], narrow[...]], axis=1)
     pad = jnp.zeros((LY, C), F32)
     flat = [row for run in rows for row in run]
     for i, (ref, x) in enumerate(flat):
@@ -131,14 +132,14 @@
                     done += 1
 
 
-PIECES = (((1, 5),), ((5, 8),), ((8, 11),), ((0, 1), (11, 16)))
+PIECES = (((1, 8),), ((0, 1), (8, 16)))
 
 
 def piece_kernel(runs, *refs):
-    if len(refs) == 4:
-        tok, weight, out, shifted = refs
+    if len(refs) == 5:
+        tok, narrow, out, shifted, weight = refs
     else:
-        tok, xlo, xhi, weight, out, shifted = refs
+        tok, xlo, xhi, narrow, out, shifted, weight = refs
     rows = []
     for first, end in runs:
         run = [(tok, x) for x in range(max(first - 1, 0), min(end + 1, LX))]
@@ -147,7 +148,7 @@
         if end == LX:
             run = run + [(xhi, 0)]
         rows.append(run)
-    conv_rows(rows, weight, out, shifted)
+    conv_rows(rows, narrow, out, shifted, weight)
 
 
 def piece(at, *operands):
@@ -157,9 +158,8 @@
     return call(
         functools.partial(piece_kernel, runs),
         jax.ShapeDtypeStruct((made, LY, MERGED), F32),
-        [VMEM((made + 2 * len(runs), LY, wide), F32)],
+        [VMEM((made + 2 * len(runs), LY, wide), F32), VMEM((27, W), F32)],
         name=f"conv{at}",
-        cost=pl.CostEstimate(flops=1, bytes_accessed=1, transcendentals=0),
     )(*operands)
 
 
@@ -185,7 +185,8 @@
 
 def edge_kernel(*refs):
     pieces, refs = refs[: len(PIECES)], refs[len(PIECES) :]
-    ylo, yhi, weight, z_fwd, field, freq, ylo_s, yhi_s, edge = refs
+    ylo, yhi, narrow, z_fwd, field, freq, ylo_s, yhi_s, edge, weight = refs
+    weight[...] = jnp.concatenate([narrow[...], narrow[...]], axis=1)
     pad = jnp.zeros((LX + 2, C), F32)
     ylo_s[...] = jnp.concatenate([pad, ylo[...].astype(F32), pad], axis=1)
     yhi_s[...] = jnp.concatenate([pad, yhi[...].astype(F32), pad], axis=1)
@@ -304,13 +305,12 @@
                 out[x, :, z * W : (z + 1) * W] = value[z * LY : (z + 1) * LY].astype(BF16)
 
 
-def call(kernel, outs, scratch=(), name=None, cost=None):
+def call(kernel, outs, scratch=(), name=None):
     return pl.pallas_call(
         kernel,
         out_shape=outs,
         scratch_shapes=list(scratch),
         compiler_params=pltpu.CompilerParams(vmem_limit_bytes=20 * 2**20),
-        cost_estimate=cost,
         name=name,
     )
 
@@ -332,33 +332,26 @@
 
 def body(tokens, conv_weight, inner_weight, outer_weight):
     z_fwd, z_inv, y_fwd, y_inv, x_fwd, x_inv, pick = (jnp.asarray(m) for m in matrices())
-    weight = jnp.concatenate([conv_weight, conv_weight], axis=1)
     inner = jnp.concatenate([block_diagonal(w, 256) for w in inner_weight], axis=1)
     outer = [block_diagonal(w, C) for w in outer_weight]
     outer = jnp.concatenate([outer[0], outer[0], outer[1], outer[1]], axis=1)
 
     wide = MERGED + 2 * C
     xlo = lax.ppermute(tokens[LX - 1 :], "px", pairs(PX, 1))
-    piece0 = piece(0, tokens, weight)
-    piece0, bottom, xlo = lax.optimization_barrier((piece0, tokens[:1], xlo))
-    xhi = lax.ppermute(bottom, "px", pairs(PX, -1))
-    tokens, bottom = lax.optimization_barrier((tokens, bottom))
-    piece1 = piece(1, tokens, weight)
-    piece1, xlo, xhi = lax.optimization_barrier((piece1, xlo, xhi))
+    xhi = lax.ppermute(tokens[:1], "px", pairs(PX, -1))
+    piece0 = piece(0, tokens, conv_weight)
+    piece0, xlo, xhi = lax.optimization_barrier((piece0, xlo, xhi))
     first, last = call(rows_kernel, [shape(LX + 2, MERGED)] * 2, name="y_rows")(tokens, xlo, xhi, pick)
     ylo = lax.ppermute(last, "py", pairs(PY, 1))
-    tokens, last = lax.optimization_barrier((tokens, last))
-    piece2 = piece(2, tokens, weight)
-    piece2, first = lax.optimization_barrier((piece2, first))
     yhi = lax.ppermute(first, "py", pairs(PY, -1))
-    piece3 = piece(3, tokens, xlo, xhi, weight)
-    piece3, inner, outer = lax.optimization_barrier((piece3, inner, outer))
+    piece1 = piece(1, tokens, xlo, xhi, conv_weight)
+    piece1, inner, outer = lax.optimization_barrier((piece1, inner, outer))
     field, freq = call(
         edge_kernel,
         [shape(LX, ZH * LY, W), shape(KZ, XP, 2 * LY, W)],
-        [VMEM((LX + 2, wide), F32), VMEM((LX + 2, wide), F32), VMEM((2, LX, MERGED), F32)],
+        [VMEM((LX + 2, wide), F32), VMEM((LX + 2, wide), F32), VMEM((2, LX, MERGED), F32), VMEM((27, W), F32)],
         name="edge_z",
-    )(piece0, piece1, piece2, piece3, ylo, yhi, weight, z_fwd)
+    )(piece0, piece1, ylo, yhi, conv_weight, z_fwd)
     rows = VMEM((W // 128, 2 * XP * Q, 128), F32)
     freq = lax.all_to_all(freq, "py", 0, 0, tiled=True)
     freq = call(y_forward_kernel, shape(PX, Q // PX, 2 * XP, W), [rows], name="y_fwd")(freq, y_fwd)

time: 136 us -> 130 us (0.956)
  waiting for transfers between devices: 4.68 us -> 2.27 us
  blocking collectives: 93.2 us -> 91.3 us
  Pallas kernels: 19.3 us -> 17.7 us
    ppermute x1, waiting for transfers between devices: 2.06 us -> 0.01 us  [body(): xhi = lax.ppermute(tokens[:1], 'px', pairs(PX, -1))]
    pallas_call x4 -> x2, Pallas kernels: 9.49 us -> 7.9 us  [piece(): call(functools.partial(piece_kernel, runs), jax.ShapeDtypeStruct((made, L...]
  transfers between devices with their start and end apart: 4 -> 4, of which waited for: 2 -> 1; matrix products, arithmetic and copies ran while one was open for 2% -> 2% of each run, Pallas kernels for 7% -> 6%
where the time goes in v4:
time: 130 us; the launch traced here: 129 us
  blocking collectives  91.3 us (70%)
  Pallas kernels  17.7 us (14%)
  starting transfers between devices  12.3 us (9%)
  local copies, waits for them, and re-layouts  4.75 us (4%)
  waiting for transfers between devices  2.27 us (2%)
    all_to_all x2, blocking collectives, body(): freq = lax.all_to_all(freq, 'py', 0, 0, tiled=True)  56.7 us
    all_to_all x2, blocking collectives, body(): freq = lax.all_to_all(freq, 'px', 0, 0, tiled=True)  34.6 us
    pallas_call x2, Pallas kernels, piece(): call(functools.partial(piece_kernel, runs), jax.ShapeDtypeStruct((made, L...  7.9 us
    ppermute x1, starting transfers between devices, body(): xlo = lax.ppermute(tokens[LX - 1:], 'px', pairs(PX, 1))  4.66 us
    ppermute x1, starting transfers between devices, body(): ylo = lax.ppermute(last, 'py', pairs(PY, 1))  4.39 us
    pallas_call x1, Pallas kernels, body(): pl.pallas_call(z_inverse_kernel, out_shape=shape(LX, LY, MERGED), grid=(s...  2.91 us
    pallas_call x1, Pallas kernels, body(): call(edge_kernel, [shape(LX, ZH * LY, W), shape(KZ, XP, 2 * LY, W)], [VME...  2.75 us
  transfers between devices with their start and end apart: 4, of which 1 were waited for; matrix products, arithmetic and copies ran while one was open for 2% of the time, Pallas kernels for 6%

profile of v4, /device:TPU:1, one launch (start us, length us, event | category | flops | bytes accessed | tf_op | source)
XLA Modules:
  0.0 128.9 jit_solution(10202042682195878030)
XLA Ops:
  0.0 1.0 fusion
  1.0 1.3 %collective-permute-start.1 = (bf16[1,8,6144]{2,1,0:T(8,128)(2,1)S(1)}, bf16[1,8,6144]{2,1,0:T(8,128)(2,1)S(1)}, u32[]{:S(2)}, u32[]{:S(2)}) collective-permute-start(bf16[1,8,6144]{2,1,0:T(8,128)(2,1)S(1)} %get-tuple-element.25), channel_id=1, source_target_pairs={{16,0},{32,16},{48,32},{64,48},{80,64},{96,80},{112,96},{17,1},{33... | collective-permute-start | bytes 294920 | tf_op jit(solution)/shard_map/ppermute | solution.py:341
  2.3 4.7 %collective-permute-start = (bf16[1,8,6144]{2,1,0:T(8,128)(2,1)S(1)}, bf16[1,8,6144]{2,1,0:T(8,128)(2,1)S(1)}, u32[]{:S(2)}, u32[]{:S(2)}) collective-permute-start(bf16[1,8,6144]{2,1,0:T(8,128)(2,1)S(1)} %get-tuple-element.26), channel_id=1, source_target_pairs={{0,16},{16,32},{32,48},{48,64},{64,80},{80,96},{96,112},{1,17},{17... | collective-permute-start | bytes 294920 | tf_op jit(solution)/shard_map/ppermute | solution.py:340
  6.9 0.8 slice_bitcast_fusion.7
  7.7 0.8 slice_bitcast_fusion.3
  8.5 1.4 %copy-done = bf16[16,8,6144]{2,1,0:T(8,128)(2,1)S(1)} copy-done((bf16[16,8,6144]{2,1,0:T(8,128)(2,1)S(1)}, bf16[16,8,6144]{2,1,0:T(8,128)(2,1)}, u32[]{:S(2)}) %copy-start) | copy-done | bytes 1572888
  9.9 0.8 copy-done.1
  10.7 3.5 %conv0.1.refs_0_ = f32[7,8,6144]{2,1,0:T(8,128)S(1)} custom-call(bf16[16,8,6144]{2,1,0:T(8,128)(2,1)S(1)} %copy-done, f32[27,192]{1,0:T(8,128)S(1)} %copy-done.1), custom_call_target="tpu_custom_call" | custom-call | tf_op jit(solution)/shard_map/conv0/pallas_call | solution.py:158
  14.2 0.1 pad_add_fusion.2
  14.4 0.0 collective-permute-done.1.refs_2_.xhi
  14.4 0.0 collective-permute-done.refs_1_.xlo
  14.4 0.4 y_rows.1
  14.8 4.4 %collective-permute-start.2 = (bf16[18,6144]{1,0:T(8,128)(2,1)S(1)}, bf16[18,6144]{1,0:T(8,128)(2,1)S(1)}, u32[]{:S(2)}, u32[]{:S(2)}) collective-permute-start(bf16[18,6144]{1,0:T(8,128)(2,1)S(1)} %get-tuple-element.19), channel_id=1, source_target_pairs={{0,1},{1,2},{2,3},{3,4},{4,5},{5,6},{6,7},{7,8},{8,9},{9,10},{10,1... | collective-permute-start | bytes 663560 | tf_op jit(solution)/shard_map/ppermute | solution.py:345
  19.2 1.9 %collective-permute-start.3 = (bf16[18,6144]{1,0:T(8,128)(2,1)S(1)}, bf16[18,6144]{1,0:T(8,128)(2,1)S(1)}, u32[]{:S(2)}, u32[]{:S(2)}) collective-permute-start(bf16[18,6144]{1,0:T(8,128)(2,1)S(1)} %get-tuple-element.20), channel_id=1, source_target_pairs={{1,0},{2,1},{3,2},{4,3},{5,4},{6,5},{7,6},{8,7},{9,8},{10,9},{11,1... | collective-permute-start | bytes 663560 | tf_op jit(solution)/shard_map/ppermute | solution.py:346
  21.1 0.1 pad_add_fusion
  21.2 0.2 pad_maximum_fusion.outer
  21.4 0.0 copy-start.3
  21.4 4.4 %conv1.1.refs_1_ = f32[9,8,6144]{2,1,0:T(8,128)S(1)} custom-call(bf16[16,8,6144]{2,1,0:T(8,128)(2,1)S(1)} %copy-done, bf16[1,8,6144]{2,1,0:T(8,128)(2,1)S(1)} %collective-permute-done.refs_1_.xlo, bf16[1,8,6144]{2,1,0:T(8,128)(2,1)S(1)} %collective-permute-done.1.refs_2_.xhi, f32[27,192]{1,0:T(8,128)S(1)} %copy-done.1), custom_call_target="tpu_custom_call" | custom-call | tf_op jit(solution)/shard_map/conv1/pallas_call | solution.py:158
  25.8 0.0 collective-permute-done.2.refs_2_
  25.8 2.3 %collective-permute-done.3.refs_3_ = bf16[18,6144]{1,0:T(8,128)(2,1)S(1)} collective-permute-done((bf16[18,6144]{1,0:T(8,128)(2,1)S(1)}, bf16[18,6144]{1,0:T(8,128)(2,1)S(1)}, u32[]{:S(2)}, u32[]{:S(2)}) %collective-permute-start.3) | collective-permute-done | bytes 221216 | tf_op jit(solution)/shard_map/ppermute | solution.py:346
  28.1 2.7 %edge_z.1 = (bf16[16,128,384]{2,1,0:T(8,128)(2,1)S(1)}, bf16[16,8,16,384]{3,2,1,0:T(8,128)(2,1)S(1)}) custom-call(f32[7,8,6144]{2,1,0:T(8,128)S(1)} %conv0.1.refs_0_, f32[9,8,6144]{2,1,0:T(8,128)S(1)} %conv1.1.refs_1_, bf16[18,6144]{1,0:T(8,128)(2,1)S(1)} %collective-permute-done.2.refs_2_, bf16[18,6144]{1,0:T(8,128)(2,1)S(1)} %collective-permute-done.3.refs_3_, ...), custom_call_target="tpu_custom_call" | custom-call | tf_op jit(solution)/shard_map/edge_z/pallas_call | solution.py:349
  30.8 0.0 copy-start.7
  30.8 27.4 %all_to_all.20.given = bf16[16,8,16,384]{3,2,1,0:T(8,128)(2,1)S(1)} all-to-all(bf16[16,8,16,384]{3,2,1,0:T(8,128)(2,1)S(1)} %get-tuple-element.21), channel_id=1, replica_groups=mesh['px'=8,'py'=16] {'py'}, dimensions={0} | all-to-all | bytes 3145728 | tf_op jit(solution)/shard_map/all_to_all | solution.py:356
  58.2 0.0 copy-done.7
  58.2 0.8 y_fwd.2
  59.0 19.4 %all_to_all.21.given = bf16[8,8,16,384]{3,2,1,0:T(8,128)(2,1)S(1)} all-to-all(bf16[8,8,16,384]{3,2,1,0:T(8,128)(2,1)S(1)} %y_fwd.2), channel_id=1, replica_groups=mesh['px'=8,'py'=16] {'px'}, dimensions={0} | all-to-all | bytes 1572864 | tf_op jit(solution)/shard_map/all_to_all | solution.py:358
  78.5 2.4 %spec.1 = bf16[8,8,16,384]{3,2,1,0:T(8,128)(2,1)S(1)} custom-call(bf16[8,8,16,384]{3,2,1,0:T(8,128)(2,1)S(1)} %all_to_all.21.given, bf16[256,128]{1,0:T(8,128)(2,1)S(1)} %copy-done.6, bf16[256,128]{1,0:T(8,128)(2,1)S(1)} %copy-done.5, bf16[256,512]{1,0:T(8,128)(2,1)S(1)} %pad_maximum_fusion.1.inner, bf16[256,768]{1,0:T(8,128)(2,1)S(1)} %pad_maximum_fusion.outer), custom_call_target="tpu_custom_call" | custom-call | tf_op jit(solution)/shard_map/spec/pallas_call | solution.py:359
  80.9 15.2 %all_to_all.22.given = bf16[8,8,16,384]{3,2,1,0:T(8,128)(2,1)S(1)} all-to-all(bf16[8,8,16,384]{3,2,1,0:T(8,128)(2,1)S(1)} %spec.1), channel_id=1, replica_groups=mesh['px'=8,'py'=16] {'px'}, dimensions={0} | all-to-all | bytes 1572864 | tf_op jit(solution)/shard_map/all_to_all | solution.py:362
  96.1 0.6 y_inv.2
  96.6 0.0 copy-start.2
  96.6 29.3 %all_to_all.23.given = bf16[16,8,16,384]{3,2,1,0:T(8,128)(2,1)S(1)} all-to-all(bf16[16,8,16,384]{3,2,1,0:T(8,128)(2,1)S(1)} %y_inv.2), channel_id=1, replica_groups=mesh['px'=8,'py'=16] {'py'}, dimensions={0} | all-to-all | bytes 3145728 | tf_op jit(solution)/shard_map/all_to_all | solution.py:364
  126.0 2.9 %z_inv.2 = bf16[16,8,6144]{2,1,0:T(8,128)(2,1)} custom-call(bf16[16,8,16,384]{3,2,1,0:T(8,128)(2,1)S(1)} %all_to_all.23.given, bf16[256,256]{1,0:T(8,128)(2,1)S(1)} %copy-done.2, bf16[16,128,384]{2,1,0:T(8,128)(2,1)S(1)} %get-tuple-element.24.field), custom_call_target="tpu_custom_call" | custom-call | tf_op jit(solution)/shard_map/z_inv/pallas_call | solution.py:366
  (13 shorter events, 0.0 us)
Async XLA Ops:
  1.0 13.4 %collective-permute-start.1 = (bf16[1,8,6144]{2,1,0:T(8,128)(2,1)S(1)}, bf16[1,8,6144]{2,1,0:T(8,128)(2,1)S(1)}, u32[]{:S(2)}, u32[]{:S(2)}) collective-permute-start(bf16[1,8,6144]{2,1,0:T(8,128)(2,1)S(1)} %get-tuple-element.25), channel_id=1, source_target_pairs={{16,0},{32,16},{48,32},{64,48},{80,64},{96,80},{112,96},{17,1},{33... | collective-permute-start | bytes 294920 | tf_op jit(solution)/shard_map/ppermute | solution.py:341
  2.3 12.1 %collective-permute-start = (bf16[1,8,6144]{2,1,0:T(8,128)(2,1)S(1)}, bf16[1,8,6144]{2,1,0:T(8,128)(2,1)S(1)}, u32[]{:S(2)}, u32[]{:S(2)}) collective-permute-start(bf16[1,8,6144]{2,1,0:T(8,128)(2,1)S(1)} %get-tuple-element.26), channel_id=1, source_target_pairs={{0,16},{16,32},{32,48},{48,64},{64,80},{80,96},{96,112},{1,17},{17... | collective-permute-start | bytes 294920 | tf_op jit(solution)/shard_map/ppermute | solution.py:340
  8.5 1.4 %copy-start = (bf16[16,8,6144]{2,1,0:T(8,128)(2,1)S(1)}, bf16[16,8,6144]{2,1,0:T(8,128)(2,1)}, u32[]{:S(2)}) copy-start(bf16[16,8,6144]{2,1,0:T(8,128)(2,1)} %tok.1) | copy-start | bytes 4718596
  9.9 0.8 copy-start.1
  10.7 3.7 %copy-start.8 = (bf16[64,144]{1,0:T(8,128)(2,1)S(1)}, bf16[64,144]{1,0:T(8,128)(2,1)}, u32[]{:S(2)}) copy-start(bf16[64,144]{1,0:T(8,128)(2,1)} %constant.23.clone.pick) | copy-start | bytes 55300
  14.8 11.0 %collective-permute-start.2 = (bf16[18,6144]{1,0:T(8,128)(2,1)S(1)}, bf16[18,6144]{1,0:T(8,128)(2,1)S(1)}, u32[]{:S(2)}, u32[]{:S(2)}) collective-permute-start(bf16[18,6144]{1,0:T(8,128)(2,1)S(1)} %get-tuple-element.19), channel_id=1, source_target_pairs={{0,1},{1,2},{2,3},{3,4},{4,5},{5,6},{6,7},{7,8},{8,9},{9,10},{10,1... | collective-permute-start | bytes 663560 | tf_op jit(solution)/shard_map/ppermute | solution.py:345
  19.2 8.9 %collective-permute-start.3 = (bf16[18,6144]{1,0:T(8,128)(2,1)S(1)}, bf16[18,6144]{1,0:T(8,128)(2,1)S(1)}, u32[]{:S(2)}, u32[]{:S(2)}) collective-permute-start(bf16[18,6144]{1,0:T(8,128)(2,1)S(1)} %get-tuple-element.20), channel_id=1, source_target_pairs={{1,0},{2,1},{3,2},{4,3},{5,4},{6,5},{7,6},{8,7},{9,8},{10,9},{11,1... | collective-permute-start | bytes 663560 | tf_op jit(solution)/shard_map/ppermute | solution.py:346
  21.4 6.7 %copy-start.3 = (bf16[256,256]{1,0:T(8,128)(2,1)S(1)}, bf16[256,256]{1,0:T(8,128)(2,1)}, u32[]{:S(2)}) copy-start(bf16[256,256]{1,0:T(8,128)(2,1)} %constant.17.clone.refs_5_) | copy-start | bytes 393220
  30.8 27.4 %copy-start.7 = (bf16[128,256]{1,0:T(8,128)(2,1)S(1)}, bf16[128,256]{1,0:T(8,128)(2,1)}, u32[]{:S(2)}) copy-start(bf16[128,256]{1,0:T(8,128)(2,1)} %constant.19.clone.y_fwd) | copy-start | bytes 196612
  58.2 20.3 %copy-start.5 = (bf16[256,128]{1,0:T(8,128)(2,1)S(1)}, bf16[256,128]{1,0:T(8,128)(2,1)}, u32[]{:S(2)}) copy-start(bf16[256,128]{1,0:T(8,128)(2,1)} %constant.22.clone.x_inv) | copy-start | bytes 196612
  58.2 20.3 %copy-start.6 = (bf16[256,128]{1,0:T(8,128)(2,1)S(1)}, bf16[256,128]{1,0:T(8,128)(2,1)}, u32[]{:S(2)}) copy-start(bf16[256,128]{1,0:T(8,128)(2,1)} %constant.21.clone.x_fwd) | copy-start | bytes 196612
  78.5 17.6 %copy-start.4 = (bf16[256,128]{1,0:T(8,128)(2,1)S(1)}, bf16[256,128]{1,0:T(8,128)(2,1)}, u32[]{:S(2)}) copy-start(bf16[256,128]{1,0:T(8,128)(2,1)} %constant.20.clone.y_inv) | copy-start | bytes 196612
  96.6 29.4 %copy-start.2 = (bf16[256,256]{1,0:T(8,128)(2,1)S(1)}, bf16[256,256]{1,0:T(8,128)(2,1)}, u32[]{:S(2)}) copy-start(bf16[256,256]{1,0:T(8,128)(2,1)} %constant.18.clone.z_inv) | copy-start | bytes 393220

commit v5 on v3

--- a/solution.py
+++ b/solution.py
@@ -131,35 +131,55 @@
                     done += 1
 
 
-PIECES = (((1, 5),), ((5, 8),), ((8, 11),), ((0, 1), (11, 16)))
-
-
-def piece_kernel(runs, *refs):
-    if len(refs) == 4:
-        tok, weight, out, shifted = refs
-    else:
-        tok, xlo, xhi, weight, out, shifted = refs
+PIECES = (((1, 8),), ((0, 1), (8, 16)))
+
+
+def odd(axis):
+    return lax.rem(lax.axis_index(axis), 2) == 1
+
+
+def by_order(axis, first, second):
+    second, first = second.astype(F32), first.astype(F32)
+    up = odd(axis)
+    return jnp.where(up, first, second), jnp.where(up, second, first)
+
+
+def start_kernel(tok, narrow_hbm, first, second, weight, narrow, sem):
+    copy = pltpu.make_async_copy(narrow_hbm, narrow, sem)
+    copy.start()
+    below, above = tok[0].astype(F32), tok[LX - 1].astype(F32)
+    up = odd("px")
+    first[0] = jnp.where(up, below, above).astype(BF16)
+    second[0] = jnp.where(up, above, below).astype(BF16)
+    copy.wait()
+    weight[...] = jnp.concatenate([narrow[...], narrow[...]], axis=1)
+
+
+def inside_kernel(tok, weight, out, shifted):
+    conv_rows([[(tok, x) for x in range(first - 1, end + 1)] for first, end in PIECES[0]], weight, out, shifted)
+
+
+def border_kernel(tok, first, second, weight, out, shifted, sides):
+    sides[0], sides[1] = by_order("px", first[0], second[0])
     rows = []
-    for first, end in runs:
-        run = [(tok, x) for x in range(max(first - 1, 0), min(end + 1, LX))]
-        if first == 0:
-            run = [(xlo, 0)] + run
+    for start, end in PIECES[1]:
+        run = [(tok, x) for x in range(max(start - 1, 0), min(end + 1, LX))]
+        if start == 0:
+            run = [(sides, 0)] + run
         if end == LX:
-            run = run + [(xhi, 0)]
+            run = run + [(sides, 1)]
         rows.append(run)
     conv_rows(rows, weight, out, shifted)
 
 
-def piece(at, *operands):
+def piece(at, kernel, extra, *operands):
     runs = PIECES[at]
     made = sum(end - first for first, end in runs)
-    wide = MERGED + 2 * C
     return call(
-        functools.partial(piece_kernel, runs),
+        kernel,
         jax.ShapeDtypeStruct((made, LY, MERGED), F32),
-        [VMEM((made + 2 * len(runs), LY, wide), F32)],
+        [VMEM((made + 2 * len(runs), LY, MERGED + 2 * C), F32)] + extra,
         name=f"conv{at}",
-        cost=pl.CostEstimate(flops=1, bytes_accessed=1, transcendentals=0),
     )(*operands)
 
 
@@ -172,23 +192,26 @@
             row += end - first
 
 
-def rows_kernel(tok, xlo, xhi, pick, first, last):
+def rows_kernel(tok, first, second, pick, send_first, send_second):
     step = MERGED // 4
+    up = odd("py")
     for j in range(4):
         here = slice(j * step, (j + 1) * step)
-        parts = [ref[:, :, here].astype(F32) for ref in (xlo, tok, xhi)]
-        data = jnp.concatenate(parts, axis=0).reshape((LX + 2) * LY, step).astype(BF16)
-        out = dot(pick[...], data).astype(BF16)
-        first[:, here] = out[: LX + 2]
-        last[:, here] = out[32 : 32 + LX + 2]
+        lo, hi = by_order("px", first[:, :, here], second[:, :, here])
+        data = jnp.concatenate([lo, tok[:, :, here].astype(F32), hi], axis=0)
+        out = dot(pick[...], data.reshape((LX + 2) * LY, step).astype(BF16))
+        below, above = out[: LX + 2], out[32 : 32 + LX + 2]
+        send_first[:, here] = jnp.where(up, below, above).astype(BF16)
+        send_second[:, here] = jnp.where(up, above, below).astype(BF16)
 
 
 def edge_kernel(*refs):
     pieces, refs = refs[: len(PIECES)], refs[len(PIECES) :]
-    ylo, yhi, weight, z_fwd, field, freq, ylo_s, yhi_s, edge = refs
+    first, second, weight, z_fwd, field, freq, ylo, yhi, ylo_s, yhi_s, edge = refs
     pad = jnp.zeros((LX + 2, C), F32)
-    ylo_s[...] = jnp.concatenate([pad, ylo[...].astype(F32), pad], axis=1)
-    yhi_s[...] = jnp.concatenate([pad, yhi[...].astype(F32), pad], axis=1)
+    ylo[...], yhi[...] = by_order("py", first[...], second[...])
+    ylo_s[...] = jnp.concatenate([pad, ylo[...], pad], axis=1)
+    yhi_s[...] = jnp.concatenate([pad, yhi[...], pad], axis=1)
 
     @pl.loop(0, MERGED // 128)
     def _(j):
@@ -197,7 +220,7 @@
         here = pl.ds(at, 128)
         phase = pl.multiple_of(lax.rem(j, 3) * 128, 128)
         for side, rows, rows_s, b in ((0, ylo, ylo_s, 0), (1, yhi, yhi_s, 2)):
-            mid = rows[:, here].astype(F32)
+            mid = rows[:, here]
             before = rows_s[:, here]
             behind = rows_s[:, pl.ds(after, 128)]
             total = None
@@ -255,7 +278,21 @@
     return v - jnp.clip(v, -shrink_level, shrink_level)
 
 
-def spectrum_kernel(given, x_fwd, x_inv, inner, outer, out, rows):
+def lay_out(weight, width, copies, out):
+    for b in range(C // CB):
+        columns = []
+        for part in range(2):
+            block = weight[part, b].astype(F32)
+            columns += [jnp.zeros((CB, b * CB), F32)] * (b > 0) + [block]
+            columns += [jnp.zeros((CB, width - (b + 1) * CB), F32)] * (width > (b + 1) * CB)
+            columns += columns[-2:] * (copies - 1)
+        out[b * CB : (b + 1) * CB] = jnp.concatenate(columns, axis=1).astype(BF16)
+    out[C:] = jnp.zeros((256 - C, out.shape[1]), BF16)
+
+
+def spectrum_kernel(given, x_fwd, x_inv, inner_weight, outer_weight, out, rows, inner, outer):
+    lay_out(inner_weight, 256, 1, inner)
+    lay_out(outer_weight, C, 2, outer)
     count = Q // PX
     low = low_half(2 * PX * XP)
     data = [given[:, q].reshape(2 * PX * XP, W) for q in range(count)]
@@ -304,13 +341,13 @@
                 out[x, :, z * W : (z + 1) * W] = value[z * LY : (z + 1) * LY].astype(BF16)
 
 
-def call(kernel, outs, scratch=(), name=None, cost=None):
+def call(kernel, outs, scratch=(), name=None, in_specs=None):
     return pl.pallas_call(
         kernel,
         out_shape=outs,
         scratch_shapes=list(scratch),
+        **({} if in_specs is None else {"in_specs": in_specs}),
         compiler_params=pltpu.CompilerParams(vmem_limit_bytes=20 * 2**20),
-        cost_estimate=cost,
         name=name,
     )
 
@@ -319,52 +356,44 @@
     return jax.ShapeDtypeStruct(dims, BF16)
 
 
-def block_diagonal(weight, width):
-    total = 0
-    for b in range(C // CB):
-        total = total + jnp.pad(weight[b], ((b * CB, 256 - (b + 1) * CB), (b * CB, width - (b + 1) * CB)))
-    return total
-
-
-def pairs(count, step):
-    return [(i, i + step) for i in range(count) if 0 <= i + step < count]
+def swap_pairs(value, axis, count, start):
+    low = range(start, count - 1, 2)
+    return lax.ppermute(value, axis, [(i, i + 1) for i in low] + [(i + 1, i) for i in low])
 
 
 def body(tokens, conv_weight, inner_weight, outer_weight):
     z_fwd, z_inv, y_fwd, y_inv, x_fwd, x_inv, pick = (jnp.asarray(m) for m in matrices())
-    weight = jnp.concatenate([conv_weight, conv_weight], axis=1)
-    inner = jnp.concatenate([block_diagonal(w, 256) for w in inner_weight], axis=1)
-    outer = [block_diagonal(w, C) for w in outer_weight]
-    outer = jnp.concatenate([outer[0], outer[0], outer[1], outer[1]], axis=1)
-
     wide = MERGED + 2 * C
-    xlo = lax.ppermute(tokens[LX - 1 :], "px", pairs(PX, 1))
-    piece0 = piece(0, tokens, weight)
-    piece0, bottom, xlo = lax.optimization_barrier((piece0, tokens[:1], xlo))
-    xhi = lax.ppermute(bottom, "px", pairs(PX, -1))
-    tokens, bottom = lax.optimization_barrier((tokens, bottom))
-    piece1 = piece(1, tokens, weight)
-    piece1, xlo, xhi = lax.optimization_barrier((piece1, xlo, xhi))
-    first, last = call(rows_kernel, [shape(LX + 2, MERGED)] * 2, name="y_rows")(tokens, xlo, xhi, pick)
-    ylo = lax.ppermute(last, "py", pairs(PY, 1))
-    tokens, last = lax.optimization_barrier((tokens, last))
-    piece2 = piece(2, tokens, weight)
-    piece2, first = lax.optimization_barrier((piece2, first))
-    yhi = lax.ppermute(first, "py", pairs(PY, -1))
-    piece3 = piece(3, tokens, xlo, xhi, weight)
-    piece3, inner, outer = lax.optimization_barrier((piece3, inner, outer))
+    first, second, weight = call(
+        start_kernel,
+        [shape(1, LY, MERGED)] * 2 + [jax.ShapeDtypeStruct((27, W), F32)],
+        [VMEM((27, C), F32), pltpu.SemaphoreType.DMA],
+        name="x_rows",
+        in_specs=[pl.BlockSpec(memory_space=VMEM), pl.BlockSpec(memory_space=pl.ANY)],
+    )(tokens, conv_weight)
+    first = swap_pairs(first, "px", PX, 0)
+    second = swap_pairs(second, "px", PX, 1)
+    inside = piece(0, inside_kernel, [], tokens, weight)
+    inside, first, second = lax.optimization_barrier((inside, first, second))
+    y_first, y_second = call(rows_kernel, [shape(LX + 2, MERGED)] * 2, name="y_rows")(
+        tokens, first, second, pick
+    )
+    y_first = swap_pairs(y_first, "py", PY, 0)
+    y_second = swap_pairs(y_second, "py", PY, 1)
+    border = piece(1, border_kernel, [VMEM((2, LY, MERGED), F32)], tokens, first, second, weight)
     field, freq = call(
         edge_kernel,
         [shape(LX, ZH * LY, W), shape(KZ, XP, 2 * LY, W)],
-        [VMEM((LX + 2, wide), F32), VMEM((LX + 2, wide), F32), VMEM((2, LX, MERGED), F32)],
+        [VMEM((LX + 2, MERGED), F32)] * 2 + [VMEM((LX + 2, wide), F32)] * 2 + [VMEM((2, LX, MERGED), F32)],
         name="edge_z",
-    )(piece0, piece1, piece2, piece3, ylo, yhi, weight, z_fwd)
+    )(inside, border, y_first, y_second, weight, z_fwd)
     rows = VMEM((W // 128, 2 * XP * Q, 128), F32)
     freq = lax.all_to_all(freq, "py", 0, 0, tiled=True)
     freq = call(y_forward_kernel, shape(PX, Q // PX, 2 * XP, W), [rows], name="y_fwd")(freq, y_fwd)
     freq = lax.all_to_all(freq, "px", 0, 0, tiled=True)
-    freq = call(spectrum_kernel, shape(PX, XP, 2 * Q // PX, W), [rows], name="spec")(
-        freq, x_fwd, x_inv, inner, outer
+    mixing = [VMEM((256, 512), BF16), VMEM((256, 4 * C), BF16)]
+    freq = call(spectrum_kernel, shape(PX, XP, 2 * Q // PX, W), [rows] + mixing, name="spec")(
+        freq, x_fwd, x_inv, inner_weight, outer_weight
     )
     freq = lax.all_to_all(freq, "px", 0, 0, tiled=True)
     freq = call(y_inverse_kernel, shape(PY, XP, 2 * LY, W), name="y_inv")(freq, y_inv)

time: 136 us -> 125 us (0.919)
  starting transfers between devices: 12.4 us -> 7.05 us
  local copies, waits for them, and re-layouts: 3.99 us -> 2.21 us
  waiting for transfers between devices: 4.68 us -> 3.08 us
    ppermute x4, starting transfers between devices: 12.4 us -> 7.05 us  [swap_pairs(): lax.ppermute(value, axis, [(i, i + 1) for i in low] + [(i + 1, i) for i i...]
    ppermute x4, waiting for transfers between devices: 4.68 us -> 3.08 us  [swap_pairs(): lax.ppermute(value, axis, [(i, i + 1) for i in low] + [(i + 1, i) for i i...]
    squeeze x2 -> x0, local copies, waits for them, and re-layouts: 1.6 us -> none  [block_diagonal(): weight[b]]
    pallas_call x5 -> x4, Pallas kernels: 11.9 us -> 10.5 us  [the longest x2 7.92 us: piece(): call(kernel, jax.ShapeDtypeStruct((made, LY, MERGED), F32), [VMEM((made +...]
  transfers between devices with their start and end apart: 4 -> 4, of which waited for: 2 -> 1; matrix products, arithmetic and copies ran while one was open for 2% -> 0% of each run, Pallas kernels for 7% -> 6%
where the time goes in v5:
time: 125 us; the launch traced here: 124 us
  blocking collectives  93.6 us (75%)
  Pallas kernels  18 us (14%)
  starting transfers between devices  7.05 us (6%)
  waiting for transfers between devices  3.08 us (2%)
  local copies, waits for them, and re-layouts  2.21 us (2%)
    all_to_all x2, blocking collectives, body(): freq = lax.all_to_all(freq, 'py', 0, 0, tiled=True)  57 us
    all_to_all x2, blocking collectives, body(): freq = lax.all_to_all(freq, 'px', 0, 0, tiled=True)  36.6 us
    pallas_call x2, Pallas kernels, piece(): call(kernel, jax.ShapeDtypeStruct((made, LY, MERGED), F32), [VMEM((made +...  7.92 us
    ppermute x4, starting transfers between devices, swap_pairs(): lax.ppermute(value, axis, [(i, i + 1) for i in low] + [(i + 1, i) for i i...  7.05 us
    ppermute x4, waiting for transfers between devices, swap_pairs(): lax.ppermute(value, axis, [(i, i + 1) for i in low] + [(i + 1, i) for i i...  3.08 us
    pallas_call x1, Pallas kernels, body(): pl.pallas_call(z_inverse_kernel, out_shape=shape(LX, LY, MERGED), grid=(s...  2.91 us
    pallas_call x1, Pallas kernels, body(): call(edge_kernel, [shape(LX, ZH * LY, W), shape(KZ, XP, 2 * LY, W)], [VME...  2.82 us
  transfers between devices with their start and end apart: 4, of which 1 were waited for; matrix products, arithmetic and copies ran while one was open for 0% of the time, Pallas kernels for 6%

profile of v5, /device:TPU:1, one launch (start us, length us, event | category | flops | bytes accessed | tf_op | source)
XLA Modules:
  0.0 124.2 jit_solution(17434379848200554819)
XLA Ops:
  0.0 1.4 %copy-done = bf16[16,8,6144]{2,1,0:T(8,128)(2,1)S(1)} copy-done((bf16[16,8,6144]{2,1,0:T(8,128)(2,1)S(1)}, bf16[16,8,6144]{2,1,0:T(8,128)(2,1)}, u32[]{:S(2)}) %copy-start) | copy-done | bytes 1572888
  1.4 0.8 copy-done.10
  2.2 0.2 x_rows.1
  2.3 0.0 copy-start.9
  2.3 2.2 %collective-permute-start = (bf16[1,8,6144]{2,1,0:T(8,128)(2,1)S(1)}, bf16[1,8,6144]{2,1,0:T(8,128)(2,1)S(1)}, u32[]{:S(2)}, u32[]{:S(2)}) collective-permute-start(bf16[1,8,6144]{2,1,0:T(8,128)(2,1)S(1)} %get-tuple-element.16), channel_id=1, source_target_pairs={{0,16},{32,48},{64,80},{96,112},{16,0},{48,32},{80,64},{112,96},{1... | collective-permute-start | bytes 294920 | tf_op jit(solution)/shard_map/ppermute | solution.py:361
  4.5 0.7 collective-permute-start.1
  5.2 3.5 %conv0.1.refs_0_ = f32[7,8,6144]{2,1,0:T(8,128)S(1)} custom-call(bf16[16,8,6144]{2,1,0:T(8,128)(2,1)S(1)} %copy-done, f32[27,384]{1,0:T(8,128)S(1)} %get-tuple-element.15.weight.refs_4_), custom_call_target="tpu_custom_call" | custom-call | tf_op jit(solution)/shard_map/conv0/pallas_call | solution.py:178
  8.7 0.0 collective-permute-done.first
  8.8 0.0 collective-permute-done.1.second
  8.8 0.0 copy-done.9
  8.8 0.4 y_rows.1
  9.2 1.0 collective-permute-start.2
  10.2 3.2 %collective-permute-start.3 = (bf16[18,6144]{1,0:T(8,128)(2,1)S(1)}, bf16[18,6144]{1,0:T(8,128)(2,1)S(1)}, u32[]{:S(2)}, u32[]{:S(2)}) collective-permute-start(bf16[18,6144]{1,0:T(8,128)(2,1)S(1)} %get-tuple-element.22), channel_id=1, source_target_pairs={{1,2},{3,4},{5,6},{7,8},{9,10},{11,12},{13,14},{2,1},{4,3},{6,5},{... | collective-permute-start | bytes 663560 | tf_op jit(solution)/shard_map/ppermute | solution.py:361
  13.4 4.4 %conv1.1.refs_1_ = f32[9,8,6144]{2,1,0:T(8,128)S(1)} custom-call(bf16[16,8,6144]{2,1,0:T(8,128)(2,1)S(1)} %copy-done, bf16[1,8,6144]{2,1,0:T(8,128)(2,1)S(1)} %collective-permute-done.first, bf16[1,8,6144]{2,1,0:T(8,128)(2,1)S(1)} %collective-permute-done.1.second, f32[27,384]{1,0:T(8,128)S(1)} %get-tuple-element.15.weight.refs_4_), custom_call_target="tpu_custom_call" | custom-call | tf_op jit(solution)/shard_map/conv1/pallas_call | solution.py:178
  17.8 0.0 collective-permute-done.2.refs_2_
  17.8 3.1 %collective-permute-done.3.refs_3_ = bf16[18,6144]{1,0:T(8,128)(2,1)S(1)} collective-permute-done((bf16[18,6144]{1,0:T(8,128)(2,1)S(1)}, bf16[18,6144]{1,0:T(8,128)(2,1)S(1)}, u32[]{:S(2)}, u32[]{:S(2)}) %collective-permute-start.3) | collective-permute-done | bytes 221216 | tf_op jit(solution)/shard_map/ppermute | solution.py:361
  20.9 2.8 %edge_z.1 = (bf16[16,128,384]{2,1,0:T(8,128)(2,1)S(1)}, bf16[16,8,16,384]{3,2,1,0:T(8,128)(2,1)S(1)}) custom-call(f32[7,8,6144]{2,1,0:T(8,128)S(1)} %conv0.1.refs_0_, f32[9,8,6144]{2,1,0:T(8,128)S(1)} %conv1.1.refs_1_, bf16[18,6144]{1,0:T(8,128)(2,1)S(1)} %collective-permute-done.2.refs_2_, bf16[18,6144]{1,0:T(8,128)(2,1)S(1)} %collective-permute-done.3.refs_3_, ...), custom_call_target="tpu_custom_call" | custom-call | tf_op jit(solution)/shard_map/edge_z/pallas_call | solution.py:384
  23.7 0.0 copy-start.6
  23.7 28.2 %all_to_all.20.given = bf16[16,8,16,384]{3,2,1,0:T(8,128)(2,1)S(1)} all-to-all(bf16[16,8,16,384]{3,2,1,0:T(8,128)(2,1)S(1)} %get-tuple-element.23), channel_id=1, replica_groups=mesh['px'=8,'py'=16] {'py'}, dimensions={0} | all-to-all | bytes 3145728 | tf_op jit(solution)/shard_map/all_to_all | solution.py:391
  52.0 0.0 copy-done.6
  52.0 0.0 copy-start.8
  52.0 0.9 y_fwd.2
  52.9 21.4 %all_to_all.21.given = bf16[8,8,16,384]{3,2,1,0:T(8,128)(2,1)S(1)} all-to-all(bf16[8,8,16,384]{3,2,1,0:T(8,128)(2,1)S(1)} %y_fwd.2), channel_id=1, replica_groups=mesh['px'=8,'py'=16] {'px'}, dimensions={0} | all-to-all | bytes 1572864 | tf_op jit(solution)/shard_map/all_to_all | solution.py:393
  74.2 0.0 copy-done.7
  74.2 0.0 copy-done.8
  74.3 0.0 copy-start.5
  74.3 2.4 %spec.1 = bf16[8,8,16,384]{3,2,1,0:T(8,128)(2,1)S(1)} custom-call(bf16[8,8,16,384]{3,2,1,0:T(8,128)(2,1)S(1)} %all_to_all.21.given, bf16[256,128]{1,0:T(8,128)(2,1)S(1)} %copy-done.8, bf16[256,128]{1,0:T(8,128)(2,1)S(1)} %copy-done.7, bf16[2,2,96,96]{3,2,1,0:T(8,128)(2,1)S(1)} %copy-done.3, bf16[2,2,96,96]{3,2,1,0:T(8,128)(2,1)S(1)} %copy-done.4), custom_call_target="tpu_custom_call" | custom-call | tf_op jit(solution)/shard_map/spec/pallas_call | solution.py:395
  76.7 15.2 %all_to_all.22.given = bf16[8,8,16,384]{3,2,1,0:T(8,128)(2,1)S(1)} all-to-all(bf16[8,8,16,384]{3,2,1,0:T(8,128)(2,1)S(1)} %spec.1), channel_id=1, replica_groups=mesh['px'=8,'py'=16] {'px'}, dimensions={0} | all-to-all | bytes 1572864 | tf_op jit(solution)/shard_map/all_to_all | solution.py:398
  91.9 0.6 y_inv.2
  92.4 0.0 copy-start.1
  92.5 28.8 %all_to_all.23.given = bf16[16,8,16,384]{3,2,1,0:T(8,128)(2,1)S(1)} all-to-all(bf16[16,8,16,384]{3,2,1,0:T(8,128)(2,1)S(1)} %y_inv.2), channel_id=1, replica_groups=mesh['px'=8,'py'=16] {'py'}, dimensions={0} | all-to-all | bytes 3145728 | tf_op jit(solution)/shard_map/all_to_all | solution.py:400
  121.3 2.9 %z_inv.2 = bf16[16,8,6144]{2,1,0:T(8,128)(2,1)} custom-call(bf16[16,8,16,384]{3,2,1,0:T(8,128)(2,1)S(1)} %all_to_all.23.given, bf16[256,256]{1,0:T(8,128)(2,1)S(1)} %copy-done.1, bf16[16,128,384]{2,1,0:T(8,128)(2,1)S(1)} %get-tuple-element.24.field), custom_call_target="tpu_custom_call" | custom-call | tf_op jit(solution)/shard_map/z_inv/pallas_call | solution.py:402
  (11 shorter events, 0.0 us)
Async XLA Ops:
  0.0 1.4 %copy-start = (bf16[16,8,6144]{2,1,0:T(8,128)(2,1)S(1)}, bf16[16,8,6144]{2,1,0:T(8,128)(2,1)}, u32[]{:S(2)}) copy-start(bf16[16,8,6144]{2,1,0:T(8,128)(2,1)} %tok.7) | copy-start | bytes 4718596
  1.4 0.8 copy-start.10
  2.3 6.4 %copy-start.9 = (bf16[64,144]{1,0:T(8,128)(2,1)S(1)}, bf16[64,144]{1,0:T(8,128)(2,1)}, u32[]{:S(2)}) copy-start(bf16[64,144]{1,0:T(8,128)(2,1)} %constant.20.clone.pick) | copy-start | bytes 55300
  2.3 6.4 %collective-permute-start = (bf16[1,8,6144]{2,1,0:T(8,128)(2,1)S(1)}, bf16[1,8,6144]{2,1,0:T(8,128)(2,1)S(1)}, u32[]{:S(2)}, u32[]{:S(2)}) collective-permute-start(bf16[1,8,6144]{2,1,0:T(8,128)(2,1)S(1)} %get-tuple-element.16), channel_id=1, source_target_pairs={{0,16},{32,48},{64,80},{96,112},{16,0},{48,32},{80,64},{112,96},{1... | collective-permute-start | bytes 294920 | tf_op jit(solution)/shard_map/ppermute | solution.py:361
  4.5 4.2 %collective-permute-start.1 = (bf16[1,8,6144]{2,1,0:T(8,128)(2,1)S(1)}, bf16[1,8,6144]{2,1,0:T(8,128)(2,1)S(1)}, u32[]{:S(2)}, u32[]{:S(2)}) collective-permute-start(bf16[1,8,6144]{2,1,0:T(8,128)(2,1)S(1)} %get-tuple-element.17), channel_id=1, source_target_pairs={{16,32},{48,64},{80,96},{32,16},{64,48},{96,80},{17,33},{49,65},{8... | collective-permute-start | bytes 294920 | tf_op jit(solution)/shard_map/ppermute | solution.py:361
  9.2 8.6 %collective-permute-start.2 = (bf16[18,6144]{1,0:T(8,128)(2,1)S(1)}, bf16[18,6144]{1,0:T(8,128)(2,1)S(1)}, u32[]{:S(2)}, u32[]{:S(2)}) collective-permute-start(bf16[18,6144]{1,0:T(8,128)(2,1)S(1)} %get-tuple-element.21), channel_id=1, source_target_pairs={{0,1},{2,3},{4,5},{6,7},{8,9},{10,11},{12,13},{14,15},{1,0},{3,2},... | collective-permute-start | bytes 663560 | tf_op jit(solution)/shard_map/ppermute | solution.py:361
  10.2 10.7 %copy-start.2 = (bf16[256,256]{1,0:T(8,128)(2,1)S(1)}, bf16[256,256]{1,0:T(8,128)(2,1)}, u32[]{:S(2)}) copy-start(bf16[256,256]{1,0:T(8,128)(2,1)} %constant.14.clone.refs_5_) | copy-start | bytes 393220
  10.2 10.7 %collective-permute-start.3 = (bf16[18,6144]{1,0:T(8,128)(2,1)S(1)}, bf16[18,6144]{1,0:T(8,128)(2,1)S(1)}, u32[]{:S(2)}, u32[]{:S(2)}) collective-permute-start(bf16[18,6144]{1,0:T(8,128)(2,1)S(1)} %get-tuple-element.22), channel_id=1, source_target_pairs={{1,2},{3,4},{5,6},{7,8},{9,10},{11,12},{13,14},{2,1},{4,3},{6,5},{... | collective-permute-start | bytes 663560 | tf_op jit(solution)/shard_map/ppermute | solution.py:361
  23.7 28.3 %copy-start.6 = (bf16[128,256]{1,0:T(8,128)(2,1)S(1)}, bf16[128,256]{1,0:T(8,128)(2,1)}, u32[]{:S(2)}) copy-start(bf16[128,256]{1,0:T(8,128)(2,1)} %constant.16.clone.y_fwd) | copy-start | bytes 196612
  52.0 22.3 %copy-start.3 = (bf16[2,2,96,96]{3,2,1,0:T(8,128)(2,1)S(1)}, bf16[2,2,96,96]{3,2,1,0:T(8,128)(2,1)}, u32[]{:S(2)}) copy-start(bf16[2,2,96,96]{3,2,1,0:T(8,128)(2,1)} %inner_weight.1) | copy-start | bytes 221188
  52.0 22.3 %copy-start.4 = (bf16[2,2,96,96]{3,2,1,0:T(8,128)(2,1)S(1)}, bf16[2,2,96,96]{3,2,1,0:T(8,128)(2,1)}, u32[]{:S(2)}) copy-start(bf16[2,2,96,96]{3,2,1,0:T(8,128)(2,1)} %outer_weight.1) | copy-start | bytes 221188
  52.0 22.3 %copy-start.7 = (bf16[256,128]{1,0:T(8,128)(2,1)S(1)}, bf16[256,128]{1,0:T(8,128)(2,1)}, u32[]{:S(2)}) copy-start(bf16[256,128]{1,0:T(8,128)(2,1)} %constant.19.clone.x_inv) | copy-start | bytes 196612
  52.0 22.3 %copy-start.8 = (bf16[256,128]{1,0:T(8,128)(2,1)S(1)}, bf16[256,128]{1,0:T(8,128)(2,1)}, u32[]{:S(2)}) copy-start(bf16[256,128]{1,0:T(8,128)(2,1)} %constant.18.clone.x_fwd) | copy-start | bytes 196612
  74.3 17.6 %copy-start.5 = (bf16[256,128]{1,0:T(8,128)(2,1)S(1)}, bf16[256,128]{1,0:T(8,128)(2,1)}, u32[]{:S(2)}) copy-start(bf16[256,128]{1,0:T(8,128)(2,1)} %constant.17.clone.y_inv) | copy-start | bytes 196612
  92.4 28.8 %copy-start.1 = (bf16[256,256]{1,0:T(8,128)(2,1)S(1)}, bf16[256,256]{1,0:T(8,128)(2,1)}, u32[]{:S(2)}) copy-start(bf16[256,256]{1,0:T(8,128)(2,1)} %constant.15.clone.z_inv) | copy-start | bytes 393220

commit v6 on v2

v6 whole, which is shorter than its diff:
```python
import functools
import math

import jax
import jax.numpy as jnp
import ml_dtypes
import numpy as np
from jax import lax
from jax.experimental import pallas as pl
from jax.experimental.pallas import tpu as pltpu
from jax.sharding import PartitionSpec as P

shrink_level = 0.2
F32 = jnp.float32
BF16 = jnp.bfloat16
VMEM = pltpu.VMEM

PX, PY = 8, 16
LX, LY = 16, 8
Z, KZ, C, CB = 32, 16, 192, 96
W = 2 * C
MERGED = Z * C
XP = LX // 2
XE = XP + 1
ZH = Z // 2
Q = 64


def tables(length, modes, weights):
    product = np.asarray(modes)[:, None] * np.arange(length)[None, :] % length
    angle = product.astype(np.float32) * np.float32(2.0 * math.pi / length)
    factor = np.asarray(weights, np.float32)[:, None] / np.float32(math.sqrt(length))
    rounded = [(f(angle) * factor).astype(ml_dtypes.bfloat16) for f in (np.cos, np.sin)]
    return [t.astype(np.float64) for t in rounded]


def kept(length):
    return np.concatenate([np.arange(length // 4), np.arange(length - length // 4, length)])


def forward(cos, sin):
    return np.stack([np.stack([cos, sin], 1), np.stack([-sin, cos], 1)])


def backward(cos, sin):
    cos, sin = cos.T, sin.T
    return np.stack([np.stack([cos, -sin], 1), np.stack([sin, cos], 1)])


def as_bf16(matrix):
    return np.ascontiguousarray(matrix).astype(ml_dtypes.bfloat16)


@functools.cache
def matrices():
    eye = np.eye(LY)
    one = np.ones(KZ)
    cz, sz = tables(Z, np.arange(KZ), one)
    both = np.stack([cz, -sz], 1).reshape(KZ, 2, ZH, 2)
    z_fwd = np.einsum("kpzs,yw->kpyszw", both, eye).reshape(KZ * 2 * LY, 2 * ZH * LY)
    two = np.where(np.arange(KZ) == 0, 1.0, 2.0)
    cz, sz = tables(Z, np.arange(KZ), two)
    both = np.stack([cz, -sz], 1).reshape(KZ, 2, ZH, 2)
    z_inv = np.einsum("kpzs,yw->szykpw", both, eye).reshape(2 * ZH * LY, KZ * 2 * LY)
    n = PY * LY
    cy, sy = tables(n, kept(n), np.ones(Q))
    y_fwd = forward(cy, sy).reshape(2, PX, Q // PX, 2, PY, LY).transpose(1, 0, 2, 4, 3, 5)
    y_fwd = y_fwd.reshape(2 * Q, 2 * n)
    y_inv = backward(cy, sy).reshape(2, PY, LY, 2, PX, Q // PX)
    y_inv = y_inv.transpose(1, 0, 2, 4, 3, 5).reshape(2 * n, 2 * Q)
    n = PX * LX
    cx, sx = tables(n, kept(n), np.ones(Q))
    x_fwd = forward(cx, sx)
    extra = np.zeros((2, Q, 2, PX, 1, 2))
    extra[..., 1:, 0, 0] = x_fwd[..., LX - 1 : n - LX : LX]
    extra[..., :-1, 0, 1] = x_fwd[..., LX::LX]
    x_fwd = np.concatenate([x_fwd.reshape(2, Q, 2, PX, XP, 2), extra], axis=4)
    x_fwd = x_fwd.transpose(5, 0, 1, 3, 4, 2).reshape(4 * Q, 2 * PX * XE)
    x_inv = backward(cx, sx).reshape(2, PX, XP, 2, 2, Q)
    x_inv = x_inv.transpose(3, 0, 1, 2, 4, 5).reshape(4 * PX * XP, 2 * Q)
    pick = np.zeros((2, LX, LX, LY))
    for x in range(LX):
        pick[0, x, x, 0] = pick[1, x, x, LY - 1] = 1
    pick = pick.reshape(2 * LX, LX * LY)
    return [as_bf16(m) for m in (z_fwd, z_inv, y_fwd, y_inv, x_fwd, x_inv, pick)]


def dot(a, b):
    return jnp.dot(a, b, preferred_element_type=F32)


def low_half(rows):
    return lax.broadcasted_iota(jnp.int32, (rows, W), 1) < C


def swap(value):
    return pltpu.roll(value, C, 1)


def odd(axis):
    return lax.rem(lax.axis_index(axis), 2) == 1


def by_order(axis, first, second):
    second, first = second.astype(F32), first.astype(F32)
    up = odd(axis)
    return jnp.where(up, first, second), jnp.where(up, second, first)


def rows_kernel(tok, pick, send_first, send_second):
    step = MERGED // 4
    up = odd("py")
    for j in range(4):
        here = slice(j * step, (j + 1) * step)
        data = tok[:, :, here].astype(F32).reshape(LX * LY, step).astype(BF16)
        out = dot(pick[...], data)
        send_first[:, here] = jnp.where(up, out[:LX], out[LX:]).astype(BF16)
        send_second[:, here] = jnp.where(up, out[LX:], out[:LX]).astype(BF16)


def conv_kernel(tok, narrow, out, shifted, weight):
    weight[...] = jnp.concatenate([narrow[...], narrow[...]], axis=1)
    pad = jnp.zeros((LY, C), F32)
    for x in range(LX):
        shifted[x] = jnp.concatenate([pad, tok[x].astype(F32), pad], axis=1)
    row_at = lax.broadcasted_iota(jnp.int32, (LY, 128), 0)

    @pl.loop(0, MERGED // 128)
    def _(j):
        at = pl.multiple_of(j * 128, 128)
        after = pl.multiple_of(j * 128 + W, 128)
        here = pl.ds(at, 128)
        phase = pl.multiple_of(lax.rem(j, 3) * 128, 128)
        wide = [jnp.broadcast_to(weight[t : t + 1, pl.ds(phase, 128)], (LY, 128)) for t in range(27)]
        sums = {}
        for x in range(LX + 2):
            if x < LX:
                mid = tok[x, :, here].astype(F32)
                before = shifted[x, :, here]
                behind = shifted[x, :, pl.ds(after, 128)]
                for a in range(3):
                    to = x + 2 - a
                    for b in range(3):
                        t = a * 9 + b * 3
                        term = before * wide[t] + mid * wide[t + 1] + behind * wide[t + 2]
                        sums[to, b] = sums[to, b] + term if (to, b) in sums else term
            down = pltpu.roll(sums.pop((x, 0)), 1, 0)
            up = pltpu.roll(sums.pop((x, 2)), LY - 1, 0)
            down = jnp.where(row_at == 0, 0.0, down)
            up = jnp.where(row_at == LY - 1, 0.0, up)
            out[x, :, here] = sums.pop((x, 1)) + down + up


def edge_kernel(
    conv, first, second, narrow, z_fwd, field, freq, to_below, to_above, ylo, yhi, ylo_s, yhi_s, edge, weight
):
    weight[...] = jnp.concatenate([narrow[...], narrow[...]], axis=1)
    for rows, rows_s, value in zip((ylo, yhi), (ylo_s, yhi_s), by_order("py", first[...], second[...])):
        none = jnp.zeros((2, MERGED), F32)
        value = jnp.concatenate([none, value, none], axis=0)
        rows[...] = value
        pad = jnp.zeros((LX + 4, C), F32)
        rows_s[...] = jnp.concatenate([pad, value, pad], axis=1)

    @pl.loop(0, MERGED // 128)
    def _(j):
        at = pl.multiple_of(j * 128, 128)
        after = pl.multiple_of(j * 128 + W, 128)
        here = pl.ds(at, 128)
        phase = pl.multiple_of(lax.rem(j, 3) * 128, 128)
        for side, rows, rows_s, b in ((0, ylo, ylo_s, 0), (1, yhi, yhi_s, 2)):
            mid = rows[:, here]
            before = rows_s[:, here]
            behind = rows_s[:, pl.ds(after, 128)]
            total = None
            for a in range(3):
                t = a * 9 + b * 3
                taps = [weight[t + e : t + e + 1, pl.ds(phase, 128)] for e in range(3)]
                term = before * taps[0] + mid * taps[1] + behind * taps[2]
                term = term[a : a + LX + 2]
                total = term if total is None else total + term
            edge[side, :, here] = total

    low = low_half(ZH * LY)
    row_at = lax.broadcasted_iota(jnp.int32, (LY, W), 0)
    for xp in range(XE):
        parts = []
        for x in (2 * xp, 2 * xp + 1) if xp < XP else (-1, LX):
            at = x + 1
            rows = []
            for z in range(ZH):
                here = slice(z * W, (z + 1) * W)
                more = jnp.where(row_at == 0, edge[0, at : at + 1, here], 0.0)
                more = jnp.where(row_at == LY - 1, edge[1, at : at + 1, here], more)
                rows.append(conv[at, :, here] + more)
            part = jnp.concatenate(rows, axis=0)
            if xp < XP:
                field[x] = part.astype(BF16)
            parts.append(part)
        first, second = parts
        if xp == XP:
            to_below[...] = first.astype(BF16)
            to_above[...] = second.astype(BF16)
        even = jnp.where(low, first, swap(second)).astype(BF16)
        odd_z = jnp.where(low, swap(first), second).astype(BF16)
        out = dot(z_fwd[...], jnp.concatenate([even, odd_z], axis=0))
        freq[:, xp] = out.astype(BF16).reshape(KZ, 2 * LY, W)


def y_forward_kernel(given, y_fwd, out):
    for xp in range(XE):
        data = given[:, xp].reshape(2 * PY * LY, W)
        out[:, xp] = dot(y_fwd[...], data).astype(BF16).reshape(PX, 2 * Q // PX, W)


def gather(rows, out):
    count = 2 * XP * Q // PX
    for d in range(PX):
        block = [rows[t, pl.ds(d * count, count), :] for t in range(W // 128)]
        out[d] = jnp.concatenate(block, axis=1).astype(BF16).reshape(out.shape[1:])


def shrink(v):
    return v - jnp.clip(v, -shrink_level, shrink_level)


def lay_out(weight, width, copies, out):
    for b in range(C // CB):
        columns = []
        for part in range(2):
            block = weight[part, b].astype(F32)
            columns += [jnp.zeros((CB, b * CB), F32)] * (b > 0) + [block]
            columns += [jnp.zeros((CB, width - (b + 1) * CB), F32)] * (width > (b + 1) * CB)
            columns += columns[-2:] * (copies - 1)
        out[b * CB : (b + 1) * CB] = jnp.concatenate(columns, axis=1).astype(BF16)
    out[C:] = jnp.zeros((256 - C, out.shape[1]), BF16)


def spectrum_kernel(given, x_fwd, x_inv, inner_weight, outer_weight, out, rows, arrived, inner, outer):
    lay_out(inner_weight, 256, 1, inner)
    lay_out(outer_weight, C, 2, outer)
    count = Q // PX
    low = low_half(2 * PX * XP)
    wide = given[...].astype(F32).reshape(2 * count * PX * XE, W)
    for t in range(W // 128):
        arrived[t] = wide[:, t * 128 : (t + 1) * 128]
    data = []
    for q in range(count):
        some = [arrived[t, pl.ds(q, 2 * PX * XE, stride=count), :] for t in range(W // 128)]
        data.append(jnp.concatenate(some, axis=1).astype(BF16))
    both = dot(x_fwd[...], jnp.concatenate(data, axis=1))
    spec = []
    for q in range(count):
        part = both[:, q * W : (q + 1) * W]
        part = part[: 2 * Q] + swap(part[2 * Q :])
        spec.append(part[:, :256].astype(BF16))
    mixed = dot(jnp.concatenate(spec, axis=0), inner[...]).reshape(count, 2, Q, 512)
    hidden_r = jnp.tanh(mixed[:, 0, :, :256] - mixed[:, 1, :, 256:])
    hidden_i = jnp.tanh(mixed[:, 0, :, 256:] + mixed[:, 1, :, :256])
    hidden = jnp.stack([hidden_r, hidden_i], axis=1).astype(BF16).reshape(count * 2 * Q, 256)
    mixed = dot(hidden, outer[...]).reshape(count, 2, Q, 2 * W)
    filt_r = shrink(mixed[:, 0, :, :W] - mixed[:, 1, :, W:]).astype(BF16)
    filt_i = shrink(mixed[:, 0, :, W:] + mixed[:, 1, :, :W]).astype(BF16)
    filt = [jnp.concatenate([filt_r[q], filt_i[q]], axis=0) for q in range(count)]
    both = dot(x_inv[...], jnp.concatenate(filt, axis=1))
    for q in range(count):
        part = both[:, q * W : (q + 1) * W]
        back = jnp.where(low, part[: 2 * PX * XP], part[2 * PX * XP :])
        for part in range(2):
            for t in range(W // 128):
                rows[t, pl.ds(part * count + q, PX * XP, stride=2 * count), :] = back[
                    part * PX * XP : (part + 1) * PX * XP, t * 128 : (t + 1) * 128
                ]
    gather(rows, out)


def y_inverse_kernel(given, y_inv, out):
    for xp in range(XP):
        data = given[:, xp].reshape(2 * Q, W)
        out[:, xp] = dot(y_inv[...], data).astype(BF16).reshape(PY, 2 * LY, W)


def z_inverse_kernel(given, z_inv, field, below, above, out):
    low = low_half(ZH * LY)
    step, pairs = pl.program_id(0), given.shape[1]
    below = jnp.where(step == 0, below[...].astype(F32), 0.0)
    above = jnp.where(step == XP // pairs - 1, above[...].astype(F32), 0.0)
    for xp in range(pairs):
        data = given[:, xp].reshape(2 * KZ * LY, W)
        value = dot(z_inv[...], data)
        even, odd = value[: ZH * LY], value[ZH * LY :]
        first = jnp.where(low, even, swap(odd)) + field[2 * xp].astype(F32)
        second = jnp.where(low, swap(even), odd) + field[2 * xp + 1].astype(F32)
        if xp == 0:
            first = first + below
        if xp == pairs - 1:
            second = second + above
        for x, value in ((2 * xp, first), (2 * xp + 1, second)):
            for z in range(ZH):
                out[x, :, z * W : (z + 1) * W] = value[z * LY : (z + 1) * LY].astype(BF16)


def call(kernel, outs, scratch=(), name=None, in_specs=None):
    return pl.pallas_call(
        kernel,
        out_shape=outs,
        scratch_shapes=list(scratch),
        **({} if in_specs is None else {"in_specs": in_specs}),
        compiler_params=pltpu.CompilerParams(vmem_limit_bytes=20 * 2**20),
        name=name,
    )


def shape(*dims):
    return jax.ShapeDtypeStruct(dims, BF16)


def swap_pairs(value, axis, count, start):
    low = range(start, count - 1, 2)
    return lax.ppermute(value, axis, [(i, i + 1) for i in low] + [(i + 1, i) for i in low])


def body(tokens, conv_weight, inner_weight, outer_weight):
    z_fwd, z_inv, y_fwd, y_inv, x_fwd, x_inv, pick = (jnp.asarray(m) for m in matrices())
    wide = MERGED + 2 * C
    first, second = call(rows_kernel, [shape(LX, MERGED)] * 2, name="y_rows")(tokens, pick)
    second = swap_pairs(second, "py", PY, 1)
    first = swap_pairs(first, "py", PY, 0)
    conv = call(
        conv_kernel,
        jax.ShapeDtypeStruct((LX + 2, LY, MERGED), F32),
        [VMEM((LX, LY, wide), F32), VMEM((27, W), F32)],
        name="conv",
    )(tokens, conv_weight)
    rows = [VMEM((LX + 4, MERGED), F32)] * 2 + [VMEM((LX + 4, wide), F32)] * 2
    field, freq, to_below, to_above = call(
        edge_kernel,
        [shape(LX, ZH * LY, W), shape(KZ, XE, 2 * LY, W)] + [shape(ZH * LY, W)] * 2,
        rows + [VMEM((2, LX + 2, MERGED), F32), VMEM((27, W), F32)],
        name="edge_z",
    )(conv, first, second, conv_weight, z_fwd)
    rows = VMEM((W // 128, 2 * XP * Q, 128), F32)
    up = odd("px")
    first = swap_pairs(jnp.where(up, to_below, to_above), "px", PX, 0)
    second = swap_pairs(jnp.where(up, to_above, to_below), "px", PX, 1)
    below, above = jnp.where(up, first, second), jnp.where(up, second, first)
    freq = lax.all_to_all(freq, "py", 0, 0, tiled=True)
    freq, below, above = lax.optimization_barrier((freq, below, above))
    freq = call(y_forward_kernel, shape(PX, XE, 2 * Q // PX, W), name="y_fwd")(freq, y_fwd)
    freq = lax.all_to_all(freq, "px", 0, 0, tiled=True)
    mixing = [VMEM((256, 512), BF16), VMEM((256, 4 * C), BF16)]
    freq = call(spectrum_kernel, shape(PX, XP, 2 * Q // PX, W), [rows, VMEM((W // 128, 2 * XE * Q, 128), F32)] + mixing, name="spec")(
        freq, x_fwd, x_inv, inner_weight, outer_weight
    )
    freq = lax.all_to_all(freq, "px", 0, 0, tiled=True)
    freq = call(y_inverse_kernel, shape(PY, XP, 2 * LY, W), name="y_inv")(freq, y_inv)
    freq = lax.all_to_all(freq, "py", 0, 0, tiled=True)
    steps = 4
    return pl.pallas_call(
        z_inverse_kernel,
        out_shape=shape(LX, LY, MERGED),
        grid=(steps,),
        in_specs=[
            pl.BlockSpec((KZ, XP // steps, 2 * LY, W), lambda i: (0, i, 0, 0)),
            pl.BlockSpec(z_inv.shape, lambda i: (0, 0)),
            pl.BlockSpec((LX // steps, ZH * LY, W), lambda i: (i, 0, 0)),
            pl.BlockSpec((ZH * LY, W), lambda i: (0, 0)),
            pl.BlockSpec((ZH * LY, W), lambda i: (0, 0)),
        ],
        out_specs=pl.BlockSpec((LX // steps, LY, MERGED), lambda i: (i, 0, 0)),
        compiler_params=pltpu.CompilerParams(vmem_limit_bytes=20 * 2**20),
        name="z_inv",
    )(freq, z_inv, field, below, above)


def solution(mesh):
    in_specs = (P("px", "py", None), P(), P(), P())
    out_specs = P("px", "py", None)
    return jax.shard_map(body, mesh=mesh, in_specs=in_specs, out_specs=out_specs, check_vma=False)
```

time: 131 us -> 120 us (0.916)
  blocking collectives: 91.6 us -> 64.2 us
  waiting for transfers between devices: 0.91 us -> 18.9 us
  starting transfers between devices: 12.4 us -> 15.7 us
  local copies, waits for them, and re-layouts: 5.12 us -> 2.98 us
  Pallas kernels: 20 us -> 18.1 us
    all_to_all x2 -> x1, blocking collectives: 57 us -> 28.6 us  [body(): freq = lax.all_to_all(freq, 'py', 0, 0, tiled=True)]
    all_to_all x0 -> x1, waiting for transfers between devices: none -> 16.1 us  [body(): freq = lax.all_to_all(freq, 'py', 0, 0, tiled=True)]
    all_to_all x0 -> x1, starting transfers between devices: none -> 6.31 us  [body(): freq = lax.all_to_all(freq, 'py', 0, 0, tiled=True)]
    slice x2 -> x0, local copies, waits for them, and re-layouts: 3.52 us -> none  [the longest x1 2.52 us: halos_y(): tokens[:, y]]
    ppermute x4, starting transfers between devices: 12.4 us -> 9.36 us  [swap_pairs(): lax.ppermute(value, axis, [(i, i + 1) for i in low] + [(i + 1, i) for i i...]
    ppermute x4, waiting for transfers between devices: 0.91 us -> 2.88 us  [swap_pairs(): lax.ppermute(value, axis, [(i, i + 1) for i in low] + [(i + 1, i) for i i...]
    pallas_call x5, Pallas kernels: 16.5 us -> 14.7 us  [the longest x1 6.95 us: body(): call(conv_kernel, jax.ShapeDtypeStruct((LX + 2, LY, MERGED), F32), [VMEM(...]
    unnamed x24 -> x22, local copies, waits for them, and re-layouts: 1.51 us -> 2.98 us
  transfers between devices with their start and end apart: 4 -> 5, of which waited for: 1 -> 2; matrix products, arithmetic and copies ran while one was open for 3% -> 0% of each run, Pallas kernels for 6% -> 6%
where the time goes in v6:
time: 120 us
  blocking collectives  64.2 us (54%)
  waiting for transfers between devices  18.9 us (16%)
  Pallas kernels  18.1 us (15%)
  starting transfers between devices  15.7 us (13%)
  local copies, waits for them, and re-layouts  2.98 us (2%)
    all_to_all x2, blocking collectives, body(): freq = lax.all_to_all(freq, 'px', 0, 0, tiled=True)  35.6 us
    all_to_all x1, blocking collectives, body(): freq = lax.all_to_all(freq, 'py', 0, 0, tiled=True)  28.6 us
    all_to_all x1, waiting for transfers between devices, body(): freq = lax.all_to_all(freq, 'py', 0, 0, tiled=True)  16.1 us
    ppermute x4, starting transfers between devices, swap_pairs(): lax.ppermute(value, axis, [(i, i + 1) for i in low] + [(i + 1, i) for i i...  9.36 us
    pallas_call x1, Pallas kernels, body(): call(conv_kernel, jax.ShapeDtypeStruct((LX + 2, LY, MERGED), F32), [VMEM(...  6.95 us
    all_to_all x1, starting transfers between devices, body(): freq = lax.all_to_all(freq, 'py', 0, 0, tiled=True)  6.31 us
    pallas_call x1, Pallas kernels, body(): call(edge_kernel, [shape(LX, ZH * LY, W), shape(KZ, XE, 2 * LY, W)] + [sh...  4.35 us
    unnamed x22, local copies, waits for them, and re-layouts  2.98 us
  transfers between devices with their start and end apart: 5, of which 2 were waited for; matrix products, arithmetic and copies ran while one was open for 0% of the time, Pallas kernels for 6%

profile of v6, /device:TPU:1, one launch (start us, length us, event | category | flops | bytes accessed | tf_op | source)
XLA Modules:
  0.0 120.1 jit_solution(17679796404066685952)
XLA Ops:
  0.0 1.4 %copy-done = bf16[16,8,6144]{2,1,0:T(8,128)(2,1)S(1)} copy-done((bf16[16,8,6144]{2,1,0:T(8,128)(2,1)S(1)}, bf16[16,8,6144]{2,1,0:T(8,128)(2,1)}, u32[]{:S(2)}) %copy-start) | copy-done | bytes 1572888
  1.4 0.7 copy-done.10
  2.1 0.3 y_rows.1
  2.5 1.5 %collective-permute-start = (bf16[16,6144]{1,0:T(8,128)(2,1)S(1)}, bf16[16,6144]{1,0:T(8,128)(2,1)S(1)}, u32[]{:S(2)}, u32[]{:S(2)}) collective-permute-start(bf16[16,6144]{1,0:T(8,128)(2,1)S(1)} %get-tuple-element.14), channel_id=1, source_target_pairs={{0,1},{2,3},{4,5},{6,7},{8,9},{10,11},{12,13},{14,15},{1,0},{3,2},... | collective-permute-start | bytes 589832 | tf_op jit(solution)/shard_map/ppermute | solution.py:320
  4.0 3.2 %collective-permute-start.1 = (bf16[16,6144]{1,0:T(8,128)(2,1)S(1)}, bf16[16,6144]{1,0:T(8,128)(2,1)S(1)}, u32[]{:S(2)}, u32[]{:S(2)}) collective-permute-start(bf16[16,6144]{1,0:T(8,128)(2,1)S(1)} %get-tuple-element.15), channel_id=1, source_target_pairs={{1,2},{3,4},{5,6},{7,8},{9,10},{11,12},{13,14},{2,1},{4,3},{6,5},{... | collective-permute-start | bytes 589832 | tf_op jit(solution)/shard_map/ppermute | solution.py:320
  7.2 0.0 copy-done.1
  7.2 6.9 %conv.1 = f32[18,8,6144]{2,1,0:T(8,128)S(1)} custom-call(bf16[16,8,6144]{2,1,0:T(8,128)(2,1)S(1)} %copy-done, f32[27,192]{1,0:T(8,128)S(1)} %copy-done.1), custom_call_target="tpu_custom_call" | custom-call | tf_op jit(solution)/shard_map/conv/pallas_call | solution.py:329
  14.2 0.0 collective-permute-done.first
  14.2 0.0 collective-permute-done.1.second
  14.2 0.0 copy-done.4
  14.2 4.4 %edge_z.1 = (bf16[16,128,384]{2,1,0:T(8,128)(2,1)S(1)}, bf16[16,9,16,384]{3,2,1,0:T(8,128)(2,1)}, bf16[128,384]{1,0:T(8,128)(2,1)S(1)}, bf16[128,384]{1,0:T(8,128)(2,1)S(1)}) custom-call(f32[18,8,6144]{2,1,0:T(8,128)S(1)} %conv.1, bf16[16,6144]{1,0:T(8,128)(2,1)S(1)} %collective-permute-done.first, bf16[16,6144]{1,0:T(8,128)(2,1)S(1)} %collective-permute-done.1.second, ...), custom_call_target="tpu_custom_call" | custom-call | tf_op jit(solution)/shard_map/edge_z/pallas_call | solution.py:336
  18.6 6.3 %all-to-all-start = ((bf16[16,9,16,384]{3,2,1,0:T(8,128)(2,1)}), bf16[16,9,16,384]{3,2,1,0:T(8,128)(2,1)S(1)}, u32[]{:S(2)}, u32[]{:S(2)}) async-start(bf16[16,9,16,384]{3,2,1,0:T(8,128)(2,1)} %get-tuple-element.16), calls=%async_computation | async-start | bytes 3538944 | tf_op jit(solution)/shard_map/all_to_all | solution.py:347
  24.9 0.7 collective-permute-start.3
  25.6 3.9 %collective-permute-start.2 = (bf16[128,384]{1,0:T(8,128)(2,1)S(1)}, bf16[128,384]{1,0:T(8,128)(2,1)S(1)}, u32[]{:S(2)}, u32[]{:S(2)}) collective-permute-start(bf16[128,384]{1,0:T(8,128)(2,1)S(1)} %get-tuple-element.26), channel_id=1, source_target_pairs={{0,16},{32,48},{64,80},{96,112},{16,0},{48,32},{80,64},{112,96},{1... | collective-permute-start | bytes 294920 | tf_op jit(solution)/shard_map/ppermute | solution.py:320
  29.5 0.0 collective-permute-done.3
  29.5 2.9 %collective-permute-done.2 = bf16[128,384]{1,0:T(8,128)(2,1)S(1)} collective-permute-done((bf16[128,384]{1,0:T(8,128)(2,1)S(1)}, bf16[128,384]{1,0:T(8,128)(2,1)S(1)}, u32[]{:S(2)}, u32[]{:S(2)}) %collective-permute-start.2) | collective-permute-done | bytes 98336 | tf_op jit(solution)/shard_map/ppermute | solution.py:320
  32.4 16.1 %all-to-all-done.given = bf16[16,9,16,384]{3,2,1,0:T(8,128)(2,1)S(1)} async-done(((bf16[16,9,16,384]{3,2,1,0:T(8,128)(2,1)}), bf16[16,9,16,384]{3,2,1,0:T(8,128)(2,1)S(1)}, u32[]{:S(2)}, u32[]{:S(2)}) %all-to-all-start) | async-done | bytes 1769504 | tf_op jit(solution)/shard_map/all_to_all | solution.py:347
  48.5 0.8 copy-done.9
  49.3 0.5 y_fwd.2
  49.8 20.7 %all_to_all.20.given = bf16[8,9,16,384]{3,2,1,0:T(8,128)(2,1)S(1)} all-to-all(bf16[8,9,16,384]{3,2,1,0:T(8,128)(2,1)S(1)} %y_fwd.2), channel_id=1, replica_groups=mesh['px'=8,'py'=16] {'px'}, dimensions={0} | all-to-all | bytes 1769472 | tf_op jit(solution)/shard_map/all_to_all | solution.py:350
  70.4 0.0 copy-done.3
  70.5 0.0 copy-done.5
  70.5 0.0 copy-done.6
  70.5 0.0 copy-done.8
  70.5 0.0 copy-start.7
  70.5 2.6 %spec.1 = bf16[8,8,16,384]{3,2,1,0:T(8,128)(2,1)S(1)} custom-call(bf16[8,9,16,384]{3,2,1,0:T(8,128)(2,1)S(1)} %all_to_all.20.given, bf16[256,144]{1,0:T(8,128)(2,1)S(1)} %copy-done.3, bf16[256,128]{1,0:T(8,128)(2,1)S(1)} %copy-done.8, bf16[2,2,96,96]{3,2,1,0:T(8,128)(2,1)S(1)} %copy-done.5, bf16[2,2,96,96]{3,2,1,0:T(8,128)(2,1)S(1)} %copy-done.6), custom_call_target="tpu_custom_call" | custom-call | tf_op jit(solution)/shard_map/spec/pallas_call | solution.py:352
  73.1 15.0 %all_to_all.21.given = bf16[8,8,16,384]{3,2,1,0:T(8,128)(2,1)S(1)} all-to-all(bf16[8,8,16,384]{3,2,1,0:T(8,128)(2,1)S(1)} %spec.1), channel_id=1, replica_groups=mesh['px'=8,'py'=16] {'px'}, dimensions={0} | all-to-all | bytes 1572864 | tf_op jit(solution)/shard_map/all_to_all | solution.py:355
  88.0 0.6 y_inv.2
  88.6 0.0 copy-start.2
  88.6 28.6 %all_to_all.22.given = bf16[16,8,16,384]{3,2,1,0:T(8,128)(2,1)S(1)} all-to-all(bf16[16,8,16,384]{3,2,1,0:T(8,128)(2,1)S(1)} %y_inv.2), channel_id=1, replica_groups=mesh['px'=8,'py'=16] {'py'}, dimensions={0} | all-to-all | bytes 3145728 | tf_op jit(solution)/shard_map/all_to_all | solution.py:357
  117.1 0.0 copy-done.2
  117.2 2.9 %z_inv.2 = bf16[16,8,6144]{2,1,0:T(8,128)(2,1)} custom-call(bf16[16,8,16,384]{3,2,1,0:T(8,128)(2,1)S(1)} %all_to_all.22.given, bf16[256,256]{1,0:T(8,128)(2,1)S(1)} %copy-done.2, bf16[16,128,384]{2,1,0:T(8,128)(2,1)S(1)} %get-tuple-element.20.field, bf16[128,384]{1,0:T(8,128)(2,1)S(1)} %get-tuple-element.21.below, bf16[128,384]{1,0:T(8,128)(2,1)S(1)} %get-tuple-element.22.above), custom_call_target="tpu_custom_call" | custom-call | tf_op jit(solution)/shard_map/z_inv/pallas_call | solution.py:359
  (12 shorter events, 0.1 us)
Async XLA Ops:
  0.0 1.4 %copy-start = (bf16[16,8,6144]{2,1,0:T(8,128)(2,1)S(1)}, bf16[16,8,6144]{2,1,0:T(8,128)(2,1)}, u32[]{:S(2)}) copy-start(bf16[16,8,6144]{2,1,0:T(8,128)(2,1)} %tok.3) | copy-start | bytes 4718596
  1.4 0.7 copy-start.10
  2.1 5.1 %copy-start.1 = (f32[27,192]{1,0:T(8,128)S(1)}, f32[27,192]{1,0:T(8,128)}, u32[]{:S(2)}) copy-start(f32[27,192]{1,0:T(8,128)} %narrow.3) | copy-start | bytes 62212
  2.5 11.7 %collective-permute-start = (bf16[16,6144]{1,0:T(8,128)(2,1)S(1)}, bf16[16,6144]{1,0:T(8,128)(2,1)S(1)}, u32[]{:S(2)}, u32[]{:S(2)}) collective-permute-start(bf16[16,6144]{1,0:T(8,128)(2,1)S(1)} %get-tuple-element.14), channel_id=1, source_target_pairs={{0,1},{2,3},{4,5},{6,7},{8,9},{10,11},{12,13},{14,15},{1,0},{3,2},... | collective-permute-start | bytes 589832 | tf_op jit(solution)/shard_map/ppermute | solution.py:320
  4.0 10.2 %copy-start.4 = (bf16[256,256]{1,0:T(8,128)(2,1)S(1)}, bf16[256,256]{1,0:T(8,128)(2,1)}, u32[]{:S(2)}) copy-start(bf16[256,256]{1,0:T(8,128)(2,1)} %constant.26.clone.z_fwd) | copy-start | bytes 393220
  4.0 10.2 %collective-permute-start.1 = (bf16[16,6144]{1,0:T(8,128)(2,1)S(1)}, bf16[16,6144]{1,0:T(8,128)(2,1)S(1)}, u32[]{:S(2)}, u32[]{:S(2)}) collective-permute-start(bf16[16,6144]{1,0:T(8,128)(2,1)S(1)} %get-tuple-element.15), channel_id=1, source_target_pairs={{1,2},{3,4},{5,6},{7,8},{9,10},{11,12},{13,14},{2,1},{4,3},{6,5},{... | collective-permute-start | bytes 589832 | tf_op jit(solution)/shard_map/ppermute | solution.py:320
  18.6 29.9 %all-to-all-start = ((bf16[16,9,16,384]{3,2,1,0:T(8,128)(2,1)}), bf16[16,9,16,384]{3,2,1,0:T(8,128)(2,1)S(1)}, u32[]{:S(2)}, u32[]{:S(2)}) async-start(bf16[16,9,16,384]{3,2,1,0:T(8,128)(2,1)} %get-tuple-element.16), calls=%async_computation | async-start | bytes 3538944 | tf_op jit(solution)/shard_map/all_to_all | solution.py:347
  24.9 4.6 %collective-permute-start.3 = (bf16[128,384]{1,0:T(8,128)(2,1)S(1)}, bf16[128,384]{1,0:T(8,128)(2,1)S(1)}, u32[]{:S(2)}, u32[]{:S(2)}) collective-permute-start(bf16[128,384]{1,0:T(8,128)(2,1)S(1)} %get-tuple-element.25), channel_id=1, source_target_pairs={{16,32},{48,64},{80,96},{32,16},{64,48},{96,80},{17,33},{49,65},{8... | collective-permute-start | bytes 294920 | tf_op jit(solution)/shard_map/ppermute | solution.py:320
  25.6 6.8 %collective-permute-start.2 = (bf16[128,384]{1,0:T(8,128)(2,1)S(1)}, bf16[128,384]{1,0:T(8,128)(2,1)S(1)}, u32[]{:S(2)}, u32[]{:S(2)}) collective-permute-start(bf16[128,384]{1,0:T(8,128)(2,1)S(1)} %get-tuple-element.26), channel_id=1, source_target_pairs={{0,16},{32,48},{64,80},{96,112},{16,0},{48,32},{80,64},{112,96},{1... | collective-permute-start | bytes 294920 | tf_op jit(solution)/shard_map/ppermute | solution.py:320
  48.5 0.8 copy-start.9
  49.3 21.1 %copy-start.3 = (bf16[256,144]{1,0:T(8,128)(2,1)S(1)}, bf16[256,144]{1,0:T(8,128)(2,1)}, u32[]{:S(2)}) copy-start(bf16[256,144]{1,0:T(8,128)(2,1)} %constant.30.clone.x_fwd) | copy-start | bytes 221188
  49.3 21.1 %copy-start.5 = (bf16[2,2,96,96]{3,2,1,0:T(8,128)(2,1)S(1)}, bf16[2,2,96,96]{3,2,1,0:T(8,128)(2,1)}, u32[]{:S(2)}) copy-start(bf16[2,2,96,96]{3,2,1,0:T(8,128)(2,1)} %inner_weight.1) | copy-start | bytes 221188
  49.3 21.1 %copy-start.6 = (bf16[2,2,96,96]{3,2,1,0:T(8,128)(2,1)S(1)}, bf16[2,2,96,96]{3,2,1,0:T(8,128)(2,1)}, u32[]{:S(2)}) copy-start(bf16[2,2,96,96]{3,2,1,0:T(8,128)(2,1)} %outer_weight.1) | copy-start | bytes 221188
  49.3 21.1 %copy-start.8 = (bf16[256,128]{1,0:T(8,128)(2,1)S(1)}, bf16[256,128]{1,0:T(8,128)(2,1)}, u32[]{:S(2)}) copy-start(bf16[256,128]{1,0:T(8,128)(2,1)} %constant.31.clone.x_inv) | copy-start | bytes 196612
  70.5 17.5 %copy-start.7 = (bf16[256,128]{1,0:T(8,128)(2,1)S(1)}, bf16[256,128]{1,0:T(8,128)(2,1)}, u32[]{:S(2)}) copy-start(bf16[256,128]{1,0:T(8,128)(2,1)} %constant.29.clone.y_inv) | copy-start | bytes 196612
  88.6 28.6 %copy-start.2 = (bf16[256,256]{1,0:T(8,128)(2,1)S(1)}, bf16[256,256]{1,0:T(8,128)(2,1)}, u32[]{:S(2)}) copy-start(bf16[256,256]{1,0:T(8,128)(2,1)} %constant.27.clone.z_inv) | copy-start | bytes 393220

commit v7 on v6

--- a/solution.py
+++ b/solution.py
@@ -78,11 +78,7 @@
     x_fwd = x_fwd.transpose(5, 0, 1, 3, 4, 2).reshape(4 * Q, 2 * PX * XE)
     x_inv = backward(cx, sx).reshape(2, PX, XP, 2, 2, Q)
     x_inv = x_inv.transpose(3, 0, 1, 2, 4, 5).reshape(4 * PX * XP, 2 * Q)
-    pick = np.zeros((2, LX, LX, LY))
-    for x in range(LX):
-        pick[0, x, x, 0] = pick[1, x, x, LY - 1] = 1
-    pick = pick.reshape(2 * LX, LX * LY)
-    return [as_bf16(m) for m in (z_fwd, z_inv, y_fwd, y_inv, x_fwd, x_inv, pick)]
+    return [as_bf16(m) for m in (z_fwd, z_inv, y_fwd, y_inv, x_fwd, x_inv)]
 
 
 def dot(a, b):
@@ -107,13 +103,17 @@
     return jnp.where(up, first, second), jnp.where(up, second, first)
 
 
-def rows_kernel(tok, pick, send_first, send_second):
+def rows_kernel(tok, send_first, send_second):
     step = MERGED // 4
+    row = lax.broadcasted_iota(jnp.int32, (2 * LX, LX * LY), 0)
+    cell = lax.broadcasted_iota(jnp.int32, (2 * LX, LX * LY), 1)
+    wanted = jnp.where(row < LX, row * LY, (row - LX) * LY + LY - 1)
+    pick = jnp.where(cell == wanted, 1.0, 0.0).astype(BF16)
     up = odd("py")
     for j in range(4):
         here = slice(j * step, (j + 1) * step)
         data = tok[:, :, here].astype(F32).reshape(LX * LY, step).astype(BF16)
-        out = dot(pick[...], data)
+        out = dot(pick, data)
         send_first[:, here] = jnp.where(up, out[:LX], out[LX:]).astype(BF16)
         send_second[:, here] = jnp.where(up, out[LX:], out[:LX]).astype(BF16)
 
@@ -282,30 +282,26 @@
 
 def z_inverse_kernel(given, z_inv, field, below, above, out):
     low = low_half(ZH * LY)
-    step, pairs = pl.program_id(0), given.shape[1]
-    below = jnp.where(step == 0, below[...].astype(F32), 0.0)
-    above = jnp.where(step == XP // pairs - 1, above[...].astype(F32), 0.0)
-    for xp in range(pairs):
+    for xp in range(XP):
         data = given[:, xp].reshape(2 * KZ * LY, W)
         value = dot(z_inv[...], data)
         even, odd = value[: ZH * LY], value[ZH * LY :]
         first = jnp.where(low, even, swap(odd)) + field[2 * xp].astype(F32)
         second = jnp.where(low, swap(even), odd) + field[2 * xp + 1].astype(F32)
         if xp == 0:
-            first = first + below
-        if xp == pairs - 1:
-            second = second + above
+            first = first + below[...].astype(F32)
+        if xp == XP - 1:
+            second = second + above[...].astype(F32)
         for x, value in ((2 * xp, first), (2 * xp + 1, second)):
             for z in range(ZH):
                 out[x, :, z * W : (z + 1) * W] = value[z * LY : (z + 1) * LY].astype(BF16)
 
 
-def call(kernel, outs, scratch=(), name=None, in_specs=None):
+def call(kernel, outs, scratch=(), name=None):
     return pl.pallas_call(
         kernel,
         out_shape=outs,
         scratch_shapes=list(scratch),
-        **({} if in_specs is None else {"in_specs": in_specs}),
         compiler_params=pltpu.CompilerParams(vmem_limit_bytes=20 * 2**20),
         name=name,
     )
@@ -321,15 +317,18 @@
 
 
 def body(tokens, conv_weight, inner_weight, outer_weight):
-    z_fwd, z_inv, y_fwd, y_inv, x_fwd, x_inv, pick = (jnp.asarray(m) for m in matrices())
+    z_fwd, z_inv, y_fwd, y_inv, x_fwd, x_inv = (jnp.asarray(m) for m in matrices())
     wide = MERGED + 2 * C
-    first, second = call(rows_kernel, [shape(LX, MERGED)] * 2, name="y_rows")(tokens, pick)
+    first, second = call(rows_kernel, [shape(LX, MERGED)] * 2, name="y_rows")(tokens)
     second = swap_pairs(second, "py", PY, 1)
     first = swap_pairs(first, "py", PY, 0)
     conv = call(
         conv_kernel,
         jax.ShapeDtypeStruct((LX + 2, LY, MERGED), F32),
-        [VMEM((LX, LY, wide), F32), VMEM((27, W), F32)],
+        [
+            VMEM((LX, LY, wide), F32),
+            VMEM((27, W), F32),
+        ],
         name="conv",
     )(tokens, conv_weight)
     rows = [VMEM((LX + 4, MERGED), F32)] * 2 + [VMEM((LX + 4, wide), F32)] * 2
@@ -340,37 +339,23 @@
         name="edge_z",
     )(conv, first, second, conv_weight, z_fwd)
     rows = VMEM((W // 128, 2 * XP * Q, 128), F32)
-    up = odd("px")
-    first = swap_pairs(jnp.where(up, to_below, to_above), "px", PX, 0)
-    second = swap_pairs(jnp.where(up, to_above, to_below), "px", PX, 1)
-    below, above = jnp.where(up, first, second), jnp.where(up, second, first)
     freq = lax.all_to_all(freq, "py", 0, 0, tiled=True)
-    freq, below, above = lax.optimization_barrier((freq, below, above))
     freq = call(y_forward_kernel, shape(PX, XE, 2 * Q // PX, W), name="y_fwd")(freq, y_fwd)
     freq = lax.all_to_all(freq, "px", 0, 0, tiled=True)
     mixing = [VMEM((256, 512), BF16), VMEM((256, 4 * C), BF16)]
     freq = call(spectrum_kernel, shape(PX, XP, 2 * Q // PX, W), [rows, VMEM((W // 128, 2 * XE * Q, 128), F32)] + mixing, name="spec")(
         freq, x_fwd, x_inv, inner_weight, outer_weight
     )
+    freq, to_below, to_above = lax.optimization_barrier((freq, to_below, to_above))
+    up = odd("px")
+    first = swap_pairs(jnp.where(up, to_below, to_above), "px", PX, 0)
+    second = swap_pairs(jnp.where(up, to_above, to_below), "px", PX, 1)
+    below, above = jnp.where(up, first, second), jnp.where(up, second, first)
     freq = lax.all_to_all(freq, "px", 0, 0, tiled=True)
+    freq, below, above = lax.optimization_barrier((freq, below, above))
     freq = call(y_inverse_kernel, shape(PY, XP, 2 * LY, W), name="y_inv")(freq, y_inv)
     freq = lax.all_to_all(freq, "py", 0, 0, tiled=True)
-    steps = 4
-    return pl.pallas_call(
-        z_inverse_kernel,
-        out_shape=shape(LX, LY, MERGED),
-        grid=(steps,),
-        in_specs=[
-            pl.BlockSpec((KZ, XP // steps, 2 * LY, W), lambda i: (0, i, 0, 0)),
-            pl.BlockSpec(z_inv.shape, lambda i: (0, 0)),
-            pl.BlockSpec((LX // steps, ZH * LY, W), lambda i: (i, 0, 0)),
-            pl.BlockSpec((ZH * LY, W), lambda i: (0, 0)),
-            pl.BlockSpec((ZH * LY, W), lambda i: (0, 0)),
-        ],
-        out_specs=pl.BlockSpec((LX // steps, LY, MERGED), lambda i: (i, 0, 0)),
-        compiler_params=pltpu.CompilerParams(vmem_limit_bytes=20 * 2**20),
-        name="z_inv",
-    )(freq, z_inv, field, below, above)
+    return call(z_inverse_kernel, shape(LX, LY, MERGED), name="z_inv")(freq, z_inv, field, below, above)
 
 
 def solution(mesh):

time: 120 us -> 117 us (0.975)
  blocking collectives: 64.2 us -> 78.3 us
  waiting for transfers between devices: 18.9 us -> 6.01 us
  starting transfers between devices: 15.7 us -> 13 us
  local copies, waits for them, and re-layouts: 2.98 us -> 1.45 us
    all_to_all x1 -> x2, blocking collectives: 28.6 us -> 57.9 us  [body(): freq = lax.all_to_all(freq, 'py', 0, 0, tiled=True)]
    all_to_all x1, waiting for transfers between devices: 16.1 us -> 0.01 us  [body(): freq = lax.all_to_all(freq, 'px', 0, 0, tiled=True)]
    all_to_all x2 -> x1, blocking collectives: 35.6 us -> 20.3 us  [body(): freq = lax.all_to_all(freq, 'px', 0, 0, tiled=True)]
    ppermute x4, waiting for transfers between devices: 2.88 us -> 6.01 us  [swap_pairs(): lax.ppermute(value, axis, [(i, i + 1) for i in low] + [(i + 1, i) for i i...]
    all_to_all x1, starting transfers between devices: 6.31 us -> 3.68 us  [body(): freq = lax.all_to_all(freq, 'px', 0, 0, tiled=True)]
    unnamed x22 -> x20, local copies, waits for them, and re-layouts: 2.98 us -> 1.45 us
    pallas_call x1, Pallas kernels: 4.35 us -> 3.09 us  [body(): call(edge_kernel, [shape(LX, ZH * LY, W), shape(KZ, XE, 2 * LY, W)] + [sh...]
  transfers between devices with their start and end apart: 5 -> 5, of which waited for: 2 -> 1; matrix products, arithmetic and copies ran while one was open for 0% -> 0% of each run, Pallas kernels for 6% -> 6%
where the time goes in v7:
time: 117 us; the launch traced here: 116 us
  blocking collectives  78.3 us (67%)
  Pallas kernels  17 us (15%)
  starting transfers between devices  13 us (11%)
  waiting for transfers between devices  6.01 us (5%)
  local copies, waits for them, and re-layouts  1.45 us (1%)
    all_to_all x2, blocking collectives, body(): freq = lax.all_to_all(freq, 'py', 0, 0, tiled=True)  57.9 us
    all_to_all x1, blocking collectives, body(): freq = lax.all_to_all(freq, 'px', 0, 0, tiled=True)  20.3 us
    ppermute x4, starting transfers between devices, swap_pairs(): lax.ppermute(value, axis, [(i, i + 1) for i in low] + [(i + 1, i) for i i...  9.28 us
    pallas_call x1, Pallas kernels, body(): call(conv_kernel, jax.ShapeDtypeStruct((LX + 2, LY, MERGED), F32), [VMEM(...  6.95 us
    ppermute x4, waiting for transfers between devices, swap_pairs(): lax.ppermute(value, axis, [(i, i + 1) for i in low] + [(i + 1, i) for i i...  6.01 us
    all_to_all x1, starting transfers between devices, body(): freq = lax.all_to_all(freq, 'px', 0, 0, tiled=True)  3.68 us
    pallas_call x1, Pallas kernels, body(): call(spectrum_kernel, shape(PX, XP, 2 * Q // PX, W), [rows, VMEM((W // 12...  3.44 us
    pallas_call x1, Pallas kernels, body(): call(edge_kernel, [shape(LX, ZH * LY, W), shape(KZ, XE, 2 * LY, W)] + [sh...  3.09 us
  transfers between devices with their start and end apart: 5, of which 1 were waited for; matrix products, arithmetic and copies ran while one was open for 0% of the time, Pallas kernels for 6%

profile of v7, /device:TPU:1, one launch (start us, length us, event | category | flops | bytes accessed | tf_op | source)
XLA Modules:
  0.0 115.9 jit_solution(9298003364153259554)
XLA Ops:
  0.0 1.4 %copy-done = bf16[16,8,6144]{2,1,0:T(8,128)(2,1)S(1)} copy-done((bf16[16,8,6144]{2,1,0:T(8,128)(2,1)S(1)}, bf16[16,8,6144]{2,1,0:T(8,128)(2,1)}, u32[]{:S(2)}) %copy-start) | copy-done | bytes 1572888
  1.4 0.3 y_rows.1
  1.8 1.5 %collective-permute-start = (bf16[16,6144]{1,0:T(8,128)(2,1)S(1)}, bf16[16,6144]{1,0:T(8,128)(2,1)S(1)}, u32[]{:S(2)}, u32[]{:S(2)}) collective-permute-start(bf16[16,6144]{1,0:T(8,128)(2,1)S(1)} %get-tuple-element.17), channel_id=1, source_target_pairs={{0,1},{2,3},{4,5},{6,7},{8,9},{10,11},{12,13},{14,15},{1,0},{3,2},... | collective-permute-start | bytes 589832 | tf_op jit(solution)/shard_map/ppermute | solution.py:316
  3.3 3.2 %collective-permute-start.1 = (bf16[16,6144]{1,0:T(8,128)(2,1)S(1)}, bf16[16,6144]{1,0:T(8,128)(2,1)S(1)}, u32[]{:S(2)}, u32[]{:S(2)}) collective-permute-start(bf16[16,6144]{1,0:T(8,128)(2,1)S(1)} %get-tuple-element.18), channel_id=1, source_target_pairs={{1,2},{3,4},{5,6},{7,8},{9,10},{11,12},{13,14},{2,1},{4,3},{6,5},{... | collective-permute-start | bytes 589832 | tf_op jit(solution)/shard_map/ppermute | solution.py:316
  6.5 0.0 copy-done.1
  6.5 6.9 %conv.1 = f32[18,8,6144]{2,1,0:T(8,128)S(1)} custom-call(bf16[16,8,6144]{2,1,0:T(8,128)(2,1)S(1)} %copy-done, f32[27,192]{1,0:T(8,128)S(1)} %copy-done.1), custom_call_target="tpu_custom_call" | custom-call | tf_op jit(solution)/shard_map/conv/pallas_call | solution.py:325
  13.5 0.0 collective-permute-done.first
  13.5 0.0 collective-permute-done.1.second
  13.5 0.0 copy-done.4
  13.5 3.1 %edge_z.1 = (bf16[16,128,384]{2,1,0:T(8,128)(2,1)S(1)}, bf16[16,9,16,384]{3,2,1,0:T(8,128)(2,1)S(1)}, bf16[128,384]{1,0:T(8,128)(2,1)S(1)}, bf16[128,384]{1,0:T(8,128)(2,1)S(1)}) custom-call(f32[18,8,6144]{2,1,0:T(8,128)S(1)} %conv.1, bf16[16,6144]{1,0:T(8,128)(2,1)S(1)} %collective-permute-done.first, bf16[16,6144]{1,0:T(8,128)(2,1)S(1)} %collective-permute-done.1.second, ...), custom_call_target="tpu_custom_call" | custom-call | tf_op jit(solution)/shard_map/edge_z/pallas_call | solution.py:335
  16.6 0.0 copy-start.9
  16.6 29.8 %all_to_all.20.given = bf16[16,9,16,384]{3,2,1,0:T(8,128)(2,1)S(1)} all-to-all(bf16[16,9,16,384]{3,2,1,0:T(8,128)(2,1)S(1)} %get-tuple-element.19), channel_id=1, replica_groups=mesh['px'=8,'py'=16] {'py'}, dimensions={0} | all-to-all | bytes 3538944 | tf_op jit(solution)/shard_map/all_to_all | solution.py:342
  46.4 0.0 copy-done.9
  46.4 0.0 copy-start.8
  46.4 0.5 y_fwd.2
  46.9 20.3 %all_to_all.21.given = bf16[8,9,16,384]{3,2,1,0:T(8,128)(2,1)S(1)} all-to-all(bf16[8,9,16,384]{3,2,1,0:T(8,128)(2,1)S(1)} %y_fwd.2), channel_id=1, replica_groups=mesh['px'=8,'py'=16] {'px'}, dimensions={0} | all-to-all | bytes 1769472 | tf_op jit(solution)/shard_map/all_to_all | solution.py:344
  67.2 0.0 copy-done.3
  67.2 0.0 copy-done.5
  67.2 0.0 copy-done.6
  67.2 0.0 copy-done.8
  67.2 3.4 %spec.1 = bf16[8,8,16,384]{3,2,1,0:T(8,128)(2,1)} custom-call(bf16[8,9,16,384]{3,2,1,0:T(8,128)(2,1)S(1)} %all_to_all.21.given, bf16[256,144]{1,0:T(8,128)(2,1)S(1)} %copy-done.3, bf16[256,128]{1,0:T(8,128)(2,1)S(1)} %copy-done.8, bf16[2,2,96,96]{3,2,1,0:T(8,128)(2,1)S(1)} %copy-done.5, bf16[2,2,96,96]{3,2,1,0:T(8,128)(2,1)S(1)} %copy-done.6), custom_call_target="tpu_custom_call" | custom-call | tf_op jit(solution)/shard_map/spec/pallas_call | solution.py:346
  70.7 3.7 %all-to-all-start.2 = ((bf16[8,8,16,384]{3,2,1,0:T(8,128)(2,1)}), bf16[8,8,16,384]{3,2,1,0:T(8,128)(2,1)S(1)}, u32[]{:S(2)}, u32[]{:S(2)}) async-start(bf16[8,8,16,384]{3,2,1,0:T(8,128)(2,1)} %spec.1), calls=%async_computation.2 | async-start | bytes 1572864 | tf_op jit(solution)/shard_map/all_to_all | solution.py:354
  74.4 0.7 collective-permute-start.3
  75.1 3.9 %collective-permute-start.2 = (bf16[128,384]{1,0:T(8,128)(2,1)S(1)}, bf16[128,384]{1,0:T(8,128)(2,1)S(1)}, u32[]{:S(2)}, u32[]{:S(2)}) collective-permute-start(bf16[128,384]{1,0:T(8,128)(2,1)S(1)} %get-tuple-element.32), channel_id=1, source_target_pairs={{0,16},{32,48},{64,80},{96,112},{16,0},{48,32},{80,64},{112,96},{1... | collective-permute-start | bytes 294920 | tf_op jit(solution)/shard_map/ppermute | solution.py:316
  78.9 0.0 collective-permute-done.3
  78.9 6.0 %collective-permute-done.2 = bf16[128,384]{1,0:T(8,128)(2,1)S(1)} collective-permute-done((bf16[128,384]{1,0:T(8,128)(2,1)S(1)}, bf16[128,384]{1,0:T(8,128)(2,1)S(1)}, u32[]{:S(2)}, u32[]{:S(2)}) %collective-permute-start.2) | collective-permute-done | bytes 98336 | tf_op jit(solution)/shard_map/ppermute | solution.py:316
  85.0 0.0 all-to-all-done.2.given
  85.0 0.6 y_inv.2
  85.5 0.0 copy-start.2
  85.6 28.2 %all_to_all.22.given = bf16[16,8,16,384]{3,2,1,0:T(8,128)(2,1)S(1)} all-to-all(bf16[16,8,16,384]{3,2,1,0:T(8,128)(2,1)S(1)} %y_inv.2), channel_id=1, replica_groups=mesh['px'=8,'py'=16] {'py'}, dimensions={0} | all-to-all | bytes 3145728 | tf_op jit(solution)/shard_map/all_to_all | solution.py:357
  113.7 0.0 copy-done.2
  113.7 2.2 %z_inv.2 = bf16[16,8,6144]{2,1,0:T(8,128)(2,1)} custom-call(bf16[16,8,16,384]{3,2,1,0:T(8,128)(2,1)S(1)} %all_to_all.22.given, bf16[256,256]{1,0:T(8,128)(2,1)S(1)} %copy-done.2, bf16[16,128,384]{2,1,0:T(8,128)(2,1)S(1)} %get-tuple-element.26.field, bf16[128,384]{1,0:T(8,128)(2,1)S(1)} %get-tuple-element.27.below, bf16[128,384]{1,0:T(8,128)(2,1)S(1)} %get-tuple-element.28.above), custom_call_target="tpu_custom_call" | custom-call | tf_op jit(solution)/shard_map/z_inv/pallas_call | solution.py:358
  (10 shorter events, 0.1 us)
Async XLA Ops:
  0.0 1.4 %copy-start = (bf16[16,8,6144]{2,1,0:T(8,128)(2,1)S(1)}, bf16[16,8,6144]{2,1,0:T(8,128)(2,1)}, u32[]{:S(2)}) copy-start(bf16[16,8,6144]{2,1,0:T(8,128)(2,1)} %tok.3) | copy-start | bytes 4718596
  1.4 5.1 %copy-start.1 = (f32[27,192]{1,0:T(8,128)S(1)}, f32[27,192]{1,0:T(8,128)}, u32[]{:S(2)}) copy-start(f32[27,192]{1,0:T(8,128)} %narrow.3) | copy-start | bytes 62212
  1.8 11.7 %collective-permute-start = (bf16[16,6144]{1,0:T(8,128)(2,1)S(1)}, bf16[16,6144]{1,0:T(8,128)(2,1)S(1)}, u32[]{:S(2)}, u32[]{:S(2)}) collective-permute-start(bf16[16,6144]{1,0:T(8,128)(2,1)S(1)} %get-tuple-element.17), channel_id=1, source_target_pairs={{0,1},{2,3},{4,5},{6,7},{8,9},{10,11},{12,13},{14,15},{1,0},{3,2},... | collective-permute-start | bytes 589832 | tf_op jit(solution)/shard_map/ppermute | solution.py:316
  3.3 10.2 %copy-start.4 = (bf16[256,256]{1,0:T(8,128)(2,1)S(1)}, bf16[256,256]{1,0:T(8,128)(2,1)}, u32[]{:S(2)}) copy-start(bf16[256,256]{1,0:T(8,128)(2,1)} %constant.24.clone.z_fwd) | copy-start | bytes 393220
  3.3 10.2 %collective-permute-start.1 = (bf16[16,6144]{1,0:T(8,128)(2,1)S(1)}, bf16[16,6144]{1,0:T(8,128)(2,1)S(1)}, u32[]{:S(2)}, u32[]{:S(2)}) collective-permute-start(bf16[16,6144]{1,0:T(8,128)(2,1)S(1)} %get-tuple-element.18), channel_id=1, source_target_pairs={{1,2},{3,4},{5,6},{7,8},{9,10},{11,12},{13,14},{2,1},{4,3},{6,5},{... | collective-permute-start | bytes 589832 | tf_op jit(solution)/shard_map/ppermute | solution.py:316
  16.6 29.8 %copy-start.9 = (bf16[128,256]{1,0:T(8,128)(2,1)S(1)}, bf16[128,256]{1,0:T(8,128)(2,1)}, u32[]{:S(2)}) copy-start(bf16[128,256]{1,0:T(8,128)(2,1)} %constant.26.clone.y_fwd) | copy-start | bytes 196612
  46.4 20.8 %copy-start.3 = (bf16[256,144]{1,0:T(8,128)(2,1)S(1)}, bf16[256,144]{1,0:T(8,128)(2,1)}, u32[]{:S(2)}) copy-start(bf16[256,144]{1,0:T(8,128)(2,1)} %constant.28.clone.x_fwd) | copy-start | bytes 221188
  46.4 20.8 %copy-start.5 = (bf16[2,2,96,96]{3,2,1,0:T(8,128)(2,1)S(1)}, bf16[2,2,96,96]{3,2,1,0:T(8,128)(2,1)}, u32[]{:S(2)}) copy-start(bf16[2,2,96,96]{3,2,1,0:T(8,128)(2,1)} %inner_weight.1) | copy-start | bytes 221188
  46.4 20.8 %copy-start.6 = (bf16[2,2,96,96]{3,2,1,0:T(8,128)(2,1)S(1)}, bf16[2,2,96,96]{3,2,1,0:T(8,128)(2,1)}, u32[]{:S(2)}) copy-start(bf16[2,2,96,96]{3,2,1,0:T(8,128)(2,1)} %outer_weight.1) | copy-start | bytes 221188
  46.4 20.8 %copy-start.8 = (bf16[256,128]{1,0:T(8,128)(2,1)S(1)}, bf16[256,128]{1,0:T(8,128)(2,1)}, u32[]{:S(2)}) copy-start(bf16[256,128]{1,0:T(8,128)(2,1)} %constant.29.clone.x_inv) | copy-start | bytes 196612
  70.7 14.3 %copy-start.7 = (bf16[256,128]{1,0:T(8,128)(2,1)S(1)}, bf16[256,128]{1,0:T(8,128)(2,1)}, u32[]{:S(2)}) copy-start(bf16[256,128]{1,0:T(8,128)(2,1)} %constant.27.clone.y_inv) | copy-start | bytes 196612
  70.7 14.3 %all-to-all-start.2 = ((bf16[8,8,16,384]{3,2,1,0:T(8,128)(2,1)}), bf16[8,8,16,384]{3,2,1,0:T(8,128)(2,1)S(1)}, u32[]{:S(2)}, u32[]{:S(2)}) async-start(bf16[8,8,16,384]{3,2,1,0:T(8,128)(2,1)} %spec.1), calls=%async_computation.2 | async-start | bytes 1572864 | tf_op jit(solution)/shard_map/all_to_all | solution.py:354
  74.4 4.5 %collective-permute-start.3 = (bf16[128,384]{1,0:T(8,128)(2,1)S(1)}, bf16[128,384]{1,0:T(8,128)(2,1)S(1)}, u32[]{:S(2)}, u32[]{:S(2)}) collective-permute-start(bf16[128,384]{1,0:T(8,128)(2,1)S(1)} %get-tuple-element.31), channel_id=1, source_target_pairs={{16,32},{48,64},{80,96},{32,16},{64,48},{96,80},{17,33},{49,65},{8... | collective-permute-start | bytes 294920 | tf_op jit(solution)/shard_map/ppermute | solution.py:316
  75.1 9.9 %collective-permute-start.2 = (bf16[128,384]{1,0:T(8,128)(2,1)S(1)}, bf16[128,384]{1,0:T(8,128)(2,1)S(1)}, u32[]{:S(2)}, u32[]{:S(2)}) collective-permute-start(bf16[128,384]{1,0:T(8,128)(2,1)S(1)} %get-tuple-element.32), channel_id=1, source_target_pairs={{0,16},{32,48},{64,80},{96,112},{16,0},{48,32},{80,64},{112,96},{1... | collective-permute-start | bytes 294920 | tf_op jit(solution)/shard_map/ppermute | solution.py:316
  85.5 28.2 %copy-start.2 = (bf16[256,256]{1,0:T(8,128)(2,1)S(1)}, bf16[256,256]{1,0:T(8,128)(2,1)}, u32[]{:S(2)}) copy-start(bf16[256,256]{1,0:T(8,128)(2,1)} %constant.25.clone.z_inv) | copy-start | bytes 393220

commit v8 on v7

--- a/solution.py
+++ b/solution.py
@@ -99,8 +99,9 @@
 
 def by_order(axis, first, second):
     second, first = second.astype(F32), first.astype(F32)
-    up = odd(axis)
-    return jnp.where(up, first, second), jnp.where(up, second, first)
+    up, at = odd(axis), lax.axis_index(axis)
+    below, above = jnp.where(up, first, second), jnp.where(up, second, first)
+    return jnp.where(at == 0, 0.0, below), jnp.where(at == lax.axis_size(axis) - 1, 0.0, above)
 
 
 def rows_kernel(tok, send_first, send_second):
@@ -148,7 +149,7 @@
             up = pltpu.roll(sums.pop((x, 2)), LY - 1, 0)
             down = jnp.where(row_at == 0, 0.0, down)
             up = jnp.where(row_at == LY - 1, 0.0, up)
-            out[x, :, here] = sums.pop((x, 1)) + down + up
+            out[j, x * LY : (x + 1) * LY, :] = sums.pop((x, 1)) + down + up
 
 
 def edge_kernel(
@@ -168,6 +169,7 @@
         after = pl.multiple_of(j * 128 + W, 128)
         here = pl.ds(at, 128)
         phase = pl.multiple_of(lax.rem(j, 3) * 128, 128)
+        edge[j] = jnp.zeros(edge.shape[1:], F32)
         for side, rows, rows_s, b in ((0, ylo, ylo_s, 0), (1, yhi, yhi_s, 2)):
             mid = rows[:, here]
             before = rows_s[:, here]
@@ -179,30 +181,26 @@
                 term = before * taps[0] + mid * taps[1] + behind * taps[2]
                 term = term[a : a + LX + 2]
                 total = term if total is None else total + term
-            edge[side, :, here] = total
+            cells = pl.ds(side * (LY - 1), LX + 2, stride=LY)
+            edge[j, cells, :] = total
 
     low = low_half(ZH * LY)
-    row_at = lax.broadcasted_iota(jnp.int32, (LY, W), 0)
     for xp in range(XE):
         parts = []
         for x in (2 * xp, 2 * xp + 1) if xp < XP else (-1, LX):
-            at = x + 1
-            rows = []
-            for z in range(ZH):
-                here = slice(z * W, (z + 1) * W)
-                more = jnp.where(row_at == 0, edge[0, at : at + 1, here], 0.0)
-                more = jnp.where(row_at == LY - 1, edge[1, at : at + 1, here], more)
-                rows.append(conv[at, :, here] + more)
-            part = jnp.concatenate(rows, axis=0)
+            rows = slice((x + 1) * LY, (x + 2) * LY)
+            part = (conv[:, rows, :] + edge[:, rows, :]).reshape(ZH, W // 128, LY, 128)
+            part = jnp.concatenate([part[:, t].reshape(ZH * LY, 128) for t in range(W // 128)], axis=1)
+            part = part.astype(BF16)
             if xp < XP:
-                field[x] = part.astype(BF16)
+                field[x] = part
             parts.append(part)
         first, second = parts
         if xp == XP:
-            to_below[...] = first.astype(BF16)
-            to_above[...] = second.astype(BF16)
-        even = jnp.where(low, first, swap(second)).astype(BF16)
-        odd_z = jnp.where(low, swap(first), second).astype(BF16)
+            to_below[...] = first
+            to_above[...] = second
+        even = jnp.where(low, first, swap(second))
+        odd_z = jnp.where(low, swap(first), second)
         out = dot(z_fwd[...], jnp.concatenate([even, odd_z], axis=0))
         freq[:, xp] = out.astype(BF16).reshape(KZ, 2 * LY, W)
 
@@ -280,9 +278,11 @@
         out[:, xp] = dot(y_inv[...], data).astype(BF16).reshape(PY, 2 * LY, W)
 
 
-def z_inverse_kernel(given, z_inv, field, below, above, out):
+def z_inverse_kernel(given, z_inv, field, below, above, out_hbm, out, sems):
     low = low_half(ZH * LY)
+    copies = []
     for xp in range(XP):
+        here = pl.ds(2 * xp, 2)
         data = given[:, xp].reshape(2 * KZ * LY, W)
         value = dot(z_inv[...], data)
         even, odd = value[: ZH * LY], value[ZH * LY :]
@@ -295,13 +295,18 @@
         for x, value in ((2 * xp, first), (2 * xp + 1, second)):
             for z in range(ZH):
                 out[x, :, z * W : (z + 1) * W] = value[z * LY : (z + 1) * LY].astype(BF16)
-
-
-def call(kernel, outs, scratch=(), name=None):
+        copies.append(pltpu.make_async_copy(out.at[here], out_hbm.at[here], sems.at[xp]))
+        copies[xp].start()
+    for copy in copies:
+        copy.wait()
+
+
+def call(kernel, outs, scratch=(), name=None, **specs):
     return pl.pallas_call(
         kernel,
         out_shape=outs,
         scratch_shapes=list(scratch),
+        **specs,
         compiler_params=pltpu.CompilerParams(vmem_limit_bytes=20 * 2**20),
         name=name,
     )
@@ -311,20 +316,21 @@
     return jax.ShapeDtypeStruct(dims, BF16)
 
 
-def swap_pairs(value, axis, count, start):
-    low = range(start, count - 1, 2)
-    return lax.ppermute(value, axis, [(i, i + 1) for i in low] + [(i + 1, i) for i in low])
+def swap_pairs(value, axis, count, start, ends=False):
+    low = range(start, count if ends else count - 1, 2)
+    return lax.ppermute(value, axis, [(i, (i + 1) % count) for i in low] + [((i + 1) % count, i) for i in low])
 
 
 def body(tokens, conv_weight, inner_weight, outer_weight):
     z_fwd, z_inv, y_fwd, y_inv, x_fwd, x_inv = (jnp.asarray(m) for m in matrices())
     wide = MERGED + 2 * C
     first, second = call(rows_kernel, [shape(LX, MERGED)] * 2, name="y_rows")(tokens)
-    second = swap_pairs(second, "py", PY, 1)
+    second = swap_pairs(second, "py", PY, 1, True)
     first = swap_pairs(first, "py", PY, 0)
+    filtered = jax.ShapeDtypeStruct((MERGED // 128, (LX + 2) * LY, 128), F32)
     conv = call(
         conv_kernel,
-        jax.ShapeDtypeStruct((LX + 2, LY, MERGED), F32),
+        filtered,
         [
             VMEM((LX, LY, wide), F32),
             VMEM((27, W), F32),
@@ -335,7 +341,7 @@
     field, freq, to_below, to_above = call(
         edge_kernel,
         [shape(LX, ZH * LY, W), shape(KZ, XE, 2 * LY, W)] + [shape(ZH * LY, W)] * 2,
-        rows + [VMEM((2, LX + 2, MERGED), F32), VMEM((27, W), F32)],
+        rows + [VMEM(filtered.shape, F32), VMEM((27, W), F32)],
         name="edge_z",
     )(conv, first, second, conv_weight, z_fwd)
     rows = VMEM((W // 128, 2 * XP * Q, 128), F32)
@@ -355,7 +361,13 @@
     freq, below, above = lax.optimization_barrier((freq, below, above))
     freq = call(y_inverse_kernel, shape(PY, XP, 2 * LY, W), name="y_inv")(freq, y_inv)
     freq = lax.all_to_all(freq, "py", 0, 0, tiled=True)
-    return call(z_inverse_kernel, shape(LX, LY, MERGED), name="z_inv")(freq, z_inv, field, below, above)
+    return call(
+        z_inverse_kernel,
+        shape(LX, LY, MERGED),
+        [VMEM((LX, LY, MERGED), BF16), pltpu.SemaphoreType.DMA((XP,))],
+        name="z_inv",
+        out_specs=pl.BlockSpec(memory_space=pl.ANY),
+    )(freq, z_inv, field, below, above)
 
 
 def solution(mesh):

time: 117 us -> 114 us (0.974)
  starting transfers between devices: 13 us -> 11 us
    ppermute x4, starting transfers between devices: 9.28 us -> 7.31 us  [swap_pairs(): lax.ppermute(value, axis, [(i, (i + 1) % count) for i in low] + [((i + 1)...]
where the time goes in v8:
time: 114 us; the launch traced here: 113 us
  blocking collectives  78.3 us (69%)
  Pallas kernels  16.3 us (14%)
  starting transfers between devices  11 us (10%)
  waiting for transfers between devices  6.01 us (5%)
  local copies, waits for them, and re-layouts  1.45 us (1%)
    all_to_all x2, blocking collectives, body(): freq = lax.all_to_all(freq, 'py', 0, 0, tiled=True)  58.2 us
    all_to_all x1, blocking collectives, body(): freq = lax.all_to_all(freq, 'px', 0, 0, tiled=True)  20.1 us
    ppermute x4, starting transfers between devices, swap_pairs(): lax.ppermute(value, axis, [(i, (i + 1) % count) for i in low] + [((i + 1)...  7.31 us
    pallas_call x1, Pallas kernels, body(): call(conv_kernel, filtered, [VMEM((LX, LY, wide), F32), VMEM((27, W), F32...  6.94 us
    ppermute x4, waiting for transfers between devices, swap_pairs(): lax.ppermute(value, axis, [(i, (i + 1) % count) for i in low] + [((i + 1)...  6.01 us
    all_to_all x1, starting transfers between devices, body(): freq = lax.all_to_all(freq, 'px', 0, 0, tiled=True)  3.68 us
    pallas_call x1, Pallas kernels, body(): call(spectrum_kernel, shape(PX, XP, 2 * Q // PX, W), [rows, VMEM((W // 12...  3.45 us
    pallas_call x1, Pallas kernels, body(): call(edge_kernel, [shape(LX, ZH * LY, W), shape(KZ, XE, 2 * LY, W)] + [sh...  2.74 us
  transfers between devices with their start and end apart: 5, of which 1 were waited for; matrix products, arithmetic and copies ran while one was open for 0% of the time, Pallas kernels for 6%

profile of v8, /device:TPU:1, one launch (start us, length us, event | category | flops | bytes accessed | tf_op | source)
XLA Modules:
  0.0 113.2 jit_solution(7927507069068842711)
XLA Ops:
  0.0 1.4 %copy-done = bf16[16,8,6144]{2,1,0:T(8,128)(2,1)S(1)} copy-done((bf16[16,8,6144]{2,1,0:T(8,128)(2,1)S(1)}, bf16[16,8,6144]{2,1,0:T(8,128)(2,1)}, u32[]{:S(2)}) %copy-start) | copy-done | bytes 1572888
  1.4 0.3 y_rows.1
  1.8 1.5 %collective-permute-start = (bf16[16,6144]{1,0:T(8,128)(2,1)S(1)}, bf16[16,6144]{1,0:T(8,128)(2,1)S(1)}, u32[]{:S(2)}, u32[]{:S(2)}) collective-permute-start(bf16[16,6144]{1,0:T(8,128)(2,1)S(1)} %get-tuple-element.17), channel_id=1, source_target_pairs={{0,1},{2,3},{4,5},{6,7},{8,9},{10,11},{12,13},{14,15},{1,0},{3,2},... | collective-permute-start | bytes 589832 | tf_op jit(solution)/shard_map/ppermute | solution.py:321
  3.3 1.3 %collective-permute-start.1 = (bf16[16,6144]{1,0:T(8,128)(2,1)S(1)}, bf16[16,6144]{1,0:T(8,128)(2,1)S(1)}, u32[]{:S(2)}, u32[]{:S(2)}) collective-permute-start(bf16[16,6144]{1,0:T(8,128)(2,1)S(1)} %get-tuple-element.18), channel_id=1, source_target_pairs={{1,2},{3,4},{5,6},{7,8},{9,10},{11,12},{13,14},{15,0},{2,1},{4,3},... | collective-permute-start | bytes 589832 | tf_op jit(solution)/shard_map/ppermute | solution.py:321
  4.5 0.0 copy-done.1
  4.5 6.9 %conv.1 = f32[48,144,128]{2,1,0:T(8,128)S(1)} custom-call(bf16[16,8,6144]{2,1,0:T(8,128)(2,1)S(1)} %copy-done, f32[27,192]{1,0:T(8,128)S(1)} %copy-done.1), custom_call_target="tpu_custom_call" | custom-call | tf_op jit(solution)/shard_map/conv/pallas_call | solution.py:331
  11.5 0.0 collective-permute-done.first
  11.5 0.0 collective-permute-done.1.second
  11.5 0.0 copy-done.4
  11.5 2.7 %edge_z.1 = (bf16[16,128,384]{2,1,0:T(8,128)(2,1)S(1)}, bf16[16,9,16,384]{3,2,1,0:T(8,128)(2,1)S(1)}, bf16[128,384]{1,0:T(8,128)(2,1)S(1)}, bf16[128,384]{1,0:T(8,128)(2,1)S(1)}) custom-call(f32[48,144,128]{2,1,0:T(8,128)S(1)} %conv.1, bf16[16,6144]{1,0:T(8,128)(2,1)S(1)} %collective-permute-done.first, bf16[16,6144]{1,0:T(8,128)(2,1)S(1)} %collective-permute-done.1.second, ...), custom_call_target="tpu_custom_call" | custom-call | tf_op jit(solution)/shard_map/edge_z/pallas_call | solution.py:341
  14.3 0.0 copy-start.9
  14.3 30.0 %all_to_all.20.given = bf16[16,9,16,384]{3,2,1,0:T(8,128)(2,1)S(1)} all-to-all(bf16[16,9,16,384]{3,2,1,0:T(8,128)(2,1)S(1)} %get-tuple-element.19), channel_id=1, replica_groups=mesh['px'=8,'py'=16] {'py'}, dimensions={0} | all-to-all | bytes 3538944 | tf_op jit(solution)/shard_map/all_to_all | solution.py:348
  44.3 0.0 copy-done.9
  44.3 0.0 copy-start.8
  44.3 0.5 y_fwd.2
  44.8 20.1 %all_to_all.21.given = bf16[8,9,16,384]{3,2,1,0:T(8,128)(2,1)S(1)} all-to-all(bf16[8,9,16,384]{3,2,1,0:T(8,128)(2,1)S(1)} %y_fwd.2), channel_id=1, replica_groups=mesh['px'=8,'py'=16] {'px'}, dimensions={0} | all-to-all | bytes 1769472 | tf_op jit(solution)/shard_map/all_to_all | solution.py:350
  64.9 0.0 copy-done.3
  64.9 0.0 copy-done.5
  64.9 0.0 copy-done.6
  64.9 0.0 copy-done.8
  64.9 3.5 %spec.1 = bf16[8,8,16,384]{3,2,1,0:T(8,128)(2,1)} custom-call(bf16[8,9,16,384]{3,2,1,0:T(8,128)(2,1)S(1)} %all_to_all.21.given, bf16[256,144]{1,0:T(8,128)(2,1)S(1)} %copy-done.3, bf16[256,128]{1,0:T(8,128)(2,1)S(1)} %copy-done.8, bf16[2,2,96,96]{3,2,1,0:T(8,128)(2,1)S(1)} %copy-done.5, bf16[2,2,96,96]{3,2,1,0:T(8,128)(2,1)S(1)} %copy-done.6), custom_call_target="tpu_custom_call" | custom-call | tf_op jit(solution)/shard_map/spec/pallas_call | solution.py:352
  68.3 3.7 %all-to-all-start.2 = ((bf16[8,8,16,384]{3,2,1,0:T(8,128)(2,1)}), bf16[8,8,16,384]{3,2,1,0:T(8,128)(2,1)S(1)}, u32[]{:S(2)}, u32[]{:S(2)}) async-start(bf16[8,8,16,384]{3,2,1,0:T(8,128)(2,1)} %spec.1), calls=%async_computation.2 | async-start | bytes 1572864 | tf_op jit(solution)/shard_map/all_to_all | solution.py:360
  72.1 0.7 collective-permute-start.3
  72.7 3.9 %collective-permute-start.2 = (bf16[128,384]{1,0:T(8,128)(2,1)S(1)}, bf16[128,384]{1,0:T(8,128)(2,1)S(1)}, u32[]{:S(2)}, u32[]{:S(2)}) collective-permute-start(bf16[128,384]{1,0:T(8,128)(2,1)S(1)} %get-tuple-element.32), channel_id=1, source_target_pairs={{0,16},{32,48},{64,80},{96,112},{16,0},{48,32},{80,64},{112,96},{1... | collective-permute-start | bytes 294920 | tf_op jit(solution)/shard_map/ppermute | solution.py:321
  76.6 0.0 collective-permute-done.3
  76.6 6.0 %collective-permute-done.2 = bf16[128,384]{1,0:T(8,128)(2,1)S(1)} collective-permute-done((bf16[128,384]{1,0:T(8,128)(2,1)S(1)}, bf16[128,384]{1,0:T(8,128)(2,1)S(1)}, u32[]{:S(2)}, u32[]{:S(2)}) %collective-permute-start.2) | collective-permute-done | bytes 98336 | tf_op jit(solution)/shard_map/ppermute | solution.py:321
  82.6 0.0 all-to-all-done.2.given
  82.7 0.0 copy-done.7
  82.7 0.6 y_inv.2
  83.2 0.0 copy-start.2
  83.2 28.2 %all_to_all.22.given = bf16[16,8,16,384]{3,2,1,0:T(8,128)(2,1)S(1)} all-to-all(bf16[16,8,16,384]{3,2,1,0:T(8,128)(2,1)S(1)} %y_inv.2), channel_id=1, replica_groups=mesh['px'=8,'py'=16] {'py'}, dimensions={0} | all-to-all | bytes 3145728 | tf_op jit(solution)/shard_map/all_to_all | solution.py:363
  111.4 1.8 %z_inv.2 = bf16[16,8,6144]{2,1,0:T(8,128)(2,1)} custom-call(bf16[16,8,16,384]{3,2,1,0:T(8,128)(2,1)S(1)} %all_to_all.22.given, bf16[256,256]{1,0:T(8,128)(2,1)S(1)} %copy-done.2, bf16[16,128,384]{2,1,0:T(8,128)(2,1)S(1)} %get-tuple-element.26.field, bf16[128,384]{1,0:T(8,128)(2,1)S(1)} %get-tuple-element.27.below, bf16[128,384]{1,0:T(8,128)(2,1)S(1)} %get-tuple-element.28.above), custom_call_target="tpu_custom_call" | custom-call | tf_op jit(solution)/shard_map/z_inv/pallas_call | solution.py:364
  (10 shorter events, 0.1 us)
Async XLA Ops:
  0.0 1.4 %copy-start = (bf16[16,8,6144]{2,1,0:T(8,128)(2,1)S(1)}, bf16[16,8,6144]{2,1,0:T(8,128)(2,1)}, u32[]{:S(2)}) copy-start(bf16[16,8,6144]{2,1,0:T(8,128)(2,1)} %tok.3) | copy-start | bytes 4718596
  1.4 3.1 %copy-start.1 = (f32[27,192]{1,0:T(8,128)S(1)}, f32[27,192]{1,0:T(8,128)}, u32[]{:S(2)}) copy-start(f32[27,192]{1,0:T(8,128)} %narrow.3) | copy-start | bytes 62212
  1.8 9.7 %collective-permute-start = (bf16[16,6144]{1,0:T(8,128)(2,1)S(1)}, bf16[16,6144]{1,0:T(8,128)(2,1)S(1)}, u32[]{:S(2)}, u32[]{:S(2)}) collective-permute-start(bf16[16,6144]{1,0:T(8,128)(2,1)S(1)} %get-tuple-element.17), channel_id=1, source_target_pairs={{0,1},{2,3},{4,5},{6,7},{8,9},{10,11},{12,13},{14,15},{1,0},{3,2},... | collective-permute-start | bytes 589832 | tf_op jit(solution)/shard_map/ppermute | solution.py:321
  3.3 8.3 %copy-start.4 = (bf16[256,256]{1,0:T(8,128)(2,1)S(1)}, bf16[256,256]{1,0:T(8,128)(2,1)}, u32[]{:S(2)}) copy-start(bf16[256,256]{1,0:T(8,128)(2,1)} %constant.24.clone.z_fwd) | copy-start | bytes 393220
  3.3 8.3 %collective-permute-start.1 = (bf16[16,6144]{1,0:T(8,128)(2,1)S(1)}, bf16[16,6144]{1,0:T(8,128)(2,1)S(1)}, u32[]{:S(2)}, u32[]{:S(2)}) collective-permute-start(bf16[16,6144]{1,0:T(8,128)(2,1)S(1)} %get-tuple-element.18), channel_id=1, source_target_pairs={{1,2},{3,4},{5,6},{7,8},{9,10},{11,12},{13,14},{15,0},{2,1},{4,3},... | collective-permute-start | bytes 589832 | tf_op jit(solution)/shard_map/ppermute | solution.py:321
  14.3 30.0 %copy-start.9 = (bf16[128,256]{1,0:T(8,128)(2,1)S(1)}, bf16[128,256]{1,0:T(8,128)(2,1)}, u32[]{:S(2)}) copy-start(bf16[128,256]{1,0:T(8,128)(2,1)} %constant.26.clone.y_fwd) | copy-start | bytes 196612
  44.3 20.6 %copy-start.3 = (bf16[256,144]{1,0:T(8,128)(2,1)S(1)}, bf16[256,144]{1,0:T(8,128)(2,1)}, u32[]{:S(2)}) copy-start(bf16[256,144]{1,0:T(8,128)(2,1)} %constant.28.clone.x_fwd) | copy-start | bytes 221188
  44.3 20.6 %copy-start.5 = (bf16[2,2,96,96]{3,2,1,0:T(8,128)(2,1)S(1)}, bf16[2,2,96,96]{3,2,1,0:T(8,128)(2,1)}, u32[]{:S(2)}) copy-start(bf16[2,2,96,96]{3,2,1,0:T(8,128)(2,1)} %inner_weight.1) | copy-start | bytes 221188
  44.3 20.6 %copy-start.6 = (bf16[2,2,96,96]{3,2,1,0:T(8,128)(2,1)S(1)}, bf16[2,2,96,96]{3,2,1,0:T(8,128)(2,1)}, u32[]{:S(2)}) copy-start(bf16[2,2,96,96]{3,2,1,0:T(8,128)(2,1)} %outer_weight.1) | copy-start | bytes 221188
  44.3 20.6 %copy-start.8 = (bf16[256,128]{1,0:T(8,128)(2,1)S(1)}, bf16[256,128]{1,0:T(8,128)(2,1)}, u32[]{:S(2)}) copy-start(bf16[256,128]{1,0:T(8,128)(2,1)} %constant.29.clone.x_inv) | copy-start | bytes 196612
  68.3 14.3 %copy-start.7 = (bf16[256,128]{1,0:T(8,128)(2,1)S(1)}, bf16[256,128]{1,0:T(8,128)(2,1)}, u32[]{:S(2)}) copy-start(bf16[256,128]{1,0:T(8,128)(2,1)} %constant.27.clone.y_inv) | copy-start | bytes 196612
  68.3 14.3 %all-to-all-start.2 = ((bf16[8,8,16,384]{3,2,1,0:T(8,128)(2,1)}), bf16[8,8,16,384]{3,2,1,0:T(8,128)(2,1)S(1)}, u32[]{:S(2)}, u32[]{:S(2)}) async-start(bf16[8,8,16,384]{3,2,1,0:T(8,128)(2,1)} %spec.1), calls=%async_computation.2 | async-start | bytes 1572864 | tf_op jit(solution)/shard_map/all_to_all | solution.py:360
  72.1 4.5 %collective-permute-start.3 = (bf16[128,384]{1,0:T(8,128)(2,1)S(1)}, bf16[128,384]{1,0:T(8,128)(2,1)S(1)}, u32[]{:S(2)}, u32[]{:S(2)}) collective-permute-start(bf16[128,384]{1,0:T(8,128)(2,1)S(1)} %get-tuple-element.31), channel_id=1, source_target_pairs={{16,32},{48,64},{80,96},{32,16},{64,48},{96,80},{17,33},{49,65},{8... | collective-permute-start | bytes 294920 | tf_op jit(solution)/shard_map/ppermute | solution.py:321
  72.7 9.9 %collective-permute-start.2 = (bf16[128,384]{1,0:T(8,128)(2,1)S(1)}, bf16[128,384]{1,0:T(8,128)(2,1)S(1)}, u32[]{:S(2)}, u32[]{:S(2)}) collective-permute-start(bf16[128,384]{1,0:T(8,128)(2,1)S(1)} %get-tuple-element.32), channel_id=1, source_target_pairs={{0,16},{32,48},{64,80},{96,112},{16,0},{48,32},{80,64},{112,96},{1... | collective-permute-start | bytes 294920 | tf_op jit(solution)/shard_map/ppermute | solution.py:321
  83.2 28.2 %copy-start.2 = (bf16[256,256]{1,0:T(8,128)(2,1)S(1)}, bf16[256,256]{1,0:T(8,128)(2,1)}, u32[]{:S(2)}) copy-start(bf16[256,256]{1,0:T(8,128)(2,1)} %constant.25.clone.z_inv) | copy-start | bytes 393220

commit v9 on v8

--- a/solution.py
+++ b/solution.py
@@ -280,6 +280,7 @@
 
 def z_inverse_kernel(given, z_inv, field, below, above, out_hbm, out, sems):
     low = low_half(ZH * LY)
+    below, above = by_order("px", below[...], above[...])
     copies = []
     for xp in range(XP):
         here = pl.ds(2 * xp, 2)
@@ -289,9 +290,9 @@
         first = jnp.where(low, even, swap(odd)) + field[2 * xp].astype(F32)
         second = jnp.where(low, swap(even), odd) + field[2 * xp + 1].astype(F32)
         if xp == 0:
-            first = first + below[...].astype(F32)
+            first = first + below
         if xp == XP - 1:
-            second = second + above[...].astype(F32)
+            second = second + above
         for x, value in ((2 * xp, first), (2 * xp + 1, second)):
             for z in range(ZH):
                 out[x, :, z * W : (z + 1) * W] = value[z * LY : (z + 1) * LY].astype(BF16)
@@ -316,17 +317,26 @@
     return jax.ShapeDtypeStruct(dims, BF16)
 
 
-def swap_pairs(value, axis, count, start, ends=False):
-    low = range(start, count if ends else count - 1, 2)
-    return lax.ppermute(value, axis, [(i, (i + 1) % count) for i in low] + [((i + 1) % count, i) for i in low])
+def swap_pairs(value, axis, start):
+    pairs = []
+    for x in range(PX):
+        for y in range(PY):
+            at, count = (x, PX) if axis == "px" else (y, PY)
+            to = at + 1 if (at - start) % 2 == 0 else at - 1
+            if 0 <= to < count:
+                x_to, y_to = (to, y) if axis == "px" else (x, to)
+            else:
+                x_to, y_to = (x, y ^ 1) if axis == "px" else (x ^ 1, y)
+            pairs.append((x * PY + y, x_to * PY + y_to))
+    return lax.ppermute(value, ("px", "py"), pairs)
 
 
 def body(tokens, conv_weight, inner_weight, outer_weight):
     z_fwd, z_inv, y_fwd, y_inv, x_fwd, x_inv = (jnp.asarray(m) for m in matrices())
     wide = MERGED + 2 * C
     first, second = call(rows_kernel, [shape(LX, MERGED)] * 2, name="y_rows")(tokens)
-    second = swap_pairs(second, "py", PY, 1, True)
-    first = swap_pairs(first, "py", PY, 0)
+    second = swap_pairs(second, "py", 1)
+    first = swap_pairs(first, "py", 0)
     filtered = jax.ShapeDtypeStruct((MERGED // 128, (LX + 2) * LY, 128), F32)
     conv = call(
         conv_kernel,
@@ -354,12 +364,11 @@
     )
     freq, to_below, to_above = lax.optimization_barrier((freq, to_below, to_above))
     up = odd("px")
-    first = swap_pairs(jnp.where(up, to_below, to_above), "px", PX, 0)
-    second = swap_pairs(jnp.where(up, to_above, to_below), "px", PX, 1)
-    below, above = jnp.where(up, first, second), jnp.where(up, second, first)
+    first = swap_pairs(jnp.where(up, to_below, to_above), "px", 0)
+    second = swap_pairs(jnp.where(up, to_above, to_below), "px", 1)
     freq = lax.all_to_all(freq, "px", 0, 0, tiled=True)
-    freq, below, above = lax.optimization_barrier((freq, below, above))
     freq = call(y_inverse_kernel, shape(PY, XP, 2 * LY, W), name="y_inv")(freq, y_inv)
+    freq, first, second = lax.optimization_barrier((freq, first, second))
     freq = lax.all_to_all(freq, "py", 0, 0, tiled=True)
     return call(
         z_inverse_kernel,
@@ -367,7 +376,7 @@
         [VMEM((LX, LY, MERGED), BF16), pltpu.SemaphoreType.DMA((XP,))],
         name="z_inv",
         out_specs=pl.BlockSpec(memory_space=pl.ANY),
-    )(freq, z_inv, field, below, above)
+    )(freq, z_inv, field, first, second)
 
 
 def solution(mesh):

time: 114 us -> 113 us (level)
    ppermute x4, waiting for transfers between devices: 6.01 us -> 0.01 us  [swap_pairs(): return lax.ppermute(value, ('px', 'py'), pairs)]
    all_to_all x1, waiting for transfers between devices: 0.01 us -> 5.23 us  [body(): freq = lax.all_to_all(freq, 'px', 0, 0, tiled=True)]
  transfers between devices with their start and end apart: 5 -> 5, of which waited for: 1 -> 1; matrix products, arithmetic and copies ran while one was open for 0% -> 0% of each run, Pallas kernels for 6% -> 7%
where the time goes in v9:
time: 113 us
  blocking collectives  79.1 us (70%)
  Pallas kernels  16.3 us (14%)
  starting transfers between devices  10.9 us (10%)
  waiting for transfers between devices  5.24 us (5%)
  local copies, waits for them, and re-layouts  1.45 us (1%)
    all_to_all x2, blocking collectives, body(): freq = lax.all_to_all(freq, 'py', 0, 0, tiled=True)  58.9 us
    all_to_all x1, blocking collectives, body(): freq = lax.all_to_all(freq, 'px', 0, 0, tiled=True)  20.2 us
    ppermute x4, starting transfers between devices, swap_pairs(): return lax.ppermute(value, ('px', 'py'), pairs)  7.33 us
    pallas_call x1, Pallas kernels, body(): call(conv_kernel, filtered, [VMEM((LX, LY, wide), F32), VMEM((27, W), F32...  6.94 us
    all_to_all x1, waiting for transfers between devices, body(): freq = lax.all_to_all(freq, 'px', 0, 0, tiled=True)  5.23 us
    all_to_all x1, starting transfers between devices, body(): freq = lax.all_to_all(freq, 'px', 0, 0, tiled=True)  3.55 us
    pallas_call x1, Pallas kernels, body(): call(spectrum_kernel, shape(PX, XP, 2 * Q // PX, W), [rows, VMEM((W // 12...  3.45 us
    pallas_call x1, Pallas kernels, body(): call(edge_kernel, [shape(LX, ZH * LY, W), shape(KZ, XE, 2 * LY, W)] + [sh...  2.74 us
  transfers between devices with their start and end apart: 5, of which 1 were waited for; matrix products, arithmetic and copies ran while one was open for 0% of the time, Pallas kernels for 7%

profile of v9, /device:TPU:1, one launch (start us, length us, event | category | flops | bytes accessed | tf_op | source)
XLA Modules:
  0.0 113.1 jit_solution(1805438966353689158)
XLA Ops:
  0.0 1.4 %copy-done = bf16[16,8,6144]{2,1,0:T(8,128)(2,1)S(1)} copy-done((bf16[16,8,6144]{2,1,0:T(8,128)(2,1)S(1)}, bf16[16,8,6144]{2,1,0:T(8,128)(2,1)}, u32[]{:S(2)}) %copy-start) | copy-done | bytes 1572888
  1.4 0.3 y_rows.1
  1.8 1.5 %collective-permute-start = (bf16[16,6144]{1,0:T(8,128)(2,1)S(1)}, bf16[16,6144]{1,0:T(8,128)(2,1)S(1)}, u32[]{:S(2)}, u32[]{:S(2)}) collective-permute-start(bf16[16,6144]{1,0:T(8,128)(2,1)S(1)} %get-tuple-element.17), channel_id=1, source_target_pairs={{0,1},{1,0},{2,3},{3,2},{4,5},{5,4},{6,7},{7,6},{8,9},{9,8},{10,11... | collective-permute-start | bytes 589832 | tf_op jit(solution)/shard_map/ppermute | solution.py:331
  3.3 1.3 %collective-permute-start.1 = (bf16[16,6144]{1,0:T(8,128)(2,1)S(1)}, bf16[16,6144]{1,0:T(8,128)(2,1)S(1)}, u32[]{:S(2)}, u32[]{:S(2)}) collective-permute-start(bf16[16,6144]{1,0:T(8,128)(2,1)S(1)} %get-tuple-element.18), channel_id=1, source_target_pairs={{0,16},{1,2},{2,1},{3,4},{4,3},{5,6},{6,5},{7,8},{8,7},{9,10},{10,... | collective-permute-start | bytes 589832 | tf_op jit(solution)/shard_map/ppermute | solution.py:331
  4.5 0.0 copy-done.1
  4.5 6.9 %conv.1 = f32[48,144,128]{2,1,0:T(8,128)S(1)} custom-call(bf16[16,8,6144]{2,1,0:T(8,128)(2,1)S(1)} %copy-done, f32[27,192]{1,0:T(8,128)S(1)} %copy-done.1), custom_call_target="tpu_custom_call" | custom-call | tf_op jit(solution)/shard_map/conv/pallas_call | solution.py:341
  11.5 0.0 collective-permute-done.first
  11.5 0.0 collective-permute-done.1.second
  11.5 0.0 copy-done.4
  11.5 2.7 %edge_z.1 = (bf16[16,128,384]{2,1,0:T(8,128)(2,1)S(1)}, bf16[16,9,16,384]{3,2,1,0:T(8,128)(2,1)S(1)}, bf16[128,384]{1,0:T(8,128)(2,1)S(1)}, bf16[128,384]{1,0:T(8,128)(2,1)S(1)}) custom-call(f32[48,144,128]{2,1,0:T(8,128)S(1)} %conv.1, bf16[16,6144]{1,0:T(8,128)(2,1)S(1)} %collective-permute-done.first, bf16[16,6144]{1,0:T(8,128)(2,1)S(1)} %collective-permute-done.1.second, ...), custom_call_target="tpu_custom_call" | custom-call | tf_op jit(solution)/shard_map/edge_z/pallas_call | solution.py:351
  14.3 0.0 copy-start.9
  14.3 29.9 %all_to_all.20.given = bf16[16,9,16,384]{3,2,1,0:T(8,128)(2,1)S(1)} all-to-all(bf16[16,9,16,384]{3,2,1,0:T(8,128)(2,1)S(1)} %get-tuple-element.19), channel_id=1, replica_groups=mesh['px'=8,'py'=16] {'py'}, dimensions={0} | all-to-all | bytes 3538944 | tf_op jit(solution)/shard_map/all_to_all | solution.py:358
  44.2 0.0 copy-done.9
  44.2 0.0 copy-start.8
  44.2 0.5 y_fwd.2
  44.7 20.2 %all_to_all.21.given = bf16[8,9,16,384]{3,2,1,0:T(8,128)(2,1)S(1)} all-to-all(bf16[8,9,16,384]{3,2,1,0:T(8,128)(2,1)S(1)} %y_fwd.2), channel_id=1, replica_groups=mesh['px'=8,'py'=16] {'px'}, dimensions={0} | all-to-all | bytes 1769472 | tf_op jit(solution)/shard_map/all_to_all | solution.py:360
  64.9 0.0 copy-done.3
  64.9 0.0 copy-done.5
  64.9 0.0 copy-done.6
  64.9 0.0 copy-start.7
  64.9 3.5 %spec.1 = bf16[8,8,16,384]{3,2,1,0:T(8,128)(2,1)} custom-call(bf16[8,9,16,384]{3,2,1,0:T(8,128)(2,1)S(1)} %all_to_all.21.given, bf16[256,144]{1,0:T(8,128)(2,1)S(1)} %copy-done.3, bf16[256,128]{1,0:T(8,128)(2,1)S(1)} %copy-done.8, bf16[2,2,96,96]{3,2,1,0:T(8,128)(2,1)S(1)} %copy-done.5, bf16[2,2,96,96]{3,2,1,0:T(8,128)(2,1)S(1)} %copy-done.6), custom_call_target="tpu_custom_call" | custom-call | tf_op jit(solution)/shard_map/spec/pallas_call | solution.py:362
  68.4 3.5 %all-to-all-start.2 = ((bf16[8,8,16,384]{3,2,1,0:T(8,128)(2,1)}), bf16[8,8,16,384]{3,2,1,0:T(8,128)(2,1)S(1)}, u32[]{:S(2)}, u32[]{:S(2)}) async-start(bf16[8,8,16,384]{3,2,1,0:T(8,128)(2,1)} %spec.1), calls=%async_computation.2 | async-start | bytes 1572864 | tf_op jit(solution)/shard_map/all_to_all | solution.py:369
  72.0 1.4 %collective-permute-start.2 = (bf16[128,384]{1,0:T(8,128)(2,1)S(1)}, bf16[128,384]{1,0:T(8,128)(2,1)S(1)}, u32[]{:S(2)}, u32[]{:S(2)}) collective-permute-start(bf16[128,384]{1,0:T(8,128)(2,1)S(1)} %get-tuple-element.30), channel_id=1, source_target_pairs={{0,16},{1,17},{2,18},{3,19},{4,20},{5,21},{6,22},{7,23},{8,24},{9,... | collective-permute-start | bytes 294920 | tf_op jit(solution)/shard_map/ppermute | solution.py:331
  73.4 3.1 %collective-permute-start.3 = (bf16[128,384]{1,0:T(8,128)(2,1)S(1)}, bf16[128,384]{1,0:T(8,128)(2,1)S(1)}, u32[]{:S(2)}, u32[]{:S(2)}) collective-permute-start(bf16[128,384]{1,0:T(8,128)(2,1)S(1)} %get-tuple-element.29), channel_id=1, source_target_pairs={{0,1},{1,0},{2,3},{3,2},{4,5},{5,4},{6,7},{7,6},{8,9},{9,8},{10,11... | collective-permute-start | bytes 294920 | tf_op jit(solution)/shard_map/ppermute | solution.py:331
  76.5 5.2 %all-to-all-done.2.given = bf16[8,8,16,384]{3,2,1,0:T(8,128)(2,1)S(1)} async-done(((bf16[8,8,16,384]{3,2,1,0:T(8,128)(2,1)}), bf16[8,8,16,384]{3,2,1,0:T(8,128)(2,1)S(1)}, u32[]{:S(2)}, u32[]{:S(2)}) %all-to-all-start.2) | async-done | bytes 786464 | tf_op jit(solution)/shard_map/all_to_all | solution.py:369
  81.7 0.6 y_inv.2
  82.3 0.0 copy-start.2
  82.3 0.0 collective-permute-done.2.below
  82.3 0.0 collective-permute-done.3.above
  82.3 29.0 %all_to_all.22.given = bf16[16,8,16,384]{3,2,1,0:T(8,128)(2,1)S(1)} all-to-all(bf16[16,8,16,384]{3,2,1,0:T(8,128)(2,1)S(1)} %y_inv.2), channel_id=1, replica_groups=mesh['px'=8,'py'=16] {'py'}, dimensions={0} | all-to-all | bytes 3145728 | tf_op jit(solution)/shard_map/all_to_all | solution.py:372
  111.3 0.0 copy-done.2
  111.3 1.8 %z_inv.2 = bf16[16,8,6144]{2,1,0:T(8,128)(2,1)} custom-call(bf16[16,8,16,384]{3,2,1,0:T(8,128)(2,1)S(1)} %all_to_all.22.given, bf16[256,256]{1,0:T(8,128)(2,1)S(1)} %copy-done.2, bf16[16,128,384]{2,1,0:T(8,128)(2,1)S(1)} %get-tuple-element.26.field, bf16[128,384]{1,0:T(8,128)(2,1)S(1)} %collective-permute-done.2.below, ...), custom_call_target="tpu_custom_call" | custom-call | tf_op jit(solution)/shard_map/z_inv/pallas_call | solution.py:373
  (9 shorter events, 0.0 us)
Async XLA Ops:
  0.0 1.4 %copy-start = (bf16[16,8,6144]{2,1,0:T(8,128)(2,1)S(1)}, bf16[16,8,6144]{2,1,0:T(8,128)(2,1)}, u32[]{:S(2)}) copy-start(bf16[16,8,6144]{2,1,0:T(8,128)(2,1)} %tok.3) | copy-start | bytes 4718596
  1.4 3.1 %copy-start.1 = (f32[27,192]{1,0:T(8,128)S(1)}, f32[27,192]{1,0:T(8,128)}, u32[]{:S(2)}) copy-start(f32[27,192]{1,0:T(8,128)} %narrow.3) | copy-start | bytes 62212
  1.8 9.7 %collective-permute-start = (bf16[16,6144]{1,0:T(8,128)(2,1)S(1)}, bf16[16,6144]{1,0:T(8,128)(2,1)S(1)}, u32[]{:S(2)}, u32[]{:S(2)}) collective-permute-start(bf16[16,6144]{1,0:T(8,128)(2,1)S(1)} %get-tuple-element.17), channel_id=1, source_target_pairs={{0,1},{1,0},{2,3},{3,2},{4,5},{5,4},{6,7},{7,6},{8,9},{9,8},{10,11... | collective-permute-start | bytes 589832 | tf_op jit(solution)/shard_map/ppermute | solution.py:331
  3.3 8.3 %copy-start.4 = (bf16[256,256]{1,0:T(8,128)(2,1)S(1)}, bf16[256,256]{1,0:T(8,128)(2,1)}, u32[]{:S(2)}) copy-start(bf16[256,256]{1,0:T(8,128)(2,1)} %constant.24.clone.z_fwd) | copy-start | bytes 393220
  3.3 8.3 %collective-permute-start.1 = (bf16[16,6144]{1,0:T(8,128)(2,1)S(1)}, bf16[16,6144]{1,0:T(8,128)(2,1)S(1)}, u32[]{:S(2)}, u32[]{:S(2)}) collective-permute-start(bf16[16,6144]{1,0:T(8,128)(2,1)S(1)} %get-tuple-element.18), channel_id=1, source_target_pairs={{0,16},{1,2},{2,1},{3,4},{4,3},{5,6},{6,5},{7,8},{8,7},{9,10},{10,... | collective-permute-start | bytes 589832 | tf_op jit(solution)/shard_map/ppermute | solution.py:331
  14.3 29.9 %copy-start.9 = (bf16[128,256]{1,0:T(8,128)(2,1)S(1)}, bf16[128,256]{1,0:T(8,128)(2,1)}, u32[]{:S(2)}) copy-start(bf16[128,256]{1,0:T(8,128)(2,1)} %constant.26.clone.y_fwd) | copy-start | bytes 196612
  44.2 20.7 %copy-start.3 = (bf16[256,144]{1,0:T(8,128)(2,1)S(1)}, bf16[256,144]{1,0:T(8,128)(2,1)}, u32[]{:S(2)}) copy-start(bf16[256,144]{1,0:T(8,128)(2,1)} %constant.28.clone.x_fwd) | copy-start | bytes 221188
  44.2 20.7 %copy-start.5 = (bf16[2,2,96,96]{3,2,1,0:T(8,128)(2,1)S(1)}, bf16[2,2,96,96]{3,2,1,0:T(8,128)(2,1)}, u32[]{:S(2)}) copy-start(bf16[2,2,96,96]{3,2,1,0:T(8,128)(2,1)} %inner_weight.1) | copy-start | bytes 221188
  44.2 20.7 %copy-start.6 = (bf16[2,2,96,96]{3,2,1,0:T(8,128)(2,1)S(1)}, bf16[2,2,96,96]{3,2,1,0:T(8,128)(2,1)}, u32[]{:S(2)}) copy-start(bf16[2,2,96,96]{3,2,1,0:T(8,128)(2,1)} %outer_weight.1) | copy-start | bytes 221188
  44.2 20.7 %copy-start.8 = (bf16[256,128]{1,0:T(8,128)(2,1)S(1)}, bf16[256,128]{1,0:T(8,128)(2,1)}, u32[]{:S(2)}) copy-start(bf16[256,128]{1,0:T(8,128)(2,1)} %constant.29.clone.x_inv) | copy-start | bytes 196612
  64.9 16.8 %copy-start.7 = (bf16[256,128]{1,0:T(8,128)(2,1)S(1)}, bf16[256,128]{1,0:T(8,128)(2,1)}, u32[]{:S(2)}) copy-start(bf16[256,128]{1,0:T(8,128)(2,1)} %constant.27.clone.y_inv) | copy-start | bytes 196612
  68.4 13.4 %all-to-all-start.2 = ((bf16[8,8,16,384]{3,2,1,0:T(8,128)(2,1)}), bf16[8,8,16,384]{3,2,1,0:T(8,128)(2,1)S(1)}, u32[]{:S(2)}, u32[]{:S(2)}) async-start(bf16[8,8,16,384]{3,2,1,0:T(8,128)(2,1)} %spec.1), calls=%async_computation.2 | async-start | bytes 1572864 | tf_op jit(solution)/shard_map/all_to_all | solution.py:369
  72.0 10.4 %collective-permute-start.2 = (bf16[128,384]{1,0:T(8,128)(2,1)S(1)}, bf16[128,384]{1,0:T(8,128)(2,1)S(1)}, u32[]{:S(2)}, u32[]{:S(2)}) collective-permute-start(bf16[128,384]{1,0:T(8,128)(2,1)S(1)} %get-tuple-element.30), channel_id=1, source_target_pairs={{0,16},{1,17},{2,18},{3,19},{4,20},{5,21},{6,22},{7,23},{8,24},{9,... | collective-permute-start | bytes 294920 | tf_op jit(solution)/shard_map/ppermute | solution.py:331
  73.4 8.9 %collective-permute-start.3 = (bf16[128,384]{1,0:T(8,128)(2,1)S(1)}, bf16[128,384]{1,0:T(8,128)(2,1)S(1)}, u32[]{:S(2)}, u32[]{:S(2)}) collective-permute-start(bf16[128,384]{1,0:T(8,128)(2,1)S(1)} %get-tuple-element.29), channel_id=1, source_target_pairs={{0,1},{1,0},{2,3},{3,2},{4,5},{5,4},{6,7},{7,6},{8,9},{9,8},{10,11... | collective-permute-start | bytes 294920 | tf_op jit(solution)/shard_map/ppermute | solution.py:331
  82.3 29.0 %copy-start.2 = (bf16[256,256]{1,0:T(8,128)(2,1)S(1)}, bf16[256,256]{1,0:T(8,128)(2,1)}, u32[]{:S(2)}) copy-start(bf16[256,256]{1,0:T(8,128)(2,1)} %constant.25.clone.z_inv) | copy-start | bytes 393220

commit v10 on v9

--- a/solution.py
+++ b/solution.py
@@ -157,10 +157,8 @@
 ):
     weight[...] = jnp.concatenate([narrow[...], narrow[...]], axis=1)
     for rows, rows_s, value in zip((ylo, yhi), (ylo_s, yhi_s), by_order("py", first[...], second[...])):
-        none = jnp.zeros((2, MERGED), F32)
-        value = jnp.concatenate([none, value, none], axis=0)
         rows[...] = value
-        pad = jnp.zeros((LX + 4, C), F32)
+        pad = jnp.zeros((LX, C), F32)
         rows_s[...] = jnp.concatenate([pad, value, pad], axis=1)
 
     @pl.loop(0, MERGED // 128)
@@ -169,7 +167,7 @@
         after = pl.multiple_of(j * 128 + W, 128)
         here = pl.ds(at, 128)
         phase = pl.multiple_of(lax.rem(j, 3) * 128, 128)
-        edge[j] = jnp.zeros(edge.shape[1:], F32)
+        edge[j, : (LX + 2) * LY, :] = jnp.zeros(((LX + 2) * LY, 128), F32)
         for side, rows, rows_s, b in ((0, ylo, ylo_s, 0), (1, yhi, yhi_s, 2)):
             mid = rows[:, here]
             before = rows_s[:, here]
@@ -179,7 +177,8 @@
                 t = a * 9 + b * 3
                 taps = [weight[t + e : t + e + 1, pl.ds(phase, 128)] for e in range(3)]
                 term = before * taps[0] + mid * taps[1] + behind * taps[2]
-                term = term[a : a + LX + 2]
+                around = [jnp.zeros((n, 128), F32) for n in (2 - a, a) if n]
+                term = jnp.concatenate([term] + around if a == 2 else around[:1] + [term] + around[1:], axis=0)
                 total = term if total is None else total + term
             cells = pl.ds(side * (LY - 1), LX + 2, stride=LY)
             edge[j, cells, :] = total
@@ -347,11 +346,11 @@
         ],
         name="conv",
     )(tokens, conv_weight)
-    rows = [VMEM((LX + 4, MERGED), F32)] * 2 + [VMEM((LX + 4, wide), F32)] * 2
+    rows = [VMEM((LX, MERGED), F32)] * 2 + [VMEM((LX, wide), F32)] * 2
     field, freq, to_below, to_above = call(
         edge_kernel,
         [shape(LX, ZH * LY, W), shape(KZ, XE, 2 * LY, W)] + [shape(ZH * LY, W)] * 2,
-        rows + [VMEM(filtered.shape, F32), VMEM((27, W), F32)],
+        rows + [VMEM((MERGED // 128, 24 * LY, 128), F32), VMEM((27, W), F32)],
         name="edge_z",
     )(conv, first, second, conv_weight, z_fwd)
     rows = VMEM((W // 128, 2 * XP * Q, 128), F32)

time: 113 us -> 113 us (level)
  no operation moved by 1% of the time
where the time goes in v10:
time: 113 us
  blocking collectives  79.1 us (70%)
  Pallas kernels  16.2 us (14%)
  starting transfers between devices  10.9 us (10%)
  waiting for transfers between devices  5.25 us (5%)
  local copies, waits for them, and re-layouts  1.45 us (1%)
    all_to_all x2, blocking collectives, body(): freq = lax.all_to_all(freq, 'py', 0, 0, tiled=True)  58.9 us
    all_to_all x1, blocking collectives, body(): freq = lax.all_to_all(freq, 'px', 0, 0, tiled=True)  20.2 us
    ppermute x4, starting transfers between devices, swap_pairs(): return lax.ppermute(value, ('px', 'py'), pairs)  7.33 us
    pallas_call x1, Pallas kernels, body(): call(conv_kernel, filtered, [VMEM((LX, LY, wide), F32), VMEM((27, W), F32...  6.94 us
    all_to_all x1, waiting for transfers between devices, body(): freq = lax.all_to_all(freq, 'px', 0, 0, tiled=True)  5.24 us
    all_to_all x1, starting transfers between devices, body(): freq = lax.all_to_all(freq, 'px', 0, 0, tiled=True)  3.55 us
    pallas_call x1, Pallas kernels, body(): call(spectrum_kernel, shape(PX, XP, 2 * Q // PX, W), [rows, VMEM((W // 12...  3.45 us
    pallas_call x1, Pallas kernels, body(): call(edge_kernel, [shape(LX, ZH * LY, W), shape(KZ, XE, 2 * LY, W)] + [sh...  2.6 us
  transfers between devices with their start and end apart: 5, of which 1 were waited for; matrix products, arithmetic and copies ran while one was open for 0% of the time, Pallas kernels for 7%

profile of v10, /device:TPU:1, one launch (start us, length us, event | category | flops | bytes accessed | tf_op | source)
XLA Modules:
  0.0 113.0 jit_solution(6504380442354934146)
XLA Ops:
  0.0 1.4 %copy-done = bf16[16,8,6144]{2,1,0:T(8,128)(2,1)S(1)} copy-done((bf16[16,8,6144]{2,1,0:T(8,128)(2,1)S(1)}, bf16[16,8,6144]{2,1,0:T(8,128)(2,1)}, u32[]{:S(2)}) %copy-start) | copy-done | bytes 1572888
  1.4 0.3 y_rows.1
  1.8 1.5 %collective-permute-start = (bf16[16,6144]{1,0:T(8,128)(2,1)S(1)}, bf16[16,6144]{1,0:T(8,128)(2,1)S(1)}, u32[]{:S(2)}, u32[]{:S(2)}) collective-permute-start(bf16[16,6144]{1,0:T(8,128)(2,1)S(1)} %get-tuple-element.17), channel_id=1, source_target_pairs={{0,1},{1,0},{2,3},{3,2},{4,5},{5,4},{6,7},{7,6},{8,9},{9,8},{10,11... | collective-permute-start | bytes 589832 | tf_op jit(solution)/shard_map/ppermute | solution.py:330
  3.3 1.3 %collective-permute-start.1 = (bf16[16,6144]{1,0:T(8,128)(2,1)S(1)}, bf16[16,6144]{1,0:T(8,128)(2,1)S(1)}, u32[]{:S(2)}, u32[]{:S(2)}) collective-permute-start(bf16[16,6144]{1,0:T(8,128)(2,1)S(1)} %get-tuple-element.18), channel_id=1, source_target_pairs={{0,16},{1,2},{2,1},{3,4},{4,3},{5,6},{6,5},{7,8},{8,7},{9,10},{10,... | collective-permute-start | bytes 589832 | tf_op jit(solution)/shard_map/ppermute | solution.py:330
  4.5 0.0 copy-done.1
  4.5 6.9 %conv.1 = f32[48,144,128]{2,1,0:T(8,128)S(1)} custom-call(bf16[16,8,6144]{2,1,0:T(8,128)(2,1)S(1)} %copy-done, f32[27,192]{1,0:T(8,128)S(1)} %copy-done.1), custom_call_target="tpu_custom_call" | custom-call | tf_op jit(solution)/shard_map/conv/pallas_call | solution.py:340
  11.5 0.0 collective-permute-done.first
  11.5 0.0 collective-permute-done.1.second
  11.5 0.0 copy-done.4
  11.5 2.6 %edge_z.1 = (bf16[16,128,384]{2,1,0:T(8,128)(2,1)S(1)}, bf16[16,9,16,384]{3,2,1,0:T(8,128)(2,1)S(1)}, bf16[128,384]{1,0:T(8,128)(2,1)S(1)}, bf16[128,384]{1,0:T(8,128)(2,1)S(1)}) custom-call(f32[48,144,128]{2,1,0:T(8,128)S(1)} %conv.1, bf16[16,6144]{1,0:T(8,128)(2,1)S(1)} %collective-permute-done.first, bf16[16,6144]{1,0:T(8,128)(2,1)S(1)} %collective-permute-done.1.second, ...), custom_call_target="tpu_custom_call" | custom-call | tf_op jit(solution)/shard_map/edge_z/pallas_call | solution.py:350
  14.1 0.0 copy-start.9
  14.1 29.9 %all_to_all.20.given = bf16[16,9,16,384]{3,2,1,0:T(8,128)(2,1)S(1)} all-to-all(bf16[16,9,16,384]{3,2,1,0:T(8,128)(2,1)S(1)} %get-tuple-element.19), channel_id=1, replica_groups=mesh['px'=8,'py'=16] {'py'}, dimensions={0} | all-to-all | bytes 3538944 | tf_op jit(solution)/shard_map/all_to_all | solution.py:357
  44.1 0.0 copy-done.9
  44.1 0.0 copy-start.8
  44.1 0.5 y_fwd.2
  44.6 20.2 %all_to_all.21.given = bf16[8,9,16,384]{3,2,1,0:T(8,128)(2,1)S(1)} all-to-all(bf16[8,9,16,384]{3,2,1,0:T(8,128)(2,1)S(1)} %y_fwd.2), channel_id=1, replica_groups=mesh['px'=8,'py'=16] {'px'}, dimensions={0} | all-to-all | bytes 1769472 | tf_op jit(solution)/shard_map/all_to_all | solution.py:359
  64.7 0.0 copy-done.3
  64.7 0.0 copy-done.5
  64.7 0.0 copy-done.6
  64.8 0.0 copy-done.8
  64.8 0.0 copy-start.7
  64.8 3.4 %spec.1 = bf16[8,8,16,384]{3,2,1,0:T(8,128)(2,1)} custom-call(bf16[8,9,16,384]{3,2,1,0:T(8,128)(2,1)S(1)} %all_to_all.21.given, bf16[256,144]{1,0:T(8,128)(2,1)S(1)} %copy-done.3, bf16[256,128]{1,0:T(8,128)(2,1)S(1)} %copy-done.8, bf16[2,2,96,96]{3,2,1,0:T(8,128)(2,1)S(1)} %copy-done.5, bf16[2,2,96,96]{3,2,1,0:T(8,128)(2,1)S(1)} %copy-done.6), custom_call_target="tpu_custom_call" | custom-call | tf_op jit(solution)/shard_map/spec/pallas_call | solution.py:361
  68.2 3.5 %all-to-all-start.2 = ((bf16[8,8,16,384]{3,2,1,0:T(8,128)(2,1)}), bf16[8,8,16,384]{3,2,1,0:T(8,128)(2,1)S(1)}, u32[]{:S(2)}, u32[]{:S(2)}) async-start(bf16[8,8,16,384]{3,2,1,0:T(8,128)(2,1)} %spec.1), calls=%async_computation.2 | async-start | bytes 1572864 | tf_op jit(solution)/shard_map/all_to_all | solution.py:368
  71.8 1.4 %collective-permute-start.2 = (bf16[128,384]{1,0:T(8,128)(2,1)S(1)}, bf16[128,384]{1,0:T(8,128)(2,1)S(1)}, u32[]{:S(2)}, u32[]{:S(2)}) collective-permute-start(bf16[128,384]{1,0:T(8,128)(2,1)S(1)} %get-tuple-element.30), channel_id=1, source_target_pairs={{0,16},{1,17},{2,18},{3,19},{4,20},{5,21},{6,22},{7,23},{8,24},{9,... | collective-permute-start | bytes 294920 | tf_op jit(solution)/shard_map/ppermute | solution.py:330
  73.3 3.1 %collective-permute-start.3 = (bf16[128,384]{1,0:T(8,128)(2,1)S(1)}, bf16[128,384]{1,0:T(8,128)(2,1)S(1)}, u32[]{:S(2)}, u32[]{:S(2)}) collective-permute-start(bf16[128,384]{1,0:T(8,128)(2,1)S(1)} %get-tuple-element.29), channel_id=1, source_target_pairs={{0,1},{1,0},{2,3},{3,2},{4,5},{5,4},{6,7},{7,6},{8,9},{9,8},{10,11... | collective-permute-start | bytes 294920 | tf_op jit(solution)/shard_map/ppermute | solution.py:330
  76.4 5.2 %all-to-all-done.2.given = bf16[8,8,16,384]{3,2,1,0:T(8,128)(2,1)S(1)} async-done(((bf16[8,8,16,384]{3,2,1,0:T(8,128)(2,1)}), bf16[8,8,16,384]{3,2,1,0:T(8,128)(2,1)S(1)}, u32[]{:S(2)}, u32[]{:S(2)}) %all-to-all-start.2) | async-done | bytes 786464 | tf_op jit(solution)/shard_map/all_to_all | solution.py:368
  81.6 0.6 y_inv.2
  82.2 0.0 copy-start.2
  82.2 0.0 collective-permute-done.2.below
  82.2 0.0 collective-permute-done.3.above
  82.2 29.0 %all_to_all.22.given = bf16[16,8,16,384]{3,2,1,0:T(8,128)(2,1)S(1)} all-to-all(bf16[16,8,16,384]{3,2,1,0:T(8,128)(2,1)S(1)} %y_inv.2), channel_id=1, replica_groups=mesh['px'=8,'py'=16] {'py'}, dimensions={0} | all-to-all | bytes 3145728 | tf_op jit(solution)/shard_map/all_to_all | solution.py:371
  111.2 1.8 %z_inv.2 = bf16[16,8,6144]{2,1,0:T(8,128)(2,1)} custom-call(bf16[16,8,16,384]{3,2,1,0:T(8,128)(2,1)S(1)} %all_to_all.22.given, bf16[256,256]{1,0:T(8,128)(2,1)S(1)} %copy-done.2, bf16[16,128,384]{2,1,0:T(8,128)(2,1)S(1)} %get-tuple-element.26.field, bf16[128,384]{1,0:T(8,128)(2,1)S(1)} %collective-permute-done.2.below, ...), custom_call_target="tpu_custom_call" | custom-call | tf_op jit(solution)/shard_map/z_inv/pallas_call | solution.py:372
  (9 shorter events, 0.0 us)
Async XLA Ops:
  0.0 1.4 %copy-start = (bf16[16,8,6144]{2,1,0:T(8,128)(2,1)S(1)}, bf16[16,8,6144]{2,1,0:T(8,128)(2,1)}, u32[]{:S(2)}) copy-start(bf16[16,8,6144]{2,1,0:T(8,128)(2,1)} %tok.3) | copy-start | bytes 4718596
  1.4 3.1 %copy-start.1 = (f32[27,192]{1,0:T(8,128)S(1)}, f32[27,192]{1,0:T(8,128)}, u32[]{:S(2)}) copy-start(f32[27,192]{1,0:T(8,128)} %narrow.3) | copy-start | bytes 62212
  1.8 9.7 %collective-permute-start = (bf16[16,6144]{1,0:T(8,128)(2,1)S(1)}, bf16[16,6144]{1,0:T(8,128)(2,1)S(1)}, u32[]{:S(2)}, u32[]{:S(2)}) collective-permute-start(bf16[16,6144]{1,0:T(8,128)(2,1)S(1)} %get-tuple-element.17), channel_id=1, source_target_pairs={{0,1},{1,0},{2,3},{3,2},{4,5},{5,4},{6,7},{7,6},{8,9},{9,8},{10,11... | collective-permute-start | bytes 589832 | tf_op jit(solution)/shard_map/ppermute | solution.py:330
  3.3 8.3 %copy-start.4 = (bf16[256,256]{1,0:T(8,128)(2,1)S(1)}, bf16[256,256]{1,0:T(8,128)(2,1)}, u32[]{:S(2)}) copy-start(bf16[256,256]{1,0:T(8,128)(2,1)} %constant.24.clone.z_fwd) | copy-start | bytes 393220
  3.3 8.3 %collective-permute-start.1 = (bf16[16,6144]{1,0:T(8,128)(2,1)S(1)}, bf16[16,6144]{1,0:T(8,128)(2,1)S(1)}, u32[]{:S(2)}, u32[]{:S(2)}) collective-permute-start(bf16[16,6144]{1,0:T(8,128)(2,1)S(1)} %get-tuple-element.18), channel_id=1, source_target_pairs={{0,16},{1,2},{2,1},{3,4},{4,3},{5,6},{6,5},{7,8},{8,7},{9,10},{10,... | collective-permute-start | bytes 589832 | tf_op jit(solution)/shard_map/ppermute | solution.py:330
  14.1 29.9 %copy-start.9 = (bf16[128,256]{1,0:T(8,128)(2,1)S(1)}, bf16[128,256]{1,0:T(8,128)(2,1)}, u32[]{:S(2)}) copy-start(bf16[128,256]{1,0:T(8,128)(2,1)} %constant.26.clone.y_fwd) | copy-start | bytes 196612
  44.1 20.7 %copy-start.3 = (bf16[256,144]{1,0:T(8,128)(2,1)S(1)}, bf16[256,144]{1,0:T(8,128)(2,1)}, u32[]{:S(2)}) copy-start(bf16[256,144]{1,0:T(8,128)(2,1)} %constant.28.clone.x_fwd) | copy-start | bytes 221188
  44.1 20.7 %copy-start.5 = (bf16[2,2,96,96]{3,2,1,0:T(8,128)(2,1)S(1)}, bf16[2,2,96,96]{3,2,1,0:T(8,128)(2,1)}, u32[]{:S(2)}) copy-start(bf16[2,2,96,96]{3,2,1,0:T(8,128)(2,1)} %inner_weight.1) | copy-start | bytes 221188
  44.1 20.7 %copy-start.6 = (bf16[2,2,96,96]{3,2,1,0:T(8,128)(2,1)S(1)}, bf16[2,2,96,96]{3,2,1,0:T(8,128)(2,1)}, u32[]{:S(2)}) copy-start(bf16[2,2,96,96]{3,2,1,0:T(8,128)(2,1)} %outer_weight.1) | copy-start | bytes 221188
  44.1 20.7 %copy-start.8 = (bf16[256,128]{1,0:T(8,128)(2,1)S(1)}, bf16[256,128]{1,0:T(8,128)(2,1)}, u32[]{:S(2)}) copy-start(bf16[256,128]{1,0:T(8,128)(2,1)} %constant.29.clone.x_inv) | copy-start | bytes 196612
  64.8 16.8 %copy-start.7 = (bf16[256,128]{1,0:T(8,128)(2,1)S(1)}, bf16[256,128]{1,0:T(8,128)(2,1)}, u32[]{:S(2)}) copy-start(bf16[256,128]{1,0:T(8,128)(2,1)} %constant.27.clone.y_inv) | copy-start | bytes 196612
  68.2 13.4 %all-to-all-start.2 = ((bf16[8,8,16,384]{3,2,1,0:T(8,128)(2,1)}), bf16[8,8,16,384]{3,2,1,0:T(8,128)(2,1)S(1)}, u32[]{:S(2)}, u32[]{:S(2)}) async-start(bf16[8,8,16,384]{3,2,1,0:T(8,128)(2,1)} %spec.1), calls=%async_computation.2 | async-start | bytes 1572864 | tf_op jit(solution)/shard_map/all_to_all | solution.py:368
  71.8 10.4 %collective-permute-start.2 = (bf16[128,384]{1,0:T(8,128)(2,1)S(1)}, bf16[128,384]{1,0:T(8,128)(2,1)S(1)}, u32[]{:S(2)}, u32[]{:S(2)}) collective-permute-start(bf16[128,384]{1,0:T(8,128)(2,1)S(1)} %get-tuple-element.30), channel_id=1, source_target_pairs={{0,16},{1,17},{2,18},{3,19},{4,20},{5,21},{6,22},{7,23},{8,24},{9,... | collective-permute-start | bytes 294920 | tf_op jit(solution)/shard_map/ppermute | solution.py:330
  73.3 8.9 %collective-permute-start.3 = (bf16[128,384]{1,0:T(8,128)(2,1)S(1)}, bf16[128,384]{1,0:T(8,128)(2,1)S(1)}, u32[]{:S(2)}, u32[]{:S(2)}) collective-permute-start(bf16[128,384]{1,0:T(8,128)(2,1)S(1)} %get-tuple-element.29), channel_id=1, source_target_pairs={{0,1},{1,0},{2,3},{3,2},{4,5},{5,4},{6,7},{7,6},{8,9},{9,8},{10,11... | collective-permute-start | bytes 294920 | tf_op jit(solution)/shard_map/ppermute | solution.py:330
  82.2 29.0 %copy-start.2 = (bf16[256,256]{1,0:T(8,128)(2,1)S(1)}, bf16[256,256]{1,0:T(8,128)(2,1)}, u32[]{:S(2)}) copy-start(bf16[256,256]{1,0:T(8,128)(2,1)} %constant.25.clone.z_inv) | copy-start | bytes 393220

commit v11 on v10

--- a/solution.py
+++ b/solution.py
@@ -126,7 +126,7 @@
         shifted[x] = jnp.concatenate([pad, tok[x].astype(F32), pad], axis=1)
     row_at = lax.broadcasted_iota(jnp.int32, (LY, 128), 0)
 
-    @pl.loop(0, MERGED // 128)
+    @pl.loop(0, MERGED // 128, unroll=6)
     def _(j):
         at = pl.multiple_of(j * 128, 128)
         after = pl.multiple_of(j * 128 + W, 128)
@@ -161,7 +161,7 @@
         pad = jnp.zeros((LX, C), F32)
         rows_s[...] = jnp.concatenate([pad, value, pad], axis=1)
 
-    @pl.loop(0, MERGED // 128)
+    @pl.loop(0, MERGED // 128, unroll=6)
     def _(j):
         at = pl.multiple_of(j * 128, 128)
         after = pl.multiple_of(j * 128 + W, 128)

time: 113 us -> 112 us (level)
  transfers between devices with their start and end apart: 5 -> 5, of which waited for: 1 -> 1; matrix products, arithmetic and copies ran while one was open for 0% -> 0% of each run, Pallas kernels for 7% -> 6%
where the time goes in v11:
time: 112 us
  blocking collectives  79.1 us (71%)
  Pallas kernels  15.3 us (14%)
  starting transfers between devices  10.9 us (10%)
  waiting for transfers between devices  5.24 us (5%)
  local copies, waits for them, and re-layouts  1.45 us (1%)
    all_to_all x2, blocking collectives, body(): freq = lax.all_to_all(freq, 'py', 0, 0, tiled=True)  58.9 us
    all_to_all x1, blocking collectives, body(): freq = lax.all_to_all(freq, 'px', 0, 0, tiled=True)  20.2 us
    ppermute x4, starting transfers between devices, swap_pairs(): return lax.ppermute(value, ('px', 'py'), pairs)  7.33 us
    pallas_call x1, Pallas kernels, body(): call(conv_kernel, filtered, [VMEM((LX, LY, wide), F32), VMEM((27, W), F32...  6.53 us
    all_to_all x1, waiting for transfers between devices, body(): freq = lax.all_to_all(freq, 'px', 0, 0, tiled=True)  5.23 us
    all_to_all x1, starting transfers between devices, body(): freq = lax.all_to_all(freq, 'px', 0, 0, tiled=True)  3.55 us
    pallas_call x1, Pallas kernels, body(): call(spectrum_kernel, shape(PX, XP, 2 * Q // PX, W), [rows, VMEM((W // 12...  3.45 us
  transfers between devices with their start and end apart: 5, of which 1 were waited for; matrix products, arithmetic and copies ran while one was open for 0% of the time, Pallas kernels for 6%

profile of v11, /device:TPU:1, one launch (start us, length us, event | category | flops | bytes accessed | tf_op | source)
XLA Modules:
  0.0 112.1 jit_solution(14163291318502499890)
XLA Ops:
  0.0 1.4 %copy-done = bf16[16,8,6144]{2,1,0:T(8,128)(2,1)S(1)} copy-done((bf16[16,8,6144]{2,1,0:T(8,128)(2,1)S(1)}, bf16[16,8,6144]{2,1,0:T(8,128)(2,1)}, u32[]{:S(2)}) %copy-start) | copy-done | bytes 1572888
  1.4 0.3 y_rows.1
  1.8 1.5 %collective-permute-start = (bf16[16,6144]{1,0:T(8,128)(2,1)S(1)}, bf16[16,6144]{1,0:T(8,128)(2,1)S(1)}, u32[]{:S(2)}, u32[]{:S(2)}) collective-permute-start(bf16[16,6144]{1,0:T(8,128)(2,1)S(1)} %get-tuple-element.17), channel_id=1, source_target_pairs={{0,1},{1,0},{2,3},{3,2},{4,5},{5,4},{6,7},{7,6},{8,9},{9,8},{10,11... | collective-permute-start | bytes 589832 | tf_op jit(solution)/shard_map/ppermute | solution.py:330
  3.3 1.3 %collective-permute-start.1 = (bf16[16,6144]{1,0:T(8,128)(2,1)S(1)}, bf16[16,6144]{1,0:T(8,128)(2,1)S(1)}, u32[]{:S(2)}, u32[]{:S(2)}) collective-permute-start(bf16[16,6144]{1,0:T(8,128)(2,1)S(1)} %get-tuple-element.18), channel_id=1, source_target_pairs={{0,16},{1,2},{2,1},{3,4},{4,3},{5,6},{6,5},{7,8},{8,7},{9,10},{10,... | collective-permute-start | bytes 589832 | tf_op jit(solution)/shard_map/ppermute | solution.py:330
  4.5 0.0 copy-done.1
  4.5 6.5 %conv.1 = f32[48,144,128]{2,1,0:T(8,128)S(1)} custom-call(bf16[16,8,6144]{2,1,0:T(8,128)(2,1)S(1)} %copy-done, f32[27,192]{1,0:T(8,128)S(1)} %copy-done.1), custom_call_target="tpu_custom_call" | custom-call | tf_op jit(solution)/shard_map/conv/pallas_call | solution.py:340
  11.1 0.0 collective-permute-done.first
  11.1 0.0 collective-permute-done.1.second
  11.1 0.0 copy-done.4
  11.1 2.1 %edge_z.1 = (bf16[16,128,384]{2,1,0:T(8,128)(2,1)S(1)}, bf16[16,9,16,384]{3,2,1,0:T(8,128)(2,1)S(1)}, bf16[128,384]{1,0:T(8,128)(2,1)S(1)}, bf16[128,384]{1,0:T(8,128)(2,1)S(1)}) custom-call(f32[48,144,128]{2,1,0:T(8,128)S(1)} %conv.1, bf16[16,6144]{1,0:T(8,128)(2,1)S(1)} %collective-permute-done.first, bf16[16,6144]{1,0:T(8,128)(2,1)S(1)} %collective-permute-done.1.second, ...), custom_call_target="tpu_custom_call" | custom-call | tf_op jit(solution)/shard_map/edge_z/pallas_call | solution.py:350
  13.2 0.0 copy-start.9
  13.3 29.9 %all_to_all.20.given = bf16[16,9,16,384]{3,2,1,0:T(8,128)(2,1)S(1)} all-to-all(bf16[16,9,16,384]{3,2,1,0:T(8,128)(2,1)S(1)} %get-tuple-element.19), channel_id=1, replica_groups=mesh['px'=8,'py'=16] {'py'}, dimensions={0} | all-to-all | bytes 3538944 | tf_op jit(solution)/shard_map/all_to_all | solution.py:357
  43.2 0.0 copy-done.9
  43.2 0.0 copy-start.8
  43.2 0.5 y_fwd.2
  43.7 20.2 %all_to_all.21.given = bf16[8,9,16,384]{3,2,1,0:T(8,128)(2,1)S(1)} all-to-all(bf16[8,9,16,384]{3,2,1,0:T(8,128)(2,1)S(1)} %y_fwd.2), channel_id=1, replica_groups=mesh['px'=8,'py'=16] {'px'}, dimensions={0} | all-to-all | bytes 1769472 | tf_op jit(solution)/shard_map/all_to_all | solution.py:359
  63.8 0.0 copy-done.3
  63.8 0.0 copy-done.5
  63.9 0.0 copy-done.6
  63.9 0.0 copy-start.7
  63.9 3.4 %spec.1 = bf16[8,8,16,384]{3,2,1,0:T(8,128)(2,1)} custom-call(bf16[8,9,16,384]{3,2,1,0:T(8,128)(2,1)S(1)} %all_to_all.21.given, bf16[256,144]{1,0:T(8,128)(2,1)S(1)} %copy-done.3, bf16[256,128]{1,0:T(8,128)(2,1)S(1)} %copy-done.8, bf16[2,2,96,96]{3,2,1,0:T(8,128)(2,1)S(1)} %copy-done.5, bf16[2,2,96,96]{3,2,1,0:T(8,128)(2,1)S(1)} %copy-done.6), custom_call_target="tpu_custom_call" | custom-call | tf_op jit(solution)/shard_map/spec/pallas_call | solution.py:361
  67.3 3.5 %all-to-all-start.2 = ((bf16[8,8,16,384]{3,2,1,0:T(8,128)(2,1)}), bf16[8,8,16,384]{3,2,1,0:T(8,128)(2,1)S(1)}, u32[]{:S(2)}, u32[]{:S(2)}) async-start(bf16[8,8,16,384]{3,2,1,0:T(8,128)(2,1)} %spec.1), calls=%async_computation.2 | async-start | bytes 1572864 | tf_op jit(solution)/shard_map/all_to_all | solution.py:368
  70.9 1.4 %collective-permute-start.2 = (bf16[128,384]{1,0:T(8,128)(2,1)S(1)}, bf16[128,384]{1,0:T(8,128)(2,1)S(1)}, u32[]{:S(2)}, u32[]{:S(2)}) collective-permute-start(bf16[128,384]{1,0:T(8,128)(2,1)S(1)} %get-tuple-element.30), channel_id=1, source_target_pairs={{0,16},{1,17},{2,18},{3,19},{4,20},{5,21},{6,22},{7,23},{8,24},{9,... | collective-permute-start | bytes 294920 | tf_op jit(solution)/shard_map/ppermute | solution.py:330
  72.4 3.1 %collective-permute-start.3 = (bf16[128,384]{1,0:T(8,128)(2,1)S(1)}, bf16[128,384]{1,0:T(8,128)(2,1)S(1)}, u32[]{:S(2)}, u32[]{:S(2)}) collective-permute-start(bf16[128,384]{1,0:T(8,128)(2,1)S(1)} %get-tuple-element.29), channel_id=1, source_target_pairs={{0,1},{1,0},{2,3},{3,2},{4,5},{5,4},{6,7},{7,6},{8,9},{9,8},{10,11... | collective-permute-start | bytes 294920 | tf_op jit(solution)/shard_map/ppermute | solution.py:330
  75.5 5.2 %all-to-all-done.2.given = bf16[8,8,16,384]{3,2,1,0:T(8,128)(2,1)S(1)} async-done(((bf16[8,8,16,384]{3,2,1,0:T(8,128)(2,1)}), bf16[8,8,16,384]{3,2,1,0:T(8,128)(2,1)S(1)}, u32[]{:S(2)}, u32[]{:S(2)}) %all-to-all-start.2) | async-done | bytes 786464 | tf_op jit(solution)/shard_map/all_to_all | solution.py:368
  80.7 0.0 copy-done.7
  80.7 0.6 y_inv.2
  81.3 0.0 copy-start.2
  81.3 0.0 collective-permute-done.2.below
  81.3 0.0 collective-permute-done.3.above
  81.3 29.0 %all_to_all.22.given = bf16[16,8,16,384]{3,2,1,0:T(8,128)(2,1)S(1)} all-to-all(bf16[16,8,16,384]{3,2,1,0:T(8,128)(2,1)S(1)} %y_inv.2), channel_id=1, replica_groups=mesh['px'=8,'py'=16] {'py'}, dimensions={0} | all-to-all | bytes 3145728 | tf_op jit(solution)/shard_map/all_to_all | solution.py:371
  110.3 1.8 %z_inv.2 = bf16[16,8,6144]{2,1,0:T(8,128)(2,1)} custom-call(bf16[16,8,16,384]{3,2,1,0:T(8,128)(2,1)S(1)} %all_to_all.22.given, bf16[256,256]{1,0:T(8,128)(2,1)S(1)} %copy-done.2, bf16[16,128,384]{2,1,0:T(8,128)(2,1)S(1)} %get-tuple-element.26.field, bf16[128,384]{1,0:T(8,128)(2,1)S(1)} %collective-permute-done.2.below, ...), custom_call_target="tpu_custom_call" | custom-call | tf_op jit(solution)/shard_map/z_inv/pallas_call | solution.py:372
  (9 shorter events, 0.0 us)
Async XLA Ops:
  0.0 1.4 %copy-start = (bf16[16,8,6144]{2,1,0:T(8,128)(2,1)S(1)}, bf16[16,8,6144]{2,1,0:T(8,128)(2,1)}, u32[]{:S(2)}) copy-start(bf16[16,8,6144]{2,1,0:T(8,128)(2,1)} %tok.3) | copy-start | bytes 4718596
  1.4 3.1 %copy-start.1 = (f32[27,192]{1,0:T(8,128)S(1)}, f32[27,192]{1,0:T(8,128)}, u32[]{:S(2)}) copy-start(f32[27,192]{1,0:T(8,128)} %narrow.3) | copy-start | bytes 62212
  1.8 9.3 %collective-permute-start = (bf16[16,6144]{1,0:T(8,128)(2,1)S(1)}, bf16[16,6144]{1,0:T(8,128)(2,1)S(1)}, u32[]{:S(2)}, u32[]{:S(2)}) collective-permute-start(bf16[16,6144]{1,0:T(8,128)(2,1)S(1)} %get-tuple-element.17), channel_id=1, source_target_pairs={{0,1},{1,0},{2,3},{3,2},{4,5},{5,4},{6,7},{7,6},{8,9},{9,8},{10,11... | collective-permute-start | bytes 589832 | tf_op jit(solution)/shard_map/ppermute | solution.py:330
  3.3 7.8 %copy-start.4 = (bf16[256,256]{1,0:T(8,128)(2,1)S(1)}, bf16[256,256]{1,0:T(8,128)(2,1)}, u32[]{:S(2)}) copy-start(bf16[256,256]{1,0:T(8,128)(2,1)} %constant.24.clone.z_fwd) | copy-start | bytes 393220
  3.3 7.8 %collective-permute-start.1 = (bf16[16,6144]{1,0:T(8,128)(2,1)S(1)}, bf16[16,6144]{1,0:T(8,128)(2,1)S(1)}, u32[]{:S(2)}, u32[]{:S(2)}) collective-permute-start(bf16[16,6144]{1,0:T(8,128)(2,1)S(1)} %get-tuple-element.18), channel_id=1, source_target_pairs={{0,16},{1,2},{2,1},{3,4},{4,3},{5,6},{6,5},{7,8},{8,7},{9,10},{10,... | collective-permute-start | bytes 589832 | tf_op jit(solution)/shard_map/ppermute | solution.py:330
  13.2 29.9 %copy-start.9 = (bf16[128,256]{1,0:T(8,128)(2,1)S(1)}, bf16[128,256]{1,0:T(8,128)(2,1)}, u32[]{:S(2)}) copy-start(bf16[128,256]{1,0:T(8,128)(2,1)} %constant.26.clone.y_fwd) | copy-start | bytes 196612
  43.2 20.7 %copy-start.3 = (bf16[256,144]{1,0:T(8,128)(2,1)S(1)}, bf16[256,144]{1,0:T(8,128)(2,1)}, u32[]{:S(2)}) copy-start(bf16[256,144]{1,0:T(8,128)(2,1)} %constant.28.clone.x_fwd) | copy-start | bytes 221188
  43.2 20.7 %copy-start.5 = (bf16[2,2,96,96]{3,2,1,0:T(8,128)(2,1)S(1)}, bf16[2,2,96,96]{3,2,1,0:T(8,128)(2,1)}, u32[]{:S(2)}) copy-start(bf16[2,2,96,96]{3,2,1,0:T(8,128)(2,1)} %inner_weight.1) | copy-start | bytes 221188
  43.2 20.7 %copy-start.6 = (bf16[2,2,96,96]{3,2,1,0:T(8,128)(2,1)S(1)}, bf16[2,2,96,96]{3,2,1,0:T(8,128)(2,1)}, u32[]{:S(2)}) copy-start(bf16[2,2,96,96]{3,2,1,0:T(8,128)(2,1)} %outer_weight.1) | copy-start | bytes 221188
  43.2 20.7 %copy-start.8 = (bf16[256,128]{1,0:T(8,128)(2,1)S(1)}, bf16[256,128]{1,0:T(8,128)(2,1)}, u32[]{:S(2)}) copy-start(bf16[256,128]{1,0:T(8,128)(2,1)} %constant.29.clone.x_inv) | copy-start | bytes 196612
  63.9 16.8 %copy-start.7 = (bf16[256,128]{1,0:T(8,128)(2,1)S(1)}, bf16[256,128]{1,0:T(8,128)(2,1)}, u32[]{:S(2)}) copy-start(bf16[256,128]{1,0:T(8,128)(2,1)} %constant.27.clone.y_inv) | copy-start | bytes 196612
  67.3 13.4 %all-to-all-start.2 = ((bf16[8,8,16,384]{3,2,1,0:T(8,128)(2,1)}), bf16[8,8,16,384]{3,2,1,0:T(8,128)(2,1)S(1)}, u32[]{:S(2)}, u32[]{:S(2)}) async-start(bf16[8,8,16,384]{3,2,1,0:T(8,128)(2,1)} %spec.1), calls=%async_computation.2 | async-start | bytes 1572864 | tf_op jit(solution)/shard_map/all_to_all | solution.py:368
  70.9 10.4 %collective-permute-start.2 = (bf16[128,384]{1,0:T(8,128)(2,1)S(1)}, bf16[128,384]{1,0:T(8,128)(2,1)S(1)}, u32[]{:S(2)}, u32[]{:S(2)}) collective-permute-start(bf16[128,384]{1,0:T(8,128)(2,1)S(1)} %get-tuple-element.30), channel_id=1, source_target_pairs={{0,16},{1,17},{2,18},{3,19},{4,20},{5,21},{6,22},{7,23},{8,24},{9,... | collective-permute-start | bytes 294920 | tf_op jit(solution)/shard_map/ppermute | solution.py:330
  72.4 8.9 %collective-permute-start.3 = (bf16[128,384]{1,0:T(8,128)(2,1)S(1)}, bf16[128,384]{1,0:T(8,128)(2,1)S(1)}, u32[]{:S(2)}, u32[]{:S(2)}) collective-permute-start(bf16[128,384]{1,0:T(8,128)(2,1)S(1)} %get-tuple-element.29), channel_id=1, source_target_pairs={{0,1},{1,0},{2,3},{3,2},{4,5},{5,4},{6,7},{7,6},{8,9},{9,8},{10,11... | collective-permute-start | bytes 294920 | tf_op jit(solution)/shard_map/ppermute | solution.py:330
  81.3 29.0 %copy-start.2 = (bf16[256,256]{1,0:T(8,128)(2,1)S(1)}, bf16[256,256]{1,0:T(8,128)(2,1)}, u32[]{:S(2)}) copy-start(bf16[256,256]{1,0:T(8,128)(2,1)} %constant.25.clone.z_inv) | copy-start | bytes 393220

commit v12 on v11

--- a/solution.py
+++ b/solution.py
@@ -198,8 +198,9 @@
         if xp == XP:
             to_below[...] = first
             to_above[...] = second
-        even = jnp.where(low, first, swap(second))
-        odd_z = jnp.where(low, swap(first), second)
+        crossed = swap(jnp.where(low, second, first))
+        even = jnp.where(low, first, crossed)
+        odd_z = jnp.where(low, crossed, second)
         out = dot(z_fwd[...], jnp.concatenate([even, odd_z], axis=0))
         freq[:, xp] = out.astype(BF16).reshape(KZ, 2 * LY, W)
 
@@ -286,8 +287,9 @@
         data = given[:, xp].reshape(2 * KZ * LY, W)
         value = dot(z_inv[...], data)
         even, odd = value[: ZH * LY], value[ZH * LY :]
-        first = jnp.where(low, even, swap(odd)) + field[2 * xp].astype(F32)
-        second = jnp.where(low, swap(even), odd) + field[2 * xp + 1].astype(F32)
+        crossed = swap(jnp.where(low, odd, even))
+        first = jnp.where(low, even, crossed) + field[2 * xp].astype(F32)
+        second = jnp.where(low, crossed, odd) + field[2 * xp + 1].astype(F32)
         if xp == 0:
             first = first + below
         if xp == XP - 1:

time: 112 us -> 112 us (level)
  no operation moved by 1% of the time
where the time goes in v12:
time: 112 us
  blocking collectives  79.1 us (71%)
  Pallas kernels  14.9 us (13%)
  starting transfers between devices  10.9 us (10%)
  waiting for transfers between devices  5.24 us (5%)
  local copies, waits for them, and re-layouts  1.45 us (1%)
    all_to_all x2, blocking collectives, body(): freq = lax.all_to_all(freq, 'py', 0, 0, tiled=True)  58.9 us
    all_to_all x1, blocking collectives, body(): freq = lax.all_to_all(freq, 'px', 0, 0, tiled=True)  20.2 us
    ppermute x4, starting transfers between devices, swap_pairs(): return lax.ppermute(value, ('px', 'py'), pairs)  7.33 us
    pallas_call x1, Pallas kernels, body(): call(conv_kernel, filtered, [VMEM((LX, LY, wide), F32), VMEM((27, W), F32...  6.53 us
    all_to_all x1, waiting for transfers between devices, body(): freq = lax.all_to_all(freq, 'px', 0, 0, tiled=True)  5.23 us
    all_to_all x1, starting transfers between devices, body(): freq = lax.all_to_all(freq, 'px', 0, 0, tiled=True)  3.55 us
    pallas_call x1, Pallas kernels, body(): call(spectrum_kernel, shape(PX, XP, 2 * Q // PX, W), [rows, VMEM((W // 12...  3.45 us
  transfers between devices with their start and end apart: 5, of which 1 were waited for; matrix products, arithmetic and copies ran while one was open for 0% of the time, Pallas kernels for 6%

profile of v12, /device:TPU:1, one launch (start us, length us, event | category | flops | bytes accessed | tf_op | source)
XLA Modules:
  0.0 111.7 jit_solution(12317181221242741911)
XLA Ops:
  0.0 1.4 %copy-done = bf16[16,8,6144]{2,1,0:T(8,128)(2,1)S(1)} copy-done((bf16[16,8,6144]{2,1,0:T(8,128)(2,1)S(1)}, bf16[16,8,6144]{2,1,0:T(8,128)(2,1)}, u32[]{:S(2)}) %copy-start) | copy-done | bytes 1572888
  1.4 0.3 y_rows.1
  1.8 1.5 %collective-permute-start = (bf16[16,6144]{1,0:T(8,128)(2,1)S(1)}, bf16[16,6144]{1,0:T(8,128)(2,1)S(1)}, u32[]{:S(2)}, u32[]{:S(2)}) collective-permute-start(bf16[16,6144]{1,0:T(8,128)(2,1)S(1)} %get-tuple-element.17), channel_id=1, source_target_pairs={{0,1},{1,0},{2,3},{3,2},{4,5},{5,4},{6,7},{7,6},{8,9},{9,8},{10,11... | collective-permute-start | bytes 589832 | tf_op jit(solution)/shard_map/ppermute | solution.py:332
  3.3 1.3 %collective-permute-start.1 = (bf16[16,6144]{1,0:T(8,128)(2,1)S(1)}, bf16[16,6144]{1,0:T(8,128)(2,1)S(1)}, u32[]{:S(2)}, u32[]{:S(2)}) collective-permute-start(bf16[16,6144]{1,0:T(8,128)(2,1)S(1)} %get-tuple-element.18), channel_id=1, source_target_pairs={{0,16},{1,2},{2,1},{3,4},{4,3},{5,6},{6,5},{7,8},{8,7},{9,10},{10,... | collective-permute-start | bytes 589832 | tf_op jit(solution)/shard_map/ppermute | solution.py:332
  4.5 0.0 copy-done.1
  4.5 6.5 %conv.1 = f32[48,144,128]{2,1,0:T(8,128)S(1)} custom-call(bf16[16,8,6144]{2,1,0:T(8,128)(2,1)S(1)} %copy-done, f32[27,192]{1,0:T(8,128)S(1)} %copy-done.1), custom_call_target="tpu_custom_call" | custom-call | tf_op jit(solution)/shard_map/conv/pallas_call | solution.py:342
  11.1 0.0 collective-permute-done.first
  11.1 0.0 collective-permute-done.1.second
  11.1 0.0 copy-done.4
  11.1 1.9 %edge_z.1 = (bf16[16,128,384]{2,1,0:T(8,128)(2,1)S(1)}, bf16[16,9,16,384]{3,2,1,0:T(8,128)(2,1)S(1)}, bf16[128,384]{1,0:T(8,128)(2,1)S(1)}, bf16[128,384]{1,0:T(8,128)(2,1)S(1)}) custom-call(f32[48,144,128]{2,1,0:T(8,128)S(1)} %conv.1, bf16[16,6144]{1,0:T(8,128)(2,1)S(1)} %collective-permute-done.first, bf16[16,6144]{1,0:T(8,128)(2,1)S(1)} %collective-permute-done.1.second, ...), custom_call_target="tpu_custom_call" | custom-call | tf_op jit(solution)/shard_map/edge_z/pallas_call | solution.py:352
  13.1 0.0 copy-start.9
  13.1 29.9 %all_to_all.20.given = bf16[16,9,16,384]{3,2,1,0:T(8,128)(2,1)S(1)} all-to-all(bf16[16,9,16,384]{3,2,1,0:T(8,128)(2,1)S(1)} %get-tuple-element.19), channel_id=1, replica_groups=mesh['px'=8,'py'=16] {'py'}, dimensions={0} | all-to-all | bytes 3538944 | tf_op jit(solution)/shard_map/all_to_all | solution.py:359
  43.0 0.0 copy-done.9
  43.0 0.0 copy-start.8
  43.0 0.5 y_fwd.2
  43.5 20.2 %all_to_all.21.given = bf16[8,9,16,384]{3,2,1,0:T(8,128)(2,1)S(1)} all-to-all(bf16[8,9,16,384]{3,2,1,0:T(8,128)(2,1)S(1)} %y_fwd.2), channel_id=1, replica_groups=mesh['px'=8,'py'=16] {'px'}, dimensions={0} | all-to-all | bytes 1769472 | tf_op jit(solution)/shard_map/all_to_all | solution.py:361
  63.7 0.0 copy-done.3
  63.7 0.0 copy-done.5
  63.7 0.0 copy-done.6
  63.7 0.0 copy-done.8
  63.7 0.0 copy-start.7
  63.7 3.4 %spec.1 = bf16[8,8,16,384]{3,2,1,0:T(8,128)(2,1)} custom-call(bf16[8,9,16,384]{3,2,1,0:T(8,128)(2,1)S(1)} %all_to_all.21.given, bf16[256,144]{1,0:T(8,128)(2,1)S(1)} %copy-done.3, bf16[256,128]{1,0:T(8,128)(2,1)S(1)} %copy-done.8, bf16[2,2,96,96]{3,2,1,0:T(8,128)(2,1)S(1)} %copy-done.5, bf16[2,2,96,96]{3,2,1,0:T(8,128)(2,1)S(1)} %copy-done.6), custom_call_target="tpu_custom_call" | custom-call | tf_op jit(solution)/shard_map/spec/pallas_call | solution.py:363
  67.1 3.5 %all-to-all-start.2 = ((bf16[8,8,16,384]{3,2,1,0:T(8,128)(2,1)}), bf16[8,8,16,384]{3,2,1,0:T(8,128)(2,1)S(1)}, u32[]{:S(2)}, u32[]{:S(2)}) async-start(bf16[8,8,16,384]{3,2,1,0:T(8,128)(2,1)} %spec.1), calls=%async_computation.2 | async-start | bytes 1572864 | tf_op jit(solution)/shard_map/all_to_all | solution.py:370
  70.7 1.4 %collective-permute-start.2 = (bf16[128,384]{1,0:T(8,128)(2,1)S(1)}, bf16[128,384]{1,0:T(8,128)(2,1)S(1)}, u32[]{:S(2)}, u32[]{:S(2)}) collective-permute-start(bf16[128,384]{1,0:T(8,128)(2,1)S(1)} %get-tuple-element.30), channel_id=1, source_target_pairs={{0,16},{1,17},{2,18},{3,19},{4,20},{5,21},{6,22},{7,23},{8,24},{9,... | collective-permute-start | bytes 294920 | tf_op jit(solution)/shard_map/ppermute | solution.py:332
  72.2 3.1 %collective-permute-start.3 = (bf16[128,384]{1,0:T(8,128)(2,1)S(1)}, bf16[128,384]{1,0:T(8,128)(2,1)S(1)}, u32[]{:S(2)}, u32[]{:S(2)}) collective-permute-start(bf16[128,384]{1,0:T(8,128)(2,1)S(1)} %get-tuple-element.29), channel_id=1, source_target_pairs={{0,1},{1,0},{2,3},{3,2},{4,5},{5,4},{6,7},{7,6},{8,9},{9,8},{10,11... | collective-permute-start | bytes 294920 | tf_op jit(solution)/shard_map/ppermute | solution.py:332
  75.3 5.2 %all-to-all-done.2.given = bf16[8,8,16,384]{3,2,1,0:T(8,128)(2,1)S(1)} async-done(((bf16[8,8,16,384]{3,2,1,0:T(8,128)(2,1)}), bf16[8,8,16,384]{3,2,1,0:T(8,128)(2,1)S(1)}, u32[]{:S(2)}, u32[]{:S(2)}) %all-to-all-start.2) | async-done | bytes 786464 | tf_op jit(solution)/shard_map/all_to_all | solution.py:370
  80.5 0.6 y_inv.2
  81.1 0.0 copy-start.2
  81.1 0.0 collective-permute-done.2.below
  81.1 0.0 collective-permute-done.3.above
  81.1 29.0 %all_to_all.22.given = bf16[16,8,16,384]{3,2,1,0:T(8,128)(2,1)S(1)} all-to-all(bf16[16,8,16,384]{3,2,1,0:T(8,128)(2,1)S(1)} %y_inv.2), channel_id=1, replica_groups=mesh['px'=8,'py'=16] {'py'}, dimensions={0} | all-to-all | bytes 3145728 | tf_op jit(solution)/shard_map/all_to_all | solution.py:373
  110.1 1.6 %z_inv.2 = bf16[16,8,6144]{2,1,0:T(8,128)(2,1)} custom-call(bf16[16,8,16,384]{3,2,1,0:T(8,128)(2,1)S(1)} %all_to_all.22.given, bf16[256,256]{1,0:T(8,128)(2,1)S(1)} %copy-done.2, bf16[16,128,384]{2,1,0:T(8,128)(2,1)S(1)} %get-tuple-element.26.field, bf16[128,384]{1,0:T(8,128)(2,1)S(1)} %collective-permute-done.2.below, ...), custom_call_target="tpu_custom_call" | custom-call | tf_op jit(solution)/shard_map/z_inv/pallas_call | solution.py:374
  (9 shorter events, 0.0 us)
Async XLA Ops:
  0.0 1.4 %copy-start = (bf16[16,8,6144]{2,1,0:T(8,128)(2,1)S(1)}, bf16[16,8,6144]{2,1,0:T(8,128)(2,1)}, u32[]{:S(2)}) copy-start(bf16[16,8,6144]{2,1,0:T(8,128)(2,1)} %tok.3) | copy-start | bytes 4718596
  1.4 3.1 %copy-start.1 = (f32[27,192]{1,0:T(8,128)S(1)}, f32[27,192]{1,0:T(8,128)}, u32[]{:S(2)}) copy-start(f32[27,192]{1,0:T(8,128)} %narrow.3) | copy-start | bytes 62212
  1.8 9.3 %collective-permute-start = (bf16[16,6144]{1,0:T(8,128)(2,1)S(1)}, bf16[16,6144]{1,0:T(8,128)(2,1)S(1)}, u32[]{:S(2)}, u32[]{:S(2)}) collective-permute-start(bf16[16,6144]{1,0:T(8,128)(2,1)S(1)} %get-tuple-element.17), channel_id=1, source_target_pairs={{0,1},{1,0},{2,3},{3,2},{4,5},{5,4},{6,7},{7,6},{8,9},{9,8},{10,11... | collective-permute-start | bytes 589832 | tf_op jit(solution)/shard_map/ppermute | solution.py:332
  3.3 7.8 %copy-start.4 = (bf16[256,256]{1,0:T(8,128)(2,1)S(1)}, bf16[256,256]{1,0:T(8,128)(2,1)}, u32[]{:S(2)}) copy-start(bf16[256,256]{1,0:T(8,128)(2,1)} %constant.24.clone.z_fwd) | copy-start | bytes 393220
  3.3 7.8 %collective-permute-start.1 = (bf16[16,6144]{1,0:T(8,128)(2,1)S(1)}, bf16[16,6144]{1,0:T(8,128)(2,1)S(1)}, u32[]{:S(2)}, u32[]{:S(2)}) collective-permute-start(bf16[16,6144]{1,0:T(8,128)(2,1)S(1)} %get-tuple-element.18), channel_id=1, source_target_pairs={{0,16},{1,2},{2,1},{3,4},{4,3},{5,6},{6,5},{7,8},{8,7},{9,10},{10,... | collective-permute-start | bytes 589832 | tf_op jit(solution)/shard_map/ppermute | solution.py:332
  13.1 29.9 %copy-start.9 = (bf16[128,256]{1,0:T(8,128)(2,1)S(1)}, bf16[128,256]{1,0:T(8,128)(2,1)}, u32[]{:S(2)}) copy-start(bf16[128,256]{1,0:T(8,128)(2,1)} %constant.26.clone.y_fwd) | copy-start | bytes 196612
  43.0 20.7 %copy-start.3 = (bf16[256,144]{1,0:T(8,128)(2,1)S(1)}, bf16[256,144]{1,0:T(8,128)(2,1)}, u32[]{:S(2)}) copy-start(bf16[256,144]{1,0:T(8,128)(2,1)} %constant.28.clone.x_fwd) | copy-start | bytes 221188
  43.0 20.7 %copy-start.5 = (bf16[2,2,96,96]{3,2,1,0:T(8,128)(2,1)S(1)}, bf16[2,2,96,96]{3,2,1,0:T(8,128)(2,1)}, u32[]{:S(2)}) copy-start(bf16[2,2,96,96]{3,2,1,0:T(8,128)(2,1)} %inner_weight.1) | copy-start | bytes 221188
  43.0 20.7 %copy-start.6 = (bf16[2,2,96,96]{3,2,1,0:T(8,128)(2,1)S(1)}, bf16[2,2,96,96]{3,2,1,0:T(8,128)(2,1)}, u32[]{:S(2)}) copy-start(bf16[2,2,96,96]{3,2,1,0:T(8,128)(2,1)} %outer_weight.1) | copy-start | bytes 221188
  43.0 20.7 %copy-start.8 = (bf16[256,128]{1,0:T(8,128)(2,1)S(1)}, bf16[256,128]{1,0:T(8,128)(2,1)}, u32[]{:S(2)}) copy-start(bf16[256,128]{1,0:T(8,128)(2,1)} %constant.29.clone.x_inv) | copy-start | bytes 196612
  63.7 16.8 %copy-start.7 = (bf16[256,128]{1,0:T(8,128)(2,1)S(1)}, bf16[256,128]{1,0:T(8,128)(2,1)}, u32[]{:S(2)}) copy-start(bf16[256,128]{1,0:T(8,128)(2,1)} %constant.27.clone.y_inv) | copy-start | bytes 196612
  67.1 13.4 %all-to-all-start.2 = ((bf16[8,8,16,384]{3,2,1,0:T(8,128)(2,1)}), bf16[8,8,16,384]{3,2,1,0:T(8,128)(2,1)S(1)}, u32[]{:S(2)}, u32[]{:S(2)}) async-start(bf16[8,8,16,384]{3,2,1,0:T(8,128)(2,1)} %spec.1), calls=%async_computation.2 | async-start | bytes 1572864 | tf_op jit(solution)/shard_map/all_to_all | solution.py:370
  70.7 10.4 %collective-permute-start.2 = (bf16[128,384]{1,0:T(8,128)(2,1)S(1)}, bf16[128,384]{1,0:T(8,128)(2,1)S(1)}, u32[]{:S(2)}, u32[]{:S(2)}) collective-permute-start(bf16[128,384]{1,0:T(8,128)(2,1)S(1)} %get-tuple-element.30), channel_id=1, source_target_pairs={{0,16},{1,17},{2,18},{3,19},{4,20},{5,21},{6,22},{7,23},{8,24},{9,... | collective-permute-start | bytes 294920 | tf_op jit(solution)/shard_map/ppermute | solution.py:332
  72.2 8.9 %collective-permute-start.3 = (bf16[128,384]{1,0:T(8,128)(2,1)S(1)}, bf16[128,384]{1,0:T(8,128)(2,1)S(1)}, u32[]{:S(2)}, u32[]{:S(2)}) collective-permute-start(bf16[128,384]{1,0:T(8,128)(2,1)S(1)} %get-tuple-element.29), channel_id=1, source_target_pairs={{0,1},{1,0},{2,3},{3,2},{4,5},{5,4},{6,7},{7,6},{8,9},{9,8},{10,11... | collective-permute-start | bytes 294920 | tf_op jit(solution)/shard_map/ppermute | solution.py:332
  81.1 29.0 %copy-start.2 = (bf16[256,256]{1,0:T(8,128)(2,1)S(1)}, bf16[256,256]{1,0:T(8,128)(2,1)}, u32[]{:S(2)}) copy-start(bf16[256,256]{1,0:T(8,128)(2,1)} %constant.25.clone.z_inv) | copy-start | bytes 393220

commit v13 on v12

--- a/solution.py
+++ b/solution.py
@@ -119,8 +119,13 @@
         send_second[:, here] = jnp.where(up, out[LX:], out[:LX]).astype(BF16)
 
 
-def conv_kernel(tok, narrow, out, shifted, weight):
-    weight[...] = jnp.concatenate([narrow[...], narrow[...]], axis=1)
+def conv_kernel(tok, narrow, out, shifted, mixed):
+    taps = narrow[...]
+    w0, w1, w2 = taps[:9], taps[9:18], taps[18:]
+    for p, value in enumerate((w0, (w0 + w1 + w2) * 0.5, (w0 - w1 + w2) * 0.5, w2)):
+        value = jnp.concatenate([value, value], axis=1)
+        for t in range(9):
+            mixed[p * 9 + t] = jnp.broadcast_to(value[t : t + 1], (LY, W))
     pad = jnp.zeros((LY, C), F32)
     for x in range(LX):
         shifted[x] = jnp.concatenate([pad, tok[x].astype(F32), pad], axis=1)
@@ -132,24 +137,40 @@
         after = pl.multiple_of(j * 128 + W, 128)
         here = pl.ds(at, 128)
         phase = pl.multiple_of(lax.rem(j, 3) * 128, 128)
-        wide = [jnp.broadcast_to(weight[t : t + 1, pl.ds(phase, 128)], (LY, 128)) for t in range(27)]
-        sums = {}
-        for x in range(LX + 2):
-            if x < LX:
-                mid = tok[x, :, here].astype(F32)
-                before = shifted[x, :, here]
-                behind = shifted[x, :, pl.ds(after, 128)]
-                for a in range(3):
-                    to = x + 2 - a
-                    for b in range(3):
-                        t = a * 9 + b * 3
-                        term = before * wide[t] + mid * wide[t + 1] + behind * wide[t + 2]
-                        sums[to, b] = sums[to, b] + term if (to, b) in sums else term
-            down = pltpu.roll(sums.pop((x, 0)), 1, 0)
-            up = pltpu.roll(sums.pop((x, 2)), LY - 1, 0)
-            down = jnp.where(row_at == 0, 0.0, down)
-            up = jnp.where(row_at == LY - 1, 0.0, up)
-            out[j, x * LY : (x + 1) * LY, :] = sums.pop((x, 1)) + down + up
+        phase = pl.ds(phase, 128)
+
+        def load(x):
+            if not 0 <= x < LX:
+                return None
+            return shifted[x, :, here], tok[x, :, here].astype(F32), shifted[x, :, pl.ds(after, 128)]
+
+        def combine(one, two, sign):
+            if two is None:
+                return one
+            if one is None:
+                return two if sign > 0 else tuple(-v for v in two)
+            return tuple(u + v if sign > 0 else u - v for u, v in zip(one, two))
+
+        d0, d1 = None, None
+        for i in range(0, LX + 2, 2):
+            d2, d3 = load(i), load(i + 1)
+            points = combine(d0, d2, -1), combine(d1, d2, 1), combine(d2, d1, -1), combine(d1, d3, -1)
+            d0, d1 = d2, d3
+            sides = []
+            for b in range(3):
+                m = []
+                for p, (before, mid, behind) in enumerate(points):
+                    t = p * 9 + b * 3
+                    m.append(
+                        before * mixed[t, :, phase] + mid * mixed[t + 1, :, phase] + behind * mixed[t + 2, :, phase]
+                    )
+                sides.append((m[0] + m[1] + m[2], m[1] - m[2] - m[3]))
+            for k in range(2):
+                down = pltpu.roll(sides[0][k], 1, 0)
+                up = pltpu.roll(sides[2][k], LY - 1, 0)
+                down = jnp.where(row_at == 0, 0.0, down)
+                up = jnp.where(row_at == LY - 1, 0.0, up)
+                out[j, (i + k) * LY : (i + k + 1) * LY, :] = sides[1][k] + down + up
 
 
 def edge_kernel(
@@ -236,7 +257,7 @@
 
 def spectrum_kernel(given, x_fwd, x_inv, inner_weight, outer_weight, out, rows, arrived, inner, outer):
     lay_out(inner_weight, 256, 1, inner)
-    lay_out(outer_weight, C, 2, outer)
+    lay_out(outer_weight, 256, 1, outer)
     count = Q // PX
     low = low_half(2 * PX * XP)
     wide = given[...].astype(F32).reshape(2 * count * PX * XE, W)
@@ -256,14 +277,15 @@
     hidden_r = jnp.tanh(mixed[:, 0, :, :256] - mixed[:, 1, :, 256:])
     hidden_i = jnp.tanh(mixed[:, 0, :, 256:] + mixed[:, 1, :, :256])
     hidden = jnp.stack([hidden_r, hidden_i], axis=1).astype(BF16).reshape(count * 2 * Q, 256)
-    mixed = dot(hidden, outer[...]).reshape(count, 2, Q, 2 * W)
-    filt_r = shrink(mixed[:, 0, :, :W] - mixed[:, 1, :, W:]).astype(BF16)
-    filt_i = shrink(mixed[:, 0, :, W:] + mixed[:, 1, :, :W]).astype(BF16)
+    mixed = dot(hidden, outer[...]).reshape(count, 2, Q, 512)
+    filt_r = shrink(mixed[:, 0, :, :256] - mixed[:, 1, :, 256:]).astype(BF16)
+    filt_i = shrink(mixed[:, 0, :, 256:] + mixed[:, 1, :, :256]).astype(BF16)
     filt = [jnp.concatenate([filt_r[q], filt_i[q]], axis=0) for q in range(count)]
     both = dot(x_inv[...], jnp.concatenate(filt, axis=1))
     for q in range(count):
-        part = both[:, q * W : (q + 1) * W]
-        back = jnp.where(low, part[: 2 * PX * XP], part[2 * PX * XP :])
+        part = both[:, q * 256 : (q + 1) * 256]
+        part = jnp.concatenate([part, jnp.zeros((4 * PX * XP, W - 256), F32)], axis=1)
+        back = jnp.where(low, part[: 2 * PX * XP], swap(part[2 * PX * XP :]))
         for part in range(2):
             for t in range(W // 128):
                 rows[t, pl.ds(part * count + q, PX * XP, stride=2 * count), :] = back[
@@ -342,10 +364,7 @@
     conv = call(
         conv_kernel,
         filtered,
-        [
-            VMEM((LX, LY, wide), F32),
-            VMEM((27, W), F32),
-        ],
+        [VMEM((LX, LY, wide), F32), VMEM((36, LY, W), F32)],
         name="conv",
     )(tokens, conv_weight)
     rows = [VMEM((LX, MERGED), F32)] * 2 + [VMEM((LX, wide), F32)] * 2
@@ -359,7 +378,7 @@
     freq = lax.all_to_all(freq, "py", 0, 0, tiled=True)
     freq = call(y_forward_kernel, shape(PX, XE, 2 * Q // PX, W), name="y_fwd")(freq, y_fwd)
     freq = lax.all_to_all(freq, "px", 0, 0, tiled=True)
-    mixing = [VMEM((256, 512), BF16), VMEM((256, 4 * C), BF16)]
+    mixing = [VMEM((256, 512), BF16), VMEM((256, 512), BF16)]
     freq = call(spectrum_kernel, shape(PX, XP, 2 * Q // PX, W), [rows, VMEM((W // 128, 2 * XE * Q, 128), F32)] + mixing, name="spec")(
         freq, x_fwd, x_inv, inner_weight, outer_weight
     )

time: 112 us -> 112 us (level)
  no operation moved by 1% of the time
where the time goes in v13:
time: 112 us; the launch traced here: 111 us
  blocking collectives  79.1 us (71%)
  Pallas kernels  14.4 us (13%)
  starting transfers between devices  10.9 us (10%)
  waiting for transfers between devices  5.25 us (5%)
  local copies, waits for them, and re-layouts  1.45 us (1%)
    all_to_all x2, blocking collectives, body(): freq = lax.all_to_all(freq, 'py', 0, 0, tiled=True)  58.9 us
    all_to_all x1, blocking collectives, body(): freq = lax.all_to_all(freq, 'px', 0, 0, tiled=True)  20.2 us
    ppermute x4, starting transfers between devices, swap_pairs(): return lax.ppermute(value, ('px', 'py'), pairs)  7.33 us
    pallas_call x1, Pallas kernels, body(): call(conv_kernel, filtered, [VMEM((LX, LY, wide), F32), VMEM((36, LY, W),...  6.25 us
    all_to_all x1, waiting for transfers between devices, body(): freq = lax.all_to_all(freq, 'px', 0, 0, tiled=True)  5.24 us
    all_to_all x1, starting transfers between devices, body(): freq = lax.all_to_all(freq, 'px', 0, 0, tiled=True)  3.55 us
    pallas_call x1, Pallas kernels, body(): call(spectrum_kernel, shape(PX, XP, 2 * Q // PX, W), [rows, VMEM((W // 12...  3.29 us
  transfers between devices with their start and end apart: 5, of which 1 were waited for; matrix products, arithmetic and copies ran while one was open for 0% of the time, Pallas kernels for 6%

profile of v13, /device:TPU:1, one launch (start us, length us, event | category | flops | bytes accessed | tf_op | source)
XLA Modules:
  0.0 111.2 jit_solution(8742588257782658357)
XLA Ops:
  0.0 1.4 %copy-done = bf16[16,8,6144]{2,1,0:T(8,128)(2,1)S(1)} copy-done((bf16[16,8,6144]{2,1,0:T(8,128)(2,1)S(1)}, bf16[16,8,6144]{2,1,0:T(8,128)(2,1)}, u32[]{:S(2)}) %copy-start) | copy-done | bytes 1572888
  1.4 0.3 y_rows.1
  1.8 1.5 %collective-permute-start = (bf16[16,6144]{1,0:T(8,128)(2,1)S(1)}, bf16[16,6144]{1,0:T(8,128)(2,1)S(1)}, u32[]{:S(2)}, u32[]{:S(2)}) collective-permute-start(bf16[16,6144]{1,0:T(8,128)(2,1)S(1)} %get-tuple-element.17), channel_id=1, source_target_pairs={{0,1},{1,0},{2,3},{3,2},{4,5},{5,4},{6,7},{7,6},{8,9},{9,8},{10,11... | collective-permute-start | bytes 589832 | tf_op jit(solution)/shard_map/ppermute | solution.py:354
  3.3 1.3 %collective-permute-start.1 = (bf16[16,6144]{1,0:T(8,128)(2,1)S(1)}, bf16[16,6144]{1,0:T(8,128)(2,1)S(1)}, u32[]{:S(2)}, u32[]{:S(2)}) collective-permute-start(bf16[16,6144]{1,0:T(8,128)(2,1)S(1)} %get-tuple-element.18), channel_id=1, source_target_pairs={{0,16},{1,2},{2,1},{3,4},{4,3},{5,6},{6,5},{7,8},{8,7},{9,10},{10,... | collective-permute-start | bytes 589832 | tf_op jit(solution)/shard_map/ppermute | solution.py:354
  4.5 0.0 copy-done.1
  4.5 6.2 %conv.1 = f32[48,144,128]{2,1,0:T(8,128)S(1)} custom-call(bf16[16,8,6144]{2,1,0:T(8,128)(2,1)S(1)} %copy-done, f32[27,192]{1,0:T(8,128)S(1)} %copy-done.1), custom_call_target="tpu_custom_call" | custom-call | tf_op jit(solution)/shard_map/conv/pallas_call | solution.py:364
  10.8 0.0 collective-permute-done.first
  10.8 0.0 collective-permute-done.1.second
  10.8 0.0 copy-done.4
  10.8 1.9 %edge_z.1 = (bf16[16,128,384]{2,1,0:T(8,128)(2,1)S(1)}, bf16[16,9,16,384]{3,2,1,0:T(8,128)(2,1)S(1)}, bf16[128,384]{1,0:T(8,128)(2,1)S(1)}, bf16[128,384]{1,0:T(8,128)(2,1)S(1)}) custom-call(f32[48,144,128]{2,1,0:T(8,128)S(1)} %conv.1, bf16[16,6144]{1,0:T(8,128)(2,1)S(1)} %collective-permute-done.first, bf16[16,6144]{1,0:T(8,128)(2,1)S(1)} %collective-permute-done.1.second, ...), custom_call_target="tpu_custom_call" | custom-call | tf_op jit(solution)/shard_map/edge_z/pallas_call | solution.py:371
  12.8 0.0 copy-start.9
  12.8 29.9 %all_to_all.20.given = bf16[16,9,16,384]{3,2,1,0:T(8,128)(2,1)S(1)} all-to-all(bf16[16,9,16,384]{3,2,1,0:T(8,128)(2,1)S(1)} %get-tuple-element.19), channel_id=1, replica_groups=mesh['px'=8,'py'=16] {'py'}, dimensions={0} | all-to-all | bytes 3538944 | tf_op jit(solution)/shard_map/all_to_all | solution.py:378
  42.7 0.0 copy-done.9
  42.7 0.0 copy-start.8
  42.7 0.5 y_fwd.2
  43.2 20.2 %all_to_all.21.given = bf16[8,9,16,384]{3,2,1,0:T(8,128)(2,1)S(1)} all-to-all(bf16[8,9,16,384]{3,2,1,0:T(8,128)(2,1)S(1)} %y_fwd.2), channel_id=1, replica_groups=mesh['px'=8,'py'=16] {'px'}, dimensions={0} | all-to-all | bytes 1769472 | tf_op jit(solution)/shard_map/all_to_all | solution.py:380
  63.4 0.0 copy-done.3
  63.4 0.0 copy-done.5
  63.4 0.0 copy-done.6
  63.4 0.0 copy-done.8
  63.4 0.0 copy-start.7
  63.4 3.3 %spec.1 = bf16[8,8,16,384]{3,2,1,0:T(8,128)(2,1)} custom-call(bf16[8,9,16,384]{3,2,1,0:T(8,128)(2,1)S(1)} %all_to_all.21.given, bf16[256,144]{1,0:T(8,128)(2,1)S(1)} %copy-done.3, bf16[256,128]{1,0:T(8,128)(2,1)S(1)} %copy-done.8, bf16[2,2,96,96]{3,2,1,0:T(8,128)(2,1)S(1)} %copy-done.5, bf16[2,2,96,96]{3,2,1,0:T(8,128)(2,1)S(1)} %copy-done.6), custom_call_target="tpu_custom_call" | custom-call | tf_op jit(solution)/shard_map/spec/pallas_call | solution.py:382
  66.7 3.5 %all-to-all-start.2 = ((bf16[8,8,16,384]{3,2,1,0:T(8,128)(2,1)}), bf16[8,8,16,384]{3,2,1,0:T(8,128)(2,1)S(1)}, u32[]{:S(2)}, u32[]{:S(2)}) async-start(bf16[8,8,16,384]{3,2,1,0:T(8,128)(2,1)} %spec.1), calls=%async_computation.2 | async-start | bytes 1572864 | tf_op jit(solution)/shard_map/all_to_all | solution.py:389
  70.3 1.4 %collective-permute-start.2 = (bf16[128,384]{1,0:T(8,128)(2,1)S(1)}, bf16[128,384]{1,0:T(8,128)(2,1)S(1)}, u32[]{:S(2)}, u32[]{:S(2)}) collective-permute-start(bf16[128,384]{1,0:T(8,128)(2,1)S(1)} %get-tuple-element.30), channel_id=1, source_target_pairs={{0,16},{1,17},{2,18},{3,19},{4,20},{5,21},{6,22},{7,23},{8,24},{9,... | collective-permute-start | bytes 294920 | tf_op jit(solution)/shard_map/ppermute | solution.py:354
  71.7 3.1 %collective-permute-start.3 = (bf16[128,384]{1,0:T(8,128)(2,1)S(1)}, bf16[128,384]{1,0:T(8,128)(2,1)S(1)}, u32[]{:S(2)}, u32[]{:S(2)}) collective-permute-start(bf16[128,384]{1,0:T(8,128)(2,1)S(1)} %get-tuple-element.29), channel_id=1, source_target_pairs={{0,1},{1,0},{2,3},{3,2},{4,5},{5,4},{6,7},{7,6},{8,9},{9,8},{10,11... | collective-permute-start | bytes 294920 | tf_op jit(solution)/shard_map/ppermute | solution.py:354
  74.8 5.2 %all-to-all-done.2.given = bf16[8,8,16,384]{3,2,1,0:T(8,128)(2,1)S(1)} async-done(((bf16[8,8,16,384]{3,2,1,0:T(8,128)(2,1)}), bf16[8,8,16,384]{3,2,1,0:T(8,128)(2,1)S(1)}, u32[]{:S(2)}, u32[]{:S(2)}) %all-to-all-start.2) | async-done | bytes 786464 | tf_op jit(solution)/shard_map/all_to_all | solution.py:389
  80.1 0.6 y_inv.2
  80.6 0.0 copy-start.2
  80.7 0.0 collective-permute-done.2.below
  80.7 0.0 collective-permute-done.3.above
  80.7 29.0 %all_to_all.22.given = bf16[16,8,16,384]{3,2,1,0:T(8,128)(2,1)S(1)} all-to-all(bf16[16,8,16,384]{3,2,1,0:T(8,128)(2,1)S(1)} %y_inv.2), channel_id=1, replica_groups=mesh['px'=8,'py'=16] {'py'}, dimensions={0} | all-to-all | bytes 3145728 | tf_op jit(solution)/shard_map/all_to_all | solution.py:392
  109.7 1.6 %z_inv.2 = bf16[16,8,6144]{2,1,0:T(8,128)(2,1)} custom-call(bf16[16,8,16,384]{3,2,1,0:T(8,128)(2,1)S(1)} %all_to_all.22.given, bf16[256,256]{1,0:T(8,128)(2,1)S(1)} %copy-done.2, bf16[16,128,384]{2,1,0:T(8,128)(2,1)S(1)} %get-tuple-element.26.field, bf16[128,384]{1,0:T(8,128)(2,1)S(1)} %collective-permute-done.2.below, ...), custom_call_target="tpu_custom_call" | custom-call | tf_op jit(solution)/shard_map/z_inv/pallas_call | solution.py:393
  (9 shorter events, 0.0 us)
Async XLA Ops:
  0.0 1.4 %copy-start = (bf16[16,8,6144]{2,1,0:T(8,128)(2,1)S(1)}, bf16[16,8,6144]{2,1,0:T(8,128)(2,1)}, u32[]{:S(2)}) copy-start(bf16[16,8,6144]{2,1,0:T(8,128)(2,1)} %tok.3) | copy-start | bytes 4718596
  1.4 3.1 %copy-start.1 = (f32[27,192]{1,0:T(8,128)S(1)}, f32[27,192]{1,0:T(8,128)}, u32[]{:S(2)}) copy-start(f32[27,192]{1,0:T(8,128)} %narrow.3) | copy-start | bytes 62212
  1.8 9.0 %collective-permute-start = (bf16[16,6144]{1,0:T(8,128)(2,1)S(1)}, bf16[16,6144]{1,0:T(8,128)(2,1)S(1)}, u32[]{:S(2)}, u32[]{:S(2)}) collective-permute-start(bf16[16,6144]{1,0:T(8,128)(2,1)S(1)} %get-tuple-element.17), channel_id=1, source_target_pairs={{0,1},{1,0},{2,3},{3,2},{4,5},{5,4},{6,7},{7,6},{8,9},{9,8},{10,11... | collective-permute-start | bytes 589832 | tf_op jit(solution)/shard_map/ppermute | solution.py:354
  3.3 7.6 %copy-start.4 = (bf16[256,256]{1,0:T(8,128)(2,1)S(1)}, bf16[256,256]{1,0:T(8,128)(2,1)}, u32[]{:S(2)}) copy-start(bf16[256,256]{1,0:T(8,128)(2,1)} %constant.24.clone.z_fwd) | copy-start | bytes 393220
  3.3 7.6 %collective-permute-start.1 = (bf16[16,6144]{1,0:T(8,128)(2,1)S(1)}, bf16[16,6144]{1,0:T(8,128)(2,1)S(1)}, u32[]{:S(2)}, u32[]{:S(2)}) collective-permute-start(bf16[16,6144]{1,0:T(8,128)(2,1)S(1)} %get-tuple-element.18), channel_id=1, source_target_pairs={{0,16},{1,2},{2,1},{3,4},{4,3},{5,6},{6,5},{7,8},{8,7},{9,10},{10,... | collective-permute-start | bytes 589832 | tf_op jit(solution)/shard_map/ppermute | solution.py:354
  12.8 29.9 %copy-start.9 = (bf16[128,256]{1,0:T(8,128)(2,1)S(1)}, bf16[128,256]{1,0:T(8,128)(2,1)}, u32[]{:S(2)}) copy-start(bf16[128,256]{1,0:T(8,128)(2,1)} %constant.26.clone.y_fwd) | copy-start | bytes 196612
  42.7 20.7 %copy-start.3 = (bf16[256,144]{1,0:T(8,128)(2,1)S(1)}, bf16[256,144]{1,0:T(8,128)(2,1)}, u32[]{:S(2)}) copy-start(bf16[256,144]{1,0:T(8,128)(2,1)} %constant.28.clone.x_fwd) | copy-start | bytes 221188
  42.7 20.7 %copy-start.5 = (bf16[2,2,96,96]{3,2,1,0:T(8,128)(2,1)S(1)}, bf16[2,2,96,96]{3,2,1,0:T(8,128)(2,1)}, u32[]{:S(2)}) copy-start(bf16[2,2,96,96]{3,2,1,0:T(8,128)(2,1)} %inner_weight.1) | copy-start | bytes 221188
  42.7 20.7 %copy-start.6 = (bf16[2,2,96,96]{3,2,1,0:T(8,128)(2,1)S(1)}, bf16[2,2,96,96]{3,2,1,0:T(8,128)(2,1)}, u32[]{:S(2)}) copy-start(bf16[2,2,96,96]{3,2,1,0:T(8,128)(2,1)} %outer_weight.1) | copy-start | bytes 221188
  42.7 20.7 %copy-start.8 = (bf16[256,128]{1,0:T(8,128)(2,1)S(1)}, bf16[256,128]{1,0:T(8,128)(2,1)}, u32[]{:S(2)}) copy-start(bf16[256,128]{1,0:T(8,128)(2,1)} %constant.29.clone.x_inv) | copy-start | bytes 196612
  63.4 16.7 %copy-start.7 = (bf16[256,128]{1,0:T(8,128)(2,1)S(1)}, bf16[256,128]{1,0:T(8,128)(2,1)}, u32[]{:S(2)}) copy-start(bf16[256,128]{1,0:T(8,128)(2,1)} %constant.27.clone.y_inv) | copy-start | bytes 196612
  66.7 13.4 %all-to-all-start.2 = ((bf16[8,8,16,384]{3,2,1,0:T(8,128)(2,1)}), bf16[8,8,16,384]{3,2,1,0:T(8,128)(2,1)S(1)}, u32[]{:S(2)}, u32[]{:S(2)}) async-start(bf16[8,8,16,384]{3,2,1,0:T(8,128)(2,1)} %spec.1), calls=%async_computation.2 | async-start | bytes 1572864 | tf_op jit(solution)/shard_map/all_to_all | solution.py:389
  70.3 10.4 %collective-permute-start.2 = (bf16[128,384]{1,0:T(8,128)(2,1)S(1)}, bf16[128,384]{1,0:T(8,128)(2,1)S(1)}, u32[]{:S(2)}, u32[]{:S(2)}) collective-permute-start(bf16[128,384]{1,0:T(8,128)(2,1)S(1)} %get-tuple-element.30), channel_id=1, source_target_pairs={{0,16},{1,17},{2,18},{3,19},{4,20},{5,21},{6,22},{7,23},{8,24},{9,... | collective-permute-start | bytes 294920 | tf_op jit(solution)/shard_map/ppermute | solution.py:354
  71.7 8.9 %collective-permute-start.3 = (bf16[128,384]{1,0:T(8,128)(2,1)S(1)}, bf16[128,384]{1,0:T(8,128)(2,1)S(1)}, u32[]{:S(2)}, u32[]{:S(2)}) collective-permute-start(bf16[128,384]{1,0:T(8,128)(2,1)S(1)} %get-tuple-element.29), channel_id=1, source_target_pairs={{0,1},{1,0},{2,3},{3,2},{4,5},{5,4},{6,7},{7,6},{8,9},{9,8},{10,11... | collective-permute-start | bytes 294920 | tf_op jit(solution)/shard_map/ppermute | solution.py:354
  80.6 29.0 %copy-start.2 = (bf16[256,256]{1,0:T(8,128)(2,1)S(1)}, bf16[256,256]{1,0:T(8,128)(2,1)}, u32[]{:S(2)}) copy-start(bf16[256,256]{1,0:T(8,128)(2,1)} %constant.25.clone.z_inv) | copy-start | bytes 393220

commit v14 on v13

--- a/solution.py
+++ b/solution.py
@@ -75,7 +75,7 @@
     extra[..., 1:, 0, 0] = x_fwd[..., LX - 1 : n - LX : LX]
     extra[..., :-1, 0, 1] = x_fwd[..., LX::LX]
     x_fwd = np.concatenate([x_fwd.reshape(2, Q, 2, PX, XP, 2), extra], axis=4)
-    x_fwd = x_fwd.transpose(5, 0, 1, 3, 4, 2).reshape(4 * Q, 2 * PX * XE)
+    x_fwd = x_fwd.transpose(0, 1, 5, 3, 4, 2).reshape(2 * Q, 4 * PX * XE)
     x_inv = backward(cx, sx).reshape(2, PX, XP, 2, 2, Q)
     x_inv = x_inv.transpose(3, 0, 1, 2, 4, 5).reshape(4 * PX * XP, 2 * Q)
     return [as_bf16(m) for m in (z_fwd, z_inv, y_fwd, y_inv, x_fwd, x_inv)]
@@ -131,7 +131,7 @@
         shifted[x] = jnp.concatenate([pad, tok[x].astype(F32), pad], axis=1)
     row_at = lax.broadcasted_iota(jnp.int32, (LY, 128), 0)
 
-    @pl.loop(0, MERGED // 128, unroll=6)
+    @pl.loop(0, MERGED // 128, unroll=12)
     def _(j):
         at = pl.multiple_of(j * 128, 128)
         after = pl.multiple_of(j * 128 + W, 128)
@@ -266,13 +266,10 @@
     data = []
     for q in range(count):
         some = [arrived[t, pl.ds(q, 2 * PX * XE, stride=count), :] for t in range(W // 128)]
-        data.append(jnp.concatenate(some, axis=1).astype(BF16))
+        both = jnp.concatenate(some, axis=1).astype(BF16)
+        data.append(jnp.concatenate([both[:, :256], swap(both)[:, :256]], axis=0))
     both = dot(x_fwd[...], jnp.concatenate(data, axis=1))
-    spec = []
-    for q in range(count):
-        part = both[:, q * W : (q + 1) * W]
-        part = part[: 2 * Q] + swap(part[2 * Q :])
-        spec.append(part[:, :256].astype(BF16))
+    spec = [both[:, q * 256 : (q + 1) * 256].astype(BF16) for q in range(count)]
     mixed = dot(jnp.concatenate(spec, axis=0), inner[...]).reshape(count, 2, Q, 512)
     hidden_r = jnp.tanh(mixed[:, 0, :, :256] - mixed[:, 1, :, 256:])
     hidden_i = jnp.tanh(mixed[:, 0, :, 256:] + mixed[:, 1, :, :256])

time: 112 us -> 112 us (level)
  no operation moved by 1% of the time
where the time goes in v14:
time: 112 us; the launch traced here: 111 us
  blocking collectives  79.1 us (71%)
  Pallas kernels  14.4 us (13%)
  starting transfers between devices  10.9 us (10%)
  waiting for transfers between devices  5.24 us (5%)
  local copies, waits for them, and re-layouts  1.45 us (1%)
    all_to_all x2, blocking collectives, body(): freq = lax.all_to_all(freq, 'py', 0, 0, tiled=True)  58.9 us
    all_to_all x1, blocking collectives, body(): freq = lax.all_to_all(freq, 'px', 0, 0, tiled=True)  20.2 us
    ppermute x4, starting transfers between devices, swap_pairs(): return lax.ppermute(value, ('px', 'py'), pairs)  7.34 us
    pallas_call x1, Pallas kernels, body(): call(conv_kernel, filtered, [VMEM((LX, LY, wide), F32), VMEM((36, LY, W),...  6.22 us
    all_to_all x1, waiting for transfers between devices, body(): freq = lax.all_to_all(freq, 'px', 0, 0, tiled=True)  5.23 us
    all_to_all x1, starting transfers between devices, body(): freq = lax.all_to_all(freq, 'px', 0, 0, tiled=True)  3.55 us
    pallas_call x1, Pallas kernels, body(): call(spectrum_kernel, shape(PX, XP, 2 * Q // PX, W), [rows, VMEM((W // 12...  3.3 us
  transfers between devices with their start and end apart: 5, of which 1 were waited for; matrix products, arithmetic and copies ran while one was open for 0% of the time, Pallas kernels for 6%

profile of v14, /device:TPU:1, one launch (start us, length us, event | category | flops | bytes accessed | tf_op | source)
XLA Modules:
  0.0 111.2 jit_solution(14139121437420402194)
XLA Ops:
  0.0 1.4 %copy-done = bf16[16,8,6144]{2,1,0:T(8,128)(2,1)S(1)} copy-done((bf16[16,8,6144]{2,1,0:T(8,128)(2,1)S(1)}, bf16[16,8,6144]{2,1,0:T(8,128)(2,1)}, u32[]{:S(2)}) %copy-start) | copy-done | bytes 1572888
  1.4 0.3 y_rows.1
  1.8 1.5 %collective-permute-start = (bf16[16,6144]{1,0:T(8,128)(2,1)S(1)}, bf16[16,6144]{1,0:T(8,128)(2,1)S(1)}, u32[]{:S(2)}, u32[]{:S(2)}) collective-permute-start(bf16[16,6144]{1,0:T(8,128)(2,1)S(1)} %get-tuple-element.17), channel_id=1, source_target_pairs={{0,1},{1,0},{2,3},{3,2},{4,5},{5,4},{6,7},{7,6},{8,9},{9,8},{10,11... | collective-permute-start | bytes 589832 | tf_op jit(solution)/shard_map/ppermute | solution.py:351
  3.3 1.3 %collective-permute-start.1 = (bf16[16,6144]{1,0:T(8,128)(2,1)S(1)}, bf16[16,6144]{1,0:T(8,128)(2,1)S(1)}, u32[]{:S(2)}, u32[]{:S(2)}) collective-permute-start(bf16[16,6144]{1,0:T(8,128)(2,1)S(1)} %get-tuple-element.18), channel_id=1, source_target_pairs={{0,16},{1,2},{2,1},{3,4},{4,3},{5,6},{6,5},{7,8},{8,7},{9,10},{10,... | collective-permute-start | bytes 589832 | tf_op jit(solution)/shard_map/ppermute | solution.py:351
  4.5 0.0 copy-done.1
  4.5 6.2 %conv.1 = f32[48,144,128]{2,1,0:T(8,128)S(1)} custom-call(bf16[16,8,6144]{2,1,0:T(8,128)(2,1)S(1)} %copy-done, f32[27,192]{1,0:T(8,128)S(1)} %copy-done.1), custom_call_target="tpu_custom_call" | custom-call | tf_op jit(solution)/shard_map/conv/pallas_call | solution.py:361
  10.8 0.0 collective-permute-done.first
  10.8 0.0 collective-permute-done.1.second
  10.8 0.0 copy-done.3
  10.8 1.9 %edge_z.1 = (bf16[16,128,384]{2,1,0:T(8,128)(2,1)S(1)}, bf16[16,9,16,384]{3,2,1,0:T(8,128)(2,1)S(1)}, bf16[128,384]{1,0:T(8,128)(2,1)S(1)}, bf16[128,384]{1,0:T(8,128)(2,1)S(1)}) custom-call(f32[48,144,128]{2,1,0:T(8,128)S(1)} %conv.1, bf16[16,6144]{1,0:T(8,128)(2,1)S(1)} %collective-permute-done.first, bf16[16,6144]{1,0:T(8,128)(2,1)S(1)} %collective-permute-done.1.second, ...), custom_call_target="tpu_custom_call" | custom-call | tf_op jit(solution)/shard_map/edge_z/pallas_call | solution.py:368
  12.8 0.0 copy-start.9
  12.8 29.9 %all_to_all.20.given = bf16[16,9,16,384]{3,2,1,0:T(8,128)(2,1)S(1)} all-to-all(bf16[16,9,16,384]{3,2,1,0:T(8,128)(2,1)S(1)} %get-tuple-element.19), channel_id=1, replica_groups=mesh['px'=8,'py'=16] {'py'}, dimensions={0} | all-to-all | bytes 3538944 | tf_op jit(solution)/shard_map/all_to_all | solution.py:375
  42.7 0.0 copy-done.9
  42.7 0.0 copy-start.8
  42.7 0.5 y_fwd.2
  43.2 20.2 %all_to_all.21.given = bf16[8,9,16,384]{3,2,1,0:T(8,128)(2,1)S(1)} all-to-all(bf16[8,9,16,384]{3,2,1,0:T(8,128)(2,1)S(1)} %y_fwd.2), channel_id=1, replica_groups=mesh['px'=8,'py'=16] {'px'}, dimensions={0} | all-to-all | bytes 1769472 | tf_op jit(solution)/shard_map/all_to_all | solution.py:377
  63.3 0.0 copy-done.4
  63.4 0.0 copy-done.5
  63.4 0.0 copy-done.6
  63.4 0.0 copy-start.7
  63.4 3.3 %spec.1 = bf16[8,8,16,384]{3,2,1,0:T(8,128)(2,1)} custom-call(bf16[8,9,16,384]{3,2,1,0:T(8,128)(2,1)S(1)} %all_to_all.21.given, bf16[128,288]{1,0:T(8,128)(2,1)S(1)} %copy-done.6, bf16[256,128]{1,0:T(8,128)(2,1)S(1)} %copy-done.8, bf16[2,2,96,96]{3,2,1,0:T(8,128)(2,1)S(1)} %copy-done.4, bf16[2,2,96,96]{3,2,1,0:T(8,128)(2,1)S(1)} %copy-done.5), custom_call_target="tpu_custom_call" | custom-call | tf_op jit(solution)/shard_map/spec/pallas_call | solution.py:379
  66.7 3.5 %all-to-all-start.2 = ((bf16[8,8,16,384]{3,2,1,0:T(8,128)(2,1)}), bf16[8,8,16,384]{3,2,1,0:T(8,128)(2,1)S(1)}, u32[]{:S(2)}, u32[]{:S(2)}) async-start(bf16[8,8,16,384]{3,2,1,0:T(8,128)(2,1)} %spec.1), calls=%async_computation.2 | async-start | bytes 1572864 | tf_op jit(solution)/shard_map/all_to_all | solution.py:386
  70.3 1.4 %collective-permute-start.2 = (bf16[128,384]{1,0:T(8,128)(2,1)S(1)}, bf16[128,384]{1,0:T(8,128)(2,1)S(1)}, u32[]{:S(2)}, u32[]{:S(2)}) collective-permute-start(bf16[128,384]{1,0:T(8,128)(2,1)S(1)} %get-tuple-element.30), channel_id=1, source_target_pairs={{0,16},{1,17},{2,18},{3,19},{4,20},{5,21},{6,22},{7,23},{8,24},{9,... | collective-permute-start | bytes 294920 | tf_op jit(solution)/shard_map/ppermute | solution.py:351
  71.7 3.1 %collective-permute-start.3 = (bf16[128,384]{1,0:T(8,128)(2,1)S(1)}, bf16[128,384]{1,0:T(8,128)(2,1)S(1)}, u32[]{:S(2)}, u32[]{:S(2)}) collective-permute-start(bf16[128,384]{1,0:T(8,128)(2,1)S(1)} %get-tuple-element.29), channel_id=1, source_target_pairs={{0,1},{1,0},{2,3},{3,2},{4,5},{5,4},{6,7},{7,6},{8,9},{9,8},{10,11... | collective-permute-start | bytes 294920 | tf_op jit(solution)/shard_map/ppermute | solution.py:351
  74.8 5.2 %all-to-all-done.2.given = bf16[8,8,16,384]{3,2,1,0:T(8,128)(2,1)S(1)} async-done(((bf16[8,8,16,384]{3,2,1,0:T(8,128)(2,1)}), bf16[8,8,16,384]{3,2,1,0:T(8,128)(2,1)S(1)}, u32[]{:S(2)}, u32[]{:S(2)}) %all-to-all-start.2) | async-done | bytes 786464 | tf_op jit(solution)/shard_map/all_to_all | solution.py:386
  80.1 0.6 y_inv.2
  80.6 0.0 copy-start.2
  80.6 0.0 collective-permute-done.2.below
  80.6 0.0 collective-permute-done.3.above
  80.7 29.0 %all_to_all.22.given = bf16[16,8,16,384]{3,2,1,0:T(8,128)(2,1)S(1)} all-to-all(bf16[16,8,16,384]{3,2,1,0:T(8,128)(2,1)S(1)} %y_inv.2), channel_id=1, replica_groups=mesh['px'=8,'py'=16] {'py'}, dimensions={0} | all-to-all | bytes 3145728 | tf_op jit(solution)/shard_map/all_to_all | solution.py:389
  109.6 0.0 copy-done.2
  109.6 1.6 %z_inv.2 = bf16[16,8,6144]{2,1,0:T(8,128)(2,1)} custom-call(bf16[16,8,16,384]{3,2,1,0:T(8,128)(2,1)S(1)} %all_to_all.22.given, bf16[256,256]{1,0:T(8,128)(2,1)S(1)} %copy-done.2, bf16[16,128,384]{2,1,0:T(8,128)(2,1)S(1)} %get-tuple-element.26.field, bf16[128,384]{1,0:T(8,128)(2,1)S(1)} %collective-permute-done.2.below, ...), custom_call_target="tpu_custom_call" | custom-call | tf_op jit(solution)/shard_map/z_inv/pallas_call | solution.py:390
  (9 shorter events, 0.0 us)
Async XLA Ops:
  0.0 1.4 %copy-start = (bf16[16,8,6144]{2,1,0:T(8,128)(2,1)S(1)}, bf16[16,8,6144]{2,1,0:T(8,128)(2,1)}, u32[]{:S(2)}) copy-start(bf16[16,8,6144]{2,1,0:T(8,128)(2,1)} %tok.3) | copy-start | bytes 4718596
  1.4 3.1 %copy-start.1 = (f32[27,192]{1,0:T(8,128)S(1)}, f32[27,192]{1,0:T(8,128)}, u32[]{:S(2)}) copy-start(f32[27,192]{1,0:T(8,128)} %narrow.3) | copy-start | bytes 62212
  1.8 9.0 %collective-permute-start = (bf16[16,6144]{1,0:T(8,128)(2,1)S(1)}, bf16[16,6144]{1,0:T(8,128)(2,1)S(1)}, u32[]{:S(2)}, u32[]{:S(2)}) collective-permute-start(bf16[16,6144]{1,0:T(8,128)(2,1)S(1)} %get-tuple-element.17), channel_id=1, source_target_pairs={{0,1},{1,0},{2,3},{3,2},{4,5},{5,4},{6,7},{7,6},{8,9},{9,8},{10,11... | collective-permute-start | bytes 589832 | tf_op jit(solution)/shard_map/ppermute | solution.py:351
  3.3 7.5 %copy-start.3 = (bf16[256,256]{1,0:T(8,128)(2,1)S(1)}, bf16[256,256]{1,0:T(8,128)(2,1)}, u32[]{:S(2)}) copy-start(bf16[256,256]{1,0:T(8,128)(2,1)} %constant.24.clone.z_fwd) | copy-start | bytes 393220
  3.3 7.5 %collective-permute-start.1 = (bf16[16,6144]{1,0:T(8,128)(2,1)S(1)}, bf16[16,6144]{1,0:T(8,128)(2,1)S(1)}, u32[]{:S(2)}, u32[]{:S(2)}) collective-permute-start(bf16[16,6144]{1,0:T(8,128)(2,1)S(1)} %get-tuple-element.18), channel_id=1, source_target_pairs={{0,16},{1,2},{2,1},{3,4},{4,3},{5,6},{6,5},{7,8},{8,7},{9,10},{10,... | collective-permute-start | bytes 589832 | tf_op jit(solution)/shard_map/ppermute | solution.py:351
  12.8 29.9 %copy-start.9 = (bf16[128,256]{1,0:T(8,128)(2,1)S(1)}, bf16[128,256]{1,0:T(8,128)(2,1)}, u32[]{:S(2)}) copy-start(bf16[128,256]{1,0:T(8,128)(2,1)} %constant.26.clone.y_fwd) | copy-start | bytes 196612
  42.7 20.7 %copy-start.4 = (bf16[2,2,96,96]{3,2,1,0:T(8,128)(2,1)S(1)}, bf16[2,2,96,96]{3,2,1,0:T(8,128)(2,1)}, u32[]{:S(2)}) copy-start(bf16[2,2,96,96]{3,2,1,0:T(8,128)(2,1)} %inner_weight.1) | copy-start | bytes 221188
  42.7 20.7 %copy-start.5 = (bf16[2,2,96,96]{3,2,1,0:T(8,128)(2,1)S(1)}, bf16[2,2,96,96]{3,2,1,0:T(8,128)(2,1)}, u32[]{:S(2)}) copy-start(bf16[2,2,96,96]{3,2,1,0:T(8,128)(2,1)} %outer_weight.1) | copy-start | bytes 221188
  42.7 20.7 %copy-start.6 = (bf16[128,288]{1,0:T(8,128)(2,1)S(1)}, bf16[128,288]{1,0:T(8,128)(2,1)}, u32[]{:S(2)}) copy-start(bf16[128,288]{1,0:T(8,128)(2,1)} %constant.28.clone.x_fwd) | copy-start | bytes 221188
  42.7 20.7 %copy-start.8 = (bf16[256,128]{1,0:T(8,128)(2,1)S(1)}, bf16[256,128]{1,0:T(8,128)(2,1)}, u32[]{:S(2)}) copy-start(bf16[256,128]{1,0:T(8,128)(2,1)} %constant.29.clone.x_inv) | copy-start | bytes 196612
  63.4 16.7 %copy-start.7 = (bf16[256,128]{1,0:T(8,128)(2,1)S(1)}, bf16[256,128]{1,0:T(8,128)(2,1)}, u32[]{:S(2)}) copy-start(bf16[256,128]{1,0:T(8,128)(2,1)} %constant.27.clone.y_inv) | copy-start | bytes 196612
  66.7 13.4 %all-to-all-start.2 = ((bf16[8,8,16,384]{3,2,1,0:T(8,128)(2,1)}), bf16[8,8,16,384]{3,2,1,0:T(8,128)(2,1)S(1)}, u32[]{:S(2)}, u32[]{:S(2)}) async-start(bf16[8,8,16,384]{3,2,1,0:T(8,128)(2,1)} %spec.1), calls=%async_computation.2 | async-start | bytes 1572864 | tf_op jit(solution)/shard_map/all_to_all | solution.py:386
  70.3 10.4 %collective-permute-start.2 = (bf16[128,384]{1,0:T(8,128)(2,1)S(1)}, bf16[128,384]{1,0:T(8,128)(2,1)S(1)}, u32[]{:S(2)}, u32[]{:S(2)}) collective-permute-start(bf16[128,384]{1,0:T(8,128)(2,1)S(1)} %get-tuple-element.30), channel_id=1, source_target_pairs={{0,16},{1,17},{2,18},{3,19},{4,20},{5,21},{6,22},{7,23},{8,24},{9,... | collective-permute-start | bytes 294920 | tf_op jit(solution)/shard_map/ppermute | solution.py:351
  71.7 8.9 %collective-permute-start.3 = (bf16[128,384]{1,0:T(8,128)(2,1)S(1)}, bf16[128,384]{1,0:T(8,128)(2,1)S(1)}, u32[]{:S(2)}, u32[]{:S(2)}) collective-permute-start(bf16[128,384]{1,0:T(8,128)(2,1)S(1)} %get-tuple-element.29), channel_id=1, source_target_pairs={{0,1},{1,0},{2,3},{3,2},{4,5},{5,4},{6,7},{7,6},{8,9},{9,8},{10,11... | collective-permute-start | bytes 294920 | tf_op jit(solution)/shard_map/ppermute | solution.py:351
  80.6 29.0 %copy-start.2 = (bf16[256,256]{1,0:T(8,128)(2,1)S(1)}, bf16[256,256]{1,0:T(8,128)(2,1)}, u32[]{:S(2)}) copy-start(bf16[256,256]{1,0:T(8,128)(2,1)} %constant.25.clone.z_inv) | copy-start | bytes 393220

commit v15 on v14

--- a/solution.py
+++ b/solution.py
@@ -227,9 +227,10 @@
 
 
 def y_forward_kernel(given, y_fwd, out):
+    data = [given[:, xp].reshape(2 * PY * LY, W) for xp in range(XE)]
+    value = dot(y_fwd[...], jnp.concatenate(data, axis=1)).astype(BF16)
     for xp in range(XE):
-        data = given[:, xp].reshape(2 * PY * LY, W)
-        out[:, xp] = dot(y_fwd[...], data).astype(BF16).reshape(PX, 2 * Q // PX, W)
+        out[:, xp] = value[:, xp * W : (xp + 1) * W].reshape(PX, 2 * Q // PX, W)
 
 
 def gather(rows, out):
@@ -292,9 +293,10 @@
 
 
 def y_inverse_kernel(given, y_inv, out):
+    data = [given[:, xp].reshape(2 * Q, W) for xp in range(XP)]
+    value = dot(y_inv[...], jnp.concatenate(data, axis=1)).astype(BF16)
     for xp in range(XP):
-        data = given[:, xp].reshape(2 * Q, W)
-        out[:, xp] = dot(y_inv[...], data).astype(BF16).reshape(PY, 2 * LY, W)
+        out[:, xp] = value[:, xp * W : (xp + 1) * W].reshape(PY, 2 * LY, W)
 
 
 def z_inverse_kernel(given, z_inv, field, below, above, out_hbm, out, sems):

time: 112 us -> 112 us (level)
  no operation moved by 1% of the time
where the time goes in v15:
time: 112 us; the launch traced here: 111 us
  blocking collectives  79.1 us (71%)
  Pallas kernels  14.4 us (13%)
  starting transfers between devices  10.9 us (10%)
  waiting for transfers between devices  5.24 us (5%)
  local copies, waits for them, and re-layouts  1.45 us (1%)
    all_to_all x2, blocking collectives, body(): freq = lax.all_to_all(freq, 'py', 0, 0, tiled=True)  58.9 us
    all_to_all x1, blocking collectives, body(): freq = lax.all_to_all(freq, 'px', 0, 0, tiled=True)  20.2 us
    ppermute x4, starting transfers between devices, swap_pairs(): return lax.ppermute(value, ('px', 'py'), pairs)  7.33 us
    pallas_call x1, Pallas kernels, body(): call(conv_kernel, filtered, [VMEM((LX, LY, wide), F32), VMEM((36, LY, W),...  6.22 us
    all_to_all x1, waiting for transfers between devices, body(): freq = lax.all_to_all(freq, 'px', 0, 0, tiled=True)  5.23 us
    all_to_all x1, starting transfers between devices, body(): freq = lax.all_to_all(freq, 'px', 0, 0, tiled=True)  3.55 us
    pallas_call x1, Pallas kernels, body(): call(spectrum_kernel, shape(PX, XP, 2 * Q // PX, W), [rows, VMEM((W // 12...  3.3 us
  transfers between devices with their start and end apart: 5, of which 1 were waited for; matrix products, arithmetic and copies ran while one was open for 0% of the time, Pallas kernels for 6%

profile of v15, /device:TPU:1, one launch (start us, length us, event | category | flops | bytes accessed | tf_op | source)
XLA Modules:
  0.0 111.2 jit_solution(16013974158074556894)
XLA Ops:
  0.0 1.4 %copy-done = bf16[16,8,6144]{2,1,0:T(8,128)(2,1)S(1)} copy-done((bf16[16,8,6144]{2,1,0:T(8,128)(2,1)S(1)}, bf16[16,8,6144]{2,1,0:T(8,128)(2,1)}, u32[]{:S(2)}) %copy-start) | copy-done | bytes 1572888
  1.4 0.3 y_rows.1
  1.8 1.5 %collective-permute-start = (bf16[16,6144]{1,0:T(8,128)(2,1)S(1)}, bf16[16,6144]{1,0:T(8,128)(2,1)S(1)}, u32[]{:S(2)}, u32[]{:S(2)}) collective-permute-start(bf16[16,6144]{1,0:T(8,128)(2,1)S(1)} %get-tuple-element.17), channel_id=1, source_target_pairs={{0,1},{1,0},{2,3},{3,2},{4,5},{5,4},{6,7},{7,6},{8,9},{9,8},{10,11... | collective-permute-start | bytes 589832 | tf_op jit(solution)/shard_map/ppermute | solution.py:353
  3.3 1.3 %collective-permute-start.1 = (bf16[16,6144]{1,0:T(8,128)(2,1)S(1)}, bf16[16,6144]{1,0:T(8,128)(2,1)S(1)}, u32[]{:S(2)}, u32[]{:S(2)}) collective-permute-start(bf16[16,6144]{1,0:T(8,128)(2,1)S(1)} %get-tuple-element.18), channel_id=1, source_target_pairs={{0,16},{1,2},{2,1},{3,4},{4,3},{5,6},{6,5},{7,8},{8,7},{9,10},{10,... | collective-permute-start | bytes 589832 | tf_op jit(solution)/shard_map/ppermute | solution.py:353
  4.5 0.0 copy-done.1
  4.5 6.2 %conv.1 = f32[48,144,128]{2,1,0:T(8,128)S(1)} custom-call(bf16[16,8,6144]{2,1,0:T(8,128)(2,1)S(1)} %copy-done, f32[27,192]{1,0:T(8,128)S(1)} %copy-done.1), custom_call_target="tpu_custom_call" | custom-call | tf_op jit(solution)/shard_map/conv/pallas_call | solution.py:363
  10.8 0.0 collective-permute-done.first
  10.8 0.0 collective-permute-done.1.second
  10.8 0.0 copy-done.3
  10.8 1.9 %edge_z.1 = (bf16[16,128,384]{2,1,0:T(8,128)(2,1)S(1)}, bf16[16,9,16,384]{3,2,1,0:T(8,128)(2,1)S(1)}, bf16[128,384]{1,0:T(8,128)(2,1)S(1)}, bf16[128,384]{1,0:T(8,128)(2,1)S(1)}) custom-call(f32[48,144,128]{2,1,0:T(8,128)S(1)} %conv.1, bf16[16,6144]{1,0:T(8,128)(2,1)S(1)} %collective-permute-done.first, bf16[16,6144]{1,0:T(8,128)(2,1)S(1)} %collective-permute-done.1.second, ...), custom_call_target="tpu_custom_call" | custom-call | tf_op jit(solution)/shard_map/edge_z/pallas_call | solution.py:370
  12.8 0.0 copy-start.9
  12.8 29.9 %all_to_all.20.given = bf16[16,9,16,384]{3,2,1,0:T(8,128)(2,1)S(1)} all-to-all(bf16[16,9,16,384]{3,2,1,0:T(8,128)(2,1)S(1)} %get-tuple-element.19), channel_id=1, replica_groups=mesh['px'=8,'py'=16] {'py'}, dimensions={0} | all-to-all | bytes 3538944 | tf_op jit(solution)/shard_map/all_to_all | solution.py:377
  42.7 0.0 copy-done.9
  42.7 0.0 copy-start.8
  42.7 0.4 y_fwd.2
  43.1 20.2 %all_to_all.21.given = bf16[8,9,16,384]{3,2,1,0:T(8,128)(2,1)S(1)} all-to-all(bf16[8,9,16,384]{3,2,1,0:T(8,128)(2,1)S(1)} %y_fwd.2), channel_id=1, replica_groups=mesh['px'=8,'py'=16] {'px'}, dimensions={0} | all-to-all | bytes 1769472 | tf_op jit(solution)/shard_map/all_to_all | solution.py:379
  63.3 0.0 copy-done.4
  63.3 0.0 copy-done.5
  63.3 0.0 copy-start.7
  63.3 3.3 %spec.1 = bf16[8,8,16,384]{3,2,1,0:T(8,128)(2,1)} custom-call(bf16[8,9,16,384]{3,2,1,0:T(8,128)(2,1)S(1)} %all_to_all.21.given, bf16[128,288]{1,0:T(8,128)(2,1)S(1)} %copy-done.6, bf16[256,128]{1,0:T(8,128)(2,1)S(1)} %copy-done.8, bf16[2,2,96,96]{3,2,1,0:T(8,128)(2,1)S(1)} %copy-done.4, bf16[2,2,96,96]{3,2,1,0:T(8,128)(2,1)S(1)} %copy-done.5), custom_call_target="tpu_custom_call" | custom-call | tf_op jit(solution)/shard_map/spec/pallas_call | solution.py:381
  66.6 3.5 %all-to-all-start.2 = ((bf16[8,8,16,384]{3,2,1,0:T(8,128)(2,1)}), bf16[8,8,16,384]{3,2,1,0:T(8,128)(2,1)S(1)}, u32[]{:S(2)}, u32[]{:S(2)}) async-start(bf16[8,8,16,384]{3,2,1,0:T(8,128)(2,1)} %spec.1), calls=%async_computation.2 | async-start | bytes 1572864 | tf_op jit(solution)/shard_map/all_to_all | solution.py:388
  70.2 1.4 %collective-permute-start.2 = (bf16[128,384]{1,0:T(8,128)(2,1)S(1)}, bf16[128,384]{1,0:T(8,128)(2,1)S(1)}, u32[]{:S(2)}, u32[]{:S(2)}) collective-permute-start(bf16[128,384]{1,0:T(8,128)(2,1)S(1)} %get-tuple-element.30), channel_id=1, source_target_pairs={{0,16},{1,17},{2,18},{3,19},{4,20},{5,21},{6,22},{7,23},{8,24},{9,... | collective-permute-start | bytes 294920 | tf_op jit(solution)/shard_map/ppermute | solution.py:353
  71.7 3.1 %collective-permute-start.3 = (bf16[128,384]{1,0:T(8,128)(2,1)S(1)}, bf16[128,384]{1,0:T(8,128)(2,1)S(1)}, u32[]{:S(2)}, u32[]{:S(2)}) collective-permute-start(bf16[128,384]{1,0:T(8,128)(2,1)S(1)} %get-tuple-element.29), channel_id=1, source_target_pairs={{0,1},{1,0},{2,3},{3,2},{4,5},{5,4},{6,7},{7,6},{8,9},{9,8},{10,11... | collective-permute-start | bytes 294920 | tf_op jit(solution)/shard_map/ppermute | solution.py:353
  74.8 5.2 %all-to-all-done.2.given = bf16[8,8,16,384]{3,2,1,0:T(8,128)(2,1)S(1)} async-done(((bf16[8,8,16,384]{3,2,1,0:T(8,128)(2,1)}), bf16[8,8,16,384]{3,2,1,0:T(8,128)(2,1)S(1)}, u32[]{:S(2)}, u32[]{:S(2)}) %all-to-all-start.2) | async-done | bytes 786464 | tf_op jit(solution)/shard_map/all_to_all | solution.py:388
  80.0 0.0 copy-done.7
  80.0 0.6 y_inv.2
  80.6 0.0 copy-start.2
  80.6 0.0 collective-permute-done.2.below
  80.6 0.0 collective-permute-done.3.above
  80.6 29.0 %all_to_all.22.given = bf16[16,8,16,384]{3,2,1,0:T(8,128)(2,1)S(1)} all-to-all(bf16[16,8,16,384]{3,2,1,0:T(8,128)(2,1)S(1)} %y_inv.2), channel_id=1, replica_groups=mesh['px'=8,'py'=16] {'py'}, dimensions={0} | all-to-all | bytes 3145728 | tf_op jit(solution)/shard_map/all_to_all | solution.py:391
  109.6 0.0 copy-done.2
  109.6 1.6 %z_inv.2 = bf16[16,8,6144]{2,1,0:T(8,128)(2,1)} custom-call(bf16[16,8,16,384]{3,2,1,0:T(8,128)(2,1)S(1)} %all_to_all.22.given, bf16[256,256]{1,0:T(8,128)(2,1)S(1)} %copy-done.2, bf16[16,128,384]{2,1,0:T(8,128)(2,1)S(1)} %get-tuple-element.26.field, bf16[128,384]{1,0:T(8,128)(2,1)S(1)} %collective-permute-done.2.below, ...), custom_call_target="tpu_custom_call" | custom-call | tf_op jit(solution)/shard_map/z_inv/pallas_call | solution.py:392
  (9 shorter events, 0.0 us)
Async XLA Ops:
  0.0 1.4 %copy-start = (bf16[16,8,6144]{2,1,0:T(8,128)(2,1)S(1)}, bf16[16,8,6144]{2,1,0:T(8,128)(2,1)}, u32[]{:S(2)}) copy-start(bf16[16,8,6144]{2,1,0:T(8,128)(2,1)} %tok.3) | copy-start | bytes 4718596
  1.4 3.1 %copy-start.1 = (f32[27,192]{1,0:T(8,128)S(1)}, f32[27,192]{1,0:T(8,128)}, u32[]{:S(2)}) copy-start(f32[27,192]{1,0:T(8,128)} %narrow.3) | copy-start | bytes 62212
  1.8 9.0 %collective-permute-start = (bf16[16,6144]{1,0:T(8,128)(2,1)S(1)}, bf16[16,6144]{1,0:T(8,128)(2,1)S(1)}, u32[]{:S(2)}, u32[]{:S(2)}) collective-permute-start(bf16[16,6144]{1,0:T(8,128)(2,1)S(1)} %get-tuple-element.17), channel_id=1, source_target_pairs={{0,1},{1,0},{2,3},{3,2},{4,5},{5,4},{6,7},{7,6},{8,9},{9,8},{10,11... | collective-permute-start | bytes 589832 | tf_op jit(solution)/shard_map/ppermute | solution.py:353
  3.3 7.5 %copy-start.3 = (bf16[256,256]{1,0:T(8,128)(2,1)S(1)}, bf16[256,256]{1,0:T(8,128)(2,1)}, u32[]{:S(2)}) copy-start(bf16[256,256]{1,0:T(8,128)(2,1)} %constant.24.clone.z_fwd) | copy-start | bytes 393220
  3.3 7.5 %collective-permute-start.1 = (bf16[16,6144]{1,0:T(8,128)(2,1)S(1)}, bf16[16,6144]{1,0:T(8,128)(2,1)S(1)}, u32[]{:S(2)}, u32[]{:S(2)}) collective-permute-start(bf16[16,6144]{1,0:T(8,128)(2,1)S(1)} %get-tuple-element.18), channel_id=1, source_target_pairs={{0,16},{1,2},{2,1},{3,4},{4,3},{5,6},{6,5},{7,8},{8,7},{9,10},{10,... | collective-permute-start | bytes 589832 | tf_op jit(solution)/shard_map/ppermute | solution.py:353
  12.8 29.9 %copy-start.9 = (bf16[128,256]{1,0:T(8,128)(2,1)S(1)}, bf16[128,256]{1,0:T(8,128)(2,1)}, u32[]{:S(2)}) copy-start(bf16[128,256]{1,0:T(8,128)(2,1)} %constant.26.clone.y_fwd) | copy-start | bytes 196612
  42.7 20.6 %copy-start.4 = (bf16[2,2,96,96]{3,2,1,0:T(8,128)(2,1)S(1)}, bf16[2,2,96,96]{3,2,1,0:T(8,128)(2,1)}, u32[]{:S(2)}) copy-start(bf16[2,2,96,96]{3,2,1,0:T(8,128)(2,1)} %inner_weight.1) | copy-start | bytes 221188
  42.7 20.6 %copy-start.5 = (bf16[2,2,96,96]{3,2,1,0:T(8,128)(2,1)S(1)}, bf16[2,2,96,96]{3,2,1,0:T(8,128)(2,1)}, u32[]{:S(2)}) copy-start(bf16[2,2,96,96]{3,2,1,0:T(8,128)(2,1)} %outer_weight.1) | copy-start | bytes 221188
  42.7 20.6 %copy-start.6 = (bf16[128,288]{1,0:T(8,128)(2,1)S(1)}, bf16[128,288]{1,0:T(8,128)(2,1)}, u32[]{:S(2)}) copy-start(bf16[128,288]{1,0:T(8,128)(2,1)} %constant.28.clone.x_fwd) | copy-start | bytes 221188
  42.7 20.6 %copy-start.8 = (bf16[256,128]{1,0:T(8,128)(2,1)S(1)}, bf16[256,128]{1,0:T(8,128)(2,1)}, u32[]{:S(2)}) copy-start(bf16[256,128]{1,0:T(8,128)(2,1)} %constant.29.clone.x_inv) | copy-start | bytes 196612
  63.3 16.7 %copy-start.7 = (bf16[256,128]{1,0:T(8,128)(2,1)S(1)}, bf16[256,128]{1,0:T(8,128)(2,1)}, u32[]{:S(2)}) copy-start(bf16[256,128]{1,0:T(8,128)(2,1)} %constant.27.clone.y_inv) | copy-start | bytes 196612
  66.6 13.4 %all-to-all-start.2 = ((bf16[8,8,16,384]{3,2,1,0:T(8,128)(2,1)}), bf16[8,8,16,384]{3,2,1,0:T(8,128)(2,1)S(1)}, u32[]{:S(2)}, u32[]{:S(2)}) async-start(bf16[8,8,16,384]{3,2,1,0:T(8,128)(2,1)} %spec.1), calls=%async_computation.2 | async-start | bytes 1572864 | tf_op jit(solution)/shard_map/all_to_all | solution.py:388
  70.2 10.4 %collective-permute-start.2 = (bf16[128,384]{1,0:T(8,128)(2,1)S(1)}, bf16[128,384]{1,0:T(8,128)(2,1)S(1)}, u32[]{:S(2)}, u32[]{:S(2)}) collective-permute-start(bf16[128,384]{1,0:T(8,128)(2,1)S(1)} %get-tuple-element.30), channel_id=1, source_target_pairs={{0,16},{1,17},{2,18},{3,19},{4,20},{5,21},{6,22},{7,23},{8,24},{9,... | collective-permute-start | bytes 294920 | tf_op jit(solution)/shard_map/ppermute | solution.py:353
  71.7 8.9 %collective-permute-start.3 = (bf16[128,384]{1,0:T(8,128)(2,1)S(1)}, bf16[128,384]{1,0:T(8,128)(2,1)S(1)}, u32[]{:S(2)}, u32[]{:S(2)}) collective-permute-start(bf16[128,384]{1,0:T(8,128)(2,1)S(1)} %get-tuple-element.29), channel_id=1, source_target_pairs={{0,1},{1,0},{2,3},{3,2},{4,5},{5,4},{6,7},{7,6},{8,9},{9,8},{10,11... | collective-permute-start | bytes 294920 | tf_op jit(solution)/shard_map/ppermute | solution.py:353
  80.6 29.0 %copy-start.2 = (bf16[256,256]{1,0:T(8,128)(2,1)S(1)}, bf16[256,256]{1,0:T(8,128)(2,1)}, u32[]{:S(2)}) copy-start(bf16[256,256]{1,0:T(8,128)(2,1)} %constant.25.clone.z_inv) | copy-start | bytes 393220

commit v16 on v14

--- a/solution.py
+++ b/solution.py
@@ -303,8 +303,10 @@
     copies = []
     for xp in range(XP):
         here = pl.ds(2 * xp, 2)
-        data = given[:, xp].reshape(2 * KZ * LY, W)
-        value = dot(z_inv[...], data)
+        if xp % 2 == 0:
+            data = [given[:, i].reshape(2 * KZ * LY, W) for i in (xp, xp + 1)]
+            both = dot(z_inv[...], jnp.concatenate(data, axis=1))
+        value = both[:, xp % 2 * W : (xp % 2 + 1) * W]
         even, odd = value[: ZH * LY], value[ZH * LY :]
         crossed = swap(jnp.where(low, odd, even))
         first = jnp.where(low, even, crossed) + field[2 * xp].astype(F32)

time: 112 us -> 112 us (level)
  no operation moved by 1% of the time
where the time goes in v16:
time: 112 us; the launch traced here: 111 us
  blocking collectives  79.1 us (71%)
  Pallas kernels  14.4 us (13%)
  starting transfers between devices  10.9 us (10%)
  waiting for transfers between devices  5.24 us (5%)
  local copies, waits for them, and re-layouts  1.45 us (1%)
    all_to_all x2, blocking collectives, body(): freq = lax.all_to_all(freq, 'py', 0, 0, tiled=True)  58.9 us
    all_to_all x1, blocking collectives, body(): freq = lax.all_to_all(freq, 'px', 0, 0, tiled=True)  20.2 us
    ppermute x4, starting transfers between devices, swap_pairs(): return lax.ppermute(value, ('px', 'py'), pairs)  7.34 us
    pallas_call x1, Pallas kernels, body(): call(conv_kernel, filtered, [VMEM((LX, LY, wide), F32), VMEM((36, LY, W),...  6.22 us
    all_to_all x1, waiting for transfers between devices, body(): freq = lax.all_to_all(freq, 'px', 0, 0, tiled=True)  5.23 us
    all_to_all x1, starting transfers between devices, body(): freq = lax.all_to_all(freq, 'px', 0, 0, tiled=True)  3.55 us
    pallas_call x1, Pallas kernels, body(): call(spectrum_kernel, shape(PX, XP, 2 * Q // PX, W), [rows, VMEM((W // 12...  3.3 us
  transfers between devices with their start and end apart: 5, of which 1 were waited for; matrix products, arithmetic and copies ran while one was open for 0% of the time, Pallas kernels for 6%

profile of v16, /device:TPU:1, one launch (start us, length us, event | category | flops | bytes accessed | tf_op | source)
XLA Modules:
  0.0 111.3 jit_solution(5819112982044604823)
XLA Ops:
  0.0 1.4 %copy-done = bf16[16,8,6144]{2,1,0:T(8,128)(2,1)S(1)} copy-done((bf16[16,8,6144]{2,1,0:T(8,128)(2,1)S(1)}, bf16[16,8,6144]{2,1,0:T(8,128)(2,1)}, u32[]{:S(2)}) %copy-start) | copy-done | bytes 1572888
  1.4 0.3 y_rows.1
  1.8 1.5 %collective-permute-start = (bf16[16,6144]{1,0:T(8,128)(2,1)S(1)}, bf16[16,6144]{1,0:T(8,128)(2,1)S(1)}, u32[]{:S(2)}, u32[]{:S(2)}) collective-permute-start(bf16[16,6144]{1,0:T(8,128)(2,1)S(1)} %get-tuple-element.17), channel_id=1, source_target_pairs={{0,1},{1,0},{2,3},{3,2},{4,5},{5,4},{6,7},{7,6},{8,9},{9,8},{10,11... | collective-permute-start | bytes 589832 | tf_op jit(solution)/shard_map/ppermute | solution.py:353
  3.3 1.3 %collective-permute-start.1 = (bf16[16,6144]{1,0:T(8,128)(2,1)S(1)}, bf16[16,6144]{1,0:T(8,128)(2,1)S(1)}, u32[]{:S(2)}, u32[]{:S(2)}) collective-permute-start(bf16[16,6144]{1,0:T(8,128)(2,1)S(1)} %get-tuple-element.18), channel_id=1, source_target_pairs={{0,16},{1,2},{2,1},{3,4},{4,3},{5,6},{6,5},{7,8},{8,7},{9,10},{10,... | collective-permute-start | bytes 589832 | tf_op jit(solution)/shard_map/ppermute | solution.py:353
  4.5 0.0 copy-done.1
  4.5 6.2 %conv.1 = f32[48,144,128]{2,1,0:T(8,128)S(1)} custom-call(bf16[16,8,6144]{2,1,0:T(8,128)(2,1)S(1)} %copy-done, f32[27,192]{1,0:T(8,128)S(1)} %copy-done.1), custom_call_target="tpu_custom_call" | custom-call | tf_op jit(solution)/shard_map/conv/pallas_call | solution.py:363
  10.8 0.0 collective-permute-done.first
  10.8 0.0 collective-permute-done.1.second
  10.8 0.0 copy-done.3
  10.8 1.9 %edge_z.1 = (bf16[16,128,384]{2,1,0:T(8,128)(2,1)S(1)}, bf16[16,9,16,384]{3,2,1,0:T(8,128)(2,1)S(1)}, bf16[128,384]{1,0:T(8,128)(2,1)S(1)}, bf16[128,384]{1,0:T(8,128)(2,1)S(1)}) custom-call(f32[48,144,128]{2,1,0:T(8,128)S(1)} %conv.1, bf16[16,6144]{1,0:T(8,128)(2,1)S(1)} %collective-permute-done.first, bf16[16,6144]{1,0:T(8,128)(2,1)S(1)} %collective-permute-done.1.second, ...), custom_call_target="tpu_custom_call" | custom-call | tf_op jit(solution)/shard_map/edge_z/pallas_call | solution.py:370
  12.8 0.0 copy-start.9
  12.8 29.9 %all_to_all.20.given = bf16[16,9,16,384]{3,2,1,0:T(8,128)(2,1)S(1)} all-to-all(bf16[16,9,16,384]{3,2,1,0:T(8,128)(2,1)S(1)} %get-tuple-element.19), channel_id=1, replica_groups=mesh['px'=8,'py'=16] {'py'}, dimensions={0} | all-to-all | bytes 3538944 | tf_op jit(solution)/shard_map/all_to_all | solution.py:377
  42.7 0.0 copy-done.9
  42.7 0.0 copy-start.8
  42.7 0.5 y_fwd.2
  43.2 20.2 %all_to_all.21.given = bf16[8,9,16,384]{3,2,1,0:T(8,128)(2,1)S(1)} all-to-all(bf16[8,9,16,384]{3,2,1,0:T(8,128)(2,1)S(1)} %y_fwd.2), channel_id=1, replica_groups=mesh['px'=8,'py'=16] {'px'}, dimensions={0} | all-to-all | bytes 1769472 | tf_op jit(solution)/shard_map/all_to_all | solution.py:379
  63.3 0.0 copy-done.4
  63.4 0.0 copy-done.5
  63.4 0.0 copy-done.6
  63.4 0.0 copy-start.7
  63.4 3.3 %spec.1 = bf16[8,8,16,384]{3,2,1,0:T(8,128)(2,1)} custom-call(bf16[8,9,16,384]{3,2,1,0:T(8,128)(2,1)S(1)} %all_to_all.21.given, bf16[128,288]{1,0:T(8,128)(2,1)S(1)} %copy-done.6, bf16[256,128]{1,0:T(8,128)(2,1)S(1)} %copy-done.8, bf16[2,2,96,96]{3,2,1,0:T(8,128)(2,1)S(1)} %copy-done.4, bf16[2,2,96,96]{3,2,1,0:T(8,128)(2,1)S(1)} %copy-done.5), custom_call_target="tpu_custom_call" | custom-call | tf_op jit(solution)/shard_map/spec/pallas_call | solution.py:381
  66.7 3.5 %all-to-all-start.2 = ((bf16[8,8,16,384]{3,2,1,0:T(8,128)(2,1)}), bf16[8,8,16,384]{3,2,1,0:T(8,128)(2,1)S(1)}, u32[]{:S(2)}, u32[]{:S(2)}) async-start(bf16[8,8,16,384]{3,2,1,0:T(8,128)(2,1)} %spec.1), calls=%async_computation.2 | async-start | bytes 1572864 | tf_op jit(solution)/shard_map/all_to_all | solution.py:388
  70.3 1.4 %collective-permute-start.2 = (bf16[128,384]{1,0:T(8,128)(2,1)S(1)}, bf16[128,384]{1,0:T(8,128)(2,1)S(1)}, u32[]{:S(2)}, u32[]{:S(2)}) collective-permute-start(bf16[128,384]{1,0:T(8,128)(2,1)S(1)} %get-tuple-element.30), channel_id=1, source_target_pairs={{0,16},{1,17},{2,18},{3,19},{4,20},{5,21},{6,22},{7,23},{8,24},{9,... | collective-permute-start | bytes 294920 | tf_op jit(solution)/shard_map/ppermute | solution.py:353
  71.7 3.1 %collective-permute-start.3 = (bf16[128,384]{1,0:T(8,128)(2,1)S(1)}, bf16[128,384]{1,0:T(8,128)(2,1)S(1)}, u32[]{:S(2)}, u32[]{:S(2)}) collective-permute-start(bf16[128,384]{1,0:T(8,128)(2,1)S(1)} %get-tuple-element.29), channel_id=1, source_target_pairs={{0,1},{1,0},{2,3},{3,2},{4,5},{5,4},{6,7},{7,6},{8,9},{9,8},{10,11... | collective-permute-start | bytes 294920 | tf_op jit(solution)/shard_map/ppermute | solution.py:353
  74.8 5.2 %all-to-all-done.2.given = bf16[8,8,16,384]{3,2,1,0:T(8,128)(2,1)S(1)} async-done(((bf16[8,8,16,384]{3,2,1,0:T(8,128)(2,1)}), bf16[8,8,16,384]{3,2,1,0:T(8,128)(2,1)S(1)}, u32[]{:S(2)}, u32[]{:S(2)}) %all-to-all-start.2) | async-done | bytes 786464 | tf_op jit(solution)/shard_map/all_to_all | solution.py:388
  80.1 0.6 y_inv.2
  80.6 0.0 copy-start.2
  80.6 0.0 collective-permute-done.2.below
  80.6 0.0 collective-permute-done.3.above
  80.7 29.0 %all_to_all.22.given = bf16[16,8,16,384]{3,2,1,0:T(8,128)(2,1)S(1)} all-to-all(bf16[16,8,16,384]{3,2,1,0:T(8,128)(2,1)S(1)} %y_inv.2), channel_id=1, replica_groups=mesh['px'=8,'py'=16] {'py'}, dimensions={0} | all-to-all | bytes 3145728 | tf_op jit(solution)/shard_map/all_to_all | solution.py:391
  109.6 0.0 copy-done.2
  109.6 1.6 %z_inv.2 = bf16[16,8,6144]{2,1,0:T(8,128)(2,1)} custom-call(bf16[16,8,16,384]{3,2,1,0:T(8,128)(2,1)S(1)} %all_to_all.22.given, bf16[256,256]{1,0:T(8,128)(2,1)S(1)} %copy-done.2, bf16[16,128,384]{2,1,0:T(8,128)(2,1)S(1)} %get-tuple-element.26.field, bf16[128,384]{1,0:T(8,128)(2,1)S(1)} %collective-permute-done.2.below, ...), custom_call_target="tpu_custom_call" | custom-call | tf_op jit(solution)/shard_map/z_inv/pallas_call | solution.py:392
  (9 shorter events, 0.0 us)
Async XLA Ops:
  0.0 1.4 %copy-start = (bf16[16,8,6144]{2,1,0:T(8,128)(2,1)S(1)}, bf16[16,8,6144]{2,1,0:T(8,128)(2,1)}, u32[]{:S(2)}) copy-start(bf16[16,8,6144]{2,1,0:T(8,128)(2,1)} %tok.3) | copy-start | bytes 4718596
  1.4 3.1 %copy-start.1 = (f32[27,192]{1,0:T(8,128)S(1)}, f32[27,192]{1,0:T(8,128)}, u32[]{:S(2)}) copy-start(f32[27,192]{1,0:T(8,128)} %narrow.3) | copy-start | bytes 62212
  1.8 9.0 %collective-permute-start = (bf16[16,6144]{1,0:T(8,128)(2,1)S(1)}, bf16[16,6144]{1,0:T(8,128)(2,1)S(1)}, u32[]{:S(2)}, u32[]{:S(2)}) collective-permute-start(bf16[16,6144]{1,0:T(8,128)(2,1)S(1)} %get-tuple-element.17), channel_id=1, source_target_pairs={{0,1},{1,0},{2,3},{3,2},{4,5},{5,4},{6,7},{7,6},{8,9},{9,8},{10,11... | collective-permute-start | bytes 589832 | tf_op jit(solution)/shard_map/ppermute | solution.py:353
  3.3 7.5 %copy-start.3 = (bf16[256,256]{1,0:T(8,128)(2,1)S(1)}, bf16[256,256]{1,0:T(8,128)(2,1)}, u32[]{:S(2)}) copy-start(bf16[256,256]{1,0:T(8,128)(2,1)} %constant.24.clone.z_fwd) | copy-start | bytes 393220
  3.3 7.5 %collective-permute-start.1 = (bf16[16,6144]{1,0:T(8,128)(2,1)S(1)}, bf16[16,6144]{1,0:T(8,128)(2,1)S(1)}, u32[]{:S(2)}, u32[]{:S(2)}) collective-permute-start(bf16[16,6144]{1,0:T(8,128)(2,1)S(1)} %get-tuple-element.18), channel_id=1, source_target_pairs={{0,16},{1,2},{2,1},{3,4},{4,3},{5,6},{6,5},{7,8},{8,7},{9,10},{10,... | collective-permute-start | bytes 589832 | tf_op jit(solution)/shard_map/ppermute | solution.py:353
  12.8 29.9 %copy-start.9 = (bf16[128,256]{1,0:T(8,128)(2,1)S(1)}, bf16[128,256]{1,0:T(8,128)(2,1)}, u32[]{:S(2)}) copy-start(bf16[128,256]{1,0:T(8,128)(2,1)} %constant.26.clone.y_fwd) | copy-start | bytes 196612
  42.7 20.7 %copy-start.4 = (bf16[2,2,96,96]{3,2,1,0:T(8,128)(2,1)S(1)}, bf16[2,2,96,96]{3,2,1,0:T(8,128)(2,1)}, u32[]{:S(2)}) copy-start(bf16[2,2,96,96]{3,2,1,0:T(8,128)(2,1)} %inner_weight.1) | copy-start | bytes 221188
  42.7 20.7 %copy-start.5 = (bf16[2,2,96,96]{3,2,1,0:T(8,128)(2,1)S(1)}, bf16[2,2,96,96]{3,2,1,0:T(8,128)(2,1)}, u32[]{:S(2)}) copy-start(bf16[2,2,96,96]{3,2,1,0:T(8,128)(2,1)} %outer_weight.1) | copy-start | bytes 221188
  42.7 20.7 %copy-start.6 = (bf16[128,288]{1,0:T(8,128)(2,1)S(1)}, bf16[128,288]{1,0:T(8,128)(2,1)}, u32[]{:S(2)}) copy-start(bf16[128,288]{1,0:T(8,128)(2,1)} %constant.28.clone.x_fwd) | copy-start | bytes 221188
  42.7 20.7 %copy-start.8 = (bf16[256,128]{1,0:T(8,128)(2,1)S(1)}, bf16[256,128]{1,0:T(8,128)(2,1)}, u32[]{:S(2)}) copy-start(bf16[256,128]{1,0:T(8,128)(2,1)} %constant.29.clone.x_inv) | copy-start | bytes 196612
  63.4 16.7 %copy-start.7 = (bf16[256,128]{1,0:T(8,128)(2,1)S(1)}, bf16[256,128]{1,0:T(8,128)(2,1)}, u32[]{:S(2)}) copy-start(bf16[256,128]{1,0:T(8,128)(2,1)} %constant.27.clone.y_inv) | copy-start | bytes 196612
  66.7 13.4 %all-to-all-start.2 = ((bf16[8,8,16,384]{3,2,1,0:T(8,128)(2,1)}), bf16[8,8,16,384]{3,2,1,0:T(8,128)(2,1)S(1)}, u32[]{:S(2)}, u32[]{:S(2)}) async-start(bf16[8,8,16,384]{3,2,1,0:T(8,128)(2,1)} %spec.1), calls=%async_computation.2 | async-start | bytes 1572864 | tf_op jit(solution)/shard_map/all_to_all | solution.py:388
  70.3 10.4 %collective-permute-start.2 = (bf16[128,384]{1,0:T(8,128)(2,1)S(1)}, bf16[128,384]{1,0:T(8,128)(2,1)S(1)}, u32[]{:S(2)}, u32[]{:S(2)}) collective-permute-start(bf16[128,384]{1,0:T(8,128)(2,1)S(1)} %get-tuple-element.30), channel_id=1, source_target_pairs={{0,16},{1,17},{2,18},{3,19},{4,20},{5,21},{6,22},{7,23},{8,24},{9,... | collective-permute-start | bytes 294920 | tf_op jit(solution)/shard_map/ppermute | solution.py:353
  71.7 8.9 %collective-permute-start.3 = (bf16[128,384]{1,0:T(8,128)(2,1)S(1)}, bf16[128,384]{1,0:T(8,128)(2,1)S(1)}, u32[]{:S(2)}, u32[]{:S(2)}) collective-permute-start(bf16[128,384]{1,0:T(8,128)(2,1)S(1)} %get-tuple-element.29), channel_id=1, source_target_pairs={{0,1},{1,0},{2,3},{3,2},{4,5},{5,4},{6,7},{7,6},{8,9},{9,8},{10,11... | collective-permute-start | bytes 294920 | tf_op jit(solution)/shard_map/ppermute | solution.py:353
  80.6 29.0 %copy-start.2 = (bf16[256,256]{1,0:T(8,128)(2,1)S(1)}, bf16[256,256]{1,0:T(8,128)(2,1)}, u32[]{:S(2)}) copy-start(bf16[256,256]{1,0:T(8,128)(2,1)} %constant.25.clone.z_inv) | copy-start | bytes 393220
